TPU v7x, 32 devices: a whole 2x2x4 slice. The times are simulated.
32 devices in a mesh: dp: 8 (over y, x, core), seq: 4 (over z).
Axes of the slice: x: 2, y: 2, z: 4, core: 2. Of those that a mesh axis runs over, the one named last changes fastest.
Arguments:
- q_space: bfloat16 [8, 640, 1152], P('dp', 'seq'), may hold values from -64 to 64
- k_space: bfloat16 [8, 640, 1152], P('dp', 'seq'), may hold values from -6 to 6
- v_space: bfloat16 [8, 640, 1152], P('dp', 'seq'), may hold values from -6 to 6
- q_time: bfloat16 [8, 640, 1152], P('dp', 'seq'), may hold values from -64 to 64
- k_time: bfloat16 [8, 640, 1152], P('dp', 'seq'), may hold values from -6 to 6
- v_time: bfloat16 [8, 640, 1152], P('dp', 'seq'), may hold values from -6 to 6
- weight: bfloat16 [1152, 1152], P('dp'), may hold values from -0.1875 to 0.1875
- target: bfloat16 [8, 640, 1152], P('dp', 'seq'), may hold values from -6 to 6
Outputs:
- grad_q_space: bfloat16 [8, 640, 1152], P('dp', 'seq')
- grad_k_space: bfloat16 [8, 640, 1152], P('dp', 'seq')
- grad_v_space: bfloat16 [8, 640, 1152], P('dp', 'seq')
- grad_q_time: bfloat16 [8, 640, 1152], P('dp', 'seq')
- grad_k_time: bfloat16 [8, 640, 1152], P('dp', 'seq')
- grad_v_time: bfloat16 [8, 640, 1152], P('dp', 'seq')
- weight_grad: float32 [1152, 1152], P('seq')
All inputs are finite; a program needn't handle non-finite values.
Results may differ from a plain program's by a relative error of at most 0.025.
Values may be sent and summed in bfloat16 or wider, within the bound.
No kernel may reach another device: no remote copies, remote signals or barrier semaphores. Data moves between devices by JAX's collectives and lax.ppermute only.
A program may use at most 64 MiB of HBM per device.

v0:
```python
import math

import jax
import jax.numpy as jnp
from jax import lax
from jax.sharding import PartitionSpec as P

HEAD_DIM = 72


def form_pair(layout):
    if layout == "space":
        return ("blhe", "bmhe")
    return ("lbhe", "mbhe")


def split_heads(array):
    return array.reshape(array.shape[:-1] + (array.shape[-1] // HEAD_DIM, HEAD_DIM))


def attend_forward(query, key_data, values, layout):
    query_form, key_form = form_pair(layout)
    scaling = 1.0 / math.sqrt(HEAD_DIM)
    logits = (
        jnp.einsum(
            query_form + "," + key_form + "->bhlm",
            query,
            key_data,
            preferred_element_type=jnp.float32,
        )
        * scaling
    )
    row_max = jnp.max(logits, axis=-1, keepdims=True)
    lifted = jnp.exp(logits - row_max)
    attention = lifted / jnp.sum(lifted, axis=-1, keepdims=True)
    rounded = attention.astype(jnp.bfloat16)
    result = jnp.einsum(
        "bhlm," + key_form + "->" + query_form, rounded, values, preferred_element_type=jnp.float32
    )
    return (attention, rounded, result)


def attend_backward(query, key_data, values, attention, rounded, step_grad, layout):
    query_form, key_form = form_pair(layout)
    scaling = 1.0 / math.sqrt(HEAD_DIM)
    upstream = jnp.einsum(
        query_form + "," + key_form + "->bhlm",
        step_grad,
        values,
        preferred_element_type=jnp.float32,
    )
    grad_values = jnp.einsum(
        "bhlm," + query_form + "->" + key_form,
        rounded,
        step_grad,
        preferred_element_type=jnp.float32,
    ).astype(jnp.bfloat16)
    grad_scores = (
        attention * (upstream - jnp.sum(attention * upstream, axis=-1, keepdims=True))
    ).astype(jnp.bfloat16)
    grad_query = (
        jnp.einsum(
            "bhlm," + key_form + "->" + query_form,
            grad_scores,
            key_data,
            preferred_element_type=jnp.float32,
        )
        * scaling
    ).astype(jnp.bfloat16)
    grad_keys = (
        jnp.einsum(
            "bhlm," + query_form + "->" + key_form,
            grad_scores,
            query,
            preferred_element_type=jnp.float32,
        )
        * scaling
    ).astype(jnp.bfloat16)
    return (grad_query, grad_keys, grad_values)


def time_side(time_q, time_k, time_v, out_space, target_rows, full_weight):
    heads_q = split_heads(time_q)
    heads_k = split_heads(time_k)
    heads_v = split_heads(time_v)
    attention_t, rounded_t, result_t = attend_forward(heads_q, heads_k, heads_v, "time")
    combined = (out_space.astype(jnp.float32) + result_t.reshape(out_space.shape)).astype(
        jnp.bfloat16
    )
    projected = jnp.einsum("fnd,dc->fnc", combined, full_weight, preferred_element_type=jnp.float32)
    output_grad = (projected - target_rows.astype(jnp.float32)).astype(jnp.bfloat16)
    step_grad = jnp.einsum(
        "fnc,dc->fnd", output_grad, full_weight, preferred_element_type=jnp.float32
    ).astype(jnp.bfloat16)
    grads_time = attend_backward(
        heads_q, heads_k, heads_v, attention_t, rounded_t, split_heads(step_grad), "time"
    )
    grad_q, grad_k, grad_v = [item.reshape(out_space.shape) for item in grads_time]
    return (step_grad, grad_q, grad_k, grad_v, combined, output_grad)


def shards(q_space, k_space, v_space, q_time, k_time, v_time, weight, target):
    space_q = split_heads(q_space)
    space_k = split_heads(k_space)
    space_v = split_heads(v_space)
    attention_s, rounded_s, result_s = attend_forward(space_q, space_k, space_v, "space")
    out_space = result_s.astype(jnp.bfloat16).reshape(q_space.shape)
    full_weight = lax.all_gather(weight, "dp", axis=0, tiled=True)
    groups = lax.axis_size("seq")
    width = q_space.shape[2]
    per_block = q_space.shape[1] // groups

    def blocked(array):
        return array.reshape(1, groups, per_block, width)

    def per_patch(pieces):
        flat = [item[:, 0] for item in pieces]
        outcome = time_side(flat[0], flat[1], flat[2], flat[3], flat[4], full_weight)
        return tuple((item[:, None] for item in outcome))

    mapped = per_patch(
        (
            lax.all_to_all(blocked(q_time), "seq", split_axis=1, concat_axis=0, tiled=True),
            lax.all_to_all(blocked(k_time), "seq", split_axis=1, concat_axis=0, tiled=True),
            lax.all_to_all(blocked(v_time), "seq", split_axis=1, concat_axis=0, tiled=True),
            lax.all_to_all(blocked(out_space), "seq", split_axis=1, concat_axis=0, tiled=True),
            lax.all_to_all(blocked(target), "seq", split_axis=1, concat_axis=0, tiled=True),
        )
    )
    returned = tuple((item[:, 0] for item in mapped))
    step_grad, grad_qt, grad_kt, grad_vt, combined, output_grad = returned
    home = (
        lax.all_to_all(step_grad, "seq", split_axis=0, concat_axis=1, tiled=True),
        lax.all_to_all(grad_qt, "seq", split_axis=0, concat_axis=1, tiled=True),
        lax.all_to_all(grad_kt, "seq", split_axis=0, concat_axis=1, tiled=True),
        lax.all_to_all(grad_vt, "seq", split_axis=0, concat_axis=1, tiled=True),
    )
    grads_space = attend_backward(
        space_q, space_k, space_v, attention_s, rounded_s, split_heads(home[0]), "space"
    )
    grad_qs, grad_ks, grad_vs = [item.reshape(q_space.shape) for item in grads_space]
    flat_comb = combined.reshape(-1, combined.shape[-1])
    flat_grad = output_grad.reshape(-1, output_grad.shape[-1])
    share = lax.psum_scatter(
        lax.dot_general(
            flat_comb, flat_grad, (((0,), (0,)), ((), ())), preferred_element_type=jnp.float32
        ).astype(jnp.bfloat16),
        "seq",
        scatter_dimension=0,
        tiled=True,
    )
    total = lax.psum(share, "dp").astype(jnp.float32)
    scaling = 1.0 / math.sqrt(lax.axis_size("dp") * lax.axis_size("seq") * q_space.shape[1])
    return (grad_qs, grad_ks, grad_vs, home[1], home[2], home[3], total * scaling)


def solution(mesh):
    return jax.shard_map(
        shards,
        mesh=mesh,
        in_specs=(
            P("dp", "seq", None),
            P("dp", "seq", None),
            P("dp", "seq", None),
            P("dp", "seq", None),
            P("dp", "seq", None),
            P("dp", "seq", None),
            P("dp", None),
            P("dp", "seq", None),
        ),
        out_specs=(
            P("dp", "seq", None),
            P("dp", "seq", None),
            P("dp", "seq", None),
            P("dp", "seq", None),
            P("dp", "seq", None),
            P("dp", "seq", None),
            P("seq", None),
        ),
        check_vma=False,
    )
```

profile of v0, /device:TPU:0, one launch (start us, length us, event | category | flops | bytes accessed | tf_op | source)
XLA Modules:
  0.0 243.0 jit_solution(15579420141537322185)
XLA Ops:
  7.2 0.7 all-gather.2.cloned.1.call-update
  7.9 17.6 %all_to_all.90 = bf16[1,4,40,1152]{3,2,0,1:T(8,128)(2,1)} all-to-all(bf16[1,4,40,1152]{3,2,0,1:T(8,128)(2,1)} %bitcast.120), channel_id=1, replica_groups=mesh['dp'=8,'seq'=4] {'seq'}, dimensions={1} | all-to-all | bytes 737280 | tf_op jit(solution)/shard_map/all_to_all | solution.py:124
  25.5 3.5 %all-to-all-start.1 = ((bf16[1,4,40,1152]{3,2,0,1:T(8,128)(2,1)}), bf16[1,4,40,1152]{3,2,0,1:T(8,128)(2,1)S(1)}, u32[]{:S(2)}, u32[]{:S(2)}) async-start(bf16[1,4,40,1152]{3,2,0,1:T(8,128)(2,1)} %bitcast.121), calls=%async_computation.1 | async-start | bytes 737280 | tf_op jit(solution)/shard_map/all_to_all | solution.py:123
  29.0 1.1 copy.104
  30.1 0.2 copy.105
  30.4 8.7 %all-to-all-done.1 = bf16[1,4,40,1152]{3,2,0,1:T(8,128)(2,1)S(1)} async-done(((bf16[1,4,40,1152]{3,2,0,1:T(8,128)(2,1)}), bf16[1,4,40,1152]{3,2,0,1:T(8,128)(2,1)S(1)}, u32[]{:S(2)}, u32[]{:S(2)}) %all-to-all-start.1) | async-done | bytes 368672 | tf_op jit(solution)/shard_map/all_to_all | solution.py:123
  39.0 4.1 %all-to-all-start.3 = ((bf16[1,4,40,1152]{3,2,0,1:T(8,128)(2,1)}), bf16[1,4,40,1152]{3,2,0,1:T(8,128)(2,1)}, u32[]{:S(2)}, u32[]{:S(2)}) async-start(bf16[1,4,40,1152]{3,2,0,1:T(8,128)(2,1)} %bitcast.8), calls=%async_computation.3 | async-start | bytes 737280 | tf_op jit(solution)/shard_map/all_to_all | solution.py:125
  43.1 2.2 fusion.50
  45.3 2.3 copy.106
  47.6 2.2 fusion.29
  49.8 1.6 copy.69
  51.5 1.4 reshape_reshape.3
  52.9 5.0 %all-to-all-start = ((bf16[1,4,40,1152]{3,2,0,1:T(8,128)(2,1)}), bf16[1,4,40,1152]{3,2,0,1:T(8,128)(2,1)S(1)}, u32[]{:S(2)}, u32[]{:S(2)}) async-start(bf16[1,4,40,1152]{3,2,0,1:T(8,128)(2,1)} %bitcast.3), calls=%async_computation | async-start | bytes 737280 | tf_op jit(solution)/shard_map/all_to_all | solution.py:126
  58.0 1.1 reshape_squeeze.10
  59.1 1.1 reshape_squeeze.9
  60.3 5.4 %all-to-all-done = bf16[1,4,40,1152]{3,2,0,1:T(8,128)(2,1)S(1)} async-done(((bf16[1,4,40,1152]{3,2,0,1:T(8,128)(2,1)}), bf16[1,4,40,1152]{3,2,0,1:T(8,128)(2,1)S(1)}, u32[]{:S(2)}, u32[]{:S(2)}) %all-to-all-start) | async-done | bytes 368672 | tf_op jit(solution)/shard_map/all_to_all | solution.py:126
  65.6 3.7 %all-to-all-start.4 = ((bf16[1,4,40,1152]{3,2,0,1:T(8,128)(2,1)}), bf16[1,4,40,1152]{3,2,0,1:T(8,128)(2,1)S(1)}, u32[]{:S(2)}, u32[]{:S(2)}) async-start(bf16[1,4,40,1152]{3,2,0,1:T(8,128)(2,1)} %bitcast.11), calls=%async_computation.4 | async-start | bytes 737280 | tf_op jit(solution)/shard_map/all_to_all | solution.py:127
  69.3 3.4 %fusion.49 = (f32[40,16,4]{2,1,0:T(8,128)S(1)}, f32[40,16,4,4]{2,3,1,0:T(4,128)}) fusion(bf16[4,40,16,72]{3,2,1,0:T(8,128)(2,1)S(1)} %reshape_squeeze.10, bf16[4,40,16,72]{3,2,1,0:T(8,128)(2,1)S(1)} %reshape_squeeze.9), kind=kOutput, calls=%fused_computation.58 | convolution fusion | flops 1505283 | bytes 788480 | tf_op jit(solution)/shard_map/sub | solution.py:34
  72.7 2.2 reshape_squeeze.11
  75.0 0.8 copy-done.15
  75.8 2.4 convolution_bitcast_fusion.1
  78.2 0.1 copy.76
  78.3 0.6 reshape.161
  79.0 0.7 copy-done.21
  79.7 2.6 %fusion.10 = bf16[4,40,1152]{2,1,0:T(8,128)(2,1)S(1)} fusion(bf16[1152,1152]{1,0:T(8,128)(2,1)} %all-gather.2.cloned.1.call-done, bf16[1,4,40,1152]{3,2,0,1:T(8,128)(2,1)} %copy-done.21, f32[4,40,1152]{2,1,0:T(8,128)S(1)} %reshape.161, bf16[1,4,40,1152]{3,2,0,1:T(8,128)(2,1)} %copy-done.19), kind=kOutput, calls=%fused_computation.12 | convolution fusion | flops 425779200 | bytes 4497408 | tf_op jit(solution)/shard_map/fnd,dc->fnc/dot_general | solution.py:90
  82.3 2.5 %fusion.2 = bf16[1152,1152]{1,0:T(8,128)(2,1)} fusion(bf16[4,40,1152]{2,1,0:T(8,128)(2,1)S(1)} %fusion.10, f32[4,40,1152]{2,1,0:T(8,128)S(1)} %reshape.161, bf16[1,4,40,1152]{3,2,0,1:T(8,128)(2,1)S(1)} %copy-done.20), kind=kOutput, calls=%fused_computation.3 | convolution fusion | flops 426553344 | bytes 4128768 | tf_op jit(solution)/shard_map/dot_general | solution.py:145
  84.9 1.7 copy-done
  86.6 2.8 %fusion.13 = bf16[4,40,1152]{2,1,0:T(8,128)(2,1)} fusion(bf16[4,40,1152]{2,1,0:T(8,128)(2,1)} %copy-done.18, bf16[1152,1152]{1,0:T(8,128)(2,1)S(1)} %copy-done), kind=kOutput, calls=%fused_computation.13 | convolution fusion | flops 424857600 | bytes 3391488 | tf_op jit(solution)/shard_map/fnc,dc->fnd/dot_general | solution.py:92
  89.4 2.1 reshape.167
  91.6 3.8 %multiply_reduce_fusion.2 = (f32[40,16,4]{2,1,0:T(8,128)S(1)}, f32[40,16,4,4]{2,3,1,0:T(4,128)S(1)}) fusion(f32[40,16,4,4]{2,3,1,0:T(4,128)} %get-tuple-element.29, f32[40,16,4]{2,1,0:T(8,128)} %copy-done.24, bf16[4,40,16,72]{3,2,1,0:T(8,128)(2,1)} %copy-done.15, bf16[4,40,16,72]{3,2,1,0:T(8,128)(2,1)S(1)} %reshape.167), kind=kOutput, calls=%fused_computation.33 | convolution fusion | flops 1502720 | bytes 839680 | tf_op jit(solution)/shard_map/lbhe,mbhe->bhlm/dot_general | solution.py:46
  95.4 2.1 multiply_convert_fusion.1
  97.4 0.9 fusion.27
  98.3 0.1 copy.92
  98.4 1.7 squeeze_broadcast_in_dim_reshape.10
  100.1 5.1 %all-to-all-start.7 = ((bf16[4,40,1152]{2,1,0:T(8,128)(2,1)}), bf16[4,40,1152]{2,1,0:T(8,128)(2,1)S(1)}, u32[]{:S(2)}, u32[]{:S(2)}) async-start(bf16[4,40,1152]{2,1,0:T(8,128)(2,1)} %squeeze_broadcast_in_dim_reshape.10), calls=%async_computation.7 | async-start | bytes 737280 | tf_op jit(solution)/shard_map/all_to_all | solution.py:135
  105.1 2.1 fusion.28
  107.3 0.1 copy.90
  107.4 0.7 squeeze_broadcast_in_dim_reshape.9
  108.1 17.9 %all-to-all-done.7 = bf16[4,40,1152]{2,1,0:T(8,128)(2,1)S(1)} async-done(((bf16[4,40,1152]{2,1,0:T(8,128)(2,1)}), bf16[4,40,1152]{2,1,0:T(8,128)(2,1)S(1)}, u32[]{:S(2)}, u32[]{:S(2)}) %all-to-all-start.7) | async-done | bytes 368672 | tf_op jit(solution)/shard_map/all_to_all | solution.py:135
  126.0 21.9 %all_to_all.91 = bf16[4,40,1152]{2,1,0:T(8,128)(2,1)} all-to-all(bf16[4,40,1152]{2,1,0:T(8,128)(2,1)S(1)} %squeeze_broadcast_in_dim_reshape.9), channel_id=1, replica_groups=mesh['dp'=8,'seq'=4] {'seq'}, dimensions={0} | all-to-all | bytes 737280 | tf_op jit(solution)/shard_map/all_to_all | solution.py:134
  147.9 4.1 %all-to-all-start.5 = ((bf16[4,40,1152]{2,1,0:T(8,128)(2,1)}), bf16[4,40,1152]{2,1,0:T(8,128)(2,1)}, u32[]{:S(2)}, u32[]{:S(2)}) async-start(bf16[4,40,1152]{2,1,0:T(8,128)(2,1)} %fusion.13), calls=%async_computation.5 | async-start | bytes 737280 | tf_op jit(solution)/shard_map/all_to_all | solution.py:133
  152.0 2.2 fusion.26
  154.3 0.1 copy.94
  154.4 1.4 squeeze_broadcast_in_dim_reshape.11
  155.8 6.1 %all-to-all-done.5 = bf16[4,40,1152]{2,1,0:T(8,128)(2,1)} async-done(((bf16[4,40,1152]{2,1,0:T(8,128)(2,1)}), bf16[4,40,1152]{2,1,0:T(8,128)(2,1)}, u32[]{:S(2)}, u32[]{:S(2)}) %all-to-all-start.5) | async-done | bytes 368672 | tf_op jit(solution)/shard_map/all_to_all | solution.py:133
  161.9 4.4 %all-to-all-start.8 = ((bf16[4,40,1152]{2,1,0:T(8,128)(2,1)}), bf16[4,40,1152]{2,1,0:T(8,128)(2,1)}, u32[]{:S(2)}, u32[]{:S(2)}) async-start(bf16[4,40,1152]{2,1,0:T(8,128)(2,1)} %squeeze_broadcast_in_dim_reshape.11), calls=%async_computation.8 | async-start | bytes 737280 | tf_op jit(solution)/shard_map/all_to_all | solution.py:136
  166.3 2.1 reshape.163
  168.4 1.4 copy.78
  169.8 2.0 multiply_reduce_fusion
  171.8 0.1 copy-done.3
  171.9 0.5 multiply_convert_fusion
  172.4 0.5 copy-done.6
  173.0 0.6 fusion.24
  173.5 1.0 copy.96
  174.5 0.3 fusion.23
  174.8 1.0 copy.95
  175.8 0.1 copy-done.17
  175.9 2.3 convolution_convert_fusion.1
  178.2 1.0 copy.97
  179.2 51.8 %all-reduce.2.cloned.1.call-done = bf16[288,1152]{1,0:T(8,128)(2,1)} async-done(((bf16[288,1152]{1,0:T(8,128)(2,1)}), bf16[288,1152]{1,0:T(8,128)(2,1)}) %all-reduce.2.cloned.1.call-update) | async-done | bytes 663568 | tf_op jit(solution)/shard_map/psum | solution.py:152
  230.9 2.3 convert_multiply_fusion
  233.2 0.7 copy.135
  233.9 0.7 copy.136
  234.7 1.8 copy.137
  (56 shorter events, 0.2 us)
Async XLA Ops:
  7.2 21.8 %copy-start.22 = (bf16[1,160,1152]{2,1,0:T(8,128)(2,1)S(1)}, bf16[1,160,1152]{2,1,0:T(8,128)(2,1)}, u32[]{:S(2)}) copy-start(bf16[1,160,1152]{2,1,0:T(8,128)(2,1)} %param.8) | copy-start | bytes 1105924
  7.2 22.9 %copy-start.23 = (bf16[1,160,1152]{2,1,0:T(8,128)(2,1)S(1)}, bf16[1,160,1152]{2,1,0:T(8,128)(2,1)}, u32[]{:S(2)}) copy-start(bf16[1,160,1152]{2,1,0:T(8,128)(2,1)} %param.9) | copy-start | bytes 1105924
  7.2 72.5 %all-gather.2.cloned.1.call-start = ((), (), s32[]{:S(2)}) async-start(), calls=%async_computation.10 | async-start | bytes 2985984 | tf_op jit(solution)/shard_map/all_gather | solution.py:108
  25.5 13.5 %all-to-all-start.1 = ((bf16[1,4,40,1152]{3,2,0,1:T(8,128)(2,1)}), bf16[1,4,40,1152]{3,2,0,1:T(8,128)(2,1)S(1)}, u32[]{:S(2)}, u32[]{:S(2)}) async-start(bf16[1,4,40,1152]{3,2,0,1:T(8,128)(2,1)} %bitcast.121), calls=%async_computation.1 | async-start | bytes 737280 | tf_op jit(solution)/shard_map/all_to_all | solution.py:123
  30.3 15.0 %copy-start.4 = (bf16[1,160,1152]{1,2,0:T(8,128)(2,1)}, bf16[1,160,1152]{1,2,0:T(8,128)(2,1)S(1)}, u32[]{:S(2)}) copy-start(bf16[1,160,1152]{1,2,0:T(8,128)(2,1)S(1)} %copy.105) | copy-start | bytes 1105924
  39.0 4.1 %copy-start.10 = (bf16[1,4,40,1152]{3,2,0,1:T(8,128)(2,1)}, bf16[1,4,40,1152]{3,2,0,1:T(8,128)(2,1)S(1)}, u32[]{:S(2)}) copy-start(bf16[1,4,40,1152]{3,2,0,1:T(8,128)(2,1)S(1)} %all-to-all-done.1) | copy-start | bytes 1105924
  39.0 13.9 %all-to-all-start.3 = ((bf16[1,4,40,1152]{3,2,0,1:T(8,128)(2,1)}), bf16[1,4,40,1152]{3,2,0,1:T(8,128)(2,1)}, u32[]{:S(2)}, u32[]{:S(2)}) async-start(bf16[1,4,40,1152]{3,2,0,1:T(8,128)(2,1)} %bitcast.8), calls=%async_computation.3 | async-start | bytes 737280 | tf_op jit(solution)/shard_map/all_to_all | solution.py:125
  45.3 4.5 %copy-start.1 = (f32[16,160,160]{1,2,0:T(8,128)}, f32[16,160,160]{1,2,0:T(8,128)S(1)}, u32[]{:S(2)}) copy-start(f32[16,160,160]{1,2,0:T(8,128)S(1)} %get-tuple-element.31) | copy-start | bytes 4915204
  51.5 6.5 %copy-start.12 = (bf16[1,4,40,1152]{3,2,0,1:T(8,128)(2,1)S(1)}, bf16[1,4,40,1152]{3,2,0,1:T(8,128)(2,1)}, u32[]{:S(2)}) copy-start(bf16[1,4,40,1152]{3,2,0,1:T(8,128)(2,1)} %all_to_all.90) | copy-start | bytes 1105924
  51.5 7.6 %copy-start.11 = (bf16[1,4,40,1152]{3,2,0,1:T(8,128)(2,1)S(1)}, bf16[1,4,40,1152]{3,2,0,1:T(8,128)(2,1)}, u32[]{:S(2)}) copy-start(bf16[1,4,40,1152]{3,2,0,1:T(8,128)(2,1)} %copy-done.10) | copy-start | bytes 1105924
  52.9 12.7 %all-to-all-start = ((bf16[1,4,40,1152]{3,2,0,1:T(8,128)(2,1)}), bf16[1,4,40,1152]{3,2,0,1:T(8,128)(2,1)S(1)}, u32[]{:S(2)}, u32[]{:S(2)}) async-start(bf16[1,4,40,1152]{3,2,0,1:T(8,128)(2,1)} %bitcast.3), calls=%async_computation | async-start | bytes 737280 | tf_op jit(solution)/shard_map/all_to_all | solution.py:126
  60.3 12.5 %copy-start.13 = (bf16[4,40,16,72]{3,2,1,0:T(8,128)(2,1)}, bf16[4,40,16,72]{3,2,1,0:T(8,128)(2,1)S(1)}, u32[]{:S(2)}) copy-start(bf16[4,40,16,72]{3,2,1,0:T(8,128)(2,1)S(1)} %reshape_squeeze.9) | copy-start | bytes 1105924
  65.6 3.7 %copy-start.19 = (bf16[1,4,40,1152]{3,2,0,1:T(8,128)(2,1)}, bf16[1,4,40,1152]{3,2,0,1:T(8,128)(2,1)S(1)}, u32[]{:S(2)}) copy-start(bf16[1,4,40,1152]{3,2,0,1:T(8,128)(2,1)S(1)} %all-to-all-done) | copy-start | bytes 1105924
  65.6 13.3 %all-to-all-start.4 = ((bf16[1,4,40,1152]{3,2,0,1:T(8,128)(2,1)}), bf16[1,4,40,1152]{3,2,0,1:T(8,128)(2,1)S(1)}, u32[]{:S(2)}, u32[]{:S(2)}) async-start(bf16[1,4,40,1152]{3,2,0,1:T(8,128)(2,1)} %bitcast.11), calls=%async_computation.4 | async-start | bytes 737280 | tf_op jit(solution)/shard_map/all_to_all | solution.py:127
  69.3 106.4 %reduce-scatter.2.cloned.1.call-start = ((), (), s32[]{:S(2)}) async-start(), calls=%async_computation.11 | async-start | bytes 3317760 | tf_op jit(solution)/shard_map/reduce_scatter | solution.py:144
  72.7 2.2 copy-start.24
  75.0 0.9 copy-start.15
  78.9 3.4 %copy-start.20 = (bf16[1,4,40,1152]{3,2,0,1:T(8,128)(2,1)S(1)}, bf16[1,4,40,1152]{3,2,0,1:T(8,128)(2,1)}, u32[]{:S(2)}) copy-start(bf16[1,4,40,1152]{3,2,0,1:T(8,128)(2,1)} %copy-done.19) | copy-start | bytes 1105924
  78.9 0.7 copy-start.21
  82.3 2.5 %copy-start.18 = (bf16[4,40,1152]{2,1,0:T(8,128)(2,1)}, bf16[4,40,1152]{2,1,0:T(8,128)(2,1)S(1)}, u32[]{:S(2)}) copy-start(bf16[4,40,1152]{2,1,0:T(8,128)(2,1)S(1)} %fusion.10) | copy-start | bytes 1105924
  84.8 1.8 copy-start
  91.5 3.8 %copy-start.25 = (f32[40,16,4]{2,1,0:T(8,128)S(1)}, f32[40,16,4]{2,1,0:T(8,128)}, u32[]{:S(2)}) copy-start(f32[40,16,4]{2,1,0:T(8,128)} %copy-done.24) | copy-start | bytes 30724
  95.3 2.1 copy-start.14
  97.4 0.9 copy-start.16
  100.1 25.9 %all-to-all-start.7 = ((bf16[4,40,1152]{2,1,0:T(8,128)(2,1)}), bf16[4,40,1152]{2,1,0:T(8,128)(2,1)S(1)}, u32[]{:S(2)}, u32[]{:S(2)}) async-start(bf16[4,40,1152]{2,1,0:T(8,128)(2,1)} %squeeze_broadcast_in_dim_reshape.10), calls=%async_computation.7 | async-start | bytes 737280 | tf_op jit(solution)/shard_map/all_to_all | solution.py:135
  126.0 28.3 %copy-start.7 = (bf16[4,40,1152]{2,1,0:T(8,128)(2,1)}, bf16[4,40,1152]{2,1,0:T(8,128)(2,1)S(1)}, u32[]{:S(2)}) copy-start(bf16[4,40,1152]{2,1,0:T(8,128)(2,1)S(1)} %all-to-all-done.7) | copy-start | bytes 1105924
  147.9 14.0 %all-to-all-start.5 = ((bf16[4,40,1152]{2,1,0:T(8,128)(2,1)}), bf16[4,40,1152]{2,1,0:T(8,128)(2,1)}, u32[]{:S(2)}, u32[]{:S(2)}) async-start(bf16[4,40,1152]{2,1,0:T(8,128)(2,1)} %fusion.13), calls=%async_computation.5 | async-start | bytes 737280 | tf_op jit(solution)/shard_map/all_to_all | solution.py:133
  161.9 7.9 %copy-start.2 = (f32[16,160,160]{1,2,0:T(8,128)S(1)}, f32[16,160,160]{1,2,0:T(8,128)}, u32[]{:S(2)}) copy-start(f32[16,160,160]{1,2,0:T(8,128)} %copy-done.1) | copy-start | bytes 4915204
  161.9 13.9 %all-to-all-start.8 = ((bf16[4,40,1152]{2,1,0:T(8,128)(2,1)}), bf16[4,40,1152]{2,1,0:T(8,128)(2,1)}, u32[]{:S(2)}, u32[]{:S(2)}) async-start(bf16[4,40,1152]{2,1,0:T(8,128)(2,1)} %squeeze_broadcast_in_dim_reshape.11), calls=%async_computation.8 | async-start | bytes 737280 | tf_op jit(solution)/shard_map/all_to_all | solution.py:136
  166.2 64.7 %all-reduce.2.cloned.1.call-start = ((), (), s32[]{:S(2)}) async-start(), calls=%async_computation.12 | async-start | bytes 1327104 | tf_op jit(solution)/shard_map/psum | solution.py:152
  169.8 2.1 copy-start.3
  171.9 1.1 copy-start.6
  173.0 1.5 copy-start.5
  174.8 1.1 copy-start.17
  178.2 55.0 %copy-start.9 = (bf16[4,40,1152]{2,1,0:T(8,128)(2,1)S(1)}, bf16[4,40,1152]{2,1,0:T(8,128)(2,1)}, u32[]{:S(2)}) copy-start(bf16[4,40,1152]{2,1,0:T(8,128)(2,1)} %all_to_all.91) | copy-start | bytes 1105924
  179.2 54.8 %copy-start.8 = (bf16[4,40,1152]{2,1,0:T(8,128)(2,1)S(1)}, bf16[4,40,1152]{2,1,0:T(8,128)(2,1)}, u32[]{:S(2)}) copy-start(bf16[4,40,1152]{2,1,0:T(8,128)(2,1)} %copy-done.7) | copy-start | bytes 1105924
Sparse Core Ops, SparseCore 0:
  9.9 32.9 all-gather.1
  85.0 66.0 reduce-scatter.1
  175.9 54.9 all-reduce.1
where the time goes:
time: 244 us; the launch traced here: 243 us
  waiting for transfers between devices  90.5 us (37%)
  blocking collectives  39.5 us (16%)
  matrix products  32.3 us (13%)
  local copies, waits for them, and re-layouts  31.8 us (13%)
  starting transfers between devices  30 us (12%)
  between operations  14.2 us (6%)
  other arithmetic  4.82 us (2%)
    psum x1, waiting for transfers between devices, shards(): total = lax.psum(share, 'dp').astype(jnp.float32)  51.8 us
    all_to_all x1, blocking collectives, shards(): lax.all_to_all(grad_qt, 'seq', split_axis=0, concat_axis=1, tiled=True)  21.9 us
    all_to_all x1, waiting for transfers between devices, shards(): lax.all_to_all(grad_kt, 'seq', split_axis=0, concat_axis=1, tiled=True)  17.9 us
    all_to_all x1, blocking collectives, shards(): lax.all_to_all(blocked(k_time), 'seq', split_axis=1, concat_axis=0, tiled...  17.6 us
    unnamed x58, local copies, waits for them, and re-layouts  10.2 us
    all_to_all x1, waiting for transfers between devices, shards(): lax.all_to_all(blocked(q_time), 'seq', split_axis=1, concat_axis=0, tiled...  8.66 us
    all_to_all x1, waiting for transfers between devices, shards(): lax.all_to_all(step_grad, 'seq', split_axis=0, concat_axis=1, tiled=True)  6.06 us
    another operation x4, local copies, waits for them, and re-layouts  6.03 us
  transfers between devices with their start and end apart: 10, of which 5 were waited for; matrix products, arithmetic and copies ran while one was open for 22% of the time, Pallas kernels for 0%

commit v1 on v0

v1 whole, which is shorter than its diff:
```python
import functools
import math

import jax
import jax.numpy as jnp
from jax import lax
from jax.experimental import pallas as pl
from jax.experimental.pallas import tpu as pltpu
from jax.sharding import PartitionSpec as P

HEAD_DIM = 72
LANES = 128
VMEM_BYTES = 24 * 1024 * 1024
F32 = jnp.float32
BF16 = jnp.bfloat16
NT = (((1,), (1,)), ((), ()))
NN = (((1,), (0,)), ((), ()))
TN = (((0,), (0,)), ((), ()))


def dot(left, right, form):
    return lax.dot_general(left, right, form, preferred_element_type=F32)


def windows(width):
    found = []
    for head in range(width // HEAD_DIM):
        first = head * HEAD_DIM
        start = first // LANES * LANES
        size = -(-(first + HEAD_DIM - start) // LANES) * LANES
        found.append((start, size, first - start))
    return found


def head_only(block, offset):
    lane = lax.broadcasted_iota(jnp.int32, (1, block.shape[1]), 1)
    inside = (lane >= offset) & (lane < offset + HEAD_DIM)
    return jnp.where(inside, block, jnp.zeros_like(block))


def same_patch(rows, per_block):
    left = lax.broadcasted_iota(jnp.int32, (rows, 1), 0) % per_block
    right = lax.broadcasted_iota(jnp.int32, (1, rows), 1) % per_block
    return left == right


def forward_kernel(per_block, q_ref, k_ref, v_ref, out_ref, probs_ref, total):
    rows, width = q_ref.shape
    scaling = 1.0 / math.sqrt(HEAD_DIM)
    keep = None if per_block is None else same_patch(rows, per_block)
    total[...] = jnp.zeros_like(total)
    for head, (start, size, offset) in enumerate(windows(width)):
        lanes = slice(start, start + size)
        logits = dot(head_only(q_ref[:, lanes], offset), k_ref[:, lanes], NT) * scaling
        if keep is not None:
            logits = jnp.where(keep, logits, -1e30)
        lifted = jnp.exp(logits - jnp.max(logits, axis=-1, keepdims=True))
        probs = lifted * (1.0 / jnp.sum(lifted, axis=-1, keepdims=True))
        probs_ref[head] = probs
        total[:, lanes] += dot(probs.astype(BF16), head_only(v_ref[:, lanes], offset), NN)
    out_ref[...] = total[...].astype(out_ref.dtype)


def backward_kernel(
    q_ref, k_ref, v_ref, g_ref, probs_ref, dq_ref, dk_ref, dv_ref, dq_sum, dk_sum, dv_sum
):
    scaling = 1.0 / math.sqrt(HEAD_DIM)
    dq_sum[...] = jnp.zeros_like(dq_sum)
    dk_sum[...] = jnp.zeros_like(dk_sum)
    dv_sum[...] = jnp.zeros_like(dv_sum)
    for head, (start, size, offset) in enumerate(windows(q_ref.shape[1])):
        lanes = slice(start, start + size)
        probs = probs_ref[head]
        step = head_only(g_ref[:, lanes], offset)
        upstream = dot(step, v_ref[:, lanes], NT)
        dv_sum[:, lanes] += dot(probs.astype(BF16), step, TN)
        mean = jnp.sum(probs * upstream, axis=-1, keepdims=True)
        dscore = (probs * (upstream - mean)).astype(BF16)
        dq_sum[:, lanes] += dot(dscore, head_only(k_ref[:, lanes], offset), NN)
        dk_sum[:, lanes] += dot(dscore, head_only(q_ref[:, lanes], offset), TN)
    dq_ref[...] = (dq_sum[...] * scaling).astype(BF16)
    dk_ref[...] = (dk_sum[...] * scaling).astype(BF16)
    dv_ref[...] = dv_sum[...].astype(BF16)


def project_kernel(space_ref, time_ref, weight_ref, target_ref, comb_ref, og_ref, step_ref):
    comb = (space_ref[...].astype(F32) + time_ref[...].astype(F32)).astype(BF16)
    comb_ref[...] = comb
    projected = dot(comb, weight_ref[...], NN)
    og = (projected - target_ref[...].astype(F32)).astype(BF16)
    og_ref[...] = og
    step_ref[...] = dot(og, weight_ref[...], NT).astype(BF16)


def call(body, outs, scratch, flops, moved, *args):
    return pl.pallas_call(
        body,
        out_shape=outs,
        scratch_shapes=scratch,
        cost_estimate=pl.CostEstimate(flops=flops, bytes_accessed=moved, transcendentals=0),
        compiler_params=pltpu.CompilerParams(vmem_limit_bytes=VMEM_BYTES),
    )(*args)


def attend_forward(q, k, v, per_block):
    rows, width = q.shape
    heads = width // HEAD_DIM
    return call(
        functools.partial(forward_kernel, per_block),
        (
            jax.ShapeDtypeStruct((rows, width), BF16),
            jax.ShapeDtypeStruct((heads, rows, rows), F32),
        ),
        [pltpu.VMEM((rows, width), F32)],
        4 * 10**9,
        8 * 10**6,
        q,
        k,
        v,
    )


def attend_backward(q, k, v, step, probs):
    rows, width = q.shape
    return call(
        backward_kernel,
        (jax.ShapeDtypeStruct((rows, width), BF16),) * 3,
        [pltpu.VMEM((rows, width), F32)] * 3,
        6 * 10**9,
        8 * 10**6,
        q,
        k,
        v,
        step,
        probs,
    )


def project(space, time, weight, target):
    return call(
        project_kernel,
        (jax.ShapeDtypeStruct(space.shape, BF16),) * 3,
        [],
        3 * 10**9,
        5 * 10**6,
        space,
        time,
        weight,
        target,
    )


def swap(array, axis, bits):
    size = lax.axis_size(axis)
    return lax.ppermute(array, axis, [(i, i ^ bits) for i in range(size)])


def pick(array, index):
    return lax.dynamic_index_in_dim(array, index, 0, keepdims=False)


def in_order(pieces, me):
    stacked = jnp.stack(pieces)
    return jnp.concatenate([pick(stacked, me ^ i) for i in range(len(pieces))], axis=0)


def gather_weight(weight):
    size = lax.axis_size("dp")
    me = lax.axis_index("dp")
    chips = jnp.stack([weight] + [swap(weight, "dp", 2 * i) for i in range(1, size // 2)])
    other = swap(chips, "dp", 1)
    pieces = jnp.stack([chips, other], axis=1).reshape((size,) + weight.shape)
    return jnp.concatenate([pick(pieces, me ^ i) for i in range(size)], axis=0)


def grad_kernel(chip_size, core_ref, chip_ref, comb_ref, og_ref, out_ref, total):
    size = out_ref.shape[-1]
    first = pl.multiple_of(core_ref[0] * (og_ref.shape[-1] - size), LANES)
    term = dot(comb_ref[0], og_ref[0, :, pl.ds(first, size)], TN)
    term += dot(comb_ref[1], og_ref[1, :, pl.ds(first, size)], TN)
    total[...] = term.reshape(total.shape)
    for i in range(chip_size):
        out_ref[i] = total[:, chip_ref[0] ^ i].astype(BF16)


def weight_gradient(comb, og, scaling):
    width = comb.shape[-1]
    chip_size = lax.axis_size("dp") // 2
    groups = lax.axis_size("seq")
    me, seq = lax.axis_index("dp"), lax.axis_index("seq")
    core, chip = me % 2, me // 2
    rows = width // groups // chip_size
    if rows * groups * chip_size != width or rows % 8 != 0:
        term = dot(comb, og, TN).astype(BF16)
        share = lax.psum_scatter(term, "seq", scatter_dimension=0, tiled=True)
        return lax.psum(share, "dp").astype(F32) * scaling
    size = -(-width // (2 * LANES)) * LANES
    pair = jnp.stack([comb, og])
    other = swap(pair, "dp", 1)
    pieces = pl.pallas_call(
        functools.partial(grad_kernel, chip_size),
        out_shape=jax.ShapeDtypeStruct((chip_size, groups, rows, size), BF16),
        in_specs=[pl.BlockSpec(memory_space=pltpu.SMEM)] * 2
        + [pl.BlockSpec(memory_space=pltpu.VMEM)] * 2,
        scratch_shapes=[pltpu.VMEM((groups, chip_size, rows, size), F32)],
        cost_estimate=pl.CostEstimate(flops=3 * 10**9, bytes_accessed=4 * 10**6, transcendentals=0),
        compiler_params=pltpu.CompilerParams(vmem_limit_bytes=VMEM_BYTES),
    )(core.reshape(1), chip.reshape(1), jnp.stack([comb, other[0]]), jnp.stack([og, other[1]]))
    share = pieces[0].astype(F32)
    for i in range(1, chip_size):
        share += swap(pieces[i], "dp", 2 * i).astype(F32)
    share = share.astype(BF16)
    total = pick(share, seq).astype(F32)
    for i in range(1, groups):
        total += swap(pick(share, seq ^ i), "seq", i).astype(F32)
    total = total.astype(BF16)
    mine = in_order([total] + [swap(total, "dp", 2 * i) for i in range(1, chip_size)], chip)
    other = swap(mine, "dp", 1)
    low = jnp.where(core == 0, mine, other)
    high = jnp.where(core == 0, other, mine)
    whole = jnp.concatenate([low, high[:, 2 * size - width :]], axis=1)
    return whole.astype(F32) * scaling


def shards(q_space, k_space, v_space, q_time, k_time, v_time, weight, target):
    groups = lax.axis_size("seq")
    me = lax.axis_index("seq")
    rows, width = q_space.shape[1:]
    per_block = rows // groups
    home = (rows, width)

    def block(array, index):
        return lax.dynamic_slice_in_dim(array, index * per_block, per_block, axis=-2)

    times = [item.reshape(home) for item in (q_time, k_time, v_time)]
    sent = [jnp.stack([block(item, me ^ i) for item in times]) for i in range(groups)]
    there = [sent[0]] + [swap(sent[i], "seq", i) for i in range(1, groups)]
    time_q, time_k, time_v = jnp.concatenate(there, axis=1)
    full_weight = gather_weight(weight)
    space_q, space_k, space_v = [item.reshape(home) for item in (q_space, k_space, v_space)]
    out_space, probs_s = attend_forward(space_q, space_k, space_v, None)
    out_time, probs_t = attend_forward(time_q, time_k, time_v, per_block)

    def come_home(array):
        parts = array.reshape(array.shape[:-2] + (groups, per_block, width))
        parts = [parts[..., i, :, :] for i in range(groups)]
        return [parts[0]] + [swap(parts[i], "seq", i) for i in range(1, groups)]

    time_home = in_order(come_home(out_time), me)
    comb, og, step = project(out_space, time_home, full_weight, target.reshape(home))
    step_there = jnp.concatenate(
        [block(step, me)] + [swap(block(step, me ^ i), "seq", i) for i in range(1, groups)]
    )
    time_grads = attend_backward(time_q, time_k, time_v, step_there, probs_t)
    back = [in_order(come_home(item), me) for item in time_grads]
    space_grads = attend_backward(space_q, space_k, space_v, step, probs_s)
    scaling = 1.0 / math.sqrt(lax.axis_size("dp") * groups * rows)
    weight_grad = weight_gradient(comb, og, scaling)
    outs = [item.reshape(q_space.shape) for item in list(space_grads) + back]
    return tuple(outs) + (weight_grad,)


def solution(mesh):
    tokens = P("dp", "seq", None)
    return jax.shard_map(
        shards,
        mesh=mesh,
        in_specs=(tokens,) * 6 + (P("dp", None), tokens),
        out_specs=(tokens,) * 6 + (P("seq", None),),
        check_vma=False,
    )
```

time: 244 us -> 131 us (0.54)
  waiting for transfers between devices: 90.5 us -> 47 us
  blocking collectives: 39.5 us -> 0 us
  matrix products: 32.3 us -> 0 us
  local copies, waits for them, and re-layouts: 31.8 us -> 6.02 us
  starting transfers between devices: 30 us -> 52 us
  Pallas kernels: 0 us -> 16.3 us
  between operations: 14.2 us -> 1.13 us
  other arithmetic: 4.82 us -> 8.02 us
    ppermute x0 -> x33, starting transfers between devices: none -> 52 us  [swap(): return lax.ppermute(array, axis, [(i, i ^ bits) for i in range(size)])]
    psum x1 -> x0, waiting for transfers between devices: 51.8 us -> none  [shards(): total = lax.psum(share, 'dp').astype(jnp.float32)]
    ppermute x0 -> x33, waiting for transfers between devices: none -> 47 us  [swap(): return lax.ppermute(array, axis, [(i, i ^ bits) for i in range(size)])]
    all_to_all x2 -> x0, blocking collectives: 39.5 us -> none  [the longest x1 21.9 us: shards(): lax.all_to_all(grad_qt, 'seq', split_axis=0, concat_axis=1, tiled=True)]
    all_to_all x7 -> x0, waiting for transfers between devices: 38 us -> none  [the longest x1 17.9 us: shards(): lax.all_to_all(grad_kt, 'seq', split_axis=0, concat_axis=1, tiled=True)]
    all_to_all x7 -> x0, starting transfers between devices: 29.9 us -> none  [the longest x1 5.06 us: shards(): lax.all_to_all(grad_kt, 'seq', split_axis=0, concat_axis=1, tiled=True)]
    dot_general x13 -> x0, matrix products: 26.8 us -> none  [the longest x2 5.77 us: attend_backward(): jnp.einsum(query_form + ',' + key_form + '->bhlm', step_grad, values, pre...]
    pallas_call x0 -> x6, Pallas kernels: none -> 16.3 us  [the longest x5 15.1 us: call(): pl.pallas_call(body, out_shape=outs, scratch_shapes=scratch, cost_estimat...]
  transfers between devices with their start and end apart: 10 -> 33, of which waited for: 5 -> 14; matrix products, arithmetic and copies ran while one was open for 22% -> 3% of each run, Pallas kernels for 0% -> 11%
where the time goes in v1:
time: 131 us; the launch traced here: 130 us
  starting transfers between devices  52 us (40%)
  waiting for transfers between devices  47 us (36%)
  Pallas kernels  16.3 us (12%)
  other arithmetic  8.02 us (6%)
  local copies, waits for them, and re-layouts  6.02 us (5%)
    ppermute x33, starting transfers between devices, swap(): return lax.ppermute(array, axis, [(i, i ^ bits) for i in range(size)])  52 us
    ppermute x33, waiting for transfers between devices, swap(): return lax.ppermute(array, axis, [(i, i ^ bits) for i in range(size)])  47 us
    pallas_call x5, Pallas kernels, call(): pl.pallas_call(body, out_shape=outs, scratch_shapes=scratch, cost_estimat...  15.1 us
    another operation x2, other arithmetic, gather_weight(): pieces = jnp.stack([chips, other], axis=1).reshape((size,) + weight.shape)  3.33 us
    unnamed x27, local copies, waits for them, and re-layouts  2.95 us
  transfers between devices with their start and end apart: 33, of which 14 were waited for; matrix products, arithmetic and copies ran while one was open for 3% of the time, Pallas kernels for 11%

profile of v1, /device:TPU:0, one launch (start us, length us, event | category | flops | bytes accessed | tf_op | source)
XLA Modules:
  0.0 130.5 jit_solution(14800076577748082275)
XLA Ops:
  0.7 1.1 constant_dynamic-slice_fusion.15
  1.8 1.3 constant_dynamic-slice_fusion.13
  3.1 3.1 %collective-permute-start = (bf16[3,40,1152]{2,1,0:T(8,128)(2,1)S(1)}, bf16[3,40,1152]{2,1,0:T(8,128)(2,1)S(1)}, u32[]{:S(2)}, u32[]{:S(2)}) collective-permute-start(bf16[3,40,1152]{2,1,0:T(8,128)(2,1)S(1)} %pad_maximum_fusion.14), channel_id=1, source_target_pairs={{0,1},{1,0},{2,3},{3,2},{4,5},{5,4},{6,7},{7,6},{8,9},{9,8},{10,11... | collective-permute-start | bytes 829448 | tf_op jit(solution)/shard_map/ppermute | solution.py:155
  6.2 2.7 %collective-permute-start.1 = (bf16[3,40,1152]{2,1,0:T(8,128)(2,1)S(1)}, bf16[3,40,1152]{2,1,0:T(8,128)(2,1)S(1)}, u32[]{:S(2)}, u32[]{:S(2)}) collective-permute-start(bf16[3,40,1152]{2,1,0:T(8,128)(2,1)S(1)} %pad_maximum_fusion.15), channel_id=1, source_target_pairs={{0,2},{1,3},{2,0},{3,1},{4,6},{5,7},{6,4},{7,5},{8,10},{9,11},{10,... | collective-permute-start | bytes 829448 | tf_op jit(solution)/shard_map/ppermute | solution.py:155
  9.0 1.7 %collective-permute-start.6 = (bf16[144,1152]{1,0:T(8,128)(2,1)S(1)}, bf16[144,1152]{1,0:T(8,128)(2,1)S(1)}, u32[]{:S(2)}, u32[]{:S(2)}) collective-permute-start(bf16[144,1152]{1,0:T(8,128)(2,1)S(1)} %copy-done.9), channel_id=1, source_target_pairs={{0,8},{4,12},{8,0},{12,4},{16,24},{20,28},{24,16},{28,20},{1,9},{5... | collective-permute-start | bytes 995336 | tf_op jit(solution)/shard_map/ppermute | solution.py:155
  10.7 1.5 %collective-permute-start.7 = (bf16[144,1152]{1,0:T(8,128)(2,1)S(1)}, bf16[144,1152]{1,0:T(8,128)(2,1)S(1)}, u32[]{:S(2)}, u32[]{:S(2)}) collective-permute-start(bf16[144,1152]{1,0:T(8,128)(2,1)S(1)} %copy-done.9), channel_id=1, source_target_pairs={{0,16},{4,20},{8,24},{12,28},{16,0},{20,4},{24,8},{28,12},{1,17},{... | collective-permute-start | bytes 995336 | tf_op jit(solution)/shard_map/ppermute | solution.py:155
  12.2 5.7 %collective-permute-done = bf16[3,40,1152]{2,1,0:T(8,128)(2,1)S(1)} collective-permute-done((bf16[3,40,1152]{2,1,0:T(8,128)(2,1)S(1)}, bf16[3,40,1152]{2,1,0:T(8,128)(2,1)S(1)}, u32[]{:S(2)}, u32[]{:S(2)}) %collective-permute-start) | collective-permute-done | bytes 276512 | tf_op jit(solution)/shard_map/ppermute | solution.py:155
  17.9 2.6 %collective-permute-start.8 = (bf16[144,1152]{1,0:T(8,128)(2,1)S(1)}, bf16[144,1152]{1,0:T(8,128)(2,1)S(1)}, u32[]{:S(2)}, u32[]{:S(2)}) collective-permute-start(bf16[144,1152]{1,0:T(8,128)(2,1)S(1)} %copy-done.9), channel_id=1, source_target_pairs={{0,24},{4,28},{8,16},{12,20},{16,8},{20,12},{24,0},{28,4},{1,25},{... | collective-permute-start | bytes 995336 | tf_op jit(solution)/shard_map/ppermute | solution.py:155
  20.5 8.1 %collective-permute-done.1 = bf16[3,40,1152]{2,1,0:T(8,128)(2,1)S(1)} collective-permute-done((bf16[3,40,1152]{2,1,0:T(8,128)(2,1)S(1)}, bf16[3,40,1152]{2,1,0:T(8,128)(2,1)S(1)}, u32[]{:S(2)}, u32[]{:S(2)}) %collective-permute-start.1) | collective-permute-done | bytes 276512 | tf_op jit(solution)/shard_map/ppermute | solution.py:155
  28.6 0.1 pad_maximum_fusion.2
  28.8 1.9 %shard_map.136 = (bf16[160,1152]{1,0:T(8,128)(2,1)S(1)}, f32[16,160,160]{2,1,0:T(8,128)S(1)}) custom-call(bf16[160,1152]{1,0:T(8,128)(2,1)S(1)} %get-tuple-element.40.q_ref, bf16[160,1152]{1,0:T(8,128)(2,1)S(1)} %get-tuple-element.39.k_ref, bf16[160,1152]{1,0:T(8,128)(2,1)S(1)} %get-tuple-element.38.v_ref), custom_call_target="tpu_custom_call" | custom-call | flops 4000000000 | bytes 8000000 | tf_op jit(solution)/shard_map/pallas_call | solution.py:96
  30.7 1.7 %fusion.6 = (bf16[4,1,144,1152]{3,2,1,0:T(8,128)(2,1)}, bf16[4,144,1152]{2,1,0:T(8,128)(2,1)}) fusion(bf16[1,144,1152]{2,1,0:T(8,128)(2,1)S(1)} %bitcast.156, bf16[1,144,1152]{2,1,0:T(8,128)(2,1)S(1)} %bitcast.155, bf16[1,144,1152]{2,1,0:T(8,128)(2,1)S(1)} %bitcast.154, bf16[1,144,1152]{2,1,0:T(8,128)(2,1)S(1)} %bitcast.153), kind=kLoop, calls=%fused_computation.89 | loop fusion | flops 1990656 | bytes 3981312 | tf_op jit(solution)/shard_map/stack | solution.py:172
  32.5 0.5 copy-done.4
  33.0 5.1 %collective-permute-start.3 = (bf16[40,1152]{1,0:T(8,128)(2,1)S(1)}, bf16[40,1152]{1,0:T(8,128)(2,1)S(1)}, u32[]{:S(2)}, u32[]{:S(2)}) collective-permute-start(bf16[40,1152]{1,0:T(8,128)(2,1)S(1)} %get-tuple-element.85), channel_id=1, source_target_pairs={{0,1},{1,0},{2,3},{3,2},{4,5},{5,4},{6,7},{7,6},{8,9},{9,8},{10,11... | collective-permute-start | bytes 276488 | tf_op jit(solution)/shard_map/ppermute | solution.py:155
  38.0 1.0 collective-permute-start.4
  39.1 1.5 %collective-permute-start.5 = (bf16[40,1152]{1,0:T(8,128)(2,1)S(1)}, bf16[40,1152]{1,0:T(8,128)(2,1)S(1)}, u32[]{:S(2)}, u32[]{:S(2)}) collective-permute-start(bf16[40,1152]{1,0:T(8,128)(2,1)S(1)} %get-tuple-element.83), channel_id=1, source_target_pairs={{0,3},{1,2},{2,1},{3,0},{4,7},{5,6},{6,5},{7,4},{8,11},{9,10},{10,... | collective-permute-start | bytes 276488 | tf_op jit(solution)/shard_map/ppermute | solution.py:155
  40.5 1.9 %shard_map.135 = (bf16[160,1152]{1,0:T(8,128)(2,1)S(1)}, f32[16,160,160]{2,1,0:T(8,128)S(1)}) custom-call(bf16[160,1152]{1,0:T(8,128)(2,1)S(1)} %bitcast.138, bf16[160,1152]{1,0:T(8,128)(2,1)S(1)} %bitcast.140, bf16[160,1152]{1,0:T(8,128)(2,1)S(1)} %bitcast.142), custom_call_target="tpu_custom_call" | custom-call | flops 4000000000 | bytes 8000000 | tf_op jit(solution)/shard_map/pallas_call | solution.py:96
  42.4 1.5 %copy-done.6 = f32[16,160,160]{2,1,0:T(8,128)} copy-done((f32[16,160,160]{2,1,0:T(8,128)}, f32[16,160,160]{2,1,0:T(8,128)S(1)}, u32[]{:S(2)}) %copy-start.6) | copy-done | bytes 1638424
  43.9 4.3 %collective-permute-done.4 = bf16[40,1152]{1,0:T(8,128)(2,1)S(1)} collective-permute-done((bf16[40,1152]{1,0:T(8,128)(2,1)S(1)}, bf16[40,1152]{1,0:T(8,128)(2,1)S(1)}, u32[]{:S(2)}, u32[]{:S(2)}) %collective-permute-start.4) | collective-permute-done | bytes 92192 | tf_op jit(solution)/shard_map/ppermute | solution.py:155
  48.4 1.6 %pad_maximum_fusion = bf16[4,2,144,1152]{3,2,1,0:T(8,128)(2,1)S(1)} fusion(bf16[4,1,144,1152]{3,2,1,0:T(8,128)(2,1)} %bitcast.20, bf16[4,1,144,1152]{3,2,1,0:T(8,128)(2,1)S(1)} %copy-done.8), kind=kLoop, calls=%fused_computation | loop fusion | flops 1327104 | bytes 5308416 | tf_op jit(solution)/shard_map/stack | solution.py:172
  50.4 0.6 copy-done
  51.1 1.5 %shard_map.137 = (bf16[160,1152]{1,0:T(8,128)(2,1)S(1)}, bf16[160,1152]{1,0:T(8,128)(2,1)S(1)}, bf16[160,1152]{1,0:T(8,128)(2,1)S(1)}) custom-call(bf16[160,1152]{1,0:T(8,128)(2,1)S(1)} %get-tuple-element.20.space_ref, bf16[160,1152]{1,0:T(8,128)(2,1)S(1)} %pad_maximum_fusion.7.time_ref, bf16[1152,1152]{1,0:T(8,128)(2,1)S(1)} %bitcast_dynamic-update-slice_fusion.weight_ref, ...), custom_call_target="tpu_custom_call" | custom-call | flops 3000000000 | bytes 5000000 | tf_op jit(solution)/shard_map/pallas_call | solution.py:96
  52.8 1.7 %collective-permute-start.10 = (bf16[40,1152]{1,0:T(8,128)(2,1)S(1)}, bf16[40,1152]{1,0:T(8,128)(2,1)S(1)}, u32[]{:S(2)}, u32[]{:S(2)}) collective-permute-start(bf16[40,1152]{1,0:T(8,128)(2,1)S(1)} %get-tuple-element.77), channel_id=1, source_target_pairs={{0,1},{1,0},{2,3},{3,2},{4,5},{5,4},{6,7},{7,6},{8,9},{9,8},{10,11... | collective-permute-start | bytes 276488 | tf_op jit(solution)/shard_map/ppermute | solution.py:155
  54.5 0.9 collective-permute-start.11
  55.4 1.8 %collective-permute-start.12 = (bf16[40,1152]{1,0:T(8,128)(2,1)S(1)}, bf16[40,1152]{1,0:T(8,128)(2,1)S(1)}, u32[]{:S(2)}, u32[]{:S(2)}) collective-permute-start(bf16[40,1152]{1,0:T(8,128)(2,1)S(1)} %get-tuple-element.75), channel_id=1, source_target_pairs={{0,3},{1,2},{2,1},{3,0},{4,7},{5,6},{6,5},{7,4},{8,11},{9,10},{10,... | collective-permute-start | bytes 276488 | tf_op jit(solution)/shard_map/ppermute | solution.py:155
  57.3 5.2 %shard_map.138 = (bf16[160,1152]{1,0:T(8,128)(2,1)}, bf16[160,1152]{1,0:T(8,128)(2,1)}, bf16[160,1152]{1,0:T(8,128)(2,1)}) custom-call(bf16[160,1152]{1,0:T(8,128)(2,1)S(1)} %bitcast.139, bf16[160,1152]{1,0:T(8,128)(2,1)S(1)} %bitcast.141, bf16[160,1152]{1,0:T(8,128)(2,1)S(1)} %bitcast.143, bf16[160,1152]{1,0:T(8,128)(2,1)S(1)} %get-tuple-element.22.g_ref, ...), custom_call_target="tpu_custom_call" | custom-call | flops 6000000000 | bytes 8000000 | tf_op jit(solution)/shard_map/pallas_call | solution.py:96
  62.5 2.3 %collective-permute-done.11 = bf16[40,1152]{1,0:T(8,128)(2,1)S(1)} collective-permute-done((bf16[40,1152]{1,0:T(8,128)(2,1)S(1)}, bf16[40,1152]{1,0:T(8,128)(2,1)S(1)}, u32[]{:S(2)}, u32[]{:S(2)}) %collective-permute-start.11) | collective-permute-done | bytes 92192 | tf_op jit(solution)/shard_map/ppermute | solution.py:155
  64.9 4.5 %shard_map.139 = (bf16[160,1152]{1,0:T(8,128)(2,1)S(1)}, bf16[160,1152]{1,0:T(8,128)(2,1)S(1)}, bf16[160,1152]{1,0:T(8,128)(2,1)S(1)}) custom-call(bf16[160,1152]{1,0:T(8,128)(2,1)S(1)} %get-tuple-element.40.q_ref, bf16[160,1152]{1,0:T(8,128)(2,1)S(1)} %get-tuple-element.39.k_ref, bf16[160,1152]{1,0:T(8,128)(2,1)S(1)} %get-tuple-element.38.v_ref, ...), custom_call_target="tpu_custom_call" | custom-call | flops 6000000000 | bytes 8000000 | tf_op jit(solution)/shard_map/pallas_call | solution.py:96
  69.5 1.9 %collective-permute-start.19 = (bf16[40,1152]{1,0:T(8,128)(2,1)S(1)}, bf16[40,1152]{1,0:T(8,128)(2,1)S(1)}, u32[]{:S(2)}, u32[]{:S(2)}) collective-permute-start(bf16[40,1152]{1,0:T(8,128)(2,1)S(1)} %get-tuple-element.57), channel_id=1, source_target_pairs={{0,1},{1,0},{2,3},{3,2},{4,5},{5,4},{6,7},{7,6},{8,9},{9,8},{10,11... | collective-permute-start | bytes 276488 | tf_op jit(solution)/shard_map/ppermute | solution.py:155
  71.3 0.9 collective-permute-start.20
  72.3 1.7 %collective-permute-start.21 = (bf16[40,1152]{1,0:T(8,128)(2,1)S(1)}, bf16[40,1152]{1,0:T(8,128)(2,1)S(1)}, u32[]{:S(2)}, u32[]{:S(2)}) collective-permute-start(bf16[40,1152]{1,0:T(8,128)(2,1)S(1)} %get-tuple-element.55), channel_id=1, source_target_pairs={{0,3},{1,2},{2,1},{3,0},{4,7},{5,6},{6,5},{7,4},{8,11},{9,10},{10,... | collective-permute-start | bytes 276488 | tf_op jit(solution)/shard_map/ppermute | solution.py:155
  74.0 1.0 collective-permute-start.16
  75.0 2.8 %collective-permute-start.17 = (bf16[40,1152]{1,0:T(8,128)(2,1)S(1)}, bf16[40,1152]{1,0:T(8,128)(2,1)S(1)}, u32[]{:S(2)}, u32[]{:S(2)}) collective-permute-start(bf16[40,1152]{1,0:T(8,128)(2,1)S(1)} %get-tuple-element.64), channel_id=1, source_target_pairs={{0,2},{1,3},{2,0},{3,1},{4,6},{5,7},{6,4},{7,5},{8,10},{9,11},{10,... | collective-permute-start | bytes 276488 | tf_op jit(solution)/shard_map/ppermute | solution.py:155
  77.8 4.1 %collective-permute-done.20 = bf16[40,1152]{1,0:T(8,128)(2,1)S(1)} collective-permute-done((bf16[40,1152]{1,0:T(8,128)(2,1)S(1)}, bf16[40,1152]{1,0:T(8,128)(2,1)S(1)}, u32[]{:S(2)}, u32[]{:S(2)}) %collective-permute-start.20) | collective-permute-done | bytes 92192 | tf_op jit(solution)/shard_map/ppermute | solution.py:155
  81.8 2.1 %collective-permute-start.18 = (bf16[40,1152]{1,0:T(8,128)(2,1)S(1)}, bf16[40,1152]{1,0:T(8,128)(2,1)S(1)}, u32[]{:S(2)}, u32[]{:S(2)}) collective-permute-start(bf16[40,1152]{1,0:T(8,128)(2,1)S(1)} %get-tuple-element.63), channel_id=1, source_target_pairs={{0,3},{1,2},{2,1},{3,0},{4,7},{5,6},{6,5},{7,4},{8,11},{9,10},{10,... | collective-permute-start | bytes 276488 | tf_op jit(solution)/shard_map/ppermute | solution.py:155
  83.9 2.6 %collective-permute-start.13 = (bf16[40,1152]{1,0:T(8,128)(2,1)S(1)}, bf16[40,1152]{1,0:T(8,128)(2,1)S(1)}, u32[]{:S(2)}, u32[]{:S(2)}) collective-permute-start(bf16[40,1152]{1,0:T(8,128)(2,1)S(1)} %get-tuple-element.73), channel_id=1, source_target_pairs={{0,1},{1,0},{2,3},{3,2},{4,5},{5,4},{6,7},{7,6},{8,9},{9,8},{10,11... | collective-permute-start | bytes 276488 | tf_op jit(solution)/shard_map/ppermute | solution.py:155
  86.6 0.5 collective-permute-start.14
  87.2 1.8 %collective-permute-done.17 = bf16[40,1152]{1,0:T(8,128)(2,1)S(1)} collective-permute-done((bf16[40,1152]{1,0:T(8,128)(2,1)S(1)}, bf16[40,1152]{1,0:T(8,128)(2,1)S(1)}, u32[]{:S(2)}, u32[]{:S(2)}) %collective-permute-start.17) | collective-permute-done | bytes 92192 | tf_op jit(solution)/shard_map/ppermute | solution.py:155
  89.0 2.8 %collective-permute-start.15 = (bf16[40,1152]{1,0:T(8,128)(2,1)S(1)}, bf16[40,1152]{1,0:T(8,128)(2,1)S(1)}, u32[]{:S(2)}, u32[]{:S(2)}) collective-permute-start(bf16[40,1152]{1,0:T(8,128)(2,1)S(1)} %get-tuple-element.71), channel_id=1, source_target_pairs={{0,3},{1,2},{2,1},{3,0},{4,7},{5,6},{6,5},{7,4},{8,11},{9,10},{10,... | collective-permute-start | bytes 276488 | tf_op jit(solution)/shard_map/ppermute | solution.py:155
  92.1 1.3 shard_map.140
  93.4 0.1 slice_bitcast_fusion.2
  93.5 1.6 %collective-permute-start.23 = (bf16[4,72,640]{2,1,0:T(8,128)(2,1)S(1)}, bf16[4,72,640]{2,1,0:T(8,128)(2,1)S(1)}, u32[]{:S(2)}, u32[]{:S(2)}) collective-permute-start(bf16[4,72,640]{2,1,0:T(8,128)(2,1)S(1)} %get-tuple-element.33), channel_id=1, source_target_pairs={{0,8},{4,12},{8,0},{12,4},{16,24},{20,28},{24,16},{28,20},{1,9},{5... | collective-permute-start | bytes 1105928 | tf_op jit(solution)/shard_map/ppermute | solution.py:155
  95.1 1.5 %collective-permute-start.24 = (bf16[4,72,640]{2,1,0:T(8,128)(2,1)S(1)}, bf16[4,72,640]{2,1,0:T(8,128)(2,1)S(1)}, u32[]{:S(2)}, u32[]{:S(2)}) collective-permute-start(bf16[4,72,640]{2,1,0:T(8,128)(2,1)S(1)} %get-tuple-element.35), channel_id=1, source_target_pairs={{0,16},{4,20},{8,24},{12,28},{16,0},{20,4},{24,8},{28,12},{1,17},{... | collective-permute-start | bytes 1105928 | tf_op jit(solution)/shard_map/ppermute | solution.py:155
  96.6 0.5 collective-permute-start.25
  97.2 7.1 %collective-permute-done.23 = bf16[4,72,640]{2,1,0:T(8,128)(2,1)S(1)} collective-permute-done((bf16[4,72,640]{2,1,0:T(8,128)(2,1)S(1)}, bf16[4,72,640]{2,1,0:T(8,128)(2,1)S(1)}, u32[]{:S(2)}, u32[]{:S(2)}) %collective-permute-start.23) | collective-permute-done | bytes 368672 | tf_op jit(solution)/shard_map/ppermute | solution.py:155
  104.3 5.2 %collective-permute-done.24 = bf16[4,72,640]{2,1,0:T(8,128)(2,1)S(1)} collective-permute-done((bf16[4,72,640]{2,1,0:T(8,128)(2,1)S(1)}, bf16[4,72,640]{2,1,0:T(8,128)(2,1)S(1)}, u32[]{:S(2)}, u32[]{:S(2)}) %collective-permute-start.24) | collective-permute-done | bytes 368672 | tf_op jit(solution)/shard_map/ppermute | solution.py:155
  109.4 0.2 fusion.2
  109.7 1.5 %collective-permute-start.26 = (bf16[72,640]{1,0:T(8,128)(2,1)S(1)}, bf16[72,640]{1,0:T(8,128)(2,1)S(1)}, u32[]{:S(2)}, u32[]{:S(2)}) collective-permute-start(bf16[72,640]{1,0:T(8,128)(2,1)S(1)} %get-tuple-element.47), channel_id=1, source_target_pairs={{0,1},{1,0},{2,3},{3,2},{4,5},{5,4},{6,7},{7,6},{8,9},{9,8},{10,11... | collective-permute-start | bytes 276488 | tf_op jit(solution)/shard_map/ppermute | solution.py:155
  111.2 2.0 %collective-permute-start.27 = (bf16[72,640]{1,0:T(8,128)(2,1)S(1)}, bf16[72,640]{1,0:T(8,128)(2,1)S(1)}, u32[]{:S(2)}, u32[]{:S(2)}) collective-permute-start(bf16[72,640]{1,0:T(8,128)(2,1)S(1)} %get-tuple-element.49), channel_id=1, source_target_pairs={{0,2},{1,3},{2,0},{3,1},{4,6},{5,7},{6,4},{7,5},{8,10},{9,11},{10,... | collective-permute-start | bytes 276488 | tf_op jit(solution)/shard_map/ppermute | solution.py:155
  113.1 1.4 %collective-permute-start.28 = (bf16[72,640]{1,0:T(8,128)(2,1)S(1)}, bf16[72,640]{1,0:T(8,128)(2,1)S(1)}, u32[]{:S(2)}, u32[]{:S(2)}) collective-permute-start(bf16[72,640]{1,0:T(8,128)(2,1)S(1)} %get-tuple-element.48), channel_id=1, source_target_pairs={{0,3},{1,2},{2,1},{3,0},{4,7},{5,6},{6,5},{7,4},{8,11},{9,10},{10,... | collective-permute-start | bytes 276488 | tf_op jit(solution)/shard_map/ppermute | solution.py:155
  114.6 2.0 %collective-permute-done.27 = bf16[72,640]{1,0:T(8,128)(2,1)S(1)} collective-permute-done((bf16[72,640]{1,0:T(8,128)(2,1)S(1)}, bf16[72,640]{1,0:T(8,128)(2,1)S(1)}, u32[]{:S(2)}, u32[]{:S(2)}) %collective-permute-start.27) | collective-permute-done | bytes 92192 | tf_op jit(solution)/shard_map/ppermute | solution.py:155
  116.6 3.0 %collective-permute-done.28 = bf16[72,640]{1,0:T(8,128)(2,1)S(1)} collective-permute-done((bf16[72,640]{1,0:T(8,128)(2,1)S(1)}, bf16[72,640]{1,0:T(8,128)(2,1)S(1)}, u32[]{:S(2)}, u32[]{:S(2)}) %collective-permute-start.28) | collective-permute-done | bytes 92192 | tf_op jit(solution)/shard_map/ppermute | solution.py:155
  119.7 1.3 collective-permute-start.29
  121.0 0.8 collective-permute-start.30
  121.8 1.4 %collective-permute-start.31 = (bf16[72,640]{1,0:T(8,128)(2,1)S(1)}, bf16[72,640]{1,0:T(8,128)(2,1)S(1)}, u32[]{:S(2)}, u32[]{:S(2)}) collective-permute-start(bf16[72,640]{1,0:T(8,128)(2,1)S(1)} %fusion.5), channel_id=1, source_target_pairs={{0,24},{4,28},{8,16},{12,20},{16,8},{20,12},{24,0},{28,4},{1,25},{... | collective-permute-start | bytes 276488 | tf_op jit(solution)/shard_map/ppermute | solution.py:155
  123.2 0.8 maximum_bitcast_fusion.2
  124.0 0.3 collective-permute-done.29
  124.3 1.2 collective-permute-done.30
  125.5 1.7 %collective-permute-done.31 = bf16[72,640]{1,0:T(8,128)(2,1)S(1)} collective-permute-done((bf16[72,640]{1,0:T(8,128)(2,1)S(1)}, bf16[72,640]{1,0:T(8,128)(2,1)S(1)}, u32[]{:S(2)}, u32[]{:S(2)}) %collective-permute-start.31) | collective-permute-done | bytes 92192 | tf_op jit(solution)/shard_map/ppermute | solution.py:155
  127.5 0.8 maximum_bitcast_fusion.1
  128.2 0.8 maximum_bitcast_fusion
  129.0 0.1 collective-permute-done.32
  129.1 0.1 broadcast_select_fusion
  129.3 1.2 convert_multiply_fusion
  (77 shorter events, 2.1 us)
Async XLA Ops:
  0.6 8.4 %copy-start.9 = (bf16[144,1152]{1,0:T(8,128)(2,1)S(1)}, bf16[144,1152]{1,0:T(8,128)(2,1)}, u32[]{:S(2)}) copy-start(bf16[144,1152]{1,0:T(8,128)(2,1)} %param.14) | copy-start | bytes 995332
  3.1 14.8 %collective-permute-start = (bf16[3,40,1152]{2,1,0:T(8,128)(2,1)S(1)}, bf16[3,40,1152]{2,1,0:T(8,128)(2,1)S(1)}, u32[]{:S(2)}, u32[]{:S(2)}) collective-permute-start(bf16[3,40,1152]{2,1,0:T(8,128)(2,1)S(1)} %pad_maximum_fusion.14), channel_id=1, source_target_pairs={{0,1},{1,0},{2,3},{3,2},{4,5},{5,4},{6,7},{7,6},{8,9},{9,8},{10,11... | collective-permute-start | bytes 829448 | tf_op jit(solution)/shard_map/ppermute | solution.py:155
  6.2 22.4 %collective-permute-start.1 = (bf16[3,40,1152]{2,1,0:T(8,128)(2,1)S(1)}, bf16[3,40,1152]{2,1,0:T(8,128)(2,1)S(1)}, u32[]{:S(2)}, u32[]{:S(2)}) collective-permute-start(bf16[3,40,1152]{2,1,0:T(8,128)(2,1)S(1)} %pad_maximum_fusion.15), channel_id=1, source_target_pairs={{0,2},{1,3},{2,0},{3,1},{4,6},{5,7},{6,4},{7,5},{8,10},{9,11},{10,... | collective-permute-start | bytes 829448 | tf_op jit(solution)/shard_map/ppermute | solution.py:155
  8.9 19.7 %collective-permute-start.2 = (bf16[3,40,1152]{2,1,0:T(8,128)(2,1)S(1)}, bf16[3,40,1152]{2,1,0:T(8,128)(2,1)S(1)}, u32[]{:S(2)}, u32[]{:S(2)}) collective-permute-start(bf16[3,40,1152]{2,1,0:T(8,128)(2,1)S(1)} %pad_maximum_fusion.16), channel_id=1, source_target_pairs={{0,3},{1,2},{2,1},{3,0},{4,7},{5,6},{6,5},{7,4},{8,11},{9,10},{10,... | collective-permute-start | bytes 829448 | tf_op jit(solution)/shard_map/ppermute | solution.py:155
  9.0 21.6 %collective-permute-start.6 = (bf16[144,1152]{1,0:T(8,128)(2,1)S(1)}, bf16[144,1152]{1,0:T(8,128)(2,1)S(1)}, u32[]{:S(2)}, u32[]{:S(2)}) collective-permute-start(bf16[144,1152]{1,0:T(8,128)(2,1)S(1)} %copy-done.9), channel_id=1, source_target_pairs={{0,8},{4,12},{8,0},{12,4},{16,24},{20,28},{24,16},{28,20},{1,9},{5... | collective-permute-start | bytes 995336 | tf_op jit(solution)/shard_map/ppermute | solution.py:155
  10.7 20.0 %collective-permute-start.7 = (bf16[144,1152]{1,0:T(8,128)(2,1)S(1)}, bf16[144,1152]{1,0:T(8,128)(2,1)S(1)}, u32[]{:S(2)}, u32[]{:S(2)}) collective-permute-start(bf16[144,1152]{1,0:T(8,128)(2,1)S(1)} %copy-done.9), channel_id=1, source_target_pairs={{0,16},{4,20},{8,24},{12,28},{16,0},{20,4},{24,8},{28,12},{1,17},{... | collective-permute-start | bytes 995336 | tf_op jit(solution)/shard_map/ppermute | solution.py:155
  17.9 12.8 %collective-permute-start.8 = (bf16[144,1152]{1,0:T(8,128)(2,1)S(1)}, bf16[144,1152]{1,0:T(8,128)(2,1)S(1)}, u32[]{:S(2)}, u32[]{:S(2)}) collective-permute-start(bf16[144,1152]{1,0:T(8,128)(2,1)S(1)} %copy-done.9), channel_id=1, source_target_pairs={{0,24},{4,28},{8,16},{12,20},{16,8},{20,12},{24,0},{28,4},{1,25},{... | collective-permute-start | bytes 995336 | tf_op jit(solution)/shard_map/ppermute | solution.py:155
  30.6 2.4 %copy-start.4 = (f32[16,160,160]{2,1,0:T(8,128)}, f32[16,160,160]{2,1,0:T(8,128)S(1)}, u32[]{:S(2)}) copy-start(f32[16,160,160]{2,1,0:T(8,128)S(1)} %get-tuple-element.27.probs_ref) | copy-start | bytes 4915204
  30.7 9.9 %copy-start.1 = (bf16[1,160,1152]{2,1,0:T(8,128)(2,1)S(1)}, bf16[1,160,1152]{2,1,0:T(8,128)(2,1)}, u32[]{:S(2)}) copy-start(bf16[1,160,1152]{2,1,0:T(8,128)(2,1)} %param.8) | copy-start | bytes 1105924
  30.7 9.8 %copy-start.2 = (bf16[1,160,1152]{2,1,0:T(8,128)(2,1)S(1)}, bf16[1,160,1152]{2,1,0:T(8,128)(2,1)}, u32[]{:S(2)}) copy-start(bf16[1,160,1152]{2,1,0:T(8,128)(2,1)} %param.9) | copy-start | bytes 1105924
  30.7 9.8 %copy-start.3 = (bf16[1,160,1152]{2,1,0:T(8,128)(2,1)S(1)}, bf16[1,160,1152]{2,1,0:T(8,128)(2,1)}, u32[]{:S(2)}) copy-start(bf16[1,160,1152]{2,1,0:T(8,128)(2,1)} %param.10) | copy-start | bytes 1105924
  32.4 16.0 %collective-permute-start.9 = (bf16[4,144,1152]{2,1,0:T(8,128)(2,1)}, bf16[4,144,1152]{2,1,0:T(8,128)(2,1)}, u32[]{:S(2)}, u32[]{:S(2)}) collective-permute-start(bf16[4,144,1152]{2,1,0:T(8,128)(2,1)} %get-tuple-element.37), channel_id=1, source_target_pairs={{0,4},{4,0},{8,12},{12,8},{16,20},{20,16},{24,28},{28,24},{1,5},{5... | collective-permute-start | bytes 3981320 | tf_op jit(solution)/shard_map/ppermute | solution.py:155
  33.0 11.0 %collective-permute-start.3 = (bf16[40,1152]{1,0:T(8,128)(2,1)S(1)}, bf16[40,1152]{1,0:T(8,128)(2,1)S(1)}, u32[]{:S(2)}, u32[]{:S(2)}) collective-permute-start(bf16[40,1152]{1,0:T(8,128)(2,1)S(1)} %get-tuple-element.85), channel_id=1, source_target_pairs={{0,1},{1,0},{2,3},{3,2},{4,5},{5,4},{6,7},{7,6},{8,9},{9,8},{10,11... | collective-permute-start | bytes 276488 | tf_op jit(solution)/shard_map/ppermute | solution.py:155
  38.0 10.2 %collective-permute-start.4 = (bf16[40,1152]{1,0:T(8,128)(2,1)S(1)}, bf16[40,1152]{1,0:T(8,128)(2,1)S(1)}, u32[]{:S(2)}, u32[]{:S(2)}) collective-permute-start(bf16[40,1152]{1,0:T(8,128)(2,1)S(1)} %get-tuple-element.84), channel_id=1, source_target_pairs={{0,2},{1,3},{2,0},{3,1},{4,6},{5,7},{6,4},{7,5},{8,10},{9,11},{10,... | collective-permute-start | bytes 276488 | tf_op jit(solution)/shard_map/ppermute | solution.py:155
  39.1 9.2 %collective-permute-start.5 = (bf16[40,1152]{1,0:T(8,128)(2,1)S(1)}, bf16[40,1152]{1,0:T(8,128)(2,1)S(1)}, u32[]{:S(2)}, u32[]{:S(2)}) collective-permute-start(bf16[40,1152]{1,0:T(8,128)(2,1)S(1)} %get-tuple-element.83), channel_id=1, source_target_pairs={{0,3},{1,2},{2,1},{3,0},{4,7},{5,6},{6,5},{7,4},{8,11},{9,10},{10,... | collective-permute-start | bytes 276488 | tf_op jit(solution)/shard_map/ppermute | solution.py:155
  42.4 1.5 %copy-start.6 = (f32[16,160,160]{2,1,0:T(8,128)}, f32[16,160,160]{2,1,0:T(8,128)S(1)}, u32[]{:S(2)}) copy-start(f32[16,160,160]{2,1,0:T(8,128)S(1)} %get-tuple-element.23.probs_ref) | copy-start | bytes 4915204
  43.9 4.5 %copy-start.8 = (bf16[4,1,144,1152]{3,2,1,0:T(8,128)(2,1)S(1)}, bf16[4,1,144,1152]{3,2,1,0:T(8,128)(2,1)}, u32[]{:S(2)}) copy-start(bf16[4,1,144,1152]{3,2,1,0:T(8,128)(2,1)} %get-tuple-element.36) | copy-start | bytes 3981316
  50.1 1.0 copy-start
  51.1 6.2 %copy-start.7 = (f32[16,160,160]{2,1,0:T(8,128)S(1)}, f32[16,160,160]{2,1,0:T(8,128)}, u32[]{:S(2)}) copy-start(f32[16,160,160]{2,1,0:T(8,128)} %copy-done.6) | copy-start | bytes 4915204
  52.7 39.2 %collective-permute-start.22 = (bf16[2,160,1152]{2,1,0:T(8,128)(2,1)S(1)}, bf16[2,160,1152]{2,1,0:T(8,128)(2,1)S(1)}, u32[]{:S(2)}, u32[]{:S(2)}) collective-permute-start(bf16[2,160,1152]{2,1,0:T(8,128)(2,1)S(1)} %pad_maximum_fusion.3), channel_id=1, source_target_pairs={{0,4},{4,0},{8,12},{12,8},{16,20},{20,16},{24,28},{28,24},{1,5},{5... | collective-permute-start | bytes 2211848 | tf_op jit(solution)/shard_map/ppermute | solution.py:155
  52.8 9.7 %collective-permute-start.10 = (bf16[40,1152]{1,0:T(8,128)(2,1)S(1)}, bf16[40,1152]{1,0:T(8,128)(2,1)S(1)}, u32[]{:S(2)}, u32[]{:S(2)}) collective-permute-start(bf16[40,1152]{1,0:T(8,128)(2,1)S(1)} %get-tuple-element.77), channel_id=1, source_target_pairs={{0,1},{1,0},{2,3},{3,2},{4,5},{5,4},{6,7},{7,6},{8,9},{9,8},{10,11... | collective-permute-start | bytes 276488 | tf_op jit(solution)/shard_map/ppermute | solution.py:155
  54.5 10.3 %collective-permute-start.11 = (bf16[40,1152]{1,0:T(8,128)(2,1)S(1)}, bf16[40,1152]{1,0:T(8,128)(2,1)S(1)}, u32[]{:S(2)}, u32[]{:S(2)}) collective-permute-start(bf16[40,1152]{1,0:T(8,128)(2,1)S(1)} %get-tuple-element.76), channel_id=1, source_target_pairs={{0,2},{1,3},{2,0},{3,1},{4,6},{5,7},{6,4},{7,5},{8,10},{9,11},{10,... | collective-permute-start | bytes 276488 | tf_op jit(solution)/shard_map/ppermute | solution.py:155
  55.4 9.4 %collective-permute-start.12 = (bf16[40,1152]{1,0:T(8,128)(2,1)S(1)}, bf16[40,1152]{1,0:T(8,128)(2,1)S(1)}, u32[]{:S(2)}, u32[]{:S(2)}) collective-permute-start(bf16[40,1152]{1,0:T(8,128)(2,1)S(1)} %get-tuple-element.75), channel_id=1, source_target_pairs={{0,3},{1,2},{2,1},{3,0},{4,7},{5,6},{6,5},{7,4},{8,11},{9,10},{10,... | collective-permute-start | bytes 276488 | tf_op jit(solution)/shard_map/ppermute | solution.py:155
  57.3 7.6 %copy-start.5 = (f32[16,160,160]{2,1,0:T(8,128)S(1)}, f32[16,160,160]{2,1,0:T(8,128)}, u32[]{:S(2)}) copy-start(f32[16,160,160]{2,1,0:T(8,128)} %copy-done.4) | copy-start | bytes 4915204
  69.5 5.5 %collective-permute-start.19 = (bf16[40,1152]{1,0:T(8,128)(2,1)S(1)}, bf16[40,1152]{1,0:T(8,128)(2,1)S(1)}, u32[]{:S(2)}, u32[]{:S(2)}) collective-permute-start(bf16[40,1152]{1,0:T(8,128)(2,1)S(1)} %get-tuple-element.57), channel_id=1, source_target_pairs={{0,1},{1,0},{2,3},{3,2},{4,5},{5,4},{6,7},{7,6},{8,9},{9,8},{10,11... | collective-permute-start | bytes 276488 | tf_op jit(solution)/shard_map/ppermute | solution.py:155
  71.3 10.5 %collective-permute-start.20 = (bf16[40,1152]{1,0:T(8,128)(2,1)S(1)}, bf16[40,1152]{1,0:T(8,128)(2,1)S(1)}, u32[]{:S(2)}, u32[]{:S(2)}) collective-permute-start(bf16[40,1152]{1,0:T(8,128)(2,1)S(1)} %get-tuple-element.56), channel_id=1, source_target_pairs={{0,2},{1,3},{2,0},{3,1},{4,6},{5,7},{6,4},{7,5},{8,10},{9,11},{10,... | collective-permute-start | bytes 276488 | tf_op jit(solution)/shard_map/ppermute | solution.py:155
  72.3 11.7 %collective-permute-start.21 = (bf16[40,1152]{1,0:T(8,128)(2,1)S(1)}, bf16[40,1152]{1,0:T(8,128)(2,1)S(1)}, u32[]{:S(2)}, u32[]{:S(2)}) collective-permute-start(bf16[40,1152]{1,0:T(8,128)(2,1)S(1)} %get-tuple-element.55), channel_id=1, source_target_pairs={{0,3},{1,2},{2,1},{3,0},{4,7},{5,6},{6,5},{7,4},{8,11},{9,10},{10,... | collective-permute-start | bytes 276488 | tf_op jit(solution)/shard_map/ppermute | solution.py:155
  74.0 12.7 %collective-permute-start.16 = (bf16[40,1152]{1,0:T(8,128)(2,1)S(1)}, bf16[40,1152]{1,0:T(8,128)(2,1)S(1)}, u32[]{:S(2)}, u32[]{:S(2)}) collective-permute-start(bf16[40,1152]{1,0:T(8,128)(2,1)S(1)} %get-tuple-element.65), channel_id=1, source_target_pairs={{0,1},{1,0},{2,3},{3,2},{4,5},{5,4},{6,7},{7,6},{8,9},{9,8},{10,11... | collective-permute-start | bytes 276488 | tf_op jit(solution)/shard_map/ppermute | solution.py:155
  75.0 14.0 %collective-permute-start.17 = (bf16[40,1152]{1,0:T(8,128)(2,1)S(1)}, bf16[40,1152]{1,0:T(8,128)(2,1)S(1)}, u32[]{:S(2)}, u32[]{:S(2)}) collective-permute-start(bf16[40,1152]{1,0:T(8,128)(2,1)S(1)} %get-tuple-element.64), channel_id=1, source_target_pairs={{0,2},{1,3},{2,0},{3,1},{4,6},{5,7},{6,4},{7,5},{8,10},{9,11},{10,... | collective-permute-start | bytes 276488 | tf_op jit(solution)/shard_map/ppermute | solution.py:155
  81.8 10.0 %collective-permute-start.18 = (bf16[40,1152]{1,0:T(8,128)(2,1)S(1)}, bf16[40,1152]{1,0:T(8,128)(2,1)S(1)}, u32[]{:S(2)}, u32[]{:S(2)}) collective-permute-start(bf16[40,1152]{1,0:T(8,128)(2,1)S(1)} %get-tuple-element.63), channel_id=1, source_target_pairs={{0,3},{1,2},{2,1},{3,0},{4,7},{5,6},{6,5},{7,4},{8,11},{9,10},{10,... | collective-permute-start | bytes 276488 | tf_op jit(solution)/shard_map/ppermute | solution.py:155
  83.9 12.7 %collective-permute-start.13 = (bf16[40,1152]{1,0:T(8,128)(2,1)S(1)}, bf16[40,1152]{1,0:T(8,128)(2,1)S(1)}, u32[]{:S(2)}, u32[]{:S(2)}) collective-permute-start(bf16[40,1152]{1,0:T(8,128)(2,1)S(1)} %get-tuple-element.73), channel_id=1, source_target_pairs={{0,1},{1,0},{2,3},{3,2},{4,5},{5,4},{6,7},{7,6},{8,9},{9,8},{10,11... | collective-permute-start | bytes 276488 | tf_op jit(solution)/shard_map/ppermute | solution.py:155
  86.6 10.5 %collective-permute-start.14 = (bf16[40,1152]{1,0:T(8,128)(2,1)S(1)}, bf16[40,1152]{1,0:T(8,128)(2,1)S(1)}, u32[]{:S(2)}, u32[]{:S(2)}) collective-permute-start(bf16[40,1152]{1,0:T(8,128)(2,1)S(1)} %get-tuple-element.72), channel_id=1, source_target_pairs={{0,2},{1,3},{2,0},{3,1},{4,6},{5,7},{6,4},{7,5},{8,10},{9,11},{10,... | collective-permute-start | bytes 276488 | tf_op jit(solution)/shard_map/ppermute | solution.py:155
  89.0 8.2 %collective-permute-start.15 = (bf16[40,1152]{1,0:T(8,128)(2,1)S(1)}, bf16[40,1152]{1,0:T(8,128)(2,1)S(1)}, u32[]{:S(2)}, u32[]{:S(2)}) collective-permute-start(bf16[40,1152]{1,0:T(8,128)(2,1)S(1)} %get-tuple-element.71), channel_id=1, source_target_pairs={{0,3},{1,2},{2,1},{3,0},{4,7},{5,6},{6,5},{7,4},{8,11},{9,10},{10,... | collective-permute-start | bytes 276488 | tf_op jit(solution)/shard_map/ppermute | solution.py:155
  93.5 10.8 %collective-permute-start.23 = (bf16[4,72,640]{2,1,0:T(8,128)(2,1)S(1)}, bf16[4,72,640]{2,1,0:T(8,128)(2,1)S(1)}, u32[]{:S(2)}, u32[]{:S(2)}) collective-permute-start(bf16[4,72,640]{2,1,0:T(8,128)(2,1)S(1)} %get-tuple-element.33), channel_id=1, source_target_pairs={{0,8},{4,12},{8,0},{12,4},{16,24},{20,28},{24,16},{28,20},{1,9},{5... | collective-permute-start | bytes 1105928 | tf_op jit(solution)/shard_map/ppermute | solution.py:155
  95.1 14.4 %collective-permute-start.24 = (bf16[4,72,640]{2,1,0:T(8,128)(2,1)S(1)}, bf16[4,72,640]{2,1,0:T(8,128)(2,1)S(1)}, u32[]{:S(2)}, u32[]{:S(2)}) collective-permute-start(bf16[4,72,640]{2,1,0:T(8,128)(2,1)S(1)} %get-tuple-element.35), channel_id=1, source_target_pairs={{0,16},{4,20},{8,24},{12,28},{16,0},{20,4},{24,8},{28,12},{1,17},{... | collective-permute-start | bytes 1105928 | tf_op jit(solution)/shard_map/ppermute | solution.py:155
  96.6 12.8 %collective-permute-start.25 = (bf16[4,72,640]{2,1,0:T(8,128)(2,1)S(1)}, bf16[4,72,640]{2,1,0:T(8,128)(2,1)S(1)}, u32[]{:S(2)}, u32[]{:S(2)}) collective-permute-start(bf16[4,72,640]{2,1,0:T(8,128)(2,1)S(1)} %get-tuple-element.34), channel_id=1, source_target_pairs={{0,24},{4,28},{8,16},{12,20},{16,8},{20,12},{24,0},{28,4},{1,25},{... | collective-permute-start | bytes 1105928 | tf_op jit(solution)/shard_map/ppermute | solution.py:155
  109.7 4.9 %collective-permute-start.26 = (bf16[72,640]{1,0:T(8,128)(2,1)S(1)}, bf16[72,640]{1,0:T(8,128)(2,1)S(1)}, u32[]{:S(2)}, u32[]{:S(2)}) collective-permute-start(bf16[72,640]{1,0:T(8,128)(2,1)S(1)} %get-tuple-element.47), channel_id=1, source_target_pairs={{0,1},{1,0},{2,3},{3,2},{4,5},{5,4},{6,7},{7,6},{8,9},{9,8},{10,11... | collective-permute-start | bytes 276488 | tf_op jit(solution)/shard_map/ppermute | solution.py:155
  111.2 5.5 %collective-permute-start.27 = (bf16[72,640]{1,0:T(8,128)(2,1)S(1)}, bf16[72,640]{1,0:T(8,128)(2,1)S(1)}, u32[]{:S(2)}, u32[]{:S(2)}) collective-permute-start(bf16[72,640]{1,0:T(8,128)(2,1)S(1)} %get-tuple-element.49), channel_id=1, source_target_pairs={{0,2},{1,3},{2,0},{3,1},{4,6},{5,7},{6,4},{7,5},{8,10},{9,11},{10,... | collective-permute-start | bytes 276488 | tf_op jit(solution)/shard_map/ppermute | solution.py:155
  113.1 6.5 %collective-permute-start.28 = (bf16[72,640]{1,0:T(8,128)(2,1)S(1)}, bf16[72,640]{1,0:T(8,128)(2,1)S(1)}, u32[]{:S(2)}, u32[]{:S(2)}) collective-permute-start(bf16[72,640]{1,0:T(8,128)(2,1)S(1)} %get-tuple-element.48), channel_id=1, source_target_pairs={{0,3},{1,2},{2,1},{3,0},{4,7},{5,6},{6,5},{7,4},{8,11},{9,10},{10,... | collective-permute-start | bytes 276488 | tf_op jit(solution)/shard_map/ppermute | solution.py:155
  119.7 4.6 %collective-permute-start.29 = (bf16[72,640]{1,0:T(8,128)(2,1)S(1)}, bf16[72,640]{1,0:T(8,128)(2,1)S(1)}, u32[]{:S(2)}, u32[]{:S(2)}) collective-permute-start(bf16[72,640]{1,0:T(8,128)(2,1)S(1)} %fusion.5), channel_id=1, source_target_pairs={{0,8},{4,12},{8,0},{12,4},{16,24},{20,28},{24,16},{28,20},{1,9},{5... | collective-permute-start | bytes 276488 | tf_op jit(solution)/shard_map/ppermute | solution.py:155
  121.0 4.6 %collective-permute-start.30 = (bf16[72,640]{1,0:T(8,128)(2,1)S(1)}, bf16[72,640]{1,0:T(8,128)(2,1)S(1)}, u32[]{:S(2)}, u32[]{:S(2)}) collective-permute-start(bf16[72,640]{1,0:T(8,128)(2,1)S(1)} %fusion.5), channel_id=1, source_target_pairs={{0,16},{4,20},{8,24},{12,28},{16,0},{20,4},{24,8},{28,12},{1,17},{... | collective-permute-start | bytes 276488 | tf_op jit(solution)/shard_map/ppermute | solution.py:155
  121.8 5.5 %collective-permute-start.31 = (bf16[72,640]{1,0:T(8,128)(2,1)S(1)}, bf16[72,640]{1,0:T(8,128)(2,1)S(1)}, u32[]{:S(2)}, u32[]{:S(2)}) collective-permute-start(bf16[72,640]{1,0:T(8,128)(2,1)S(1)} %fusion.5), channel_id=1, source_target_pairs={{0,24},{4,28},{8,16},{12,20},{16,8},{20,12},{24,0},{28,4},{1,25},{... | collective-permute-start | bytes 276488 | tf_op jit(solution)/shard_map/ppermute | solution.py:155
  127.4 1.8 %collective-permute-start.32 = (bf16[288,640]{1,0:T(8,128)(2,1)S(1)}, bf16[288,640]{1,0:T(8,128)(2,1)S(1)}, u32[]{:S(2)}, u32[]{:S(2)}) collective-permute-start(bf16[288,640]{1,0:T(8,128)(2,1)S(1)} %pad_maximum_fusion.13), channel_id=1, source_target_pairs={{0,4},{4,0},{8,12},{12,8},{16,20},{20,16},{24,28},{28,24},{1,5},{5... | collective-permute-start | bytes 1105928 | tf_op jit(solution)/shard_map/ppermute | solution.py:155

commit v2 on v1

v2 whole, which is shorter than its diff:
```python
import functools
import math

import jax
import jax.numpy as jnp
from jax import lax
from jax.experimental import pallas as pl
from jax.experimental.pallas import tpu as pltpu
from jax.sharding import PartitionSpec as P

HEAD_DIM = 72
LANES = 128
VMEM_BYTES = 24 * 1024 * 1024
COST = 10**10
SMALL = 10
F32 = jnp.float32
BF16 = jnp.bfloat16
NT = (((1,), (1,)), ((), ()))
NN = (((1,), (0,)), ((), ()))
TN = (((0,), (0,)), ((), ()))


def dot(left, right, form):
    return lax.dot_general(left, right, form, preferred_element_type=F32)


def windows(width):
    found = []
    for head in range(width // HEAD_DIM):
        first = head * HEAD_DIM
        start = first // LANES * LANES
        size = -(-(first + HEAD_DIM - start) // LANES) * LANES
        found.append((start, size, first - start))
    return found


def head_only(block, offset):
    lane = lax.broadcasted_iota(jnp.int32, (1, block.shape[1]), 1)
    inside = (lane >= offset) & (lane < offset + HEAD_DIM)
    return jnp.where(inside, block, jnp.zeros_like(block))


def same_patch(rows, per_block):
    left = lax.broadcasted_iota(jnp.int32, (rows, 1), 0) % per_block
    right = lax.broadcasted_iota(jnp.int32, (1, rows), 1) % per_block
    return left == right


def forward(per_block, q_ref, k_ref, v_ref, probs_ref, total):
    rows, width = q_ref.shape
    scaling = 1.0 / math.sqrt(HEAD_DIM)
    keep = None if per_block is None else same_patch(rows, per_block)
    total[...] = jnp.zeros_like(total)
    for head, (start, size, offset) in enumerate(windows(width)):
        lanes = slice(start, start + size)
        logits = dot(head_only(q_ref[:, lanes], offset), k_ref[:, lanes], NT) * scaling
        if keep is not None:
            logits = jnp.where(keep, logits, -1e30)
        lifted = jnp.exp(logits - jnp.max(logits, axis=-1, keepdims=True))
        probs = lifted * (1.0 / jnp.sum(lifted, axis=-1, keepdims=True))
        probs_ref[head] = probs
        total[:, lanes] += dot(probs.astype(BF16), head_only(v_ref[:, lanes], offset), NN)


def backward(q_ref, k_ref, v_ref, g_ref, probs_ref, dq_sum, dk_sum, dv_sum):
    dq_sum[...] = jnp.zeros_like(dq_sum)
    dk_sum[...] = jnp.zeros_like(dk_sum)
    dv_sum[...] = jnp.zeros_like(dv_sum)
    for head, (start, size, offset) in enumerate(windows(q_ref.shape[1])):
        lanes = slice(start, start + size)
        probs = probs_ref[head]
        step = head_only(g_ref[:, lanes], offset)
        upstream = dot(step, v_ref[:, lanes], NT)
        dv_sum[:, lanes] += dot(probs.astype(BF16), step, TN)
        mean = jnp.sum(probs * upstream, axis=-1, keepdims=True)
        dscore = (probs * (upstream - mean)).astype(BF16)
        dq_sum[:, lanes] += dot(dscore, head_only(k_ref[:, lanes], offset), NN)
        dk_sum[:, lanes] += dot(dscore, head_only(q_ref[:, lanes], offset), TN)


def space_forward_kernel(q_ref, k_ref, v_ref, out_ref, probs_ref, total):
    forward(None, q_ref, k_ref, v_ref, probs_ref, total)
    out_ref[...] = total[...].astype(BF16)


def space_backward_kernel(q_ref, k_ref, v_ref, g_ref, probs_ref, dq_ref, dk_ref, dv_ref, *sums):
    scaling = 1.0 / math.sqrt(HEAD_DIM)
    backward(q_ref, k_ref, v_ref, g_ref, probs_ref, *sums)
    dq_ref[...] = (sums[0][...] * scaling).astype(BF16)
    dk_ref[...] = (sums[1][...] * scaling).astype(BF16)
    dv_ref[...] = sums[2][...].astype(BF16)


def pack_kernel(count, where_ref, *refs):
    groups = refs[0].shape[0]
    refs, (weight_ref, low_ref, high_ref) = refs[:count] + refs[count + 1 : -2], (refs[count],) + refs[-2:]
    low_ref[...] = weight_ref[:1]
    high_ref[...] = weight_ref[1:]
    for i in range(groups):
        for j in range(count):
            refs[count + i][j] = refs[j][where_ref[1] ^ i]


def unpack_kernel(where_ref, *refs):
    count = refs[0].shape[0]
    groups = len(refs) - count
    for i in range(groups):
        for j in range(count):
            refs[groups + j][where_ref[1] ^ i] = refs[i][j]


def time_forward_kernel(groups, *refs):
    pieces, outs = refs[:groups], refs[groups : 2 * groups]
    probs_ref, qkv_ref, total = refs[2 * groups :]
    per_block = pieces[0].shape[1]
    for i in range(groups):
        qkv_ref[:, per_block * i : per_block * (i + 1), :] = pieces[i][...]
    forward(per_block, qkv_ref.at[0], qkv_ref.at[1], qkv_ref.at[2], probs_ref, total)
    for i in range(groups):
        outs[i][...] = total[per_block * i : per_block * (i + 1), :].astype(BF16)


def time_backward_kernel(groups, *refs):
    pieces, (qkv_ref, probs_ref) = refs[:groups], refs[groups : groups + 2]
    outs = refs[groups + 2 : 2 * groups + 2]
    step, *sums = refs[2 * groups + 2 :]
    per_block = pieces[0].shape[0]
    for i in range(groups):
        step[per_block * i : per_block * (i + 1), :] = pieces[i][...]
    backward(qkv_ref.at[0], qkv_ref.at[1], qkv_ref.at[2], step, probs_ref, *sums)
    scaling = 1.0 / math.sqrt(HEAD_DIM)
    for i in range(groups):
        rows = slice(per_block * i, per_block * (i + 1))
        outs[i][0] = (sums[0][rows, :] * scaling).astype(BF16)
        outs[i][1] = (sums[1][rows, :] * scaling).astype(BF16)
        outs[i][2] = sums[2][rows, :].astype(BF16)


def project_kernel(groups, where_ref, *refs):
    pieces, (space_ref, target_ref, weight_ref) = refs[:groups], refs[groups : groups + 3]
    pair_ref, home_ref = refs[groups + 3 : groups + 5]
    outs, total = refs[groups + 5 : 2 * groups + 5], refs[2 * groups + 5]
    per_block = pieces[0].shape[0]
    for i in range(groups):
        rows = slice(per_block * i, per_block * (i + 1))
        total[rows, :] = space_ref[where_ref[1] ^ i].astype(F32) + pieces[i][...].astype(F32)
    comb = total[...].astype(BF16)
    pair_ref[0] = comb
    for i in range(groups):
        rows = slice(per_block * i, per_block * (i + 1))
        total[rows, :] = target_ref[where_ref[1] ^ i].astype(F32)
    og = (dot(comb, weight_ref[...], NN) - total[...]).astype(BF16)
    pair_ref[1] = og
    total[...] = dot(og, weight_ref[...], NT)
    for i in range(groups):
        piece = total[per_block * i : per_block * (i + 1), :].astype(BF16)
        outs[i][...] = piece
        home_ref[where_ref[1] ^ i] = piece


def stack_kernel(*refs):
    for i, ref in enumerate(refs[:-1]):
        size = ref.shape[0]
        refs[-1][i * size : (i + 1) * size] = ref[...]


def weight_kernel(orders, where_ref, *refs):
    for i, ref in enumerate(refs[:-1]):
        half, other = i // 2, i % 2
        for j, bits in enumerate(orders[half]):
            refs[-1][where_ref[0] ^ (2 * bits + other), half] = ref[j]


def halve_kernel(keep_ref, came_ref, *outs):
    total = keep_ref[...] + came_ref[...].astype(F32)
    half = total.shape[0] // 2
    if half == 0:
        outs[0][...] = total.astype(outs[0].dtype)
    else:
        outs[0][...] = total[:half]
        outs[1][...] = total[half:].astype(BF16)


def turn_kernel(order, where_ref, *refs):
    *ins, keep_ref, send_ref, total = refs
    at = 0
    for keep, came in zip(ins[::2], ins[1::2]):
        rows = keep.shape[1]
        total[at : at + rows] = keep[0] + came[0].astype(F32)
        at += rows
    half = len(order) // 2
    for i, bits in enumerate(order):
        piece = total[where_ref[1] ^ bits]
        if i < half:
            keep_ref[i] = piece
        else:
            send_ref[i - half] = piece.astype(BF16)


def join_kernel(scaling, order, where_ref, mine_ref, other_ref, out_ref):
    size, width = mine_ref.shape[-1], out_ref.shape[-1]
    first = (where_ref[0] & 1) == 0
    for i, bits in enumerate(order):
        mine, other = mine_ref[i].astype(F32) * scaling, other_ref[i].astype(F32) * scaling
        chip = (where_ref[0] >> 1) ^ bits
        out_ref[chip, :, :size] = jnp.where(first, mine, other)
        out_ref[chip, :, size:] = jnp.where(first, other, mine)[:, 2 * size - width :]


def grad_kernel(orders, where_ref, mine_ref, other_ref, *refs):
    outs, total = refs[:-1], refs[-1]
    half, _, size = outs[0].shape[1:]
    first = pl.multiple_of((where_ref[0] & 1) * (mine_ref.shape[-1] - size), LANES)
    term = dot(mine_ref[0], mine_ref[1, :, pl.ds(first, size)], TN)
    term += dot(other_ref[0], other_ref[1, :, pl.ds(first, size)], TN)
    total[...] = term.reshape(total.shape)
    for i, order in enumerate(orders):
        keep_ref, send_ref = outs[2 * i : 2 * i + 2]
        stays = len(order) // 2
        for j, bits in enumerate(order):
            piece = total[half * i : half * (i + 1), (where_ref[0] >> 1) ^ bits]
            if j < stays:
                keep_ref[j] = piece
            else:
                send_ref[j - stays] = piece.astype(BF16)


def call(body, outs, scratch, where, *args, cost=COST):
    in_specs = [pl.BlockSpec(memory_space=pltpu.VMEM)] * len(args)
    if where is not None:
        in_specs = [pl.BlockSpec(memory_space=pltpu.SMEM)] + in_specs
        args = (where,) + args
    return pl.pallas_call(
        body,
        out_shape=tuple(jax.ShapeDtypeStruct(*out) for out in outs),
        in_specs=in_specs,
        out_specs=(pl.BlockSpec(memory_space=pltpu.VMEM),) * len(outs),
        scratch_shapes=[pltpu.VMEM(*item) for item in scratch],
        cost_estimate=pl.CostEstimate(flops=cost, bytes_accessed=10, transcendentals=0),
        compiler_params=pltpu.CompilerParams(vmem_limit_bytes=VMEM_BYTES),
    )(*args)


def swap(array, axis, bits):
    size = lax.axis_size(axis)
    return lax.ppermute(array, axis, [(i, i ^ bits) for i in range(size)])


def after(value, *others):
    return lax.optimization_barrier((value,) + others)[0]


def stack(left, right):
    shape = (2 * left.shape[0],) + left.shape[1:]
    return call(stack_kernel, [(shape, BF16)], [], None, left, right)[0]


def doubled(held, bits):
    order = [0]
    for bit in bits:
        held = stack(held, swap(held, "dp", 2 * bit))
        order += [item ^ bit for item in order]
    return held, order


def gather_weight(halves, where):
    size = lax.axis_size("dp")
    bits = bits_of(size // 2)
    low, low_order = doubled(halves[0], bits)
    high, high_order = doubled(halves[1], bits[::-1])
    _, rows, width = low.shape
    (full,) = call(
        functools.partial(weight_kernel, [low_order, high_order]),
        [((size, 2, rows, width), BF16)],
        [],
        where,
        low,
        swap(low, "dp", 1),
        high,
        swap(high, "dp", 1),
    )
    return full.reshape(2 * size * rows, width)


def bits_of(size):
    return [1 << i for i in range(size.bit_length() - 1)]


def halving(bits):
    order = [0]
    for bit in reversed(bits):
        order = order + [item ^ bit for item in order]
    return order


def halved(keep, came):
    count, rest = keep.shape[0], keep.shape[1:]
    if count == 1:
        return call(halve_kernel, [(keep.shape, BF16)], [], None, keep, came, cost=SMALL)
    half = (count // 2,) + rest
    return call(halve_kernel, [(half, F32), (half, BF16)], [], None, keep, came, cost=SMALL)


def weight_gradient(pair, earlier, scaling, where):
    width = pair.shape[-1]
    chip_size, groups = lax.axis_size("dp") // 2, lax.axis_size("seq")
    rows = width // groups // chip_size
    size = -(-width // (2 * LANES)) * LANES
    bits, seq_bits = bits_of(chip_size), bits_of(groups)
    ways = [bits, bits[::-1]]
    cut = (chip_size // 2, groups // 2, rows, size)
    terms = call(
        functools.partial(grad_kernel, [halving(way) for way in ways]),
        [(cut, F32), (cut, BF16)] * 2,
        [((groups, chip_size, rows, size), F32)],
        where,
        pair,
        swap(pair, "dp", 1),
    )
    state = [[terms[0], swap(terms[1], "dp", 2 * ways[0][0])]]
    state += [[terms[2], swap(terms[3], "dp", 2 * ways[1][0])]]
    state[0][0] = after(state[0][0], earlier)
    for i in range(1, len(bits)):
        for j in range(2):
            keep, send = halved(*state[j])
            state[j] = [keep, swap(send, "dp", 2 * ways[j][i])]
    order = halving(seq_bits)
    cut = (groups // 2, rows, size)
    keep, send = call(
        functools.partial(turn_kernel, order),
        [(cut, F32), (cut, BF16)],
        [((groups, rows, size), F32)],
        where,
        *state[0],
        *state[1],
        cost=SMALL,
    )
    for bit in seq_bits[:-1]:
        keep, send = halved(keep, swap(send, "seq", bit))
    (total,) = halved(keep, swap(send, "seq", seq_bits[-1]))
    mine, order = doubled(total, bits)
    (whole,) = call(
        functools.partial(join_kernel, scaling, order),
        [((chip_size, rows, width), F32)],
        [],
        where,
        mine,
        swap(mine, "dp", 1),
        cost=SMALL,
    )
    return whole.reshape(chip_size * rows, width)


def divides(width):
    cuts = lax.axis_size("seq") * lax.axis_size("dp") // 2
    return width % (cuts * 8) == 0


def shards(q_space, k_space, v_space, q_time, k_time, v_time, weight, target):
    groups = lax.axis_size("seq")
    where = jnp.stack([lax.axis_index("dp"), lax.axis_index("seq")])
    rows, width = q_space.shape[1:]
    heads = width // HEAD_DIM
    per_block = rows // groups
    blocks, piece, full = (groups, per_block, width), (per_block, width), (rows, width)

    def exchange(pieces):
        return list(pieces[:1]) + [swap(pieces[i], "seq", i) for i in range(1, groups)]

    half = (1, weight.shape[0] // 2, width)
    *sent, low, high = call(
        functools.partial(pack_kernel, 3),
        [((3,) + piece, BF16)] * groups + [(half, BF16)] * 2,
        [],
        where,
        *[item.reshape(blocks) for item in (q_time, k_time, v_time)],
        weight.reshape((2,) + half[1:]),
    )
    there = exchange(sent)
    full_weight = gather_weight((low, high), where)
    space = [item.reshape(full) for item in (q_space, k_space, v_space)]
    out_space, probs_s = call(
        space_forward_kernel,
        [(full, BF16), ((heads, rows, rows), F32)],
        [(full, F32)],
        None,
        *space,
    )
    there[0] = after(there[0], out_space, full_weight)
    *out_time, probs_t, time_qkv = call(
        functools.partial(time_forward_kernel, groups),
        [(piece, BF16)] * groups + [((heads, rows, rows), F32), ((3,) + full, BF16)],
        [(full, F32)],
        None,
        *there,
    )
    pair, step_home, *steps = call(
        functools.partial(project_kernel, groups),
        [((2,) + full, BF16), (blocks, BF16)] + [(piece, BF16)] * groups,
        [(full, F32)],
        where,
        *exchange(out_time),
        out_space.reshape(blocks),
        target.reshape(blocks),
        full_weight,
    )
    scaling = 1.0 / math.sqrt(lax.axis_size("dp") * groups * rows)
    steps = exchange(steps)
    time_grads = call(
        functools.partial(time_backward_kernel, groups),
        [((3,) + piece, BF16)] * groups,
        [(full, BF16)] + [(full, F32)] * 3,
        None,
        *steps,
        time_qkv,
        probs_t,
    )
    if divides(width):
        weight_grad = weight_gradient(pair, time_grads[0], scaling, where)
    else:
        term = dot(pair[0], pair[1], TN).astype(BF16)
        share = lax.psum_scatter(term, "seq", scatter_dimension=0, tiled=True)
        weight_grad = lax.psum(share, "dp").astype(F32) * scaling
    space_grads = call(
        space_backward_kernel,
        [(full, BF16)] * 3,
        [(full, F32)] * 3,
        None,
        *space,
        after(step_home, time_grads[0]).reshape(full),
        probs_s,
    )
    back = exchange(time_grads)
    back[0] = after(back[0], weight_grad)
    back = call(unpack_kernel, [(blocks, BF16)] * 3, [], where, *back)
    outs = [item.reshape(q_space.shape) for item in list(space_grads) + list(back)]
    return tuple(outs) + (weight_grad,)


def solution(mesh):
    tokens = P("dp", "seq", None)
    return jax.shard_map(
        shards,
        mesh=mesh,
        in_specs=(tokens,) * 6 + (P("dp", None), tokens),
        out_specs=(tokens,) * 6 + (P("seq", None),),
        check_vma=False,
    )
```

time: 131 us -> 115 us (0.88)
  starting transfers between devices: 52 us -> 38.4 us
  other arithmetic: 8.02 us -> 0.08 us
  Pallas kernels: 16.3 us -> 23.4 us
  local copies, waits for them, and re-layouts: 6.02 us -> 4.44 us
    ppermute x33 -> x28, starting transfers between devices: 52 us -> 38.4 us  [swap(): return lax.ppermute(array, axis, [(i, i ^ bits) for i in range(size)])]
    pallas_call x6 -> x21, Pallas kernels: 16.3 us -> 23.4 us  [call(): pl.pallas_call(body, out_shape=tuple((jax.ShapeDtypeStruct(*out) for out...]
    another operation x13 -> x1, other arithmetic: 3.98 us -> 0.08 us  [shards(): where = jnp.stack([lax.axis_index('dp'), lax.axis_index('seq')])]
    dynamic_slice x3 -> x0, local copies, waits for them, and re-layouts: 2.41 us -> none  [block(): lax.dynamic_slice_in_dim(array, index * per_block, per_block, axis=-2)]
    reshape x3 -> x0, other arithmetic: 2.31 us -> none  [shards(): outs = [item.reshape(q_space.shape) for item in list(space_grads) + back]]
    unnamed x27 -> x16, local copies, waits for them, and re-layouts: 2.95 us -> 4.44 us
    ppermute x33 -> x28, waiting for transfers between devices: 47 us -> 46.7 us  [swap(): return lax.ppermute(array, axis, [(i, i ^ bits) for i in range(size)])]
  transfers between devices with their start and end apart: 33 -> 28, of which waited for: 14 -> 13; matrix products, arithmetic and copies ran while one was open for 3% -> 0% of each run, Pallas kernels for 11% -> 14%
where the time goes in v2:
time: 115 us; the launch traced here: 114 us
  waiting for transfers between devices  46.7 us (41%)
  starting transfers between devices  38.4 us (33%)
  Pallas kernels  23.4 us (20%)
  local copies, waits for them, and re-layouts  4.44 us (4%)
    ppermute x28, waiting for transfers between devices, swap(): return lax.ppermute(array, axis, [(i, i ^ bits) for i in range(size)])  46.7 us
    ppermute x28, starting transfers between devices, swap(): return lax.ppermute(array, axis, [(i, i ^ bits) for i in range(size)])  38.4 us
    pallas_call x21, Pallas kernels, call(): pl.pallas_call(body, out_shape=tuple((jax.ShapeDtypeStruct(*out) for out...  23.4 us
    unnamed x16, local copies, waits for them, and re-layouts  4.44 us
  transfers between devices with their start and end apart: 28, of which 13 were waited for; matrix products, arithmetic and copies ran while one was open for 0% of the time, Pallas kernels for 14%

profile of v2, /device:TPU:0, one launch (start us, length us, event | category | flops | bytes accessed | tf_op | source)
XLA Modules:
  0.0 113.8 jit_solution(7385667191541026563)
XLA Ops:
  0.6 0.1 pad_add_fusion.where_ref
  0.7 1.0 copy-done
  1.7 1.0 copy-done.1
  2.7 1.0 copy-done.2
  3.7 1.0 copy-done.7
  4.7 0.6 shard_map.135
  5.3 3.0 %collective-permute-start = (bf16[1,72,1152]{2,1,0:T(8,128)(2,1)S(1)}, bf16[1,72,1152]{2,1,0:T(8,128)(2,1)S(1)}, u32[]{:S(2)}, u32[]{:S(2)}) collective-permute-start(bf16[1,72,1152]{2,1,0:T(8,128)(2,1)S(1)} %get-tuple-element.55.refs_0_), channel_id=1, source_target_pairs={{0,8},{4,12},{8,0},{12,4},{16,24},{20,28},{24,16},{28,20},{1,9},{5... | collective-permute-start | bytes 497672 | tf_op jit(solution)/shard_map/ppermute | solution.py:246
  8.3 1.5 %collective-permute-start.3 = (bf16[1,72,1152]{2,1,0:T(8,128)(2,1)S(1)}, bf16[1,72,1152]{2,1,0:T(8,128)(2,1)S(1)}, u32[]{:S(2)}, u32[]{:S(2)}) collective-permute-start(bf16[1,72,1152]{2,1,0:T(8,128)(2,1)S(1)} %get-tuple-element.56.refs_0_), channel_id=1, source_target_pairs={{0,16},{4,20},{8,24},{12,28},{16,0},{20,4},{24,8},{28,12},{1,17},{... | collective-permute-start | bytes 497672 | tf_op jit(solution)/shard_map/ppermute | solution.py:246
  9.8 1.6 %collective-permute-start.6 = (bf16[3,40,1152]{2,1,0:T(8,128)(2,1)S(1)}, bf16[3,40,1152]{2,1,0:T(8,128)(2,1)S(1)}, u32[]{:S(2)}, u32[]{:S(2)}) collective-permute-start(bf16[3,40,1152]{2,1,0:T(8,128)(2,1)S(1)} %get-tuple-element.58), channel_id=1, source_target_pairs={{0,1},{1,0},{2,3},{3,2},{4,5},{5,4},{6,7},{7,6},{8,9},{9,8},{10,11... | collective-permute-start | bytes 829448 | tf_op jit(solution)/shard_map/ppermute | solution.py:246
  11.4 2.6 %collective-permute-start.7 = (bf16[3,40,1152]{2,1,0:T(8,128)(2,1)S(1)}, bf16[3,40,1152]{2,1,0:T(8,128)(2,1)S(1)}, u32[]{:S(2)}, u32[]{:S(2)}) collective-permute-start(bf16[3,40,1152]{2,1,0:T(8,128)(2,1)S(1)} %get-tuple-element.59), channel_id=1, source_target_pairs={{0,2},{1,3},{2,0},{3,1},{4,6},{5,7},{6,4},{7,5},{8,10},{9,11},{10,... | collective-permute-start | bytes 829448 | tf_op jit(solution)/shard_map/ppermute | solution.py:246
  14.0 0.2 collective-permute-start.8
  14.2 0.6 collective-permute-start.1
  14.8 1.1 %collective-permute-start.4 = (bf16[2,72,1152]{2,1,0:T(8,128)(2,1)S(1)}, bf16[2,72,1152]{2,1,0:T(8,128)(2,1)S(1)}, u32[]{:S(2)}, u32[]{:S(2)}) collective-permute-start(bf16[2,72,1152]{2,1,0:T(8,128)(2,1)S(1)} %shard_map.139.refs_0_), channel_id=1, source_target_pairs={{0,8},{4,12},{8,0},{12,4},{16,24},{20,28},{24,16},{28,20},{1,9},{5... | collective-permute-start | bytes 995336 | tf_op jit(solution)/shard_map/ppermute | solution.py:246
  16.0 6.5 %collective-permute-done.1.refs_1_ = bf16[2,72,1152]{2,1,0:T(8,128)(2,1)S(1)} collective-permute-done((bf16[2,72,1152]{2,1,0:T(8,128)(2,1)S(1)}, bf16[2,72,1152]{2,1,0:T(8,128)(2,1)S(1)}, u32[]{:S(2)}, u32[]{:S(2)}) %collective-permute-start.1) | collective-permute-done | bytes 331808 | tf_op jit(solution)/shard_map/ppermute | solution.py:246
  22.6 0.0 copy-start.5
  22.6 0.1 collective-permute-start.2
  22.7 0.2 collective-permute-done.4.refs_1_
  22.9 0.3 collective-permute-start.5
  23.3 0.3 copy-done.4
  23.6 0.1 copy-done.5
  23.7 0.1 copy-done.6
  23.8 1.9 %shard_map.136 = (bf16[160,1152]{1,0:T(8,128)(2,1)S(1)}, f32[16,160,160]{2,1,0:T(8,128)S(1)}) custom-call(bf16[160,1152]{1,0:T(8,128)(2,1)S(1)} %bitcast.24, bf16[160,1152]{1,0:T(8,128)(2,1)S(1)} %bitcast.26, bf16[160,1152]{1,0:T(8,128)(2,1)S(1)} %bitcast.28), custom_call_target="tpu_custom_call" | custom-call | flops 10000000000 | bytes 10 | tf_op jit(solution)/shard_map/pallas_call | solution.py:233
  25.7 0.0 collective-permute-done.5.refs_3_
  25.7 0.7 shard_map.141
  26.5 7.2 %collective-permute-done.7.refs_2_ = bf16[3,40,1152]{2,1,0:T(8,128)(2,1)S(1)} collective-permute-done((bf16[3,40,1152]{2,1,0:T(8,128)(2,1)S(1)}, bf16[3,40,1152]{2,1,0:T(8,128)(2,1)S(1)}, u32[]{:S(2)}, u32[]{:S(2)}) %collective-permute-start.7) | collective-permute-done | bytes 276512 | tf_op jit(solution)/shard_map/ppermute | solution.py:246
  33.7 2.0 %shard_map.142 = (bf16[40,1152]{1,0:T(8,128)(2,1)S(1)}, bf16[40,1152]{1,0:T(8,128)(2,1)S(1)}, bf16[40,1152]{1,0:T(8,128)(2,1)S(1)}, bf16[40,1152]{1,0:T(8,128)(2...) custom-call(bf16[3,40,1152]{2,1,0:T(8,128)(2,1)S(1)} %get-tuple-element.57.refs_0_, ...), custom_call_target="tpu_custom_call" | custom-call | flops 10000000000 | bytes 10 | tf_op jit(solution)/shard_map/pallas_call | solution.py:233
  35.7 4.6 %collective-permute-start.9 = (bf16[40,1152]{1,0:T(8,128)(2,1)S(1)}, bf16[40,1152]{1,0:T(8,128)(2,1)S(1)}, u32[]{:S(2)}, u32[]{:S(2)}) collective-permute-start(bf16[40,1152]{1,0:T(8,128)(2,1)S(1)} %get-tuple-element.62), channel_id=1, source_target_pairs={{0,1},{1,0},{2,3},{3,2},{4,5},{5,4},{6,7},{7,6},{8,9},{9,8},{10,11... | collective-permute-start | bytes 276488 | tf_op jit(solution)/shard_map/ppermute | solution.py:246
  40.2 1.1 collective-permute-start.10
  41.3 1.4 %collective-permute-start.11 = (bf16[40,1152]{1,0:T(8,128)(2,1)S(1)}, bf16[40,1152]{1,0:T(8,128)(2,1)S(1)}, u32[]{:S(2)}, u32[]{:S(2)}) collective-permute-start(bf16[40,1152]{1,0:T(8,128)(2,1)S(1)} %get-tuple-element.64), channel_id=1, source_target_pairs={{0,3},{1,2},{2,1},{3,0},{4,7},{5,6},{6,5},{7,4},{8,11},{9,10},{10,... | collective-permute-start | bytes 276488 | tf_op jit(solution)/shard_map/ppermute | solution.py:246
  42.7 0.8 collective-permute-done.9.refs_1_
  43.5 5.0 %collective-permute-done.10.refs_2_ = bf16[40,1152]{1,0:T(8,128)(2,1)S(1)} collective-permute-done((bf16[40,1152]{1,0:T(8,128)(2,1)S(1)}, bf16[40,1152]{1,0:T(8,128)(2,1)S(1)}, u32[]{:S(2)}, u32[]{:S(2)}) %collective-permute-start.10) | collective-permute-done | bytes 92192 | tf_op jit(solution)/shard_map/ppermute | solution.py:246
  48.5 2.1 %shard_map.143 = (bf16[2,160,1152]{2,1,0:T(8,128)(2,1)S(1)}, bf16[4,40,1152]{2,1,0:T(8,128)(2,1)S(1)}, bf16[40,1152]{1,0:T(8,128)(2,1)S(1)}, bf16[40,1152]{1,0:T...) custom-call(s32[2]{0:T(128)S(1)} %pad_add_fusion.where_ref, ...), custom_call_target="tpu_custom_call" | custom-call | flops 10000000000 | bytes 10 | tf_op jit(solution)/shard_map/pallas_call | solution.py:233
  50.6 0.1 collective-permute-start.15
  50.7 1.6 %collective-permute-start.12 = (bf16[40,1152]{1,0:T(8,128)(2,1)S(1)}, bf16[40,1152]{1,0:T(8,128)(2,1)S(1)}, u32[]{:S(2)}, u32[]{:S(2)}) collective-permute-start(bf16[40,1152]{1,0:T(8,128)(2,1)S(1)} %get-tuple-element.67), channel_id=1, source_target_pairs={{0,1},{1,0},{2,3},{3,2},{4,5},{5,4},{6,7},{7,6},{8,9},{9,8},{10,11... | collective-permute-start | bytes 276488 | tf_op jit(solution)/shard_map/ppermute | solution.py:246
  52.3 1.3 %collective-permute-start.13 = (bf16[40,1152]{1,0:T(8,128)(2,1)S(1)}, bf16[40,1152]{1,0:T(8,128)(2,1)S(1)}, u32[]{:S(2)}, u32[]{:S(2)}) collective-permute-start(bf16[40,1152]{1,0:T(8,128)(2,1)S(1)} %get-tuple-element.68), channel_id=1, source_target_pairs={{0,2},{1,3},{2,0},{3,1},{4,6},{5,7},{6,4},{7,5},{8,10},{9,11},{10,... | collective-permute-start | bytes 276488 | tf_op jit(solution)/shard_map/ppermute | solution.py:246
  53.6 1.5 %collective-permute-start.14 = (bf16[40,1152]{1,0:T(8,128)(2,1)S(1)}, bf16[40,1152]{1,0:T(8,128)(2,1)S(1)}, u32[]{:S(2)}, u32[]{:S(2)}) collective-permute-start(bf16[40,1152]{1,0:T(8,128)(2,1)S(1)} %get-tuple-element.69), channel_id=1, source_target_pairs={{0,3},{1,2},{2,1},{3,0},{4,7},{5,6},{6,5},{7,4},{8,11},{9,10},{10,... | collective-permute-start | bytes 276488 | tf_op jit(solution)/shard_map/ppermute | solution.py:246
  55.1 1.8 %shard_map.146 = (f32[2,2,72,640]{3,2,1,0:T(8,128)S(1)}, bf16[2,2,72,640]{3,2,1,0:T(8,128)(2,1)S(1)}, f32[2,2,72,640]{3,2,1,0:T(8,128)S(1)}, bf16[2,2,72,640]{3,2,1,0:T(8,128)(2,1)S(1)}) custom-call(s32[2]{0:T(128)S(1)} %pad_add_fusion.where_ref, bf16[2,160,1152]{2,1,0:T(8,128)(2,1)S(1)} %get-tuple-element.78.mine_ref, ...), custom_call_target="tpu_custom_call" | custom-call | flops 10000000000 | bytes 10 | tf_op jit(solution)/shard_map/pallas_call | solution.py:233
  57.0 0.6 collective-permute-start.16
  57.5 0.5 collective-permute-start.18
  58.1 4.6 %collective-permute-done.13.refs_2_ = bf16[40,1152]{1,0:T(8,128)(2,1)S(1)} collective-permute-done((bf16[40,1152]{1,0:T(8,128)(2,1)S(1)}, bf16[40,1152]{1,0:T(8,128)(2,1)S(1)}, u32[]{:S(2)}, u32[]{:S(2)}) %collective-permute-start.13) | collective-permute-done | bytes 92192 | tf_op jit(solution)/shard_map/ppermute | solution.py:246
  62.6 4.4 %shard_map.144 = (bf16[3,40,1152]{2,1,0:T(8,128)(2,1)S(1)}, bf16[3,40,1152]{2,1,0:T(8,128)(2,1)S(1)}, bf16[3,40,1152]{2,1,0:T(8,128)(2,1)S(1)}, bf16[3,40,1152]{2,1,0:T(8,128)(2,1)S(1)}) custom-call(bf16[40,1152]{1,0:T(8,128)(2,1)S(1)} %get-tuple-element.66.refs_0_, bf16[40,1152]{1,0:T(8,128)(2,1)S(1)} %collective-permute-done.12.refs_1_, ...), custom_call_target="tpu_custom_call" | custom-call | flops 10000000000 | bytes 10 | tf_op jit(solution)/shard_map/pallas_call | solution.py:233
  67.0 0.1 collective-permute-done.16.came_ref
  67.1 0.1 shard_map.147
  67.2 0.6 collective-permute-start.17
  67.8 0.1 shard_map.148
  67.8 1.1 %collective-permute-start.19 = (bf16[1,2,72,640]{3,2,1,0:T(8,128)(2,1)S(1)}, bf16[1,2,72,640]{3,2,1,0:T(8,128)(2,1)S(1)}, u32[]{:S(2)}, u32[]{:S(2)}) collective-permute-start(bf16[1,2,72,640]{3,2,1,0:T(8,128)(2,1)S(1)} %get-tuple-element.87), channel_id=1, source_target_pairs={{0,8},{4,12},{8,0},{12,4},{16,24},{20,28},{24,16},{28,20},{1,9},{5... | collective-permute-start | bytes 552968 | tf_op jit(solution)/shard_map/ppermute | solution.py:246
  69.0 3.8 %collective-permute-done.17.refs_1_ = bf16[1,2,72,640]{3,2,1,0:T(8,128)(2,1)S(1)} collective-permute-done((bf16[1,2,72,640]{3,2,1,0:T(8,128)(2,1)S(1)}, bf16[1,2,72,640]{3,2,1,0:T(8,128)(2,1)S(1)}, u32[]{:S(2)}, u32[]{:S(2)}) %collective-permute-start.17) | collective-permute-done | bytes 184352 | tf_op jit(solution)/shard_map/ppermute | solution.py:246
  72.8 0.6 collective-permute-done.19.refs_3_
  73.5 0.7 shard_map.149
  74.1 1.8 %collective-permute-start.20 = (bf16[2,72,640]{2,1,0:T(8,128)(2,1)S(1)}, bf16[2,72,640]{2,1,0:T(8,128)(2,1)S(1)}, u32[]{:S(2)}, u32[]{:S(2)}) collective-permute-start(bf16[2,72,640]{2,1,0:T(8,128)(2,1)S(1)} %get-tuple-element.89), channel_id=1, source_target_pairs={{0,1},{1,0},{2,3},{3,2},{4,5},{5,4},{6,7},{7,6},{8,9},{9,8},{10,11... | collective-permute-start | bytes 552968 | tf_op jit(solution)/shard_map/ppermute | solution.py:246
  75.9 3.8 %collective-permute-done.20.came_ref = bf16[2,72,640]{2,1,0:T(8,128)(2,1)S(1)} collective-permute-done((bf16[2,72,640]{2,1,0:T(8,128)(2,1)S(1)}, bf16[2,72,640]{2,1,0:T(8,128)(2,1)S(1)}, u32[]{:S(2)}, u32[]{:S(2)}) %collective-permute-start.20) | collective-permute-done | bytes 184352 | tf_op jit(solution)/shard_map/ppermute | solution.py:246
  79.8 3.2 %collective-permute-start.21 = (bf16[1,72,640]{2,1,0:T(8,128)(2,1)S(1)}, bf16[1,72,640]{2,1,0:T(8,128)(2,1)S(1)}, u32[]{:S(2)}, u32[]{:S(2)}) collective-permute-start(bf16[1,72,640]{2,1,0:T(8,128)(2,1)S(1)} %get-tuple-element.91), channel_id=1, source_target_pairs={{0,2},{1,3},{2,0},{3,1},{4,6},{5,7},{6,4},{7,5},{8,10},{9,11},{10,... | collective-permute-start | bytes 276488 | tf_op jit(solution)/shard_map/ppermute | solution.py:246
  82.9 2.5 %collective-permute-done.21.came_ref = bf16[1,72,640]{2,1,0:T(8,128)(2,1)S(1)} collective-permute-done((bf16[1,72,640]{2,1,0:T(8,128)(2,1)S(1)}, bf16[1,72,640]{2,1,0:T(8,128)(2,1)S(1)}, u32[]{:S(2)}, u32[]{:S(2)}) %collective-permute-start.21) | collective-permute-done | bytes 92192 | tf_op jit(solution)/shard_map/ppermute | solution.py:246
  85.5 1.9 %collective-permute-start.22 = (bf16[1,72,640]{2,1,0:T(8,128)(2,1)S(1)}, bf16[1,72,640]{2,1,0:T(8,128)(2,1)S(1)}, u32[]{:S(2)}, u32[]{:S(2)}) collective-permute-start(bf16[1,72,640]{2,1,0:T(8,128)(2,1)S(1)} %shard_map.151.refs_0_), channel_id=1, source_target_pairs={{0,8},{4,12},{8,0},{12,4},{16,24},{20,28},{24,16},{28,20},{1,9},{5... | collective-permute-start | bytes 276488 | tf_op jit(solution)/shard_map/ppermute | solution.py:246
  87.4 2.7 %collective-permute-done.22.refs_1_ = bf16[1,72,640]{2,1,0:T(8,128)(2,1)S(1)} collective-permute-done((bf16[1,72,640]{2,1,0:T(8,128)(2,1)S(1)}, bf16[1,72,640]{2,1,0:T(8,128)(2,1)S(1)}, u32[]{:S(2)}, u32[]{:S(2)}) %collective-permute-start.22) | collective-permute-done | bytes 92192 | tf_op jit(solution)/shard_map/ppermute | solution.py:246
  90.1 1.6 %collective-permute-start.23 = (bf16[2,72,640]{2,1,0:T(8,128)(2,1)S(1)}, bf16[2,72,640]{2,1,0:T(8,128)(2,1)S(1)}, u32[]{:S(2)}, u32[]{:S(2)}) collective-permute-start(bf16[2,72,640]{2,1,0:T(8,128)(2,1)S(1)} %shard_map.152.refs_0_), channel_id=1, source_target_pairs={{0,16},{4,20},{8,24},{12,28},{16,0},{20,4},{24,8},{28,12},{1,17},{... | collective-permute-start | bytes 552968 | tf_op jit(solution)/shard_map/ppermute | solution.py:246
  91.8 1.5 %collective-permute-start.25 = (bf16[3,40,1152]{2,1,0:T(8,128)(2,1)S(1)}, bf16[3,40,1152]{2,1,0:T(8,128)(2,1)S(1)}, u32[]{:S(2)}, u32[]{:S(2)}) collective-permute-start(bf16[3,40,1152]{2,1,0:T(8,128)(2,1)S(1)} %get-tuple-element.93), channel_id=1, source_target_pairs={{0,1},{1,0},{2,3},{3,2},{4,5},{5,4},{6,7},{7,6},{8,9},{9,8},{10,11... | collective-permute-start | bytes 829448 | tf_op jit(solution)/shard_map/ppermute | solution.py:246
  93.3 1.4 %collective-permute-start.26 = (bf16[3,40,1152]{2,1,0:T(8,128)(2,1)S(1)}, bf16[3,40,1152]{2,1,0:T(8,128)(2,1)S(1)}, u32[]{:S(2)}, u32[]{:S(2)}) collective-permute-start(bf16[3,40,1152]{2,1,0:T(8,128)(2,1)S(1)} %get-tuple-element.94), channel_id=1, source_target_pairs={{0,2},{1,3},{2,0},{3,1},{4,6},{5,7},{6,4},{7,5},{8,10},{9,11},{10,... | collective-permute-start | bytes 829448 | tf_op jit(solution)/shard_map/ppermute | solution.py:246
  94.7 1.5 %collective-permute-start.27 = (bf16[3,40,1152]{2,1,0:T(8,128)(2,1)S(1)}, bf16[3,40,1152]{2,1,0:T(8,128)(2,1)S(1)}, u32[]{:S(2)}, u32[]{:S(2)}) collective-permute-start(bf16[3,40,1152]{2,1,0:T(8,128)(2,1)S(1)} %get-tuple-element.95), channel_id=1, source_target_pairs={{0,3},{1,2},{2,1},{3,0},{4,7},{5,6},{6,5},{7,4},{8,11},{9,10},{10,... | collective-permute-start | bytes 829448 | tf_op jit(solution)/shard_map/ppermute | solution.py:246
  96.2 0.1 collective-permute-start.24
  96.3 5.4 %shard_map.145 = (bf16[160,1152]{1,0:T(8,128)(2,1)}, bf16[160,1152]{1,0:T(8,128)(2,1)}, bf16[160,1152]{1,0:T(8,128)(2,1)}) custom-call(bf16[160,1152]{1,0:T(8,128)(2,1)S(1)} %bitcast.25, bf16[160,1152]{1,0:T(8,128)(2,1)S(1)} %bitcast.27, bf16[160,1152]{1,0:T(8,128)(2,1)S(1)} %bitcast.29, bf16[160,1152]{1,0:T(8,128)(2,1)S(1)} %bitcast.32, ...), custom_call_target="tpu_custom_call" | custom-call | flops 10000000000 | bytes 10 | tf_op jit(solution)/shard_map/pallas_call | solution.py:233
  101.7 1.8 %shard_map.154 = f32[4,72,1152]{2,1,0:T(8,128)} custom-call(s32[2]{0:T(128)S(1)} %pad_add_fusion.where_ref, bf16[4,72,640]{2,1,0:T(8,128)(2,1)S(1)} %shard_map.153.mine_ref, bf16[4,72,640]{2,1,0:T(8,128)(2,1)S(1)} %collective-permute-done.24.other_ref), custom_call_target="tpu_custom_call" | custom-call | flops 10 | bytes 10 | tf_op jit(solution)/shard_map/pallas_call | solution.py:233
  103.5 8.7 %collective-permute-done.26.refs_2_ = bf16[3,40,1152]{2,1,0:T(8,128)(2,1)S(1)} collective-permute-done((bf16[3,40,1152]{2,1,0:T(8,128)(2,1)S(1)}, bf16[3,40,1152]{2,1,0:T(8,128)(2,1)S(1)}, u32[]{:S(2)}, u32[]{:S(2)}) %collective-permute-start.26) | collective-permute-done | bytes 276512 | tf_op jit(solution)/shard_map/ppermute | solution.py:246
  112.2 1.6 %shard_map.155 = (bf16[4,40,1152]{2,1,0:T(8,128)(2,1)}, bf16[4,40,1152]{2,1,0:T(8,128)(2,1)}, bf16[4,40,1152]{2,1,0:T(8,128)(2,1)}) custom-call(s32[2]{0:T(128)S(1)} %pad_add_fusion.where_ref, bf16[3,40,1152]{2,1,0:T(8,128)(2,1)S(1)} %get-tuple-element.92.refs_0_, bf16[3,40,1152]{2,1,0:T(8,128)(2,1)S(1)} %collective-permute-done.25.refs_1_, ...), custom_call_target="tpu_custom_call" | custom-call | flops 10000000000 | bytes 10 | tf_op jit(solution)/shard_map/pallas_call | solution.py:233
  (30 shorter events, 0.3 us)
Async XLA Ops:
  0.7 1.0 copy-start
  1.7 1.0 copy-start.1
  2.7 1.0 copy-start.2
  3.7 1.0 copy-start.7
  5.3 8.9 %collective-permute-start = (bf16[1,72,1152]{2,1,0:T(8,128)(2,1)S(1)}, bf16[1,72,1152]{2,1,0:T(8,128)(2,1)S(1)}, u32[]{:S(2)}, u32[]{:S(2)}) collective-permute-start(bf16[1,72,1152]{2,1,0:T(8,128)(2,1)S(1)} %get-tuple-element.55.refs_0_), channel_id=1, source_target_pairs={{0,8},{4,12},{8,0},{12,4},{16,24},{20,28},{24,16},{28,20},{1,9},{5... | collective-permute-start | bytes 497672 | tf_op jit(solution)/shard_map/ppermute | solution.py:246
  8.3 6.5 %collective-permute-start.3 = (bf16[1,72,1152]{2,1,0:T(8,128)(2,1)S(1)}, bf16[1,72,1152]{2,1,0:T(8,128)(2,1)S(1)}, u32[]{:S(2)}, u32[]{:S(2)}) collective-permute-start(bf16[1,72,1152]{2,1,0:T(8,128)(2,1)S(1)} %get-tuple-element.56.refs_0_), channel_id=1, source_target_pairs={{0,16},{4,20},{8,24},{12,28},{16,0},{20,4},{24,8},{28,12},{1,17},{... | collective-permute-start | bytes 497672 | tf_op jit(solution)/shard_map/ppermute | solution.py:246
  9.8 16.7 %collective-permute-start.6 = (bf16[3,40,1152]{2,1,0:T(8,128)(2,1)S(1)}, bf16[3,40,1152]{2,1,0:T(8,128)(2,1)S(1)}, u32[]{:S(2)}, u32[]{:S(2)}) collective-permute-start(bf16[3,40,1152]{2,1,0:T(8,128)(2,1)S(1)} %get-tuple-element.58), channel_id=1, source_target_pairs={{0,1},{1,0},{2,3},{3,2},{4,5},{5,4},{6,7},{7,6},{8,9},{9,8},{10,11... | collective-permute-start | bytes 829448 | tf_op jit(solution)/shard_map/ppermute | solution.py:246
  11.4 22.3 %collective-permute-start.7 = (bf16[3,40,1152]{2,1,0:T(8,128)(2,1)S(1)}, bf16[3,40,1152]{2,1,0:T(8,128)(2,1)S(1)}, u32[]{:S(2)}, u32[]{:S(2)}) collective-permute-start(bf16[3,40,1152]{2,1,0:T(8,128)(2,1)S(1)} %get-tuple-element.59), channel_id=1, source_target_pairs={{0,2},{1,3},{2,0},{3,1},{4,6},{5,7},{6,4},{7,5},{8,10},{9,11},{10,... | collective-permute-start | bytes 829448 | tf_op jit(solution)/shard_map/ppermute | solution.py:246
  14.0 19.7 %collective-permute-start.8 = (bf16[3,40,1152]{2,1,0:T(8,128)(2,1)S(1)}, bf16[3,40,1152]{2,1,0:T(8,128)(2,1)S(1)}, u32[]{:S(2)}, u32[]{:S(2)}) collective-permute-start(bf16[3,40,1152]{2,1,0:T(8,128)(2,1)S(1)} %get-tuple-element.60), channel_id=1, source_target_pairs={{0,3},{1,2},{2,1},{3,0},{4,7},{5,6},{6,5},{7,4},{8,11},{9,10},{10,... | collective-permute-start | bytes 829448 | tf_op jit(solution)/shard_map/ppermute | solution.py:246
  14.2 8.3 %collective-permute-start.1 = (bf16[2,72,1152]{2,1,0:T(8,128)(2,1)S(1)}, bf16[2,72,1152]{2,1,0:T(8,128)(2,1)S(1)}, u32[]{:S(2)}, u32[]{:S(2)}) collective-permute-start(bf16[2,72,1152]{2,1,0:T(8,128)(2,1)S(1)} %shard_map.137.refs_0_), channel_id=1, source_target_pairs={{0,16},{4,20},{8,24},{12,28},{16,0},{20,4},{24,8},{28,12},{1,17},{... | collective-permute-start | bytes 995336 | tf_op jit(solution)/shard_map/ppermute | solution.py:246
  14.8 8.0 %collective-permute-start.4 = (bf16[2,72,1152]{2,1,0:T(8,128)(2,1)S(1)}, bf16[2,72,1152]{2,1,0:T(8,128)(2,1)S(1)}, u32[]{:S(2)}, u32[]{:S(2)}) collective-permute-start(bf16[2,72,1152]{2,1,0:T(8,128)(2,1)S(1)} %shard_map.139.refs_0_), channel_id=1, source_target_pairs={{0,8},{4,12},{8,0},{12,4},{16,24},{20,28},{24,16},{28,20},{1,9},{5... | collective-permute-start | bytes 995336 | tf_op jit(solution)/shard_map/ppermute | solution.py:246
  22.6 1.0 copy-start.4
  22.6 1.1 copy-start.5
  22.6 1.2 %copy-start.6 = (bf16[1,160,1152]{2,1,0:T(8,128)(2,1)S(1)}, bf16[1,160,1152]{2,1,0:T(8,128)(2,1)}, u32[]{:S(2)}) copy-start(bf16[1,160,1152]{2,1,0:T(8,128)(2,1)} %param.10) | copy-start | bytes 1105924
  22.6 3.1 %collective-permute-start.2 = (bf16[4,72,1152]{2,1,0:T(8,128)(2,1)S(1)}, bf16[4,72,1152]{2,1,0:T(8,128)(2,1)S(1)}, u32[]{:S(2)}, u32[]{:S(2)}) collective-permute-start(bf16[4,72,1152]{2,1,0:T(8,128)(2,1)S(1)} %shard_map.138.refs_0_), channel_id=1, source_target_pairs={{0,4},{4,0},{8,12},{12,8},{16,20},{20,16},{24,28},{28,24},{1,5},{5... | collective-permute-start | bytes 1990664 | tf_op jit(solution)/shard_map/ppermute | solution.py:246
  22.9 2.8 %collective-permute-start.5 = (bf16[4,72,1152]{2,1,0:T(8,128)(2,1)S(1)}, bf16[4,72,1152]{2,1,0:T(8,128)(2,1)S(1)}, u32[]{:S(2)}, u32[]{:S(2)}) collective-permute-start(bf16[4,72,1152]{2,1,0:T(8,128)(2,1)S(1)} %shard_map.140.refs_2_), channel_id=1, source_target_pairs={{0,4},{4,0},{8,12},{12,8},{16,20},{20,16},{24,28},{28,24},{1,5},{5... | collective-permute-start | bytes 1990664 | tf_op jit(solution)/shard_map/ppermute | solution.py:246
  26.5 22.0 %copy-start.3 = (bf16[1,160,1152]{2,1,0:T(8,128)(2,1)S(1)}, bf16[1,160,1152]{2,1,0:T(8,128)(2,1)}, u32[]{:S(2)}) copy-start(bf16[1,160,1152]{2,1,0:T(8,128)(2,1)} %param.15) | copy-start | bytes 1105924
  35.7 7.8 %collective-permute-start.9 = (bf16[40,1152]{1,0:T(8,128)(2,1)S(1)}, bf16[40,1152]{1,0:T(8,128)(2,1)S(1)}, u32[]{:S(2)}, u32[]{:S(2)}) collective-permute-start(bf16[40,1152]{1,0:T(8,128)(2,1)S(1)} %get-tuple-element.62), channel_id=1, source_target_pairs={{0,1},{1,0},{2,3},{3,2},{4,5},{5,4},{6,7},{7,6},{8,9},{9,8},{10,11... | collective-permute-start | bytes 276488 | tf_op jit(solution)/shard_map/ppermute | solution.py:246
  40.2 8.2 %collective-permute-start.10 = (bf16[40,1152]{1,0:T(8,128)(2,1)S(1)}, bf16[40,1152]{1,0:T(8,128)(2,1)S(1)}, u32[]{:S(2)}, u32[]{:S(2)}) collective-permute-start(bf16[40,1152]{1,0:T(8,128)(2,1)S(1)} %get-tuple-element.63), channel_id=1, source_target_pairs={{0,2},{1,3},{2,0},{3,1},{4,6},{5,7},{6,4},{7,5},{8,10},{9,11},{10,... | collective-permute-start | bytes 276488 | tf_op jit(solution)/shard_map/ppermute | solution.py:246
  41.3 7.2 %collective-permute-start.11 = (bf16[40,1152]{1,0:T(8,128)(2,1)S(1)}, bf16[40,1152]{1,0:T(8,128)(2,1)S(1)}, u32[]{:S(2)}, u32[]{:S(2)}) collective-permute-start(bf16[40,1152]{1,0:T(8,128)(2,1)S(1)} %get-tuple-element.64), channel_id=1, source_target_pairs={{0,3},{1,2},{2,1},{3,0},{4,7},{5,6},{6,5},{7,4},{8,11},{9,10},{10,... | collective-permute-start | bytes 276488 | tf_op jit(solution)/shard_map/ppermute | solution.py:246
  50.6 4.5 %collective-permute-start.15 = (bf16[2,160,1152]{2,1,0:T(8,128)(2,1)S(1)}, bf16[2,160,1152]{2,1,0:T(8,128)(2,1)S(1)}, u32[]{:S(2)}, u32[]{:S(2)}) collective-permute-start(bf16[2,160,1152]{2,1,0:T(8,128)(2,1)S(1)} %get-tuple-element.78.mine_ref), channel_id=1, source_target_pairs={{0,4},{4,0},{8,12},{12,8},{16,20},{20,16},{24,28},{28,24},{1,5},{5... | collective-permute-start | bytes 2211848 | tf_op jit(solution)/shard_map/ppermute | solution.py:246
  50.7 7.4 %collective-permute-start.12 = (bf16[40,1152]{1,0:T(8,128)(2,1)S(1)}, bf16[40,1152]{1,0:T(8,128)(2,1)S(1)}, u32[]{:S(2)}, u32[]{:S(2)}) collective-permute-start(bf16[40,1152]{1,0:T(8,128)(2,1)S(1)} %get-tuple-element.67), channel_id=1, source_target_pairs={{0,1},{1,0},{2,3},{3,2},{4,5},{5,4},{6,7},{7,6},{8,9},{9,8},{10,11... | collective-permute-start | bytes 276488 | tf_op jit(solution)/shard_map/ppermute | solution.py:246
  52.3 10.4 %collective-permute-start.13 = (bf16[40,1152]{1,0:T(8,128)(2,1)S(1)}, bf16[40,1152]{1,0:T(8,128)(2,1)S(1)}, u32[]{:S(2)}, u32[]{:S(2)}) collective-permute-start(bf16[40,1152]{1,0:T(8,128)(2,1)S(1)} %get-tuple-element.68), channel_id=1, source_target_pairs={{0,2},{1,3},{2,0},{3,1},{4,6},{5,7},{6,4},{7,5},{8,10},{9,11},{10,... | collective-permute-start | bytes 276488 | tf_op jit(solution)/shard_map/ppermute | solution.py:246
  53.6 9.0 %collective-permute-start.14 = (bf16[40,1152]{1,0:T(8,128)(2,1)S(1)}, bf16[40,1152]{1,0:T(8,128)(2,1)S(1)}, u32[]{:S(2)}, u32[]{:S(2)}) collective-permute-start(bf16[40,1152]{1,0:T(8,128)(2,1)S(1)} %get-tuple-element.69), channel_id=1, source_target_pairs={{0,3},{1,2},{2,1},{3,0},{4,7},{5,6},{6,5},{7,4},{8,11},{9,10},{10,... | collective-permute-start | bytes 276488 | tf_op jit(solution)/shard_map/ppermute | solution.py:246
  57.0 10.2 %collective-permute-start.16 = (bf16[2,2,72,640]{3,2,1,0:T(8,128)(2,1)S(1)}, bf16[2,2,72,640]{3,2,1,0:T(8,128)(2,1)S(1)}, u32[]{:S(2)}, u32[]{:S(2)}) collective-permute-start(bf16[2,2,72,640]{3,2,1,0:T(8,128)(2,1)S(1)} %get-tuple-element.81), channel_id=1, source_target_pairs={{0,8},{4,12},{8,0},{12,4},{16,24},{20,28},{24,16},{28,20},{1,9},{5... | collective-permute-start | bytes 1105928 | tf_op jit(solution)/shard_map/ppermute | solution.py:246
  57.5 10.2 %collective-permute-start.18 = (bf16[2,2,72,640]{3,2,1,0:T(8,128)(2,1)S(1)}, bf16[2,2,72,640]{3,2,1,0:T(8,128)(2,1)S(1)}, u32[]{:S(2)}, u32[]{:S(2)}) collective-permute-start(bf16[2,2,72,640]{3,2,1,0:T(8,128)(2,1)S(1)} %get-tuple-element.85), channel_id=1, source_target_pairs={{0,16},{4,20},{8,24},{12,28},{16,0},{20,4},{24,8},{28,12},{1,17},{... | collective-permute-start | bytes 1105928 | tf_op jit(solution)/shard_map/ppermute | solution.py:246
  67.2 5.6 %collective-permute-start.17 = (bf16[1,2,72,640]{3,2,1,0:T(8,128)(2,1)S(1)}, bf16[1,2,72,640]{3,2,1,0:T(8,128)(2,1)S(1)}, u32[]{:S(2)}, u32[]{:S(2)}) collective-permute-start(bf16[1,2,72,640]{3,2,1,0:T(8,128)(2,1)S(1)} %get-tuple-element.83), channel_id=1, source_target_pairs={{0,16},{4,20},{8,24},{12,28},{16,0},{20,4},{24,8},{28,12},{1,17},{... | collective-permute-start | bytes 552968 | tf_op jit(solution)/shard_map/ppermute | solution.py:246
  67.8 5.6 %collective-permute-start.19 = (bf16[1,2,72,640]{3,2,1,0:T(8,128)(2,1)S(1)}, bf16[1,2,72,640]{3,2,1,0:T(8,128)(2,1)S(1)}, u32[]{:S(2)}, u32[]{:S(2)}) collective-permute-start(bf16[1,2,72,640]{3,2,1,0:T(8,128)(2,1)S(1)} %get-tuple-element.87), channel_id=1, source_target_pairs={{0,8},{4,12},{8,0},{12,4},{16,24},{20,28},{24,16},{28,20},{1,9},{5... | collective-permute-start | bytes 552968 | tf_op jit(solution)/shard_map/ppermute | solution.py:246
  74.1 5.6 %collective-permute-start.20 = (bf16[2,72,640]{2,1,0:T(8,128)(2,1)S(1)}, bf16[2,72,640]{2,1,0:T(8,128)(2,1)S(1)}, u32[]{:S(2)}, u32[]{:S(2)}) collective-permute-start(bf16[2,72,640]{2,1,0:T(8,128)(2,1)S(1)} %get-tuple-element.89), channel_id=1, source_target_pairs={{0,1},{1,0},{2,3},{3,2},{4,5},{5,4},{6,7},{7,6},{8,9},{9,8},{10,11... | collective-permute-start | bytes 552968 | tf_op jit(solution)/shard_map/ppermute | solution.py:246
  79.8 5.7 %collective-permute-start.21 = (bf16[1,72,640]{2,1,0:T(8,128)(2,1)S(1)}, bf16[1,72,640]{2,1,0:T(8,128)(2,1)S(1)}, u32[]{:S(2)}, u32[]{:S(2)}) collective-permute-start(bf16[1,72,640]{2,1,0:T(8,128)(2,1)S(1)} %get-tuple-element.91), channel_id=1, source_target_pairs={{0,2},{1,3},{2,0},{3,1},{4,6},{5,7},{6,4},{7,5},{8,10},{9,11},{10,... | collective-permute-start | bytes 276488 | tf_op jit(solution)/shard_map/ppermute | solution.py:246
  85.5 4.6 %collective-permute-start.22 = (bf16[1,72,640]{2,1,0:T(8,128)(2,1)S(1)}, bf16[1,72,640]{2,1,0:T(8,128)(2,1)S(1)}, u32[]{:S(2)}, u32[]{:S(2)}) collective-permute-start(bf16[1,72,640]{2,1,0:T(8,128)(2,1)S(1)} %shard_map.151.refs_0_), channel_id=1, source_target_pairs={{0,8},{4,12},{8,0},{12,4},{16,24},{20,28},{24,16},{28,20},{1,9},{5... | collective-permute-start | bytes 276488 | tf_op jit(solution)/shard_map/ppermute | solution.py:246
  90.1 6.0 %collective-permute-start.23 = (bf16[2,72,640]{2,1,0:T(8,128)(2,1)S(1)}, bf16[2,72,640]{2,1,0:T(8,128)(2,1)S(1)}, u32[]{:S(2)}, u32[]{:S(2)}) collective-permute-start(bf16[2,72,640]{2,1,0:T(8,128)(2,1)S(1)} %shard_map.152.refs_0_), channel_id=1, source_target_pairs={{0,16},{4,20},{8,24},{12,28},{16,0},{20,4},{24,8},{28,12},{1,17},{... | collective-permute-start | bytes 552968 | tf_op jit(solution)/shard_map/ppermute | solution.py:246
  91.8 11.7 %collective-permute-start.25 = (bf16[3,40,1152]{2,1,0:T(8,128)(2,1)S(1)}, bf16[3,40,1152]{2,1,0:T(8,128)(2,1)S(1)}, u32[]{:S(2)}, u32[]{:S(2)}) collective-permute-start(bf16[3,40,1152]{2,1,0:T(8,128)(2,1)S(1)} %get-tuple-element.93), channel_id=1, source_target_pairs={{0,1},{1,0},{2,3},{3,2},{4,5},{5,4},{6,7},{7,6},{8,9},{9,8},{10,11... | collective-permute-start | bytes 829448 | tf_op jit(solution)/shard_map/ppermute | solution.py:246
  93.3 18.9 %collective-permute-start.26 = (bf16[3,40,1152]{2,1,0:T(8,128)(2,1)S(1)}, bf16[3,40,1152]{2,1,0:T(8,128)(2,1)S(1)}, u32[]{:S(2)}, u32[]{:S(2)}) collective-permute-start(bf16[3,40,1152]{2,1,0:T(8,128)(2,1)S(1)} %get-tuple-element.94), channel_id=1, source_target_pairs={{0,2},{1,3},{2,0},{3,1},{4,6},{5,7},{6,4},{7,5},{8,10},{9,11},{10,... | collective-permute-start | bytes 829448 | tf_op jit(solution)/shard_map/ppermute | solution.py:246
  94.7 17.5 %collective-permute-start.27 = (bf16[3,40,1152]{2,1,0:T(8,128)(2,1)S(1)}, bf16[3,40,1152]{2,1,0:T(8,128)(2,1)S(1)}, u32[]{:S(2)}, u32[]{:S(2)}) collective-permute-start(bf16[3,40,1152]{2,1,0:T(8,128)(2,1)S(1)} %get-tuple-element.95), channel_id=1, source_target_pairs={{0,3},{1,2},{2,1},{3,0},{4,7},{5,6},{6,5},{7,4},{8,11},{9,10},{10,... | collective-permute-start | bytes 829448 | tf_op jit(solution)/shard_map/ppermute | solution.py:246
  96.2 5.5 %collective-permute-start.24 = (bf16[4,72,640]{2,1,0:T(8,128)(2,1)S(1)}, bf16[4,72,640]{2,1,0:T(8,128)(2,1)S(1)}, u32[]{:S(2)}, u32[]{:S(2)}) collective-permute-start(bf16[4,72,640]{2,1,0:T(8,128)(2,1)S(1)} %shard_map.153.mine_ref), channel_id=1, source_target_pairs={{0,4},{4,0},{8,12},{12,8},{16,20},{20,16},{24,28},{28,24},{1,5},{5... | collective-permute-start | bytes 1105928 | tf_op jit(solution)/shard_map/ppermute | solution.py:246

commit v3 on v2

--- a/solution.py
+++ b/solution.py
@@ -91,14 +91,16 @@
     dv_ref[...] = sums[2][...].astype(BF16)
 
 
-def pack_kernel(count, where_ref, *refs):
-    groups = refs[0].shape[0]
-    refs, (weight_ref, low_ref, high_ref) = refs[:count] + refs[count + 1 : -2], (refs[count],) + refs[-2:]
+def pack_kernel(first, where_ref, *refs):
+    count = refs[-1].shape[0]
+    for i, piece_ref in enumerate(refs[count:]):
+        for j, array_ref in enumerate(refs[:count]):
+            piece_ref[j] = array_ref[where_ref[1] ^ (first + i)]
+
+
+def halves_kernel(weight_ref, low_ref, high_ref):
     low_ref[...] = weight_ref[:1]
     high_ref[...] = weight_ref[1:]
-    for i in range(groups):
-        for j in range(count):
-            refs[count + i][j] = refs[j][where_ref[1] ^ i]
 
 
 def unpack_kernel(where_ref, *refs):
@@ -250,24 +252,27 @@
     return lax.optimization_barrier((value,) + others)[0]
 
 
-def stack(left, right):
+def stack(left, right, cost=COST):
     shape = (2 * left.shape[0],) + left.shape[1:]
-    return call(stack_kernel, [(shape, BF16)], [], None, left, right)[0]
-
-
-def doubled(held, bits):
+    return call(stack_kernel, [(shape, BF16)], [], None, left, right, cost=cost)[0]
+
+
+def doubled(held, bits, earlier, last=False):
     order = [0]
     for bit in bits:
-        held = stack(held, swap(held, "dp", 2 * bit))
+        came = swap(held, "dp", 2 * bit)
+        if bit == bits[-1 if last else 0] and not last:
+            held = after(held, earlier)
+        held = stack(held, came, SMALL if last else COST)
         order += [item ^ bit for item in order]
     return held, order
 
 
-def gather_weight(halves, where):
+def gather_weight(halves, earlier, where):
     size = lax.axis_size("dp")
     bits = bits_of(size // 2)
-    low, low_order = doubled(halves[0], bits)
-    high, high_order = doubled(halves[1], bits[::-1])
+    low, low_order = doubled(halves[0], bits, earlier)
+    high, high_order = doubled(halves[1], bits[::-1], earlier)
     _, rows, width = low.shape
     (full,) = call(
         functools.partial(weight_kernel, [low_order, high_order]),
@@ -301,7 +306,7 @@
     return call(halve_kernel, [(half, F32), (half, BF16)], [], None, keep, came, cost=SMALL)
 
 
-def weight_gradient(pair, earlier, scaling, where):
+def weight_gradient(pair, earlier, beside, back, scaling, where):
     width = pair.shape[-1]
     chip_size, groups = lax.axis_size("dp") // 2, lax.axis_size("seq")
     rows = width // groups // chip_size
@@ -335,10 +340,12 @@
         *state[1],
         cost=SMALL,
     )
+    keep = after(keep, beside)
     for bit in seq_bits[:-1]:
         keep, send = halved(keep, swap(send, "seq", bit))
+    keep = after(keep, back[-1])
     (total,) = halved(keep, swap(send, "seq", seq_bits[-1]))
-    mine, order = doubled(total, bits)
+    mine, order = doubled(total, bits, back[len(back) // 2], last=True)
     (whole,) = call(
         functools.partial(join_kernel, scaling, order),
         [((chip_size, rows, width), F32)],
@@ -367,17 +374,28 @@
     def exchange(pieces):
         return list(pieces[:1]) + [swap(pieces[i], "seq", i) for i in range(1, groups)]
 
+    times = [item.reshape(blocks) for item in (q_time, k_time, v_time)]
+    sent = call(
+        functools.partial(pack_kernel, 1),
+        [((3,) + piece, BF16)] * (groups - 1),
+        [],
+        where,
+        *times,
+        cost=SMALL,
+    )
+    (own,) = call(
+        functools.partial(pack_kernel, 0),
+        [((3,) + piece, BF16)],
+        [],
+        after(where, sent[0]),
+        *times,
+    )
     half = (1, weight.shape[0] // 2, width)
-    *sent, low, high = call(
-        functools.partial(pack_kernel, 3),
-        [((3,) + piece, BF16)] * groups + [(half, BF16)] * 2,
-        [],
-        where,
-        *[item.reshape(blocks) for item in (q_time, k_time, v_time)],
-        weight.reshape((2,) + half[1:]),
-    )
-    there = exchange(sent)
-    full_weight = gather_weight((low, high), where)
+    halves = call(
+        halves_kernel, [(half, BF16)] * 2, [], None, after(weight, sent[0]).reshape((2,) + half[1:])
+    )
+    there = exchange([own, *sent])
+    full_weight = gather_weight(halves, own, where)
     space = [item.reshape(full) for item in (q_space, k_space, v_space)]
     out_space, probs_s = call(
         space_forward_kernel,
@@ -386,7 +404,7 @@
         None,
         *space,
     )
-    there[0] = after(there[0], out_space, full_weight)
+    there[0] = after(there[0], out_space)
     *out_time, probs_t, time_qkv = call(
         functools.partial(time_forward_kernel, groups),
         [(piece, BF16)] * groups + [((heads, rows, rows), F32), ((3,) + full, BF16)],
@@ -415,12 +433,6 @@
         time_qkv,
         probs_t,
     )
-    if divides(width):
-        weight_grad = weight_gradient(pair, time_grads[0], scaling, where)
-    else:
-        term = dot(pair[0], pair[1], TN).astype(BF16)
-        share = lax.psum_scatter(term, "seq", scatter_dimension=0, tiled=True)
-        weight_grad = lax.psum(share, "dp").astype(F32) * scaling
     space_grads = call(
         space_backward_kernel,
         [(full, BF16)] * 3,
@@ -431,7 +443,12 @@
         probs_s,
     )
     back = exchange(time_grads)
-    back[0] = after(back[0], weight_grad)
+    if divides(width):
+        weight_grad = weight_gradient(pair, time_grads[0], space_grads[0], back, scaling, where)
+    else:
+        term = dot(pair[0], pair[1], TN).astype(BF16)
+        share = lax.psum_scatter(term, "seq", scatter_dimension=0, tiled=True)
+        weight_grad = lax.psum(share, "dp").astype(F32) * scaling
     back = call(unpack_kernel, [(blocks, BF16)] * 3, [], where, *back)
     outs = [item.reshape(q_space.shape) for item in list(space_grads) + list(back)]
     return tuple(outs) + (weight_grad,)

time: 115 us -> 107 us (0.930)
  waiting for transfers between devices: 46.7 us -> 36.8 us
  starting transfers between devices: 38.4 us -> 40.7 us
    ppermute x28, waiting for transfers between devices: 46.7 us -> 36.8 us  [swap(): return lax.ppermute(array, axis, [(i, i ^ bits) for i in range(size)])]
    ppermute x28, starting transfers between devices: 38.4 us -> 40.7 us  [swap(): return lax.ppermute(array, axis, [(i, i ^ bits) for i in range(size)])]
    pallas_call x21 -> x23, Pallas kernels: 23.4 us -> 23.9 us  [call(): pl.pallas_call(body, out_shape=tuple((jax.ShapeDtypeStruct(*out) for out...]
    unnamed x16 -> x20, local copies, waits for them, and re-layouts: 4.44 us -> 3.96 us
  transfers between devices with their start and end apart: 28 -> 28, of which waited for: 13 -> 16; matrix products, arithmetic and copies ran while one was open for 0% -> 0% of each run, Pallas kernels for 14% -> 18%
where the time goes in v3:
time: 107 us; the launch traced here: 106 us
  starting transfers between devices  40.7 us (38%)
  waiting for transfers between devices  36.8 us (34%)
  Pallas kernels  23.9 us (22%)
  local copies, waits for them, and re-layouts  3.96 us (4%)
    ppermute x28, starting transfers between devices, swap(): return lax.ppermute(array, axis, [(i, i ^ bits) for i in range(size)])  40.7 us
    ppermute x28, waiting for transfers between devices, swap(): return lax.ppermute(array, axis, [(i, i ^ bits) for i in range(size)])  36.8 us
    pallas_call x23, Pallas kernels, call(): pl.pallas_call(body, out_shape=tuple((jax.ShapeDtypeStruct(*out) for out...  23.9 us
    unnamed x20, local copies, waits for them, and re-layouts  3.96 us
  transfers between devices with their start and end apart: 28, of which 16 were waited for; matrix products, arithmetic and copies ran while one was open for 0% of the time, Pallas kernels for 18%

profile of v3, /device:TPU:0, one launch (start us, length us, event | category | flops | bytes accessed | tf_op | source)
XLA Modules:
  0.0 106.3 jit_solution(6939818544458025134)
XLA Ops:
  0.6 0.1 pad_add_fusion.where_ref
  0.7 1.0 copy-done
  1.7 1.0 copy-done.2
  2.7 1.0 copy-done.4
  3.7 0.6 shard_map.135
  4.3 4.1 %collective-permute-start.1 = (bf16[3,40,1152]{2,1,0:T(8,128)(2,1)S(1)}, bf16[3,40,1152]{2,1,0:T(8,128)(2,1)S(1)}, u32[]{:S(2)}, u32[]{:S(2)}) collective-permute-start(bf16[3,40,1152]{2,1,0:T(8,128)(2,1)S(1)} %get-tuple-element.61), channel_id=1, source_target_pairs={{0,2},{1,3},{2,0},{3,1},{4,6},{5,7},{6,4},{7,5},{8,10},{9,11},{10,... | collective-permute-start | bytes 829448 | tf_op jit(solution)/shard_map/ppermute | solution.py:248
  8.4 1.3 %collective-permute-start.2 = (bf16[3,40,1152]{2,1,0:T(8,128)(2,1)S(1)}, bf16[3,40,1152]{2,1,0:T(8,128)(2,1)S(1)}, u32[]{:S(2)}, u32[]{:S(2)}) collective-permute-start(bf16[3,40,1152]{2,1,0:T(8,128)(2,1)S(1)} %get-tuple-element.62), channel_id=1, source_target_pairs={{0,3},{1,2},{2,1},{3,0},{4,7},{5,6},{6,5},{7,4},{8,11},{9,10},{10,... | collective-permute-start | bytes 829448 | tf_op jit(solution)/shard_map/ppermute | solution.py:248
  9.7 0.2 collective-permute-start
  10.0 1.0 copy-done.9
  11.0 1.6 %collective-permute-start.6 = (bf16[1,72,1152]{2,1,0:T(8,128)(2,1)S(1)}, bf16[1,72,1152]{2,1,0:T(8,128)(2,1)S(1)}, u32[]{:S(2)}, u32[]{:S(2)}) collective-permute-start(bf16[1,72,1152]{2,1,0:T(8,128)(2,1)S(1)} %get-tuple-element.69.refs_0_), channel_id=1, source_target_pairs={{0,8},{4,12},{8,0},{12,4},{16,24},{20,28},{24,16},{28,20},{1,9},{5... | collective-permute-start | bytes 497672 | tf_op jit(solution)/shard_map/ppermute | solution.py:248
  12.5 1.5 %collective-permute-start.9 = (bf16[1,72,1152]{2,1,0:T(8,128)(2,1)S(1)}, bf16[1,72,1152]{2,1,0:T(8,128)(2,1)S(1)}, u32[]{:S(2)}, u32[]{:S(2)}) collective-permute-start(bf16[1,72,1152]{2,1,0:T(8,128)(2,1)S(1)} %get-tuple-element.71.refs_0_), channel_id=1, source_target_pairs={{0,16},{4,20},{8,24},{12,28},{16,0},{20,4},{24,8},{28,12},{1,17},{... | collective-permute-start | bytes 497672 | tf_op jit(solution)/shard_map/ppermute | solution.py:248
  14.1 0.6 shard_map.136.refs_0_
  14.7 1.9 %shard_map.137 = (bf16[160,1152]{1,0:T(8,128)(2,1)S(1)}, f32[16,160,160]{2,1,0:T(8,128)S(1)}) custom-call(bf16[160,1152]{1,0:T(8,128)(2,1)S(1)} %bitcast.27, bf16[160,1152]{1,0:T(8,128)(2,1)S(1)} %bitcast.29, bf16[160,1152]{1,0:T(8,128)(2,1)S(1)} %bitcast.31), custom_call_target="tpu_custom_call" | custom-call | flops 10000000000 | bytes 10 | tf_op jit(solution)/shard_map/pallas_call | solution.py:235
  16.6 0.0 collective-permute-done.6.refs_1_
  16.6 1.5 %collective-permute-start.7 = (bf16[2,72,1152]{2,1,0:T(8,128)(2,1)S(1)}, bf16[2,72,1152]{2,1,0:T(8,128)(2,1)S(1)}, u32[]{:S(2)}, u32[]{:S(2)}) collective-permute-start(bf16[2,72,1152]{2,1,0:T(8,128)(2,1)S(1)} %shard_map.140.refs_0_), channel_id=1, source_target_pairs={{0,16},{4,20},{8,24},{12,28},{16,0},{20,4},{24,8},{28,12},{1,17},{... | collective-permute-start | bytes 995336 | tf_op jit(solution)/shard_map/ppermute | solution.py:248
  18.1 1.6 %collective-permute-start.10 = (bf16[2,72,1152]{2,1,0:T(8,128)(2,1)S(1)}, bf16[2,72,1152]{2,1,0:T(8,128)(2,1)S(1)}, u32[]{:S(2)}, u32[]{:S(2)}) collective-permute-start(bf16[2,72,1152]{2,1,0:T(8,128)(2,1)S(1)} %shard_map.142.refs_0_), channel_id=1, source_target_pairs={{0,8},{4,12},{8,0},{12,4},{16,24},{20,28},{24,16},{28,20},{1,9},{5... | collective-permute-start | bytes 995336 | tf_op jit(solution)/shard_map/ppermute | solution.py:248
  19.7 5.4 %collective-permute-done.7.refs_1_ = bf16[2,72,1152]{2,1,0:T(8,128)(2,1)S(1)} collective-permute-done((bf16[2,72,1152]{2,1,0:T(8,128)(2,1)S(1)}, bf16[2,72,1152]{2,1,0:T(8,128)(2,1)S(1)}, u32[]{:S(2)}, u32[]{:S(2)}) %collective-permute-start.7) | collective-permute-done | bytes 331808 | tf_op jit(solution)/shard_map/ppermute | solution.py:248
  25.1 0.1 collective-permute-start.8
  25.2 0.7 collective-permute-done.10.refs_1_
  26.0 0.1 collective-permute-start.11
  26.1 1.6 %collective-permute-done.1.refs_2_ = bf16[3,40,1152]{2,1,0:T(8,128)(2,1)S(1)} collective-permute-done((bf16[3,40,1152]{2,1,0:T(8,128)(2,1)S(1)}, bf16[3,40,1152]{2,1,0:T(8,128)(2,1)S(1)}, u32[]{:S(2)}, u32[]{:S(2)}) %collective-permute-start.1) | collective-permute-done | bytes 276512 | tf_op jit(solution)/shard_map/ppermute | solution.py:248
  27.7 0.5 collective-permute-done.refs_1_
  28.2 1.9 %shard_map.138 = (bf16[40,1152]{1,0:T(8,128)(2,1)S(1)}, bf16[40,1152]{1,0:T(8,128)(2,1)S(1)}, bf16[40,1152]{1,0:T(8,128)(2,1)S(1)}, bf16[40,1152]{1,0:T(8,128)(2...) custom-call(bf16[3,40,1152]{2,1,0:T(8,128)(2,1)S(1)} %shard_map.136.refs_0_, ...), custom_call_target="tpu_custom_call" | custom-call | flops 10000000000 | bytes 10 | tf_op jit(solution)/shard_map/pallas_call | solution.py:235
  30.2 5.4 %collective-permute-start.3 = (bf16[40,1152]{1,0:T(8,128)(2,1)S(1)}, bf16[40,1152]{1,0:T(8,128)(2,1)S(1)}, u32[]{:S(2)}, u32[]{:S(2)}) collective-permute-start(bf16[40,1152]{1,0:T(8,128)(2,1)S(1)} %get-tuple-element.64), channel_id=1, source_target_pairs={{0,1},{1,0},{2,3},{3,2},{4,5},{5,4},{6,7},{7,6},{8,9},{9,8},{10,11... | collective-permute-start | bytes 276488 | tf_op jit(solution)/shard_map/ppermute | solution.py:248
  35.6 2.0 %collective-permute-start.4 = (bf16[40,1152]{1,0:T(8,128)(2,1)S(1)}, bf16[40,1152]{1,0:T(8,128)(2,1)S(1)}, u32[]{:S(2)}, u32[]{:S(2)}) collective-permute-start(bf16[40,1152]{1,0:T(8,128)(2,1)S(1)} %get-tuple-element.65), channel_id=1, source_target_pairs={{0,2},{1,3},{2,0},{3,1},{4,6},{5,7},{6,4},{7,5},{8,10},{9,11},{10,... | collective-permute-start | bytes 276488 | tf_op jit(solution)/shard_map/ppermute | solution.py:248
  37.6 1.4 %collective-permute-start.5 = (bf16[40,1152]{1,0:T(8,128)(2,1)S(1)}, bf16[40,1152]{1,0:T(8,128)(2,1)S(1)}, u32[]{:S(2)}, u32[]{:S(2)}) collective-permute-start(bf16[40,1152]{1,0:T(8,128)(2,1)S(1)} %get-tuple-element.66), channel_id=1, source_target_pairs={{0,3},{1,2},{2,1},{3,0},{4,7},{5,6},{6,5},{7,4},{8,11},{9,10},{10,... | collective-permute-start | bytes 276488 | tf_op jit(solution)/shard_map/ppermute | solution.py:248
  39.0 0.7 shard_map.144
  39.7 0.0 collective-permute-done.3.refs_1_
  39.7 2.2 %collective-permute-done.4.refs_2_ = bf16[40,1152]{1,0:T(8,128)(2,1)S(1)} collective-permute-done((bf16[40,1152]{1,0:T(8,128)(2,1)S(1)}, bf16[40,1152]{1,0:T(8,128)(2,1)S(1)}, u32[]{:S(2)}, u32[]{:S(2)}) %collective-permute-start.4) | collective-permute-done | bytes 92192 | tf_op jit(solution)/shard_map/ppermute | solution.py:248
  42.0 3.6 %collective-permute-done.5.refs_3_ = bf16[40,1152]{1,0:T(8,128)(2,1)S(1)} collective-permute-done((bf16[40,1152]{1,0:T(8,128)(2,1)S(1)}, bf16[40,1152]{1,0:T(8,128)(2,1)S(1)}, u32[]{:S(2)}, u32[]{:S(2)}) %collective-permute-start.5) | collective-permute-done | bytes 92192 | tf_op jit(solution)/shard_map/ppermute | solution.py:248
  45.6 2.1 %shard_map.145 = (bf16[2,160,1152]{2,1,0:T(8,128)(2,1)S(1)}, bf16[4,40,1152]{2,1,0:T(8,128)(2,1)S(1)}, bf16[40,1152]{1,0:T(8,128)(2,1)S(1)}, bf16[40,1152]{1,0:T...) custom-call(s32[2]{0:T(128)S(1)} %pad_add_fusion.where_ref, ...), custom_call_target="tpu_custom_call" | custom-call | flops 10000000000 | bytes 10 | tf_op jit(solution)/shard_map/pallas_call | solution.py:235
  47.7 0.1 collective-permute-start.18
  47.7 2.0 %collective-permute-start.12 = (bf16[40,1152]{1,0:T(8,128)(2,1)S(1)}, bf16[40,1152]{1,0:T(8,128)(2,1)S(1)}, u32[]{:S(2)}, u32[]{:S(2)}) collective-permute-start(bf16[40,1152]{1,0:T(8,128)(2,1)S(1)} %get-tuple-element.74), channel_id=1, source_target_pairs={{0,1},{1,0},{2,3},{3,2},{4,5},{5,4},{6,7},{7,6},{8,9},{9,8},{10,11... | collective-permute-start | bytes 276488 | tf_op jit(solution)/shard_map/ppermute | solution.py:248
  49.8 1.5 %collective-permute-start.13 = (bf16[40,1152]{1,0:T(8,128)(2,1)S(1)}, bf16[40,1152]{1,0:T(8,128)(2,1)S(1)}, u32[]{:S(2)}, u32[]{:S(2)}) collective-permute-start(bf16[40,1152]{1,0:T(8,128)(2,1)S(1)} %get-tuple-element.75), channel_id=1, source_target_pairs={{0,2},{1,3},{2,0},{3,1},{4,6},{5,7},{6,4},{7,5},{8,10},{9,11},{10,... | collective-permute-start | bytes 276488 | tf_op jit(solution)/shard_map/ppermute | solution.py:248
  51.3 1.4 %collective-permute-start.14 = (bf16[40,1152]{1,0:T(8,128)(2,1)S(1)}, bf16[40,1152]{1,0:T(8,128)(2,1)S(1)}, u32[]{:S(2)}, u32[]{:S(2)}) collective-permute-start(bf16[40,1152]{1,0:T(8,128)(2,1)S(1)} %get-tuple-element.76), channel_id=1, source_target_pairs={{0,3},{1,2},{2,1},{3,0},{4,7},{5,6},{6,5},{7,4},{8,11},{9,10},{10,... | collective-permute-start | bytes 276488 | tf_op jit(solution)/shard_map/ppermute | solution.py:248
  52.7 1.8 %shard_map.149 = (f32[2,2,72,640]{3,2,1,0:T(8,128)S(1)}, bf16[2,2,72,640]{3,2,1,0:T(8,128)(2,1)S(1)}, f32[2,2,72,640]{3,2,1,0:T(8,128)S(1)}, bf16[2,2,72,640]{3,2,1,0:T(8,128)(2,1)S(1)}) custom-call(s32[2]{0:T(128)S(1)} %pad_add_fusion.where_ref, bf16[2,160,1152]{2,1,0:T(8,128)(2,1)S(1)} %get-tuple-element.91.mine_ref, ...), custom_call_target="tpu_custom_call" | custom-call | flops 10000000000 | bytes 10 | tf_op jit(solution)/shard_map/pallas_call | solution.py:235
  54.5 1.6 %collective-permute-start.19 = (bf16[2,2,72,640]{3,2,1,0:T(8,128)(2,1)S(1)}, bf16[2,2,72,640]{3,2,1,0:T(8,128)(2,1)S(1)}, u32[]{:S(2)}, u32[]{:S(2)}) collective-permute-start(bf16[2,2,72,640]{3,2,1,0:T(8,128)(2,1)S(1)} %get-tuple-element.94), channel_id=1, source_target_pairs={{0,8},{4,12},{8,0},{12,4},{16,24},{20,28},{24,16},{28,20},{1,9},{5... | collective-permute-start | bytes 1105928 | tf_op jit(solution)/shard_map/ppermute | solution.py:248
  56.1 1.5 %collective-permute-start.21 = (bf16[2,2,72,640]{3,2,1,0:T(8,128)(2,1)S(1)}, bf16[2,2,72,640]{3,2,1,0:T(8,128)(2,1)S(1)}, u32[]{:S(2)}, u32[]{:S(2)}) collective-permute-start(bf16[2,2,72,640]{3,2,1,0:T(8,128)(2,1)S(1)} %get-tuple-element.98), channel_id=1, source_target_pairs={{0,16},{4,20},{8,24},{12,28},{16,0},{20,4},{24,8},{28,12},{1,17},{... | collective-permute-start | bytes 1105928 | tf_op jit(solution)/shard_map/ppermute | solution.py:248
  57.6 2.1 %collective-permute-done.14.refs_3_ = bf16[40,1152]{1,0:T(8,128)(2,1)S(1)} collective-permute-done((bf16[40,1152]{1,0:T(8,128)(2,1)S(1)}, bf16[40,1152]{1,0:T(8,128)(2,1)S(1)}, u32[]{:S(2)}, u32[]{:S(2)}) %collective-permute-start.14) | collective-permute-done | bytes 92192 | tf_op jit(solution)/shard_map/ppermute | solution.py:248
  59.7 4.4 %shard_map.146 = (bf16[3,40,1152]{2,1,0:T(8,128)(2,1)S(1)}, bf16[3,40,1152]{2,1,0:T(8,128)(2,1)S(1)}, bf16[3,40,1152]{2,1,0:T(8,128)(2,1)S(1)}, bf16[3,40,1152]{2,1,0:T(8,128)(2,1)S(1)}) custom-call(bf16[40,1152]{1,0:T(8,128)(2,1)S(1)} %get-tuple-element.73.refs_0_, bf16[40,1152]{1,0:T(8,128)(2,1)S(1)} %collective-permute-done.12.refs_1_, ...), custom_call_target="tpu_custom_call" | custom-call | flops 10000000000 | bytes 10 | tf_op jit(solution)/shard_map/pallas_call | solution.py:235
  64.1 0.9 collective-permute-done.19.came_ref
  65.0 0.1 shard_map.150
  65.1 1.6 %collective-permute-start.20 = (bf16[1,2,72,640]{3,2,1,0:T(8,128)(2,1)S(1)}, bf16[1,2,72,640]{3,2,1,0:T(8,128)(2,1)S(1)}, u32[]{:S(2)}, u32[]{:S(2)}) collective-permute-start(bf16[1,2,72,640]{3,2,1,0:T(8,128)(2,1)S(1)} %get-tuple-element.96), channel_id=1, source_target_pairs={{0,16},{4,20},{8,24},{12,28},{16,0},{20,4},{24,8},{28,12},{1,17},{... | collective-permute-start | bytes 552968 | tf_op jit(solution)/shard_map/ppermute | solution.py:248
  66.7 0.1 shard_map.151
  66.7 1.6 %collective-permute-start.22 = (bf16[1,2,72,640]{3,2,1,0:T(8,128)(2,1)S(1)}, bf16[1,2,72,640]{3,2,1,0:T(8,128)(2,1)S(1)}, u32[]{:S(2)}, u32[]{:S(2)}) collective-permute-start(bf16[1,2,72,640]{3,2,1,0:T(8,128)(2,1)S(1)} %get-tuple-element.100), channel_id=1, source_target_pairs={{0,8},{4,12},{8,0},{12,4},{16,24},{20,28},{24,16},{28,20},{1,9},{5... | collective-permute-start | bytes 552968 | tf_op jit(solution)/shard_map/ppermute | solution.py:248
  68.3 2.3 %collective-permute-start.17 = (bf16[3,40,1152]{2,1,0:T(8,128)(2,1)S(1)}, bf16[3,40,1152]{2,1,0:T(8,128)(2,1)S(1)}, u32[]{:S(2)}, u32[]{:S(2)}) collective-permute-start(bf16[3,40,1152]{2,1,0:T(8,128)(2,1)S(1)} %get-tuple-element.87), channel_id=1, source_target_pairs={{0,3},{1,2},{2,1},{3,0},{4,7},{5,6},{6,5},{7,4},{8,11},{9,10},{10,... | collective-permute-start | bytes 829448 | tf_op jit(solution)/shard_map/ppermute | solution.py:248
  70.6 0.1 collective-permute-done.20.refs_1_
  70.7 1.6 %collective-permute-done.22.refs_3_ = bf16[1,2,72,640]{3,2,1,0:T(8,128)(2,1)S(1)} collective-permute-done((bf16[1,2,72,640]{3,2,1,0:T(8,128)(2,1)S(1)}, bf16[1,2,72,640]{3,2,1,0:T(8,128)(2,1)S(1)}, u32[]{:S(2)}, u32[]{:S(2)}) %collective-permute-start.22) | collective-permute-done | bytes 184352 | tf_op jit(solution)/shard_map/ppermute | solution.py:248
  72.3 0.7 shard_map.152
  73.0 1.8 %collective-permute-start.23 = (bf16[2,72,640]{2,1,0:T(8,128)(2,1)S(1)}, bf16[2,72,640]{2,1,0:T(8,128)(2,1)S(1)}, u32[]{:S(2)}, u32[]{:S(2)}) collective-permute-start(bf16[2,72,640]{2,1,0:T(8,128)(2,1)S(1)} %get-tuple-element.103), channel_id=1, source_target_pairs={{0,1},{1,0},{2,3},{3,2},{4,5},{5,4},{6,7},{7,6},{8,9},{9,8},{10,11... | collective-permute-start | bytes 552968 | tf_op jit(solution)/shard_map/ppermute | solution.py:248
  74.8 5.4 %shard_map.147 = (bf16[160,1152]{1,0:T(8,128)(2,1)}, bf16[160,1152]{1,0:T(8,128)(2,1)}, bf16[160,1152]{1,0:T(8,128)(2,1)}) custom-call(bf16[160,1152]{1,0:T(8,128)(2,1)S(1)} %bitcast.28, bf16[160,1152]{1,0:T(8,128)(2,1)S(1)} %bitcast.30, bf16[160,1152]{1,0:T(8,128)(2,1)S(1)} %bitcast.32, bf16[160,1152]{1,0:T(8,128)(2,1)S(1)} %bitcast.35, ...), custom_call_target="tpu_custom_call" | custom-call | flops 10000000000 | bytes 10 | tf_op jit(solution)/shard_map/pallas_call | solution.py:235
  80.2 0.9 collective-permute-done.23.came_ref
  81.2 0.6 collective-permute-start.24
  81.8 5.9 %collective-permute-done.24.came_ref = bf16[1,72,640]{2,1,0:T(8,128)(2,1)S(1)} collective-permute-done((bf16[1,72,640]{2,1,0:T(8,128)(2,1)S(1)}, bf16[1,72,640]{2,1,0:T(8,128)(2,1)S(1)}, u32[]{:S(2)}, u32[]{:S(2)}) %collective-permute-start.24) | collective-permute-done | bytes 92192 | tf_op jit(solution)/shard_map/ppermute | solution.py:248
  87.7 0.5 collective-permute-start.25
  88.2 3.0 %collective-permute-start.16 = (bf16[3,40,1152]{2,1,0:T(8,128)(2,1)S(1)}, bf16[3,40,1152]{2,1,0:T(8,128)(2,1)S(1)}, u32[]{:S(2)}, u32[]{:S(2)}) collective-permute-start(bf16[3,40,1152]{2,1,0:T(8,128)(2,1)S(1)} %get-tuple-element.86), channel_id=1, source_target_pairs={{0,2},{1,3},{2,0},{3,1},{4,6},{5,7},{6,4},{7,5},{8,10},{9,11},{10,... | collective-permute-start | bytes 829448 | tf_op jit(solution)/shard_map/ppermute | solution.py:248
  91.2 1.1 %collective-permute-done.25.refs_1_ = bf16[1,72,640]{2,1,0:T(8,128)(2,1)S(1)} collective-permute-done((bf16[1,72,640]{2,1,0:T(8,128)(2,1)S(1)}, bf16[1,72,640]{2,1,0:T(8,128)(2,1)S(1)}, u32[]{:S(2)}, u32[]{:S(2)}) %collective-permute-start.25) | collective-permute-done | bytes 92192 | tf_op jit(solution)/shard_map/ppermute | solution.py:248
  92.3 0.5 collective-permute-start.26
  92.8 5.1 %collective-permute-done.26.refs_1_ = bf16[2,72,640]{2,1,0:T(8,128)(2,1)S(1)} collective-permute-done((bf16[2,72,640]{2,1,0:T(8,128)(2,1)S(1)}, bf16[2,72,640]{2,1,0:T(8,128)(2,1)S(1)}, u32[]{:S(2)}, u32[]{:S(2)}) %collective-permute-start.26) | collective-permute-done | bytes 184352 | tf_op jit(solution)/shard_map/ppermute | solution.py:248
  98.0 0.1 collective-permute-start.27
  98.1 3.3 %collective-permute-done.15.refs_1_ = bf16[3,40,1152]{2,1,0:T(8,128)(2,1)S(1)} collective-permute-done((bf16[3,40,1152]{2,1,0:T(8,128)(2,1)S(1)}, bf16[3,40,1152]{2,1,0:T(8,128)(2,1)S(1)}, u32[]{:S(2)}, u32[]{:S(2)}) %collective-permute-start.15) | collective-permute-done | bytes 276512 | tf_op jit(solution)/shard_map/ppermute | solution.py:248
  101.3 1.6 %collective-permute-done.16.refs_2_ = bf16[3,40,1152]{2,1,0:T(8,128)(2,1)S(1)} collective-permute-done((bf16[3,40,1152]{2,1,0:T(8,128)(2,1)S(1)}, bf16[3,40,1152]{2,1,0:T(8,128)(2,1)S(1)}, u32[]{:S(2)}, u32[]{:S(2)}) %collective-permute-start.16) | collective-permute-done | bytes 276512 | tf_op jit(solution)/shard_map/ppermute | solution.py:248
  102.9 1.6 %shard_map.148 = (bf16[4,40,1152]{2,1,0:T(8,128)(2,1)}, bf16[4,40,1152]{2,1,0:T(8,128)(2,1)}, bf16[4,40,1152]{2,1,0:T(8,128)(2,1)}) custom-call(s32[2]{0:T(128)S(1)} %pad_add_fusion.where_ref, bf16[3,40,1152]{2,1,0:T(8,128)(2,1)S(1)} %get-tuple-element.79.refs_0_, bf16[3,40,1152]{2,1,0:T(8,128)(2,1)S(1)} %collective-permute-done.15.refs_1_, ...), custom_call_target="tpu_custom_call" | custom-call | flops 10000000000 | bytes 10 | tf_op jit(solution)/shard_map/pallas_call | solution.py:235
  104.6 1.8 %shard_map.157 = f32[4,72,1152]{2,1,0:T(8,128)} custom-call(s32[2]{0:T(128)S(1)} %pad_add_fusion.where_ref, bf16[4,72,640]{2,1,0:T(8,128)(2,1)S(1)} %shard_map.156.mine_ref, bf16[4,72,640]{2,1,0:T(8,128)(2,1)S(1)} %collective-permute-done.27.other_ref), custom_call_target="tpu_custom_call" | custom-call | flops 10 | bytes 10 | tf_op jit(solution)/shard_map/pallas_call | solution.py:235
  (36 shorter events, 0.3 us)
Async XLA Ops:
  0.7 1.0 copy-start
  1.7 1.0 copy-start.2
  2.7 1.0 copy-start.4
  4.3 23.4 %collective-permute-start.1 = (bf16[3,40,1152]{2,1,0:T(8,128)(2,1)S(1)}, bf16[3,40,1152]{2,1,0:T(8,128)(2,1)S(1)}, u32[]{:S(2)}, u32[]{:S(2)}) collective-permute-start(bf16[3,40,1152]{2,1,0:T(8,128)(2,1)S(1)} %get-tuple-element.61), channel_id=1, source_target_pairs={{0,2},{1,3},{2,0},{3,1},{4,6},{5,7},{6,4},{7,5},{8,10},{9,11},{10,... | collective-permute-start | bytes 829448 | tf_op jit(solution)/shard_map/ppermute | solution.py:248
  8.4 19.3 %collective-permute-start.2 = (bf16[3,40,1152]{2,1,0:T(8,128)(2,1)S(1)}, bf16[3,40,1152]{2,1,0:T(8,128)(2,1)S(1)}, u32[]{:S(2)}, u32[]{:S(2)}) collective-permute-start(bf16[3,40,1152]{2,1,0:T(8,128)(2,1)S(1)} %get-tuple-element.62), channel_id=1, source_target_pairs={{0,3},{1,2},{2,1},{3,0},{4,7},{5,6},{6,5},{7,4},{8,11},{9,10},{10,... | collective-permute-start | bytes 829448 | tf_op jit(solution)/shard_map/ppermute | solution.py:248
  9.7 18.5 %collective-permute-start = (bf16[3,40,1152]{2,1,0:T(8,128)(2,1)S(1)}, bf16[3,40,1152]{2,1,0:T(8,128)(2,1)S(1)}, u32[]{:S(2)}, u32[]{:S(2)}) collective-permute-start(bf16[3,40,1152]{2,1,0:T(8,128)(2,1)S(1)} %get-tuple-element.57), channel_id=1, source_target_pairs={{0,1},{1,0},{2,3},{3,2},{4,5},{5,4},{6,7},{7,6},{8,9},{9,8},{10,11... | collective-permute-start | bytes 829448 | tf_op jit(solution)/shard_map/ppermute | solution.py:248
  10.0 1.0 copy-start.9
  10.9 3.1 %copy-start.1 = (bf16[1,160,1152]{2,1,0:T(8,128)(2,1)S(1)}, bf16[1,160,1152]{2,1,0:T(8,128)(2,1)}, u32[]{:S(2)}) copy-start(bf16[1,160,1152]{2,1,0:T(8,128)(2,1)} %param.11) | copy-start | bytes 1105924
  10.9 3.1 %copy-start.3 = (bf16[1,160,1152]{2,1,0:T(8,128)(2,1)S(1)}, bf16[1,160,1152]{2,1,0:T(8,128)(2,1)}, u32[]{:S(2)}) copy-start(bf16[1,160,1152]{2,1,0:T(8,128)(2,1)} %param.12) | copy-start | bytes 1105924
  11.0 5.6 %collective-permute-start.6 = (bf16[1,72,1152]{2,1,0:T(8,128)(2,1)S(1)}, bf16[1,72,1152]{2,1,0:T(8,128)(2,1)S(1)}, u32[]{:S(2)}, u32[]{:S(2)}) collective-permute-start(bf16[1,72,1152]{2,1,0:T(8,128)(2,1)S(1)} %get-tuple-element.69.refs_0_), channel_id=1, source_target_pairs={{0,8},{4,12},{8,0},{12,4},{16,24},{20,28},{24,16},{28,20},{1,9},{5... | collective-permute-start | bytes 497672 | tf_op jit(solution)/shard_map/ppermute | solution.py:248
  12.5 2.1 %copy-start.6 = (bf16[1,160,1152]{2,1,0:T(8,128)(2,1)S(1)}, bf16[1,160,1152]{2,1,0:T(8,128)(2,1)}, u32[]{:S(2)}) copy-start(bf16[1,160,1152]{2,1,0:T(8,128)(2,1)} %param.8) | copy-start | bytes 1105924
  12.5 2.1 %copy-start.7 = (bf16[1,160,1152]{2,1,0:T(8,128)(2,1)S(1)}, bf16[1,160,1152]{2,1,0:T(8,128)(2,1)}, u32[]{:S(2)}) copy-start(bf16[1,160,1152]{2,1,0:T(8,128)(2,1)} %param.9) | copy-start | bytes 1105924
  12.5 2.1 %copy-start.8 = (bf16[1,160,1152]{2,1,0:T(8,128)(2,1)S(1)}, bf16[1,160,1152]{2,1,0:T(8,128)(2,1)}, u32[]{:S(2)}) copy-start(bf16[1,160,1152]{2,1,0:T(8,128)(2,1)} %param.10) | copy-start | bytes 1105924
  12.5 5.5 %collective-permute-start.9 = (bf16[1,72,1152]{2,1,0:T(8,128)(2,1)S(1)}, bf16[1,72,1152]{2,1,0:T(8,128)(2,1)S(1)}, u32[]{:S(2)}, u32[]{:S(2)}) collective-permute-start(bf16[1,72,1152]{2,1,0:T(8,128)(2,1)S(1)} %get-tuple-element.71.refs_0_), channel_id=1, source_target_pairs={{0,16},{4,20},{8,24},{12,28},{16,0},{20,4},{24,8},{28,12},{1,17},{... | collective-permute-start | bytes 497672 | tf_op jit(solution)/shard_map/ppermute | solution.py:248
  16.6 8.5 %collective-permute-start.7 = (bf16[2,72,1152]{2,1,0:T(8,128)(2,1)S(1)}, bf16[2,72,1152]{2,1,0:T(8,128)(2,1)S(1)}, u32[]{:S(2)}, u32[]{:S(2)}) collective-permute-start(bf16[2,72,1152]{2,1,0:T(8,128)(2,1)S(1)} %shard_map.140.refs_0_), channel_id=1, source_target_pairs={{0,16},{4,20},{8,24},{12,28},{16,0},{20,4},{24,8},{28,12},{1,17},{... | collective-permute-start | bytes 995336 | tf_op jit(solution)/shard_map/ppermute | solution.py:248
  18.1 7.8 %collective-permute-start.10 = (bf16[2,72,1152]{2,1,0:T(8,128)(2,1)S(1)}, bf16[2,72,1152]{2,1,0:T(8,128)(2,1)S(1)}, u32[]{:S(2)}, u32[]{:S(2)}) collective-permute-start(bf16[2,72,1152]{2,1,0:T(8,128)(2,1)S(1)} %shard_map.142.refs_0_), channel_id=1, source_target_pairs={{0,8},{4,12},{8,0},{12,4},{16,24},{20,28},{24,16},{28,20},{1,9},{5... | collective-permute-start | bytes 995336 | tf_op jit(solution)/shard_map/ppermute | solution.py:248
  25.1 13.8 %collective-permute-start.8 = (bf16[4,72,1152]{2,1,0:T(8,128)(2,1)S(1)}, bf16[4,72,1152]{2,1,0:T(8,128)(2,1)S(1)}, u32[]{:S(2)}, u32[]{:S(2)}) collective-permute-start(bf16[4,72,1152]{2,1,0:T(8,128)(2,1)S(1)} %shard_map.141.refs_0_), channel_id=1, source_target_pairs={{0,4},{4,0},{8,12},{12,8},{16,20},{20,16},{24,28},{28,24},{1,5},{5... | collective-permute-start | bytes 1990664 | tf_op jit(solution)/shard_map/ppermute | solution.py:248
  26.0 13.0 %collective-permute-start.11 = (bf16[4,72,1152]{2,1,0:T(8,128)(2,1)S(1)}, bf16[4,72,1152]{2,1,0:T(8,128)(2,1)S(1)}, u32[]{:S(2)}, u32[]{:S(2)}) collective-permute-start(bf16[4,72,1152]{2,1,0:T(8,128)(2,1)S(1)} %shard_map.143.refs_2_), channel_id=1, source_target_pairs={{0,4},{4,0},{8,12},{12,8},{16,20},{20,16},{24,28},{28,24},{1,5},{5... | collective-permute-start | bytes 1990664 | tf_op jit(solution)/shard_map/ppermute | solution.py:248
  30.2 9.5 %collective-permute-start.3 = (bf16[40,1152]{1,0:T(8,128)(2,1)S(1)}, bf16[40,1152]{1,0:T(8,128)(2,1)S(1)}, u32[]{:S(2)}, u32[]{:S(2)}) collective-permute-start(bf16[40,1152]{1,0:T(8,128)(2,1)S(1)} %get-tuple-element.64), channel_id=1, source_target_pairs={{0,1},{1,0},{2,3},{3,2},{4,5},{5,4},{6,7},{7,6},{8,9},{9,8},{10,11... | collective-permute-start | bytes 276488 | tf_op jit(solution)/shard_map/ppermute | solution.py:248
  35.6 6.4 %collective-permute-start.4 = (bf16[40,1152]{1,0:T(8,128)(2,1)S(1)}, bf16[40,1152]{1,0:T(8,128)(2,1)S(1)}, u32[]{:S(2)}, u32[]{:S(2)}) collective-permute-start(bf16[40,1152]{1,0:T(8,128)(2,1)S(1)} %get-tuple-element.65), channel_id=1, source_target_pairs={{0,2},{1,3},{2,0},{3,1},{4,6},{5,7},{6,4},{7,5},{8,10},{9,11},{10,... | collective-permute-start | bytes 276488 | tf_op jit(solution)/shard_map/ppermute | solution.py:248
  37.6 8.0 %copy-start.5 = (bf16[1,160,1152]{2,1,0:T(8,128)(2,1)S(1)}, bf16[1,160,1152]{2,1,0:T(8,128)(2,1)}, u32[]{:S(2)}) copy-start(bf16[1,160,1152]{2,1,0:T(8,128)(2,1)} %param.15) | copy-start | bytes 1105924
  37.6 8.0 %collective-permute-start.5 = (bf16[40,1152]{1,0:T(8,128)(2,1)S(1)}, bf16[40,1152]{1,0:T(8,128)(2,1)S(1)}, u32[]{:S(2)}, u32[]{:S(2)}) collective-permute-start(bf16[40,1152]{1,0:T(8,128)(2,1)S(1)} %get-tuple-element.66), channel_id=1, source_target_pairs={{0,3},{1,2},{2,1},{3,0},{4,7},{5,6},{6,5},{7,4},{8,11},{9,10},{10,... | collective-permute-start | bytes 276488 | tf_op jit(solution)/shard_map/ppermute | solution.py:248
  47.7 5.0 %collective-permute-start.18 = (bf16[2,160,1152]{2,1,0:T(8,128)(2,1)S(1)}, bf16[2,160,1152]{2,1,0:T(8,128)(2,1)S(1)}, u32[]{:S(2)}, u32[]{:S(2)}) collective-permute-start(bf16[2,160,1152]{2,1,0:T(8,128)(2,1)S(1)} %get-tuple-element.91.mine_ref), channel_id=1, source_target_pairs={{0,4},{4,0},{8,12},{12,8},{16,20},{20,16},{24,28},{28,24},{1,5},{5... | collective-permute-start | bytes 2211848 | tf_op jit(solution)/shard_map/ppermute | solution.py:248
  47.7 9.9 %collective-permute-start.12 = (bf16[40,1152]{1,0:T(8,128)(2,1)S(1)}, bf16[40,1152]{1,0:T(8,128)(2,1)S(1)}, u32[]{:S(2)}, u32[]{:S(2)}) collective-permute-start(bf16[40,1152]{1,0:T(8,128)(2,1)S(1)} %get-tuple-element.74), channel_id=1, source_target_pairs={{0,1},{1,0},{2,3},{3,2},{4,5},{5,4},{6,7},{7,6},{8,9},{9,8},{10,11... | collective-permute-start | bytes 276488 | tf_op jit(solution)/shard_map/ppermute | solution.py:248
  49.8 7.9 %collective-permute-start.13 = (bf16[40,1152]{1,0:T(8,128)(2,1)S(1)}, bf16[40,1152]{1,0:T(8,128)(2,1)S(1)}, u32[]{:S(2)}, u32[]{:S(2)}) collective-permute-start(bf16[40,1152]{1,0:T(8,128)(2,1)S(1)} %get-tuple-element.75), channel_id=1, source_target_pairs={{0,2},{1,3},{2,0},{3,1},{4,6},{5,7},{6,4},{7,5},{8,10},{9,11},{10,... | collective-permute-start | bytes 276488 | tf_op jit(solution)/shard_map/ppermute | solution.py:248
  51.3 8.4 %collective-permute-start.14 = (bf16[40,1152]{1,0:T(8,128)(2,1)S(1)}, bf16[40,1152]{1,0:T(8,128)(2,1)S(1)}, u32[]{:S(2)}, u32[]{:S(2)}) collective-permute-start(bf16[40,1152]{1,0:T(8,128)(2,1)S(1)} %get-tuple-element.76), channel_id=1, source_target_pairs={{0,3},{1,2},{2,1},{3,0},{4,7},{5,6},{6,5},{7,4},{8,11},{9,10},{10,... | collective-permute-start | bytes 276488 | tf_op jit(solution)/shard_map/ppermute | solution.py:248
  54.5 10.4 %collective-permute-start.19 = (bf16[2,2,72,640]{3,2,1,0:T(8,128)(2,1)S(1)}, bf16[2,2,72,640]{3,2,1,0:T(8,128)(2,1)S(1)}, u32[]{:S(2)}, u32[]{:S(2)}) collective-permute-start(bf16[2,2,72,640]{3,2,1,0:T(8,128)(2,1)S(1)} %get-tuple-element.94), channel_id=1, source_target_pairs={{0,8},{4,12},{8,0},{12,4},{16,24},{20,28},{24,16},{28,20},{1,9},{5... | collective-permute-start | bytes 1105928 | tf_op jit(solution)/shard_map/ppermute | solution.py:248
  56.1 10.6 %collective-permute-start.21 = (bf16[2,2,72,640]{3,2,1,0:T(8,128)(2,1)S(1)}, bf16[2,2,72,640]{3,2,1,0:T(8,128)(2,1)S(1)}, u32[]{:S(2)}, u32[]{:S(2)}) collective-permute-start(bf16[2,2,72,640]{3,2,1,0:T(8,128)(2,1)S(1)} %get-tuple-element.98), channel_id=1, source_target_pairs={{0,16},{4,20},{8,24},{12,28},{16,0},{20,4},{24,8},{28,12},{1,17},{... | collective-permute-start | bytes 1105928 | tf_op jit(solution)/shard_map/ppermute | solution.py:248
  65.1 5.6 %collective-permute-start.20 = (bf16[1,2,72,640]{3,2,1,0:T(8,128)(2,1)S(1)}, bf16[1,2,72,640]{3,2,1,0:T(8,128)(2,1)S(1)}, u32[]{:S(2)}, u32[]{:S(2)}) collective-permute-start(bf16[1,2,72,640]{3,2,1,0:T(8,128)(2,1)S(1)} %get-tuple-element.96), channel_id=1, source_target_pairs={{0,16},{4,20},{8,24},{12,28},{16,0},{20,4},{24,8},{28,12},{1,17},{... | collective-permute-start | bytes 552968 | tf_op jit(solution)/shard_map/ppermute | solution.py:248
  66.7 5.6 %collective-permute-start.22 = (bf16[1,2,72,640]{3,2,1,0:T(8,128)(2,1)S(1)}, bf16[1,2,72,640]{3,2,1,0:T(8,128)(2,1)S(1)}, u32[]{:S(2)}, u32[]{:S(2)}) collective-permute-start(bf16[1,2,72,640]{3,2,1,0:T(8,128)(2,1)S(1)} %get-tuple-element.100), channel_id=1, source_target_pairs={{0,8},{4,12},{8,0},{12,4},{16,24},{20,28},{24,16},{28,20},{1,9},{5... | collective-permute-start | bytes 552968 | tf_op jit(solution)/shard_map/ppermute | solution.py:248
  68.3 13.5 %collective-permute-start.17 = (bf16[3,40,1152]{2,1,0:T(8,128)(2,1)S(1)}, bf16[3,40,1152]{2,1,0:T(8,128)(2,1)S(1)}, u32[]{:S(2)}, u32[]{:S(2)}) collective-permute-start(bf16[3,40,1152]{2,1,0:T(8,128)(2,1)S(1)} %get-tuple-element.87), channel_id=1, source_target_pairs={{0,3},{1,2},{2,1},{3,0},{4,7},{5,6},{6,5},{7,4},{8,11},{9,10},{10,... | collective-permute-start | bytes 829448 | tf_op jit(solution)/shard_map/ppermute | solution.py:248
  73.0 8.1 %collective-permute-start.23 = (bf16[2,72,640]{2,1,0:T(8,128)(2,1)S(1)}, bf16[2,72,640]{2,1,0:T(8,128)(2,1)S(1)}, u32[]{:S(2)}, u32[]{:S(2)}) collective-permute-start(bf16[2,72,640]{2,1,0:T(8,128)(2,1)S(1)} %get-tuple-element.103), channel_id=1, source_target_pairs={{0,1},{1,0},{2,3},{3,2},{4,5},{5,4},{6,7},{7,6},{8,9},{9,8},{10,11... | collective-permute-start | bytes 552968 | tf_op jit(solution)/shard_map/ppermute | solution.py:248
  81.2 6.5 %collective-permute-start.24 = (bf16[1,72,640]{2,1,0:T(8,128)(2,1)S(1)}, bf16[1,72,640]{2,1,0:T(8,128)(2,1)S(1)}, u32[]{:S(2)}, u32[]{:S(2)}) collective-permute-start(bf16[1,72,640]{2,1,0:T(8,128)(2,1)S(1)} %get-tuple-element.106), channel_id=1, source_target_pairs={{0,2},{1,3},{2,0},{3,1},{4,6},{5,7},{6,4},{7,5},{8,10},{9,11},{10,... | collective-permute-start | bytes 276488 | tf_op jit(solution)/shard_map/ppermute | solution.py:248
  87.7 4.6 %collective-permute-start.25 = (bf16[1,72,640]{2,1,0:T(8,128)(2,1)S(1)}, bf16[1,72,640]{2,1,0:T(8,128)(2,1)S(1)}, u32[]{:S(2)}, u32[]{:S(2)}) collective-permute-start(bf16[1,72,640]{2,1,0:T(8,128)(2,1)S(1)} %shard_map.154.refs_0_), channel_id=1, source_target_pairs={{0,8},{4,12},{8,0},{12,4},{16,24},{20,28},{24,16},{28,20},{1,9},{5... | collective-permute-start | bytes 276488 | tf_op jit(solution)/shard_map/ppermute | solution.py:248
  88.2 13.1 %collective-permute-start.15 = (bf16[3,40,1152]{2,1,0:T(8,128)(2,1)S(1)}, bf16[3,40,1152]{2,1,0:T(8,128)(2,1)S(1)}, u32[]{:S(2)}, u32[]{:S(2)}) collective-permute-start(bf16[3,40,1152]{2,1,0:T(8,128)(2,1)S(1)} %get-tuple-element.85), channel_id=1, source_target_pairs={{0,1},{1,0},{2,3},{3,2},{4,5},{5,4},{6,7},{7,6},{8,9},{9,8},{10,11... | collective-permute-start | bytes 829448 | tf_op jit(solution)/shard_map/ppermute | solution.py:248
  88.2 14.7 %collective-permute-start.16 = (bf16[3,40,1152]{2,1,0:T(8,128)(2,1)S(1)}, bf16[3,40,1152]{2,1,0:T(8,128)(2,1)S(1)}, u32[]{:S(2)}, u32[]{:S(2)}) collective-permute-start(bf16[3,40,1152]{2,1,0:T(8,128)(2,1)S(1)} %get-tuple-element.86), channel_id=1, source_target_pairs={{0,2},{1,3},{2,0},{3,1},{4,6},{5,7},{6,4},{7,5},{8,10},{9,11},{10,... | collective-permute-start | bytes 829448 | tf_op jit(solution)/shard_map/ppermute | solution.py:248
  92.3 5.6 %collective-permute-start.26 = (bf16[2,72,640]{2,1,0:T(8,128)(2,1)S(1)}, bf16[2,72,640]{2,1,0:T(8,128)(2,1)S(1)}, u32[]{:S(2)}, u32[]{:S(2)}) collective-permute-start(bf16[2,72,640]{2,1,0:T(8,128)(2,1)S(1)} %shard_map.155.refs_0_), channel_id=1, source_target_pairs={{0,16},{4,20},{8,24},{12,28},{16,0},{20,4},{24,8},{28,12},{1,17},{... | collective-permute-start | bytes 552968 | tf_op jit(solution)/shard_map/ppermute | solution.py:248
  98.0 6.6 %collective-permute-start.27 = (bf16[4,72,640]{2,1,0:T(8,128)(2,1)S(1)}, bf16[4,72,640]{2,1,0:T(8,128)(2,1)S(1)}, u32[]{:S(2)}, u32[]{:S(2)}) collective-permute-start(bf16[4,72,640]{2,1,0:T(8,128)(2,1)S(1)} %shard_map.156.mine_ref), channel_id=1, source_target_pairs={{0,4},{4,0},{8,12},{12,8},{16,20},{20,16},{24,28},{28,24},{1,5},{5... | collective-permute-start | bytes 1105928 | tf_op jit(solution)/shard_map/ppermute | solution.py:248

commit v4 on v3

v4 whole, which is shorter than its diff:
```python
import functools
import math

import jax
import jax.numpy as jnp
from jax import lax
from jax.experimental import pallas as pl
from jax.experimental.pallas import tpu as pltpu
from jax.sharding import PartitionSpec as P

HEAD_DIM = 72
LANES = 128
VMEM_BYTES = 24 * 1024 * 1024
COST = 2 * 10**10
SMALL = 10
F32 = jnp.float32
BF16 = jnp.bfloat16
NT = (((1,), (1,)), ((), ()))
NN = (((1,), (0,)), ((), ()))
TN = (((0,), (0,)), ((), ()))


def dot(left, right, form):
    return lax.dot_general(left, right, form, preferred_element_type=F32)


def windows(width):
    found = []
    for head in range(width // HEAD_DIM):
        first = head * HEAD_DIM
        start = first // LANES * LANES
        size = -(-(first + HEAD_DIM - start) // LANES) * LANES
        found.append((start, size, first - start))
    return found


def head_only(block, offset):
    lane = lax.broadcasted_iota(jnp.int32, (1, block.shape[1]), 1)
    inside = (lane >= offset) & (lane < offset + HEAD_DIM)
    return jnp.where(inside, block, jnp.zeros_like(block))


def reverse(number, size):
    found = 0
    for i in range(size.bit_length() - 1):
        found = 2 * found + (number >> i & 1)
    return found


def by_core(core, even, odd):
    return even + core * (odd - even)


def same_patch(rows, per_block):
    left = lax.broadcasted_iota(jnp.int32, (rows, 1), 0) % per_block
    right = lax.broadcasted_iota(jnp.int32, (1, rows), 1) % per_block
    return left == right


def forward(per_block, q_ref, k_ref, v_ref, probs_ref, total):
    rows, width = q_ref.shape
    scaling = 1.0 / math.sqrt(HEAD_DIM)
    keep = None if per_block is None else same_patch(rows, per_block)
    total[...] = jnp.zeros_like(total)
    for head, (start, size, offset) in enumerate(windows(width)):
        lanes = slice(start, start + size)
        logits = dot(head_only(q_ref[:, lanes], offset), k_ref[:, lanes], NT) * scaling
        if keep is not None:
            logits = jnp.where(keep, logits, -1e30)
        lifted = jnp.exp(logits - jnp.max(logits, axis=-1, keepdims=True))
        probs = lifted * (1.0 / jnp.sum(lifted, axis=-1, keepdims=True))
        probs_ref[head] = probs
        total[:, lanes] += dot(probs.astype(BF16), head_only(v_ref[:, lanes], offset), NN)


def backward(q_ref, k_ref, v_ref, g_ref, probs_ref, dq_sum, dk_sum, dv_sum):
    dq_sum[...] = jnp.zeros_like(dq_sum)
    dk_sum[...] = jnp.zeros_like(dk_sum)
    dv_sum[...] = jnp.zeros_like(dv_sum)
    for head, (start, size, offset) in enumerate(windows(q_ref.shape[1])):
        lanes = slice(start, start + size)
        probs = probs_ref[head]
        step = head_only(g_ref[:, lanes], offset)
        upstream = dot(step, v_ref[:, lanes], NT)
        dv_sum[:, lanes] += dot(probs.astype(BF16), step, TN)
        mean = jnp.sum(probs * upstream, axis=-1, keepdims=True)
        dscore = (probs * (upstream - mean)).astype(BF16)
        dq_sum[:, lanes] += dot(dscore, head_only(k_ref[:, lanes], offset), NN)
        dk_sum[:, lanes] += dot(dscore, head_only(q_ref[:, lanes], offset), TN)


def space_forward_kernel(q_ref, k_ref, v_ref, out_ref, probs_ref, total):
    forward(None, q_ref, k_ref, v_ref, probs_ref, total)
    out_ref[...] = total[...].astype(BF16)


def space_backward_kernel(q_ref, k_ref, v_ref, g_ref, probs_ref, dq_ref, dk_ref, dv_ref, *sums):
    scaling = 1.0 / math.sqrt(HEAD_DIM)
    backward(q_ref, k_ref, v_ref, g_ref, probs_ref, *sums)
    dq_ref[...] = (sums[0][...] * scaling).astype(BF16)
    dk_ref[...] = (sums[1][...] * scaling).astype(BF16)
    dv_ref[...] = sums[2][...].astype(BF16)


def pack_kernel(first, where_ref, *refs):
    count = refs[-1].shape[0]
    for i, piece_ref in enumerate(refs[count:]):
        for j, array_ref in enumerate(refs[:count]):
            piece_ref[j] = array_ref[where_ref[1] ^ (first + i)]


def unpack_kernel(where_ref, *refs):
    count = refs[0].shape[0]
    groups = len(refs) - count
    for i in range(groups):
        for j in range(count):
            refs[groups + j][where_ref[1] ^ i] = refs[i][j]


def time_forward_kernel(groups, *refs):
    pieces, (probs_ref, qkv_ref, total) = refs[:groups], refs[groups:]
    per_block = pieces[0].shape[1]
    for i in range(groups):
        qkv_ref[:, per_block * i : per_block * (i + 1), :] = pieces[i][...]
    forward(per_block, qkv_ref.at[0], qkv_ref.at[1], qkv_ref.at[2], probs_ref, total)


def time_backward_kernel(groups, step_ref, qkv_ref, probs_ref, *refs):
    outs, sums = refs[:groups], refs[groups:]
    per_block = outs[0].shape[1]
    backward(qkv_ref.at[0], qkv_ref.at[1], qkv_ref.at[2], step_ref, probs_ref, *sums)
    scaling = 1.0 / math.sqrt(HEAD_DIM)
    for i in range(groups):
        rows = slice(per_block * i, per_block * (i + 1))
        outs[i][0] = (sums[0][rows, :] * scaling).astype(BF16)
        outs[i][1] = (sums[1][rows, :] * scaling).astype(BF16)
        outs[i][2] = sums[2][rows, :].astype(BF16)


def project_kernel(groups, *refs):
    pieces, (time_ref, weight_ref) = refs[:groups], refs[groups : groups + 2]
    pair_ref, step_ref = refs[groups + 2 : groups + 4]
    outs, total = refs[groups + 4 : 2 * groups + 4], refs[2 * groups + 4]
    per_block = pieces[0].shape[1]
    for i in range(groups):
        rows = slice(per_block * i, per_block * (i + 1))
        total[rows, :] = pieces[i][0].astype(F32) + time_ref[rows, :]
    comb = total[...].astype(BF16)
    pair_ref[0] = comb
    for i in range(groups):
        total[per_block * i : per_block * (i + 1), :] = pieces[i][1].astype(F32)
    og = (dot(comb, weight_ref[...], NN) - total[...]).astype(BF16)
    pair_ref[1] = og
    total[...] = dot(og, weight_ref[...], NT)
    step_ref[...] = total[...].astype(BF16)
    for i in range(groups):
        outs[i][0] = total[per_block * i : per_block * (i + 1), :].astype(BF16)


def copy_kernel(in_ref, out_ref):
    out_ref[...] = in_ref[...]


def stack_kernel(*refs):
    for i, ref in enumerate(refs[:-1]):
        size = ref.shape[0]
        refs[-1][i * size : (i + 1) * size] = ref[...]


def weight_kernel(where_ref, mine_ref, other_ref, out_ref):
    core, chip = where_ref[0] & 1, where_ref[0] >> 1
    size = mine_ref.shape[0]
    for i in range(size):
        back = reverse(i, size)
        out_ref[2 * (chip ^ by_core(core, i, back)) + core] = mine_ref[i]
        out_ref[2 * (chip ^ by_core(core, back, i)) + 1 - core] = other_ref[i]


def halve_kernel(keep_ref, came_ref, *outs):
    total = keep_ref[...] + came_ref[...].astype(F32)
    half = total.shape[0] // 2
    if half == 0:
        outs[0][...] = total.astype(outs[0].dtype)
    else:
        outs[0][...] = total[:half]
        outs[1][...] = total[half:].astype(BF16)


def turn_kernel(order, where_ref, mine_ref, came_ref, keep_ref, send_ref, total):
    total[...] = mine_ref[0] + came_ref[0].astype(F32)
    half = len(order) // 2
    for i, bits in enumerate(order):
        piece = total[where_ref[1] ^ bits]
        if i < half:
            keep_ref[i] = piece
        else:
            send_ref[i - half] = piece.astype(BF16)


def join_kernel(scaling, where_ref, mine_ref, other_ref, out_ref):
    core, chip = where_ref[0] & 1, where_ref[0] >> 1
    chips, _, size = mine_ref.shape
    first = core == 0
    for i in range(chips):
        back = reverse(i, chips)
        mine = mine_ref[by_core(core, i, back)].astype(F32) * scaling
        other = other_ref[by_core(core, back, i)].astype(F32) * scaling
        out_ref[chip ^ i, :, :size] = jnp.where(first, mine, other)
        out_ref[chip ^ i, :, size:] = jnp.where(first, other, mine)[:, 2 * size - out_ref.shape[-1] :]


def grad_kernel(where_ref, mine_ref, other_ref, keep_ref, send_ref, total):
    core, chip = where_ref[0] & 1, where_ref[0] >> 1
    stays, _, _, size = keep_ref.shape
    first = pl.multiple_of(core * (mine_ref.shape[-1] - size), LANES)
    term = dot(mine_ref[0], mine_ref[1, :, pl.ds(first, size)], TN)
    term += dot(other_ref[0], other_ref[1, :, pl.ds(first, size)], TN)
    total[...] = term.reshape(total.shape)
    for i in range(2 * stays):
        piece = total[:, chip ^ by_core(core, reverse(i, 2 * stays), i)]
        if i < stays:
            keep_ref[i] = piece
        else:
            send_ref[i - stays] = piece.astype(BF16)


def call(body, outs, scratch, where, *args, cost=COST):
    in_specs = [pl.BlockSpec(memory_space=pltpu.VMEM)] * len(args)
    if where is not None:
        in_specs = [pl.BlockSpec(memory_space=pltpu.SMEM)] + in_specs
        args = (where,) + args
    return pl.pallas_call(
        body,
        out_shape=tuple(jax.ShapeDtypeStruct(*out) for out in outs),
        in_specs=in_specs,
        out_specs=(pl.BlockSpec(memory_space=pltpu.VMEM),) * len(outs),
        scratch_shapes=[pltpu.VMEM(*item) for item in scratch],
        cost_estimate=pl.CostEstimate(flops=cost, bytes_accessed=10, transcendentals=0),
        compiler_params=pltpu.CompilerParams(vmem_limit_bytes=VMEM_BYTES),
    )(*args)


def swap(array, axis, bits):
    size = lax.axis_size(axis)
    return lax.ppermute(array, axis, [(i, i ^ bits) for i in range(size)])


def after(value, *others):
    return lax.optimization_barrier((value,) + others)[0]


def stack(left, right, cost=COST):
    shape = (2 * left.shape[0],) + left.shape[1:]
    return call(stack_kernel, [(shape, BF16)], [], None, left, right, cost=cost)[0]


def swap_ways(array, step, count):
    bits = (2 << step, 2 << (count - 1 - step))
    size = lax.axis_size("dp")
    return lax.ppermute(array, "dp", [(i, i ^ bits[i % 2]) for i in range(size)])


def doubled(held, count, *earlier, cost=COST):
    for step in range(count):
        came = swap_ways(held, step, count)
        if step < len(earlier):
            held = after(held, earlier[step])
        held = stack(held, came, cost)
    return held


def gather_weight(weight, earlier, where):
    size = lax.axis_size("dp")
    held = doubled(weight, (size // 2).bit_length() - 1, *earlier)
    (full,) = call(
        weight_kernel,
        [((size,) + weight.shape[1:], BF16)],
        [],
        where,
        held,
        swap(held, "dp", 1),
    )
    return full.reshape(size * weight.shape[1], weight.shape[2])


def bits_of(size):
    return [1 << i for i in range(size.bit_length() - 1)]


def halving(bits):
    order = [0]
    for bit in reversed(bits):
        order = order + [item ^ bit for item in order]
    return order


def halved(keep, came):
    count, rest = keep.shape[0], keep.shape[1:]
    if count == 1:
        return call(halve_kernel, [(keep.shape, BF16)], [], None, keep, came, cost=SMALL)
    half = (count // 2,) + rest
    return call(halve_kernel, [(half, F32), (half, BF16)], [], None, keep, came, cost=SMALL)


def gradient_terms(pair, where):
    width = pair.shape[-1]
    chip_size, groups = lax.axis_size("dp") // 2, lax.axis_size("seq")
    rows = width // groups // chip_size
    size = -(-width // (2 * LANES)) * LANES
    cut = (chip_size // 2, groups, rows, size)
    return call(
        grad_kernel,
        [(cut, F32), (cut, BF16)],
        [((groups, chip_size, rows, size), F32)],
        where,
        pair,
        swap(pair, "dp", 1),
    )


def weight_gradient(terms, width, earlier, space_backward, back, scaling, where):
    keep, send = terms
    chip_size, groups = lax.axis_size("dp") // 2, lax.axis_size("seq")
    rows, size = keep.shape[2:]
    count, seq_bits = chip_size.bit_length() - 1, bits_of(groups)
    keep = after(keep, *earlier)
    for step in range(count - 1):
        keep, send = halved(keep, swap_ways(send, step, count))
    order = halving(seq_bits)
    cut = (groups // 2, rows, size)
    keep, send = call(
        functools.partial(turn_kernel, order),
        [(cut, F32), (cut, BF16)],
        [((groups, rows, size), F32)],
        where,
        keep,
        swap_ways(send, count - 1, count),
        cost=SMALL,
    )
    for bit in seq_bits[:-1]:
        keep, send = halved(keep, swap(send, "seq", bit))
    keep = after(keep, back[-1])
    (total,) = halved(keep, swap(send, "seq", seq_bits[-1]))
    beside = space_backward(total)
    mine = doubled(total, count, total, beside[0], cost=SMALL)
    (whole,) = call(
        functools.partial(join_kernel, scaling),
        [((chip_size, rows, width), F32)],
        [],
        where,
        mine,
        swap(mine, "dp", 1),
        cost=SMALL,
    )
    return whole.reshape(chip_size * rows, width), beside


def divides(width):
    cuts = lax.axis_size("seq") * lax.axis_size("dp") // 2
    return width % (cuts * 8) == 0


def shards(q_space, k_space, v_space, q_time, k_time, v_time, weight, target):
    groups = lax.axis_size("seq")
    where = jnp.stack([lax.axis_index("dp"), lax.axis_index("seq")])
    rows, width = q_space.shape[1:]
    heads = width // HEAD_DIM
    per_block = rows // groups
    blocks, piece, full = (groups, per_block, width), (per_block, width), (rows, width)

    def exchange(pieces):
        return list(pieces[:1]) + [swap(pieces[i], "seq", i) for i in range(1, groups)]

    times = [item.reshape(blocks) for item in (q_time, k_time, v_time)]
    sent = call(
        functools.partial(pack_kernel, 1),
        [((3,) + piece, BF16)] * (groups - 1),
        [],
        where,
        *times,
        cost=SMALL,
    )
    (own,) = call(
        functools.partial(pack_kernel, 0),
        [((3,) + piece, BF16)],
        [],
        after(where, sent[0]),
        *times,
    )
    (rows_here,) = call(
        copy_kernel, [((1,) + weight.shape, BF16)], [], None, after(weight, sent[0])[None]
    )
    there = exchange([own, *sent])
    space = [item.reshape(full) for item in (q_space, k_space, v_space)]
    out_space, probs_s = call(
        space_forward_kernel,
        [(full, BF16), ((heads, rows, rows), F32)],
        [(full, F32)],
        None,
        *space,
    )
    full_weight = gather_weight(rows_here, (own, out_space), where)
    there[0] = after(there[0], out_space)
    outer = call(
        functools.partial(pack_kernel, 0),
        [((2,) + piece, BF16)] * groups,
        [],
        where,
        out_space.reshape(blocks),
        target.reshape(blocks),
        cost=SMALL,
    )
    probs_t, time_qkv, out_time = call(
        functools.partial(time_forward_kernel, groups),
        [((heads, rows, rows), F32), ((3,) + full, BF16), (full, F32)],
        [],
        None,
        *there,
    )
    pair, step, *steps = call(
        functools.partial(project_kernel, groups),
        [((2,) + full, BF16), (full, BF16)] + [((1,) + piece, BF16)] * groups,
        [(full, F32)],
        None,
        *exchange(outer),
        out_time,
        full_weight,
    )
    scaling = 1.0 / math.sqrt(lax.axis_size("dp") * groups * rows)
    if divides(width):
        terms = gradient_terms(pair, where)
        steps = [item if i == groups - 1 else after(item, terms[1]) for i, item in enumerate(steps)]
    (step_home,) = call(
        unpack_kernel, [(blocks, BF16)], [], where, *exchange(steps), cost=SMALL
    )
    time_grads = call(
        functools.partial(time_backward_kernel, groups),
        [((3,) + piece, BF16)] * groups,
        [(full, F32)] * 3,
        None,
        step,
        time_qkv,
        probs_t,
    )
    def space_backward(earlier):
        return call(
            space_backward_kernel,
            [(full, BF16)] * 3,
            [(full, F32)] * 3,
            None,
            *space,
            after(step_home, earlier).reshape(full),
            probs_s,
        )

    back = exchange(time_grads)
    if divides(width):
        weight_grad, space_grads = weight_gradient(
            terms, width, (time_grads[0], step_home), space_backward, back, scaling, where
        )
    else:
        term = dot(pair[0], pair[1], TN).astype(BF16)
        share = lax.psum_scatter(term, "seq", scatter_dimension=0, tiled=True)
        weight_grad = lax.psum(share, "dp").astype(F32) * scaling
        space_grads = space_backward(time_grads[0])
    back = call(unpack_kernel, [(blocks, BF16)] * 3, [], where, *back)
    outs = [item.reshape(q_space.shape) for item in list(space_grads) + list(back)]
    return tuple(outs) + (weight_grad,)


def solution(mesh):
    tokens = P("dp", "seq", None)
    return jax.shard_map(
        shards,
        mesh=mesh,
        in_specs=(tokens,) * 6 + (P("dp", None), tokens),
        out_specs=(tokens,) * 6 + (P("seq", None),),
        check_vma=False,
    )
```

time: 107 us -> 104 us (0.972)
  waiting for transfers between devices: 36.8 us -> 34.8 us
  starting transfers between devices: 40.7 us -> 39.5 us
    ppermute x28 -> x17, waiting for transfers between devices: 36.8 us -> 19.8 us  [swap(): return lax.ppermute(array, axis, [(i, i ^ bits) for i in range(size)])]
    ppermute x0 -> x6, waiting for transfers between devices: none -> 15 us  [swap_ways(): lax.ppermute(array, 'dp', [(i, i ^ bits[i % 2]) for i in range(size)])]
    ppermute x28 -> x17, starting transfers between devices: 40.7 us -> 31.2 us  [swap(): return lax.ppermute(array, axis, [(i, i ^ bits) for i in range(size)])]
    ppermute x0 -> x6, starting transfers between devices: none -> 8.31 us  [swap_ways(): lax.ppermute(array, 'dp', [(i, i ^ bits[i % 2]) for i in range(size)])]
    pallas_call x23 -> x22, Pallas kernels: 23.9 us -> 24.6 us  [call(): pl.pallas_call(body, out_shape=tuple((jax.ShapeDtypeStruct(*out) for out...]
  transfers between devices with their start and end apart: 28 -> 23, of which waited for: 16 -> 10; matrix products, arithmetic and copies ran while one was open for 0% -> 0% of each run, Pallas kernels for 18% -> 20%
where the time goes in v4:
time: 104 us
  starting transfers between devices  39.5 us (38%)
  waiting for transfers between devices  34.8 us (33%)
  Pallas kernels  24.6 us (24%)
  local copies, waits for them, and re-layouts  3.96 us (4%)
    ppermute x17, starting transfers between devices, swap(): return lax.ppermute(array, axis, [(i, i ^ bits) for i in range(size)])  31.2 us
    pallas_call x22, Pallas kernels, call(): pl.pallas_call(body, out_shape=tuple((jax.ShapeDtypeStruct(*out) for out...  24.6 us
    ppermute x17, waiting for transfers between devices, swap(): return lax.ppermute(array, axis, [(i, i ^ bits) for i in range(size)])  19.8 us
    ppermute x6, waiting for transfers between devices, swap_ways(): lax.ppermute(array, 'dp', [(i, i ^ bits[i % 2]) for i in range(size)])  15 us
    ppermute x6, starting transfers between devices, swap_ways(): lax.ppermute(array, 'dp', [(i, i ^ bits[i % 2]) for i in range(size)])  8.31 us
    unnamed x20, local copies, waits for them, and re-layouts  3.96 us
  transfers between devices with their start and end apart: 23, of which 10 were waited for; matrix products, arithmetic and copies ran while one was open for 0% of the time, Pallas kernels for 20%

profile of v4, /device:TPU:0, one launch (start us, length us, event | category | flops | bytes accessed | tf_op | source)
XLA Modules:
  0.0 103.8 jit_solution(8180144581254899513)
XLA Ops:
  0.6 0.1 pad_add_fusion.where_ref
  0.7 1.0 copy-done.1
  1.7 1.0 copy-done.3
  2.7 1.0 copy-done.5
  3.7 0.6 shard_map.137
  4.3 4.1 %collective-permute-start.4 = (bf16[3,40,1152]{2,1,0:T(8,128)(2,1)S(1)}, bf16[3,40,1152]{2,1,0:T(8,128)(2,1)S(1)}, u32[]{:S(2)}, u32[]{:S(2)}) collective-permute-start(bf16[3,40,1152]{2,1,0:T(8,128)(2,1)S(1)} %get-tuple-element.64), channel_id=1, source_target_pairs={{0,2},{1,3},{2,0},{3,1},{4,6},{5,7},{6,4},{7,5},{8,10},{9,11},{10,... | collective-permute-start | bytes 829448 | tf_op jit(solution)/shard_map/ppermute | solution.py:245
  8.4 1.3 %collective-permute-start.5 = (bf16[3,40,1152]{2,1,0:T(8,128)(2,1)S(1)}, bf16[3,40,1152]{2,1,0:T(8,128)(2,1)S(1)}, u32[]{:S(2)}, u32[]{:S(2)}) collective-permute-start(bf16[3,40,1152]{2,1,0:T(8,128)(2,1)S(1)} %get-tuple-element.65), channel_id=1, source_target_pairs={{0,3},{1,2},{2,1},{3,0},{4,7},{5,6},{6,5},{7,4},{8,11},{9,10},{10,... | collective-permute-start | bytes 829448 | tf_op jit(solution)/shard_map/ppermute | solution.py:245
  9.7 0.2 collective-permute-start.3
  10.0 1.0 copy-done.9
  11.0 1.6 %collective-permute-start.6 = (bf16[1,144,1152]{2,1,0:T(8,128)(2,1)S(1)}, bf16[1,144,1152]{2,1,0:T(8,128)(2,1)S(1)}, u32[]{:S(2)}, u32[]{:S(2)}) collective-permute-start(bf16[1,144,1152]{2,1,0:T(8,128)(2,1)S(1)} %shard_map.140.refs_0_), channel_id=1, source_target_pairs={{0,8},{4,20},{8,0},{12,28},{16,24},{20,4},{24,16},{28,12},{1,9},{5... | collective-permute-start | bytes 995336 | tf_op jit(solution)/shard_map/ppermute | solution.py:260
  12.5 0.6 shard_map.138.refs_0_
  13.1 0.0 copy-start.6
  13.1 0.0 copy-start.7
  13.1 0.0 copy-start.8
  13.1 5.0 %collective-permute-done.6.refs_1_ = bf16[1,144,1152]{2,1,0:T(8,128)(2,1)S(1)} collective-permute-done((bf16[1,144,1152]{2,1,0:T(8,128)(2,1)S(1)}, bf16[1,144,1152]{2,1,0:T(8,128)(2,1)S(1)}, u32[]{:S(2)}, u32[]{:S(2)}) %collective-permute-start.6) | collective-permute-done | bytes 331808 | tf_op jit(solution)/shard_map/ppermute | solution.py:260
  18.2 1.6 %collective-permute-start.7 = (bf16[2,144,1152]{2,1,0:T(8,128)(2,1)S(1)}, bf16[2,144,1152]{2,1,0:T(8,128)(2,1)S(1)}, u32[]{:S(2)}, u32[]{:S(2)}) collective-permute-start(bf16[2,144,1152]{2,1,0:T(8,128)(2,1)S(1)} %shard_map.141.refs_0_), channel_id=1, source_target_pairs={{0,16},{4,12},{8,24},{12,4},{16,0},{20,28},{24,8},{28,20},{1,17},{... | collective-permute-start | bytes 1990664 | tf_op jit(solution)/shard_map/ppermute | solution.py:260
  19.8 1.9 %shard_map.135 = (bf16[160,1152]{1,0:T(8,128)(2,1)S(1)}, f32[16,160,160]{2,1,0:T(8,128)S(1)}) custom-call(bf16[160,1152]{1,0:T(8,128)(2,1)S(1)} %bitcast.29, bf16[160,1152]{1,0:T(8,128)(2,1)S(1)} %bitcast.31, bf16[160,1152]{1,0:T(8,128)(2,1)S(1)} %bitcast.33), custom_call_target="tpu_custom_call" | custom-call | flops 20000000000 | bytes 10 | tf_op jit(solution)/shard_map/pallas_call | solution.py:232
  21.7 0.6 shard_map.136
  22.3 1.9 %collective-permute-start = (bf16[2,40,1152]{2,1,0:T(8,128)(2,1)S(1)}, bf16[2,40,1152]{2,1,0:T(8,128)(2,1)S(1)}, u32[]{:S(2)}, u32[]{:S(2)}) collective-permute-start(bf16[2,40,1152]{2,1,0:T(8,128)(2,1)S(1)} %get-tuple-element.58), channel_id=1, source_target_pairs={{0,1},{1,0},{2,3},{3,2},{4,5},{5,4},{6,7},{7,6},{8,9},{9,8},{10,11... | collective-permute-start | bytes 552968 | tf_op jit(solution)/shard_map/ppermute | solution.py:245
  24.2 4.8 %collective-permute-done.7.refs_1_ = bf16[2,144,1152]{2,1,0:T(8,128)(2,1)S(1)} collective-permute-done((bf16[2,144,1152]{2,1,0:T(8,128)(2,1)S(1)}, bf16[2,144,1152]{2,1,0:T(8,128)(2,1)S(1)}, u32[]{:S(2)}, u32[]{:S(2)}) %collective-permute-start.7) | collective-permute-done | bytes 663584 | tf_op jit(solution)/shard_map/ppermute | solution.py:260
  29.0 2.8 %collective-permute-start.1 = (bf16[2,40,1152]{2,1,0:T(8,128)(2,1)S(1)}, bf16[2,40,1152]{2,1,0:T(8,128)(2,1)S(1)}, u32[]{:S(2)}, u32[]{:S(2)}) collective-permute-start(bf16[2,40,1152]{2,1,0:T(8,128)(2,1)S(1)} %get-tuple-element.59), channel_id=1, source_target_pairs={{0,2},{1,3},{2,0},{3,1},{4,6},{5,7},{6,4},{7,5},{8,10},{9,11},{10,... | collective-permute-start | bytes 552968 | tf_op jit(solution)/shard_map/ppermute | solution.py:245
  31.8 0.1 shard_map.142.mine_ref
  31.9 1.4 %collective-permute-start.2 = (bf16[2,40,1152]{2,1,0:T(8,128)(2,1)S(1)}, bf16[2,40,1152]{2,1,0:T(8,128)(2,1)S(1)}, u32[]{:S(2)}, u32[]{:S(2)}) collective-permute-start(bf16[2,40,1152]{2,1,0:T(8,128)(2,1)S(1)} %get-tuple-element.60), channel_id=1, source_target_pairs={{0,3},{1,2},{2,1},{3,0},{4,7},{5,6},{6,5},{7,4},{8,11},{9,10},{10,... | collective-permute-start | bytes 552968 | tf_op jit(solution)/shard_map/ppermute | solution.py:245
  33.3 0.0 collective-permute-done.5.refs_3_
  33.3 0.0 collective-permute-start.8
  33.3 0.0 collective-permute-done.3.refs_1_
  33.3 2.0 %shard_map.139 = (f32[16,160,160]{2,1,0:T(8,128)S(1)}, bf16[3,160,1152]{2,1,0:T(8,128)(2,1)S(1)}, f32[160,1152]{1,0:T(8,128)S(1)}) custom-call(bf16[3,40,1152]{2,1,0:T(8,128)(2,1)S(1)} %shard_map.138.refs_0_, bf16[3,40,1152]{2,1,0:T(8,128)(2,1)S(1)} %collective-permute-done.3.refs_1_, bf16[3,40,1152]{2,1,0:T(8,128)(2,1)S(1)} %collective-permute-done.4.refs_2_, ...), custom_call_target="tpu_custom_call" | custom-call | flops 20000000000 | bytes 10 | tf_op jit(solution)/shard_map/pallas_call | solution.py:232
  35.3 1.1 %collective-permute-done.8.other_ref = bf16[4,144,1152]{2,1,0:T(8,128)(2,1)S(1)} collective-permute-done((bf16[4,144,1152]{2,1,0:T(8,128)(2,1)S(1)}, bf16[4,144,1152]{2,1,0:T(8,128)(2,1)S(1)}, u32[]{:S(2)}, u32[]{:S(2)}) %collective-permute-start.8) | collective-permute-done | bytes 1327136 | tf_op jit(solution)/shard_map/ppermute | solution.py:245
  36.3 0.7 shard_map.143
  37.1 0.0 collective-permute-done.refs_1_
  37.1 8.4 %collective-permute-done.1.refs_2_ = bf16[2,40,1152]{2,1,0:T(8,128)(2,1)S(1)} collective-permute-done((bf16[2,40,1152]{2,1,0:T(8,128)(2,1)S(1)}, bf16[2,40,1152]{2,1,0:T(8,128)(2,1)S(1)}, u32[]{:S(2)}, u32[]{:S(2)}) %collective-permute-start.1) | collective-permute-done | bytes 184352 | tf_op jit(solution)/shard_map/ppermute | solution.py:245
  45.5 0.0 collective-permute-done.2.refs_3_
  45.5 1.5 %shard_map.144 = (bf16[2,160,1152]{2,1,0:T(8,128)(2,1)S(1)}, bf16[160,1152]{1,0:T(8,128)(2,1)S(1)}, bf16[1,40,1152]{2,1,0:T(8,128)(2,1)S(1)}, bf16[1,40,1152]{2,...) custom-call(bf16[2,40,1152]{2,1,0:T(8,128)(2,1)S(1)} %get-tuple-element.57.refs_0_, ...), custom_call_target="tpu_custom_call" | custom-call | flops 20000000000 | bytes 10 | tf_op jit(solution)/shard_map/pallas_call | solution.py:232
  47.1 0.1 collective-permute-start.9
  47.1 2.9 %collective-permute-start.12 = (bf16[1,40,1152]{2,1,0:T(8,128)(2,1)S(1)}, bf16[1,40,1152]{2,1,0:T(8,128)(2,1)S(1)}, u32[]{:S(2)}, u32[]{:S(2)}) collective-permute-start(bf16[1,40,1152]{2,1,0:T(8,128)(2,1)S(1)} %get-tuple-element.78), channel_id=1, source_target_pairs={{0,3},{1,2},{2,1},{3,0},{4,7},{5,6},{6,5},{7,4},{8,11},{9,10},{10,... | collective-permute-start | bytes 276488 | tf_op jit(solution)/shard_map/ppermute | solution.py:245
  50.0 0.0 collective-permute-done.9.other_ref
  50.0 1.8 %shard_map.145 = (f32[2,4,72,640]{3,2,1,0:T(8,128)S(1)}, bf16[2,4,72,640]{3,2,1,0:T(8,128)(2,1)S(1)}) custom-call(s32[2]{0:T(128)S(1)} %pad_add_fusion.where_ref, bf16[2,160,1152]{2,1,0:T(8,128)(2,1)S(1)} %get-tuple-element.71.mine_ref, bf16[2,160,1152]{2,1,0:T(8,128)(2,1)S(1)} %collective-permute-done.9.other_ref), custom_call_target="tpu_custom_call" | custom-call | flops 20000000000 | bytes 10 | tf_op jit(solution)/shard_map/pallas_call | solution.py:232
  51.8 1.6 %collective-permute-start.13 = (bf16[2,4,72,640]{3,2,1,0:T(8,128)(2,1)S(1)}, bf16[2,4,72,640]{3,2,1,0:T(8,128)(2,1)S(1)}, u32[]{:S(2)}, u32[]{:S(2)}) collective-permute-start(bf16[2,4,72,640]{3,2,1,0:T(8,128)(2,1)S(1)} %get-tuple-element.72), channel_id=1, source_target_pairs={{0,8},{4,20},{8,0},{12,28},{16,24},{20,4},{24,16},{28,12},{1,9},{5... | collective-permute-start | bytes 2211848 | tf_op jit(solution)/shard_map/ppermute | solution.py:260
  53.4 3.5 %collective-permute-start.10 = (bf16[1,40,1152]{2,1,0:T(8,128)(2,1)S(1)}, bf16[1,40,1152]{2,1,0:T(8,128)(2,1)S(1)}, u32[]{:S(2)}, u32[]{:S(2)}) collective-permute-start(bf16[1,40,1152]{2,1,0:T(8,128)(2,1)S(1)} %get-tuple-element.75), channel_id=1, source_target_pairs={{0,1},{1,0},{2,3},{3,2},{4,5},{5,4},{6,7},{7,6},{8,9},{9,8},{10,11... | collective-permute-start | bytes 276488 | tf_op jit(solution)/shard_map/ppermute | solution.py:245
  56.9 1.6 %collective-permute-start.11 = (bf16[1,40,1152]{2,1,0:T(8,128)(2,1)S(1)}, bf16[1,40,1152]{2,1,0:T(8,128)(2,1)S(1)}, u32[]{:S(2)}, u32[]{:S(2)}) collective-permute-start(bf16[1,40,1152]{2,1,0:T(8,128)(2,1)S(1)} %get-tuple-element.77), channel_id=1, source_target_pairs={{0,2},{1,3},{2,0},{3,1},{4,6},{5,7},{6,4},{7,5},{8,10},{9,11},{10,... | collective-permute-start | bytes 276488 | tf_op jit(solution)/shard_map/ppermute | solution.py:245
  58.5 4.3 %shard_map.147 = (bf16[3,40,1152]{2,1,0:T(8,128)(2,1)S(1)}, bf16[3,40,1152]{2,1,0:T(8,128)(2,1)S(1)}, bf16[3,40,1152]{2,1,0:T(8,128)(2,1)S(1)}, bf16[3,40,1152]{2,1,0:T(8,128)(2,1)S(1)}) custom-call(bf16[160,1152]{1,0:T(8,128)(2,1)S(1)} %get-tuple-element.80.step_ref, bf16[3,160,1152]{2,1,0:T(8,128)(2,1)S(1)} %get-tuple-element.81.qkv_ref, ...), custom_call_target="tpu_custom_call" | custom-call | flops 20000000000 | bytes 10 | tf_op jit(solution)/shard_map/pallas_call | solution.py:232
  62.9 0.0 collective-permute-done.10.refs_1_
  62.9 0.5 collective-permute-done.11.refs_2_
  63.4 0.6 shard_map.146
  63.9 0.0 collective-permute-done.13.came_ref
  64.0 0.1 shard_map.148
  64.1 1.1 %collective-permute-start.14 = (bf16[1,4,72,640]{3,2,1,0:T(8,128)(2,1)S(1)}, bf16[1,4,72,640]{3,2,1,0:T(8,128)(2,1)S(1)}, u32[]{:S(2)}, u32[]{:S(2)}) collective-permute-start(bf16[1,4,72,640]{3,2,1,0:T(8,128)(2,1)S(1)} %get-tuple-element.86), channel_id=1, source_target_pairs={{0,16},{4,12},{8,24},{12,4},{16,0},{20,28},{24,8},{28,20},{1,17},{... | collective-permute-start | bytes 1105928 | tf_op jit(solution)/shard_map/ppermute | solution.py:260
  65.2 2.9 %collective-permute-start.16 = (bf16[3,40,1152]{2,1,0:T(8,128)(2,1)S(1)}, bf16[3,40,1152]{2,1,0:T(8,128)(2,1)S(1)}, u32[]{:S(2)}, u32[]{:S(2)}) collective-permute-start(bf16[3,40,1152]{2,1,0:T(8,128)(2,1)S(1)} %get-tuple-element.90), channel_id=1, source_target_pairs={{0,3},{1,2},{2,1},{3,0},{4,7},{5,6},{6,5},{7,4},{8,11},{9,10},{10,... | collective-permute-start | bytes 829448 | tf_op jit(solution)/shard_map/ppermute | solution.py:245
  68.1 3.5 %collective-permute-done.14.came_ref = bf16[1,4,72,640]{3,2,1,0:T(8,128)(2,1)S(1)} collective-permute-done((bf16[1,4,72,640]{3,2,1,0:T(8,128)(2,1)S(1)}, bf16[1,4,72,640]{3,2,1,0:T(8,128)(2,1)S(1)}, u32[]{:S(2)}, u32[]{:S(2)}) %collective-permute-start.14) | collective-permute-done | bytes 368672 | tf_op jit(solution)/shard_map/ppermute | solution.py:260
  71.7 0.7 shard_map.149
  72.3 3.0 %collective-permute-start.15 = (bf16[2,72,640]{2,1,0:T(8,128)(2,1)S(1)}, bf16[2,72,640]{2,1,0:T(8,128)(2,1)S(1)}, u32[]{:S(2)}, u32[]{:S(2)}) collective-permute-start(bf16[2,72,640]{2,1,0:T(8,128)(2,1)S(1)} %get-tuple-element.88), channel_id=1, source_target_pairs={{0,1},{1,0},{2,3},{3,2},{4,5},{5,4},{6,7},{7,6},{8,9},{9,8},{10,11... | collective-permute-start | bytes 552968 | tf_op jit(solution)/shard_map/ppermute | solution.py:245
  75.3 4.4 %collective-permute-done.15.came_ref = bf16[2,72,640]{2,1,0:T(8,128)(2,1)S(1)} collective-permute-done((bf16[2,72,640]{2,1,0:T(8,128)(2,1)S(1)}, bf16[2,72,640]{2,1,0:T(8,128)(2,1)S(1)}, u32[]{:S(2)}, u32[]{:S(2)}) %collective-permute-start.15) | collective-permute-done | bytes 184352 | tf_op jit(solution)/shard_map/ppermute | solution.py:245
  79.8 2.8 %collective-permute-start.17 = (bf16[1,72,640]{2,1,0:T(8,128)(2,1)S(1)}, bf16[1,72,640]{2,1,0:T(8,128)(2,1)S(1)}, u32[]{:S(2)}, u32[]{:S(2)}) collective-permute-start(bf16[1,72,640]{2,1,0:T(8,128)(2,1)S(1)} %get-tuple-element.92), channel_id=1, source_target_pairs={{0,2},{1,3},{2,0},{3,1},{4,6},{5,7},{6,4},{7,5},{8,10},{9,11},{10,... | collective-permute-start | bytes 276488 | tf_op jit(solution)/shard_map/ppermute | solution.py:245
  82.6 4.2 %collective-permute-done.17.came_ref = bf16[1,72,640]{2,1,0:T(8,128)(2,1)S(1)} collective-permute-done((bf16[1,72,640]{2,1,0:T(8,128)(2,1)S(1)}, bf16[1,72,640]{2,1,0:T(8,128)(2,1)S(1)}, u32[]{:S(2)}, u32[]{:S(2)}) %collective-permute-start.17) | collective-permute-done | bytes 92192 | tf_op jit(solution)/shard_map/ppermute | solution.py:245
  86.8 1.2 %collective-permute-start.20 = (bf16[1,72,640]{2,1,0:T(8,128)(2,1)S(1)}, bf16[1,72,640]{2,1,0:T(8,128)(2,1)S(1)}, u32[]{:S(2)}, u32[]{:S(2)}) collective-permute-start(bf16[1,72,640]{2,1,0:T(8,128)(2,1)S(1)} %shard_map.151.refs_0_), channel_id=1, source_target_pairs={{0,8},{4,20},{8,0},{12,28},{16,24},{20,4},{24,16},{28,12},{1,9},{5... | collective-permute-start | bytes 276488 | tf_op jit(solution)/shard_map/ppermute | solution.py:260
  88.0 0.1 collective-permute-start.18
  88.1 2.4 %collective-permute-start.19 = (bf16[3,40,1152]{2,1,0:T(8,128)(2,1)S(1)}, bf16[3,40,1152]{2,1,0:T(8,128)(2,1)S(1)}, u32[]{:S(2)}, u32[]{:S(2)}) collective-permute-start(bf16[3,40,1152]{2,1,0:T(8,128)(2,1)S(1)} %get-tuple-element.99), channel_id=1, source_target_pairs={{0,2},{1,3},{2,0},{3,1},{4,6},{5,7},{6,4},{7,5},{8,10},{9,11},{10,... | collective-permute-start | bytes 829448 | tf_op jit(solution)/shard_map/ppermute | solution.py:245
  90.5 1.7 %collective-permute-done.20.refs_1_ = bf16[1,72,640]{2,1,0:T(8,128)(2,1)S(1)} collective-permute-done((bf16[1,72,640]{2,1,0:T(8,128)(2,1)S(1)}, bf16[1,72,640]{2,1,0:T(8,128)(2,1)S(1)}, u32[]{:S(2)}, u32[]{:S(2)}) %collective-permute-start.20) | collective-permute-done | bytes 92192 | tf_op jit(solution)/shard_map/ppermute | solution.py:260
  92.3 1.3 %collective-permute-start.21 = (bf16[2,72,640]{2,1,0:T(8,128)(2,1)S(1)}, bf16[2,72,640]{2,1,0:T(8,128)(2,1)S(1)}, u32[]{:S(2)}, u32[]{:S(2)}) collective-permute-start(bf16[2,72,640]{2,1,0:T(8,128)(2,1)S(1)} %shard_map.154.refs_0_), channel_id=1, source_target_pairs={{0,16},{4,12},{8,24},{12,4},{16,0},{20,28},{24,8},{28,20},{1,17},{... | collective-permute-start | bytes 552968 | tf_op jit(solution)/shard_map/ppermute | solution.py:260
  93.6 5.4 %shard_map.152 = (bf16[160,1152]{1,0:T(8,128)(2,1)}, bf16[160,1152]{1,0:T(8,128)(2,1)}, bf16[160,1152]{1,0:T(8,128)(2,1)}) custom-call(bf16[160,1152]{1,0:T(8,128)(2,1)S(1)} %bitcast.30, bf16[160,1152]{1,0:T(8,128)(2,1)S(1)} %bitcast.32, bf16[160,1152]{1,0:T(8,128)(2,1)S(1)} %bitcast.34, bf16[160,1152]{1,0:T(8,128)(2,1)S(1)} %bitcast.21, ...), custom_call_target="tpu_custom_call" | custom-call | flops 20000000000 | bytes 10 | tf_op jit(solution)/shard_map/pallas_call | solution.py:232
  99.0 0.1 collective-permute-start.22
  99.1 1.3 %collective-permute-done.19.refs_2_ = bf16[3,40,1152]{2,1,0:T(8,128)(2,1)S(1)} collective-permute-done((bf16[3,40,1152]{2,1,0:T(8,128)(2,1)S(1)}, bf16[3,40,1152]{2,1,0:T(8,128)(2,1)S(1)}, u32[]{:S(2)}, u32[]{:S(2)}) %collective-permute-start.19) | collective-permute-done | bytes 276512 | tf_op jit(solution)/shard_map/ppermute | solution.py:245
  100.4 1.6 %shard_map.153 = (bf16[4,40,1152]{2,1,0:T(8,128)(2,1)}, bf16[4,40,1152]{2,1,0:T(8,128)(2,1)}, bf16[4,40,1152]{2,1,0:T(8,128)(2,1)}) custom-call(s32[2]{0:T(128)S(1)} %pad_add_fusion.where_ref, bf16[3,40,1152]{2,1,0:T(8,128)(2,1)S(1)} %get-tuple-element.83.refs_0_, bf16[3,40,1152]{2,1,0:T(8,128)(2,1)S(1)} %collective-permute-done.18.refs_1_, ...), custom_call_target="tpu_custom_call" | custom-call | flops 20000000000 | bytes 10 | tf_op jit(solution)/shard_map/pallas_call | solution.py:232
  102.0 1.8 %shard_map.156 = f32[4,72,1152]{2,1,0:T(8,128)} custom-call(s32[2]{0:T(128)S(1)} %pad_add_fusion.where_ref, bf16[4,72,640]{2,1,0:T(8,128)(2,1)S(1)} %shard_map.155.mine_ref, bf16[4,72,640]{2,1,0:T(8,128)(2,1)S(1)} %collective-permute-done.22.other_ref), custom_call_target="tpu_custom_call" | custom-call | flops 10 | bytes 10 | tf_op jit(solution)/shard_map/pallas_call | solution.py:232
  (25 shorter events, 0.2 us)
Async XLA Ops:
  0.7 1.0 copy-start.1
  1.7 1.0 copy-start.3
  2.7 1.0 copy-start.5
  4.3 27.6 %collective-permute-start.4 = (bf16[3,40,1152]{2,1,0:T(8,128)(2,1)S(1)}, bf16[3,40,1152]{2,1,0:T(8,128)(2,1)S(1)}, u32[]{:S(2)}, u32[]{:S(2)}) collective-permute-start(bf16[3,40,1152]{2,1,0:T(8,128)(2,1)S(1)} %get-tuple-element.64), channel_id=1, source_target_pairs={{0,2},{1,3},{2,0},{3,1},{4,6},{5,7},{6,4},{7,5},{8,10},{9,11},{10,... | collective-permute-start | bytes 829448 | tf_op jit(solution)/shard_map/ppermute | solution.py:245
  8.4 24.9 %collective-permute-start.5 = (bf16[3,40,1152]{2,1,0:T(8,128)(2,1)S(1)}, bf16[3,40,1152]{2,1,0:T(8,128)(2,1)S(1)}, u32[]{:S(2)}, u32[]{:S(2)}) collective-permute-start(bf16[3,40,1152]{2,1,0:T(8,128)(2,1)S(1)} %get-tuple-element.65), channel_id=1, source_target_pairs={{0,3},{1,2},{2,1},{3,0},{4,7},{5,6},{6,5},{7,4},{8,11},{9,10},{10,... | collective-permute-start | bytes 829448 | tf_op jit(solution)/shard_map/ppermute | solution.py:245
  9.7 23.6 %collective-permute-start.3 = (bf16[3,40,1152]{2,1,0:T(8,128)(2,1)S(1)}, bf16[3,40,1152]{2,1,0:T(8,128)(2,1)S(1)}, u32[]{:S(2)}, u32[]{:S(2)}) collective-permute-start(bf16[3,40,1152]{2,1,0:T(8,128)(2,1)S(1)} %get-tuple-element.61), channel_id=1, source_target_pairs={{0,1},{1,0},{2,3},{3,2},{4,5},{5,4},{6,7},{7,6},{8,9},{9,8},{10,11... | collective-permute-start | bytes 829448 | tf_op jit(solution)/shard_map/ppermute | solution.py:245
  10.0 1.0 copy-start.9
  10.9 1.6 %copy-start.2 = (bf16[1,160,1152]{2,1,0:T(8,128)(2,1)S(1)}, bf16[1,160,1152]{2,1,0:T(8,128)(2,1)}, u32[]{:S(2)}) copy-start(bf16[1,160,1152]{2,1,0:T(8,128)(2,1)} %param.11) | copy-start | bytes 1105924
  10.9 1.6 %copy-start.4 = (bf16[1,160,1152]{2,1,0:T(8,128)(2,1)S(1)}, bf16[1,160,1152]{2,1,0:T(8,128)(2,1)}, u32[]{:S(2)}) copy-start(bf16[1,160,1152]{2,1,0:T(8,128)(2,1)} %param.12) | copy-start | bytes 1105924
  11.0 7.2 %collective-permute-start.6 = (bf16[1,144,1152]{2,1,0:T(8,128)(2,1)S(1)}, bf16[1,144,1152]{2,1,0:T(8,128)(2,1)S(1)}, u32[]{:S(2)}, u32[]{:S(2)}) collective-permute-start(bf16[1,144,1152]{2,1,0:T(8,128)(2,1)S(1)} %shard_map.140.refs_0_), channel_id=1, source_target_pairs={{0,8},{4,20},{8,0},{12,28},{16,24},{20,4},{24,16},{28,12},{1,9},{5... | collective-permute-start | bytes 995336 | tf_op jit(solution)/shard_map/ppermute | solution.py:260
  13.1 6.7 %copy-start.6 = (bf16[1,160,1152]{2,1,0:T(8,128)(2,1)S(1)}, bf16[1,160,1152]{2,1,0:T(8,128)(2,1)}, u32[]{:S(2)}) copy-start(bf16[1,160,1152]{2,1,0:T(8,128)(2,1)} %param.8) | copy-start | bytes 1105924
  13.1 6.7 %copy-start.7 = (bf16[1,160,1152]{2,1,0:T(8,128)(2,1)S(1)}, bf16[1,160,1152]{2,1,0:T(8,128)(2,1)}, u32[]{:S(2)}) copy-start(bf16[1,160,1152]{2,1,0:T(8,128)(2,1)} %param.9) | copy-start | bytes 1105924
  13.1 6.7 %copy-start.8 = (bf16[1,160,1152]{2,1,0:T(8,128)(2,1)S(1)}, bf16[1,160,1152]{2,1,0:T(8,128)(2,1)}, u32[]{:S(2)}) copy-start(bf16[1,160,1152]{2,1,0:T(8,128)(2,1)} %param.10) | copy-start | bytes 1105924
  18.2 10.7 %collective-permute-start.7 = (bf16[2,144,1152]{2,1,0:T(8,128)(2,1)S(1)}, bf16[2,144,1152]{2,1,0:T(8,128)(2,1)S(1)}, u32[]{:S(2)}, u32[]{:S(2)}) collective-permute-start(bf16[2,144,1152]{2,1,0:T(8,128)(2,1)S(1)} %shard_map.141.refs_0_), channel_id=1, source_target_pairs={{0,16},{4,12},{8,24},{12,4},{16,0},{20,28},{24,8},{28,20},{1,17},{... | collective-permute-start | bytes 1990664 | tf_op jit(solution)/shard_map/ppermute | solution.py:260
  19.8 1.9 %copy-start = (bf16[1,160,1152]{2,1,0:T(8,128)(2,1)S(1)}, bf16[1,160,1152]{2,1,0:T(8,128)(2,1)}, u32[]{:S(2)}) copy-start(bf16[1,160,1152]{2,1,0:T(8,128)(2,1)} %param.15) | copy-start | bytes 1105924
  22.3 14.8 %collective-permute-start = (bf16[2,40,1152]{2,1,0:T(8,128)(2,1)S(1)}, bf16[2,40,1152]{2,1,0:T(8,128)(2,1)S(1)}, u32[]{:S(2)}, u32[]{:S(2)}) collective-permute-start(bf16[2,40,1152]{2,1,0:T(8,128)(2,1)S(1)} %get-tuple-element.58), channel_id=1, source_target_pairs={{0,1},{1,0},{2,3},{3,2},{4,5},{5,4},{6,7},{7,6},{8,9},{9,8},{10,11... | collective-permute-start | bytes 552968 | tf_op jit(solution)/shard_map/ppermute | solution.py:245
  29.0 16.5 %collective-permute-start.1 = (bf16[2,40,1152]{2,1,0:T(8,128)(2,1)S(1)}, bf16[2,40,1152]{2,1,0:T(8,128)(2,1)S(1)}, u32[]{:S(2)}, u32[]{:S(2)}) collective-permute-start(bf16[2,40,1152]{2,1,0:T(8,128)(2,1)S(1)} %get-tuple-element.59), channel_id=1, source_target_pairs={{0,2},{1,3},{2,0},{3,1},{4,6},{5,7},{6,4},{7,5},{8,10},{9,11},{10,... | collective-permute-start | bytes 552968 | tf_op jit(solution)/shard_map/ppermute | solution.py:245
  31.9 13.6 %collective-permute-start.2 = (bf16[2,40,1152]{2,1,0:T(8,128)(2,1)S(1)}, bf16[2,40,1152]{2,1,0:T(8,128)(2,1)S(1)}, u32[]{:S(2)}, u32[]{:S(2)}) collective-permute-start(bf16[2,40,1152]{2,1,0:T(8,128)(2,1)S(1)} %get-tuple-element.60), channel_id=1, source_target_pairs={{0,3},{1,2},{2,1},{3,0},{4,7},{5,6},{6,5},{7,4},{8,11},{9,10},{10,... | collective-permute-start | bytes 552968 | tf_op jit(solution)/shard_map/ppermute | solution.py:245
  33.3 3.1 %collective-permute-start.8 = (bf16[4,144,1152]{2,1,0:T(8,128)(2,1)S(1)}, bf16[4,144,1152]{2,1,0:T(8,128)(2,1)S(1)}, u32[]{:S(2)}, u32[]{:S(2)}) collective-permute-start(bf16[4,144,1152]{2,1,0:T(8,128)(2,1)S(1)} %shard_map.142.mine_ref), channel_id=1, source_target_pairs={{0,4},{4,0},{8,12},{12,8},{16,20},{20,16},{24,28},{28,24},{1,5},{5... | collective-permute-start | bytes 3981320 | tf_op jit(solution)/shard_map/ppermute | solution.py:245
  47.1 3.0 %collective-permute-start.9 = (bf16[2,160,1152]{2,1,0:T(8,128)(2,1)S(1)}, bf16[2,160,1152]{2,1,0:T(8,128)(2,1)S(1)}, u32[]{:S(2)}, u32[]{:S(2)}) collective-permute-start(bf16[2,160,1152]{2,1,0:T(8,128)(2,1)S(1)} %get-tuple-element.71.mine_ref), channel_id=1, source_target_pairs={{0,4},{4,0},{8,12},{12,8},{16,20},{20,16},{24,28},{28,24},{1,5},{5... | collective-permute-start | bytes 2211848 | tf_op jit(solution)/shard_map/ppermute | solution.py:245
  47.1 15.7 %collective-permute-start.12 = (bf16[1,40,1152]{2,1,0:T(8,128)(2,1)S(1)}, bf16[1,40,1152]{2,1,0:T(8,128)(2,1)S(1)}, u32[]{:S(2)}, u32[]{:S(2)}) collective-permute-start(bf16[1,40,1152]{2,1,0:T(8,128)(2,1)S(1)} %get-tuple-element.78), channel_id=1, source_target_pairs={{0,3},{1,2},{2,1},{3,0},{4,7},{5,6},{6,5},{7,4},{8,11},{9,10},{10,... | collective-permute-start | bytes 276488 | tf_op jit(solution)/shard_map/ppermute | solution.py:245
  51.8 12.1 %collective-permute-start.13 = (bf16[2,4,72,640]{3,2,1,0:T(8,128)(2,1)S(1)}, bf16[2,4,72,640]{3,2,1,0:T(8,128)(2,1)S(1)}, u32[]{:S(2)}, u32[]{:S(2)}) collective-permute-start(bf16[2,4,72,640]{3,2,1,0:T(8,128)(2,1)S(1)} %get-tuple-element.72), channel_id=1, source_target_pairs={{0,8},{4,20},{8,0},{12,28},{16,24},{20,4},{24,16},{28,12},{1,9},{5... | collective-permute-start | bytes 2211848 | tf_op jit(solution)/shard_map/ppermute | solution.py:260
  53.4 9.5 %collective-permute-start.10 = (bf16[1,40,1152]{2,1,0:T(8,128)(2,1)S(1)}, bf16[1,40,1152]{2,1,0:T(8,128)(2,1)S(1)}, u32[]{:S(2)}, u32[]{:S(2)}) collective-permute-start(bf16[1,40,1152]{2,1,0:T(8,128)(2,1)S(1)} %get-tuple-element.75), channel_id=1, source_target_pairs={{0,1},{1,0},{2,3},{3,2},{4,5},{5,4},{6,7},{7,6},{8,9},{9,8},{10,11... | collective-permute-start | bytes 276488 | tf_op jit(solution)/shard_map/ppermute | solution.py:245
  56.9 6.4 %collective-permute-start.11 = (bf16[1,40,1152]{2,1,0:T(8,128)(2,1)S(1)}, bf16[1,40,1152]{2,1,0:T(8,128)(2,1)S(1)}, u32[]{:S(2)}, u32[]{:S(2)}) collective-permute-start(bf16[1,40,1152]{2,1,0:T(8,128)(2,1)S(1)} %get-tuple-element.77), channel_id=1, source_target_pairs={{0,2},{1,3},{2,0},{3,1},{4,6},{5,7},{6,4},{7,5},{8,10},{9,11},{10,... | collective-permute-start | bytes 276488 | tf_op jit(solution)/shard_map/ppermute | solution.py:245
  64.1 7.6 %collective-permute-start.14 = (bf16[1,4,72,640]{3,2,1,0:T(8,128)(2,1)S(1)}, bf16[1,4,72,640]{3,2,1,0:T(8,128)(2,1)S(1)}, u32[]{:S(2)}, u32[]{:S(2)}) collective-permute-start(bf16[1,4,72,640]{3,2,1,0:T(8,128)(2,1)S(1)} %get-tuple-element.86), channel_id=1, source_target_pairs={{0,16},{4,12},{8,24},{12,4},{16,0},{20,28},{24,8},{28,20},{1,17},{... | collective-permute-start | bytes 1105928 | tf_op jit(solution)/shard_map/ppermute | solution.py:260
  65.2 17.4 %collective-permute-start.16 = (bf16[3,40,1152]{2,1,0:T(8,128)(2,1)S(1)}, bf16[3,40,1152]{2,1,0:T(8,128)(2,1)S(1)}, u32[]{:S(2)}, u32[]{:S(2)}) collective-permute-start(bf16[3,40,1152]{2,1,0:T(8,128)(2,1)S(1)} %get-tuple-element.90), channel_id=1, source_target_pairs={{0,3},{1,2},{2,1},{3,0},{4,7},{5,6},{6,5},{7,4},{8,11},{9,10},{10,... | collective-permute-start | bytes 829448 | tf_op jit(solution)/shard_map/ppermute | solution.py:245
  72.3 7.4 %collective-permute-start.15 = (bf16[2,72,640]{2,1,0:T(8,128)(2,1)S(1)}, bf16[2,72,640]{2,1,0:T(8,128)(2,1)S(1)}, u32[]{:S(2)}, u32[]{:S(2)}) collective-permute-start(bf16[2,72,640]{2,1,0:T(8,128)(2,1)S(1)} %get-tuple-element.88), channel_id=1, source_target_pairs={{0,1},{1,0},{2,3},{3,2},{4,5},{5,4},{6,7},{7,6},{8,9},{9,8},{10,11... | collective-permute-start | bytes 552968 | tf_op jit(solution)/shard_map/ppermute | solution.py:245
  79.8 7.0 %collective-permute-start.17 = (bf16[1,72,640]{2,1,0:T(8,128)(2,1)S(1)}, bf16[1,72,640]{2,1,0:T(8,128)(2,1)S(1)}, u32[]{:S(2)}, u32[]{:S(2)}) collective-permute-start(bf16[1,72,640]{2,1,0:T(8,128)(2,1)S(1)} %get-tuple-element.92), channel_id=1, source_target_pairs={{0,2},{1,3},{2,0},{3,1},{4,6},{5,7},{6,4},{7,5},{8,10},{9,11},{10,... | collective-permute-start | bytes 276488 | tf_op jit(solution)/shard_map/ppermute | solution.py:245
  86.8 5.5 %collective-permute-start.20 = (bf16[1,72,640]{2,1,0:T(8,128)(2,1)S(1)}, bf16[1,72,640]{2,1,0:T(8,128)(2,1)S(1)}, u32[]{:S(2)}, u32[]{:S(2)}) collective-permute-start(bf16[1,72,640]{2,1,0:T(8,128)(2,1)S(1)} %shard_map.151.refs_0_), channel_id=1, source_target_pairs={{0,8},{4,20},{8,0},{12,28},{16,24},{20,4},{24,16},{28,12},{1,9},{5... | collective-permute-start | bytes 276488 | tf_op jit(solution)/shard_map/ppermute | solution.py:260
  88.0 11.1 %collective-permute-start.18 = (bf16[3,40,1152]{2,1,0:T(8,128)(2,1)S(1)}, bf16[3,40,1152]{2,1,0:T(8,128)(2,1)S(1)}, u32[]{:S(2)}, u32[]{:S(2)}) collective-permute-start(bf16[3,40,1152]{2,1,0:T(8,128)(2,1)S(1)} %get-tuple-element.98), channel_id=1, source_target_pairs={{0,1},{1,0},{2,3},{3,2},{4,5},{5,4},{6,7},{7,6},{8,9},{9,8},{10,11... | collective-permute-start | bytes 829448 | tf_op jit(solution)/shard_map/ppermute | solution.py:245
  88.1 12.3 %collective-permute-start.19 = (bf16[3,40,1152]{2,1,0:T(8,128)(2,1)S(1)}, bf16[3,40,1152]{2,1,0:T(8,128)(2,1)S(1)}, u32[]{:S(2)}, u32[]{:S(2)}) collective-permute-start(bf16[3,40,1152]{2,1,0:T(8,128)(2,1)S(1)} %get-tuple-element.99), channel_id=1, source_target_pairs={{0,2},{1,3},{2,0},{3,1},{4,6},{5,7},{6,4},{7,5},{8,10},{9,11},{10,... | collective-permute-start | bytes 829448 | tf_op jit(solution)/shard_map/ppermute | solution.py:245
  92.3 6.7 %collective-permute-start.21 = (bf16[2,72,640]{2,1,0:T(8,128)(2,1)S(1)}, bf16[2,72,640]{2,1,0:T(8,128)(2,1)S(1)}, u32[]{:S(2)}, u32[]{:S(2)}) collective-permute-start(bf16[2,72,640]{2,1,0:T(8,128)(2,1)S(1)} %shard_map.154.refs_0_), channel_id=1, source_target_pairs={{0,16},{4,12},{8,24},{12,4},{16,0},{20,28},{24,8},{28,20},{1,17},{... | collective-permute-start | bytes 552968 | tf_op jit(solution)/shard_map/ppermute | solution.py:260
  99.0 3.0 %collective-permute-start.22 = (bf16[4,72,640]{2,1,0:T(8,128)(2,1)S(1)}, bf16[4,72,640]{2,1,0:T(8,128)(2,1)S(1)}, u32[]{:S(2)}, u32[]{:S(2)}) collective-permute-start(bf16[4,72,640]{2,1,0:T(8,128)(2,1)S(1)} %shard_map.155.mine_ref), channel_id=1, source_target_pairs={{0,4},{4,0},{8,12},{12,8},{16,20},{20,16},{24,28},{28,24},{1,5},{5... | collective-permute-start | bytes 1105928 | tf_op jit(solution)/shard_map/ppermute | solution.py:245

commit v5 on v4

--- a/solution.py
+++ b/solution.py
@@ -73,11 +73,9 @@
         total[:, lanes] += dot(probs.astype(BF16), head_only(v_ref[:, lanes], offset), NN)
 
 
-def backward(q_ref, k_ref, v_ref, g_ref, probs_ref, dq_sum, dk_sum, dv_sum):
-    dq_sum[...] = jnp.zeros_like(dq_sum)
-    dk_sum[...] = jnp.zeros_like(dk_sum)
-    dv_sum[...] = jnp.zeros_like(dv_sum)
-    for head, (start, size, offset) in enumerate(windows(q_ref.shape[1])):
+def backward(q_ref, k_ref, v_ref, g_ref, probs_ref, dq_sum, dk_sum, dv_sum, heads=slice(None)):
+    found = list(enumerate(windows(q_ref.shape[1])))
+    for head, (start, size, offset) in found[heads]:
         lanes = slice(start, start + size)
         probs = probs_ref[head]
         step = head_only(g_ref[:, lanes], offset)
@@ -94,9 +92,20 @@
     out_ref[...] = total[...].astype(BF16)
 
 
-def space_backward_kernel(q_ref, k_ref, v_ref, g_ref, probs_ref, dq_ref, dk_ref, dv_ref, *sums):
+def space_first_kernel(q_ref, k_ref, v_ref, g_ref, probs_ref, *sums):
+    for item in sums:
+        item[...] = jnp.zeros_like(item)
+    backward(q_ref, k_ref, v_ref, g_ref, probs_ref, *sums, heads=slice(probs_ref.shape[0] // 2))
+
+
+def space_backward_kernel(q_ref, k_ref, v_ref, g_ref, probs_ref, *refs):
+    firsts, (dq_ref, dk_ref, dv_ref), sums = refs[:3], refs[3:6], refs[6:]
+    for first, item in zip(firsts, sums):
+        item[...] = first[...]
+    backward(
+        q_ref, k_ref, v_ref, g_ref, probs_ref, *sums, heads=slice(probs_ref.shape[0] // 2, None)
+    )
     scaling = 1.0 / math.sqrt(HEAD_DIM)
-    backward(q_ref, k_ref, v_ref, g_ref, probs_ref, *sums)
     dq_ref[...] = (sums[0][...] * scaling).astype(BF16)
     dk_ref[...] = (sums[1][...] * scaling).astype(BF16)
     dv_ref[...] = sums[2][...].astype(BF16)
@@ -117,6 +126,20 @@
             refs[groups + j][where_ref[1] ^ i] = refs[i][j]
 
 
+def place_kernel(slots, where_ref, *refs):
+    *refs, sems = refs
+    pieces, outs = refs[: len(slots)], refs[-3:]
+    copies = []
+    for i, slot in enumerate(slots):
+        for j, out_ref in enumerate(outs):
+            block = out_ref.at[where_ref[1] ^ slot]
+            copies.append(pltpu.make_async_copy(pieces[i].at[j], block, sems.at[i, j]))
+    for copy in copies:
+        copy.start()
+    for copy in copies:
+        copy.wait()
+
+
 def time_forward_kernel(groups, *refs):
     pieces, (probs_ref, qkv_ref, total) = refs[:groups], refs[groups:]
     per_block = pieces[0].shape[1]
@@ -128,6 +151,8 @@
 def time_backward_kernel(groups, step_ref, qkv_ref, probs_ref, *refs):
     outs, sums = refs[:groups], refs[groups:]
     per_block = outs[0].shape[1]
+    for item in sums:
+        item[...] = jnp.zeros_like(item)
     backward(qkv_ref.at[0], qkv_ref.at[1], qkv_ref.at[2], step_ref, probs_ref, *sums)
     scaling = 1.0 / math.sqrt(HEAD_DIM)
     for i in range(groups):
@@ -224,6 +249,23 @@
             send_ref[i - stays] = piece.astype(BF16)
 
 
+def place(slots, pieces, arrays, shape, where):
+    whole = pl.BlockSpec(memory_space=pl.ANY)
+    count = len(slots)
+    return pl.pallas_call(
+        functools.partial(place_kernel, slots),
+        out_shape=(jax.ShapeDtypeStruct(shape, BF16),) * 3,
+        in_specs=[pl.BlockSpec(memory_space=pltpu.SMEM)]
+        + [pl.BlockSpec(memory_space=pltpu.VMEM)] * count
+        + [whole] * len(arrays),
+        out_specs=(whole,) * 3,
+        scratch_shapes=[pltpu.SemaphoreType.DMA((count, 3))],
+        input_output_aliases={1 + count + i: i for i in range(len(arrays))},
+        cost_estimate=pl.CostEstimate(flops=COST, bytes_accessed=10, transcendentals=0),
+        compiler_params=pltpu.CompilerParams(vmem_limit_bytes=VMEM_BYTES),
+    )(where, *pieces, *arrays)
+
+
 def call(body, outs, scratch, where, *args, cost=COST):
     in_specs = [pl.BlockSpec(memory_space=pltpu.VMEM)] * len(args)
     if where is not None:
@@ -318,7 +360,7 @@
     )
 
 
-def weight_gradient(terms, width, earlier, space_backward, back, scaling, where):
+def weight_gradient(terms, width, earlier, between, space_backward, back, scaling, where):
     keep, send = terms
     chip_size, groups = lax.axis_size("dp") // 2, lax.axis_size("seq")
     rows, size = keep.shape[2:]
@@ -337,6 +379,7 @@
         swap_ways(send, count - 1, count),
         cost=SMALL,
     )
+    keep = after(keep, between)
     for bit in seq_bits[:-1]:
         keep, send = halved(keep, swap(send, "seq", bit))
     keep = after(keep, back[-1])
@@ -430,9 +473,8 @@
     if divides(width):
         terms = gradient_terms(pair, where)
         steps = [item if i == groups - 1 else after(item, terms[1]) for i, item in enumerate(steps)]
-    (step_home,) = call(
-        unpack_kernel, [(blocks, BF16)], [], where, *exchange(steps), cost=SMALL
-    )
+    steps = exchange(steps)
+    (step_home,) = call(unpack_kernel, [(blocks, BF16)], [], where, *steps, cost=SMALL)
     time_grads = call(
         functools.partial(time_backward_kernel, groups),
         [((3,) + piece, BF16)] * groups,
@@ -442,6 +484,17 @@
         time_qkv,
         probs_t,
     )
+    first_heads = call(
+        space_first_kernel,
+        [(full, F32)] * 3,
+        [],
+        None,
+        *space,
+        after(step_home, time_grads[0]).reshape(full),
+        probs_s,
+        cost=SMALL,
+    )
+
     def space_backward(earlier):
         return call(
             space_backward_kernel,
@@ -451,19 +504,22 @@
             *space,
             after(step_home, earlier).reshape(full),
             probs_s,
+            *first_heads,
         )
 
     back = exchange(time_grads)
     if divides(width):
         weight_grad, space_grads = weight_gradient(
-            terms, width, (time_grads[0], step_home), space_backward, back, scaling, where
+            terms, width, (time_grads[0], *steps), first_heads[0], space_backward, back, scaling, where
         )
     else:
         term = dot(pair[0], pair[1], TN).astype(BF16)
         share = lax.psum_scatter(term, "seq", scatter_dimension=0, tiled=True)
         weight_grad = lax.psum(share, "dp").astype(F32) * scaling
         space_grads = space_backward(time_grads[0])
-    back = call(unpack_kernel, [(blocks, BF16)] * 3, [], where, *back)
+    late = range(1, groups - 1)
+    first = place([0, groups - 1], [back[0], back[-1]], [], blocks, where)
+    back = place(list(late), [back[i] for i in late], first, blocks, where)
     outs = [item.reshape(q_space.shape) for item in list(space_grads) + list(back)]
     return tuple(outs) + (weight_grad,)
 

time: 104 us -> 102 us (0.981)
  waiting for transfers between devices: 34.8 us -> 27.5 us
  starting transfers between devices: 39.5 us -> 42.9 us
  Pallas kernels: 24.6 us -> 25.9 us
    ppermute x17, waiting for transfers between devices: 19.8 us -> 12.8 us  [swap(): return lax.ppermute(array, axis, [(i, i ^ bits) for i in range(size)])]
    ppermute x6, starting transfers between devices: 8.31 us -> 12.3 us  [swap_ways(): lax.ppermute(array, 'dp', [(i, i ^ bits[i % 2]) for i in range(size)])]
    pallas_call x0 -> x2, Pallas kernels: none -> 2.77 us  [place(): pl.pallas_call(functools.partial(place_kernel, slots), out_shape=(jax.Sha...]
    pallas_call x22, Pallas kernels: 24.6 us -> 23.2 us  [call(): pl.pallas_call(body, out_shape=tuple((jax.ShapeDtypeStruct(*out) for out...]
  transfers between devices with their start and end apart: 23 -> 23, of which waited for: 10 -> 11; matrix products, arithmetic and copies ran while one was open for 0% -> 0% of each run, Pallas kernels for 20% -> 22%
where the time goes in v5:
time: 102 us; the launch traced here: 101 us
  starting transfers between devices  42.9 us (42%)
  waiting for transfers between devices  27.5 us (27%)
  Pallas kernels  25.9 us (25%)
  local copies, waits for them, and re-layouts  3.96 us (4%)
    ppermute x17, starting transfers between devices, swap(): return lax.ppermute(array, axis, [(i, i ^ bits) for i in range(size)])  30.7 us
    pallas_call x22, Pallas kernels, call(): pl.pallas_call(body, out_shape=tuple((jax.ShapeDtypeStruct(*out) for out...  23.2 us
    ppermute x6, waiting for transfers between devices, swap_ways(): lax.ppermute(array, 'dp', [(i, i ^ bits[i % 2]) for i in range(size)])  14.8 us
    ppermute x17, waiting for transfers between devices, swap(): return lax.ppermute(array, axis, [(i, i ^ bits) for i in range(size)])  12.8 us
    ppermute x6, starting transfers between devices, swap_ways(): lax.ppermute(array, 'dp', [(i, i ^ bits[i % 2]) for i in range(size)])  12.3 us
    unnamed x20, local copies, waits for them, and re-layouts  3.96 us
    pallas_call x2, Pallas kernels, place(): pl.pallas_call(functools.partial(place_kernel, slots), out_shape=(jax.Sha...  2.77 us
  transfers between devices with their start and end apart: 23, of which 11 were waited for; matrix products, arithmetic and copies ran while one was open for 0% of the time, Pallas kernels for 22%

profile of v5, /device:TPU:0, one launch (start us, length us, event | category | flops | bytes accessed | tf_op | source)
XLA Modules:
  0.0 101.3 jit_solution(6447078597789100763)
XLA Ops:
  0.6 0.1 pad_add_fusion.where_ref
  0.7 1.0 copy-done.1
  1.7 1.0 copy-done.3
  2.7 1.0 copy-done.5
  3.7 0.6 shard_map.137
  4.3 4.1 %collective-permute-start.4 = (bf16[3,40,1152]{2,1,0:T(8,128)(2,1)S(1)}, bf16[3,40,1152]{2,1,0:T(8,128)(2,1)S(1)}, u32[]{:S(2)}, u32[]{:S(2)}) collective-permute-start(bf16[3,40,1152]{2,1,0:T(8,128)(2,1)S(1)} %get-tuple-element.72), channel_id=1, source_target_pairs={{0,2},{1,3},{2,0},{3,1},{4,6},{5,7},{6,4},{7,5},{8,10},{9,11},{10,... | collective-permute-start | bytes 829448 | tf_op jit(solution)/shard_map/ppermute | solution.py:287
  8.4 1.3 %collective-permute-start.5 = (bf16[3,40,1152]{2,1,0:T(8,128)(2,1)S(1)}, bf16[3,40,1152]{2,1,0:T(8,128)(2,1)S(1)}, u32[]{:S(2)}, u32[]{:S(2)}) collective-permute-start(bf16[3,40,1152]{2,1,0:T(8,128)(2,1)S(1)} %get-tuple-element.73), channel_id=1, source_target_pairs={{0,3},{1,2},{2,1},{3,0},{4,7},{5,6},{6,5},{7,4},{8,11},{9,10},{10,... | collective-permute-start | bytes 829448 | tf_op jit(solution)/shard_map/ppermute | solution.py:287
  9.7 0.2 collective-permute-start.3
  10.0 1.0 copy-done.9
  11.0 1.6 %collective-permute-start.6 = (bf16[1,144,1152]{2,1,0:T(8,128)(2,1)S(1)}, bf16[1,144,1152]{2,1,0:T(8,128)(2,1)S(1)}, u32[]{:S(2)}, u32[]{:S(2)}) collective-permute-start(bf16[1,144,1152]{2,1,0:T(8,128)(2,1)S(1)} %shard_map.140.refs_0_), channel_id=1, source_target_pairs={{0,8},{4,20},{8,0},{12,28},{16,24},{20,4},{24,16},{28,12},{1,9},{5... | collective-permute-start | bytes 995336 | tf_op jit(solution)/shard_map/ppermute | solution.py:302
  12.5 0.6 shard_map.138.refs_0_
  13.1 0.0 copy-start.6
  13.1 0.0 copy-start.7
  13.1 0.0 copy-start.8
  13.1 5.0 %collective-permute-done.6.refs_1_ = bf16[1,144,1152]{2,1,0:T(8,128)(2,1)S(1)} collective-permute-done((bf16[1,144,1152]{2,1,0:T(8,128)(2,1)S(1)}, bf16[1,144,1152]{2,1,0:T(8,128)(2,1)S(1)}, u32[]{:S(2)}, u32[]{:S(2)}) %collective-permute-start.6) | collective-permute-done | bytes 331808 | tf_op jit(solution)/shard_map/ppermute | solution.py:302
  18.2 1.6 %collective-permute-start.7 = (bf16[2,144,1152]{2,1,0:T(8,128)(2,1)S(1)}, bf16[2,144,1152]{2,1,0:T(8,128)(2,1)S(1)}, u32[]{:S(2)}, u32[]{:S(2)}) collective-permute-start(bf16[2,144,1152]{2,1,0:T(8,128)(2,1)S(1)} %shard_map.141.refs_0_), channel_id=1, source_target_pairs={{0,16},{4,12},{8,24},{12,4},{16,0},{20,28},{24,8},{28,20},{1,17},{... | collective-permute-start | bytes 1990664 | tf_op jit(solution)/shard_map/ppermute | solution.py:302
  19.8 1.9 %shard_map.135 = (bf16[160,1152]{1,0:T(8,128)(2,1)S(1)}, f32[16,160,160]{2,1,0:T(8,128)S(1)}) custom-call(bf16[160,1152]{1,0:T(8,128)(2,1)S(1)} %bitcast.31, bf16[160,1152]{1,0:T(8,128)(2,1)S(1)} %bitcast.34, bf16[160,1152]{1,0:T(8,128)(2,1)S(1)} %bitcast.37), custom_call_target="tpu_custom_call" | custom-call | flops 20000000000 | bytes 10 | tf_op jit(solution)/shard_map/pallas_call | solution.py:274
  21.7 0.6 shard_map.136
  22.3 1.9 %collective-permute-start = (bf16[2,40,1152]{2,1,0:T(8,128)(2,1)S(1)}, bf16[2,40,1152]{2,1,0:T(8,128)(2,1)S(1)}, u32[]{:S(2)}, u32[]{:S(2)}) collective-permute-start(bf16[2,40,1152]{2,1,0:T(8,128)(2,1)S(1)} %get-tuple-element.66), channel_id=1, source_target_pairs={{0,1},{1,0},{2,3},{3,2},{4,5},{5,4},{6,7},{7,6},{8,9},{9,8},{10,11... | collective-permute-start | bytes 552968 | tf_op jit(solution)/shard_map/ppermute | solution.py:287
  24.2 4.8 %collective-permute-done.7.refs_1_ = bf16[2,144,1152]{2,1,0:T(8,128)(2,1)S(1)} collective-permute-done((bf16[2,144,1152]{2,1,0:T(8,128)(2,1)S(1)}, bf16[2,144,1152]{2,1,0:T(8,128)(2,1)S(1)}, u32[]{:S(2)}, u32[]{:S(2)}) %collective-permute-start.7) | collective-permute-done | bytes 663584 | tf_op jit(solution)/shard_map/ppermute | solution.py:302
  29.0 2.8 %collective-permute-start.1 = (bf16[2,40,1152]{2,1,0:T(8,128)(2,1)S(1)}, bf16[2,40,1152]{2,1,0:T(8,128)(2,1)S(1)}, u32[]{:S(2)}, u32[]{:S(2)}) collective-permute-start(bf16[2,40,1152]{2,1,0:T(8,128)(2,1)S(1)} %get-tuple-element.67), channel_id=1, source_target_pairs={{0,2},{1,3},{2,0},{3,1},{4,6},{5,7},{6,4},{7,5},{8,10},{9,11},{10,... | collective-permute-start | bytes 552968 | tf_op jit(solution)/shard_map/ppermute | solution.py:287
  31.8 0.1 shard_map.142.mine_ref
  31.9 1.4 %collective-permute-start.2 = (bf16[2,40,1152]{2,1,0:T(8,128)(2,1)S(1)}, bf16[2,40,1152]{2,1,0:T(8,128)(2,1)S(1)}, u32[]{:S(2)}, u32[]{:S(2)}) collective-permute-start(bf16[2,40,1152]{2,1,0:T(8,128)(2,1)S(1)} %get-tuple-element.68), channel_id=1, source_target_pairs={{0,3},{1,2},{2,1},{3,0},{4,7},{5,6},{6,5},{7,4},{8,11},{9,10},{10,... | collective-permute-start | bytes 552968 | tf_op jit(solution)/shard_map/ppermute | solution.py:287
  33.3 0.0 collective-permute-done.5.refs_3_
  33.3 0.0 collective-permute-start.8
  33.3 0.0 collective-permute-done.3.refs_1_
  33.3 2.0 %shard_map.139 = (f32[16,160,160]{2,1,0:T(8,128)S(1)}, bf16[3,160,1152]{2,1,0:T(8,128)(2,1)S(1)}, f32[160,1152]{1,0:T(8,128)S(1)}) custom-call(bf16[3,40,1152]{2,1,0:T(8,128)(2,1)S(1)} %shard_map.138.refs_0_, bf16[3,40,1152]{2,1,0:T(8,128)(2,1)S(1)} %collective-permute-done.3.refs_1_, bf16[3,40,1152]{2,1,0:T(8,128)(2,1)S(1)} %collective-permute-done.4.refs_2_, ...), custom_call_target="tpu_custom_call" | custom-call | flops 20000000000 | bytes 10 | tf_op jit(solution)/shard_map/pallas_call | solution.py:274
  35.3 1.1 %collective-permute-done.8.other_ref = bf16[4,144,1152]{2,1,0:T(8,128)(2,1)S(1)} collective-permute-done((bf16[4,144,1152]{2,1,0:T(8,128)(2,1)S(1)}, bf16[4,144,1152]{2,1,0:T(8,128)(2,1)S(1)}, u32[]{:S(2)}, u32[]{:S(2)}) %collective-permute-start.8) | collective-permute-done | bytes 1327136 | tf_op jit(solution)/shard_map/ppermute | solution.py:287
  36.3 0.7 shard_map.143
  37.1 8.4 %collective-permute-done.1.refs_2_ = bf16[2,40,1152]{2,1,0:T(8,128)(2,1)S(1)} collective-permute-done((bf16[2,40,1152]{2,1,0:T(8,128)(2,1)S(1)}, bf16[2,40,1152]{2,1,0:T(8,128)(2,1)S(1)}, u32[]{:S(2)}, u32[]{:S(2)}) %collective-permute-start.1) | collective-permute-done | bytes 184352 | tf_op jit(solution)/shard_map/ppermute | solution.py:287
  45.5 1.6 %shard_map.144 = (bf16[2,160,1152]{2,1,0:T(8,128)(2,1)S(1)}, bf16[160,1152]{1,0:T(8,128)(2,1)S(1)}, bf16[1,40,1152]{2,1,0:T(8,128)(2,1)S(1)}, bf16[1,40,1152]{2,...) custom-call(bf16[2,40,1152]{2,1,0:T(8,128)(2,1)S(1)} %get-tuple-element.65.refs_0_, ...), custom_call_target="tpu_custom_call" | custom-call | flops 20000000000 | bytes 10 | tf_op jit(solution)/shard_map/pallas_call | solution.py:274
  47.1 0.1 collective-permute-start.9
  47.1 2.9 %collective-permute-start.12 = (bf16[1,40,1152]{2,1,0:T(8,128)(2,1)S(1)}, bf16[1,40,1152]{2,1,0:T(8,128)(2,1)S(1)}, u32[]{:S(2)}, u32[]{:S(2)}) collective-permute-start(bf16[1,40,1152]{2,1,0:T(8,128)(2,1)S(1)} %get-tuple-element.86), channel_id=1, source_target_pairs={{0,3},{1,2},{2,1},{3,0},{4,7},{5,6},{6,5},{7,4},{8,11},{9,10},{10,... | collective-permute-start | bytes 276488 | tf_op jit(solution)/shard_map/ppermute | solution.py:287
  50.0 1.8 %shard_map.145 = (f32[2,4,72,640]{3,2,1,0:T(8,128)S(1)}, bf16[2,4,72,640]{3,2,1,0:T(8,128)(2,1)S(1)}) custom-call(s32[2]{0:T(128)S(1)} %pad_add_fusion.where_ref, bf16[2,160,1152]{2,1,0:T(8,128)(2,1)S(1)} %get-tuple-element.79.mine_ref, bf16[2,160,1152]{2,1,0:T(8,128)(2,1)S(1)} %collective-permute-done.9.other_ref), custom_call_target="tpu_custom_call" | custom-call | flops 20000000000 | bytes 10 | tf_op jit(solution)/shard_map/pallas_call | solution.py:274
  51.9 1.6 %collective-permute-start.13 = (bf16[2,4,72,640]{3,2,1,0:T(8,128)(2,1)S(1)}, bf16[2,4,72,640]{3,2,1,0:T(8,128)(2,1)S(1)}, u32[]{:S(2)}, u32[]{:S(2)}) collective-permute-start(bf16[2,4,72,640]{3,2,1,0:T(8,128)(2,1)S(1)} %get-tuple-element.80), channel_id=1, source_target_pairs={{0,8},{4,20},{8,0},{12,28},{16,24},{20,4},{24,16},{28,12},{1,9},{5... | collective-permute-start | bytes 2211848 | tf_op jit(solution)/shard_map/ppermute | solution.py:302
  53.4 3.5 %collective-permute-start.10 = (bf16[1,40,1152]{2,1,0:T(8,128)(2,1)S(1)}, bf16[1,40,1152]{2,1,0:T(8,128)(2,1)S(1)}, u32[]{:S(2)}, u32[]{:S(2)}) collective-permute-start(bf16[1,40,1152]{2,1,0:T(8,128)(2,1)S(1)} %get-tuple-element.83), channel_id=1, source_target_pairs={{0,1},{1,0},{2,3},{3,2},{4,5},{5,4},{6,7},{7,6},{8,9},{9,8},{10,11... | collective-permute-start | bytes 276488 | tf_op jit(solution)/shard_map/ppermute | solution.py:287
  56.9 1.6 %collective-permute-start.11 = (bf16[1,40,1152]{2,1,0:T(8,128)(2,1)S(1)}, bf16[1,40,1152]{2,1,0:T(8,128)(2,1)S(1)}, u32[]{:S(2)}, u32[]{:S(2)}) collective-permute-start(bf16[1,40,1152]{2,1,0:T(8,128)(2,1)S(1)} %get-tuple-element.85), channel_id=1, source_target_pairs={{0,2},{1,3},{2,0},{3,1},{4,6},{5,7},{6,4},{7,5},{8,10},{9,11},{10,... | collective-permute-start | bytes 276488 | tf_op jit(solution)/shard_map/ppermute | solution.py:287
  58.5 4.3 %shard_map.147 = (bf16[3,40,1152]{2,1,0:T(8,128)(2,1)S(1)}, bf16[3,40,1152]{2,1,0:T(8,128)(2,1)S(1)}, bf16[3,40,1152]{2,1,0:T(8,128)(2,1)S(1)}, bf16[3,40,1152]{2,1,0:T(8,128)(2,1)S(1)}) custom-call(bf16[160,1152]{1,0:T(8,128)(2,1)S(1)} %get-tuple-element.88.step_ref, bf16[3,160,1152]{2,1,0:T(8,128)(2,1)S(1)} %get-tuple-element.89.qkv_ref, ...), custom_call_target="tpu_custom_call" | custom-call | flops 20000000000 | bytes 10 | tf_op jit(solution)/shard_map/pallas_call | solution.py:274
  62.9 0.5 collective-permute-done.11.refs_2_
  63.4 0.0 collective-permute-done.13.came_ref
  63.4 0.1 shard_map.148
  63.5 1.6 %collective-permute-start.14 = (bf16[1,4,72,640]{3,2,1,0:T(8,128)(2,1)S(1)}, bf16[1,4,72,640]{3,2,1,0:T(8,128)(2,1)S(1)}, u32[]{:S(2)}, u32[]{:S(2)}) collective-permute-start(bf16[1,4,72,640]{3,2,1,0:T(8,128)(2,1)S(1)} %get-tuple-element.94), channel_id=1, source_target_pairs={{0,16},{4,12},{8,24},{12,4},{16,0},{20,28},{24,8},{28,20},{1,17},{... | collective-permute-start | bytes 1105928 | tf_op jit(solution)/shard_map/ppermute | solution.py:302
  65.1 2.5 %collective-permute-start.16 = (bf16[3,40,1152]{2,1,0:T(8,128)(2,1)S(1)}, bf16[3,40,1152]{2,1,0:T(8,128)(2,1)S(1)}, u32[]{:S(2)}, u32[]{:S(2)}) collective-permute-start(bf16[3,40,1152]{2,1,0:T(8,128)(2,1)S(1)} %get-tuple-element.102), channel_id=1, source_target_pairs={{0,3},{1,2},{2,1},{3,0},{4,7},{5,6},{6,5},{7,4},{8,11},{9,10},{10,... | collective-permute-start | bytes 829448 | tf_op jit(solution)/shard_map/ppermute | solution.py:287
  67.6 3.5 %collective-permute-done.14.came_ref = bf16[1,4,72,640]{3,2,1,0:T(8,128)(2,1)S(1)} collective-permute-done((bf16[1,4,72,640]{3,2,1,0:T(8,128)(2,1)S(1)}, bf16[1,4,72,640]{3,2,1,0:T(8,128)(2,1)S(1)}, u32[]{:S(2)}, u32[]{:S(2)}) %collective-permute-start.14) | collective-permute-done | bytes 368672 | tf_op jit(solution)/shard_map/ppermute | solution.py:302
  71.1 0.7 shard_map.149
  71.8 3.6 %collective-permute-start.15 = (bf16[2,72,640]{2,1,0:T(8,128)(2,1)S(1)}, bf16[2,72,640]{2,1,0:T(8,128)(2,1)S(1)}, u32[]{:S(2)}, u32[]{:S(2)}) collective-permute-start(bf16[2,72,640]{2,1,0:T(8,128)(2,1)S(1)} %get-tuple-element.100), channel_id=1, source_target_pairs={{0,1},{1,0},{2,3},{3,2},{4,5},{5,4},{6,7},{7,6},{8,9},{9,8},{10,11... | collective-permute-start | bytes 552968 | tf_op jit(solution)/shard_map/ppermute | solution.py:287
  75.3 0.6 shard_map.146
  75.9 2.4 %shard_map.150 = (f32[160,1152]{1,0:T(8,128)S(1)}, f32[160,1152]{1,0:T(8,128)S(1)}, f32[160,1152]{1,0:T(8,128)S(1)}) custom-call(bf16[160,1152]{1,0:T(8,128)(2,1)S(1)} %bitcast.32, bf16[160,1152]{1,0:T(8,128)(2,1)S(1)} %bitcast.35, bf16[160,1152]{1,0:T(8,128)(2,1)S(1)} %bitcast.38, bf16[160,1152]{1,0:T(8,128)(2,1)S(1)} %bitcast.21, ...), custom_call_target="tpu_custom_call" | custom-call | flops 10 | bytes 10 | tf_op jit(solution)/shard_map/pallas_call | solution.py:274
  78.4 0.7 collective-permute-done.15.came_ref
  79.2 3.4 %collective-permute-start.17 = (bf16[1,72,640]{2,1,0:T(8,128)(2,1)S(1)}, bf16[1,72,640]{2,1,0:T(8,128)(2,1)S(1)}, u32[]{:S(2)}, u32[]{:S(2)}) collective-permute-start(bf16[1,72,640]{2,1,0:T(8,128)(2,1)S(1)} %get-tuple-element.104), channel_id=1, source_target_pairs={{0,2},{1,3},{2,0},{3,1},{4,6},{5,7},{6,4},{7,5},{8,10},{9,11},{10,... | collective-permute-start | bytes 276488 | tf_op jit(solution)/shard_map/ppermute | solution.py:287
  82.6 0.8 collective-permute-start.18
  83.3 0.6 collective-permute-start.19
  83.9 1.8 %collective-permute-done.17.came_ref = bf16[1,72,640]{2,1,0:T(8,128)(2,1)S(1)} collective-permute-done((bf16[1,72,640]{2,1,0:T(8,128)(2,1)S(1)}, bf16[1,72,640]{2,1,0:T(8,128)(2,1)S(1)}, u32[]{:S(2)}, u32[]{:S(2)}) %collective-permute-start.17) | collective-permute-done | bytes 92192 | tf_op jit(solution)/shard_map/ppermute | solution.py:287
  85.7 3.9 %collective-permute-start.20 = (bf16[1,72,640]{2,1,0:T(8,128)(2,1)S(1)}, bf16[1,72,640]{2,1,0:T(8,128)(2,1)S(1)}, u32[]{:S(2)}, u32[]{:S(2)}) collective-permute-start(bf16[1,72,640]{2,1,0:T(8,128)(2,1)S(1)} %shard_map.152.refs_0_), channel_id=1, source_target_pairs={{0,8},{4,20},{8,0},{12,28},{16,24},{20,4},{24,16},{28,12},{1,9},{5... | collective-permute-start | bytes 276488 | tf_op jit(solution)/shard_map/ppermute | solution.py:302
  89.6 1.4 %shard_map.154 = (bf16[4,40,1152]{2,1,0:T(8,128)(2,1)}, bf16[4,40,1152]{2,1,0:T(8,128)(2,1)}, bf16[4,40,1152]{2,1,0:T(8,128)(2,1)}) custom-call(s32[2]{0:T(128)S(1)} %pad_add_fusion.where_ref, bf16[3,40,1152]{2,1,0:T(8,128)(2,1)S(1)} %get-tuple-element.91.refs_0_, bf16[3,40,1152]{2,1,0:T(8,128)(2,1)S(1)} %collective-permute-done.16.refs_1_), custom_call_target="tpu_custom_call" | custom-call | flops 20000000000 | bytes 10 | tf_op jit(solution)/shard_map/pallas_call | solution.py:255
  91.0 1.1 %collective-permute-done.20.refs_1_ = bf16[1,72,640]{2,1,0:T(8,128)(2,1)S(1)} collective-permute-done((bf16[1,72,640]{2,1,0:T(8,128)(2,1)S(1)}, bf16[1,72,640]{2,1,0:T(8,128)(2,1)S(1)}, u32[]{:S(2)}, u32[]{:S(2)}) %collective-permute-start.20) | collective-permute-done | bytes 92192 | tf_op jit(solution)/shard_map/ppermute | solution.py:302
  92.1 2.1 %collective-permute-start.21 = (bf16[2,72,640]{2,1,0:T(8,128)(2,1)S(1)}, bf16[2,72,640]{2,1,0:T(8,128)(2,1)S(1)}, u32[]{:S(2)}, u32[]{:S(2)}) collective-permute-start(bf16[2,72,640]{2,1,0:T(8,128)(2,1)S(1)} %shard_map.156.refs_0_), channel_id=1, source_target_pairs={{0,16},{4,12},{8,24},{12,4},{16,0},{20,28},{24,8},{28,20},{1,17},{... | collective-permute-start | bytes 552968 | tf_op jit(solution)/shard_map/ppermute | solution.py:302
  94.3 3.2 %shard_map.153 = (bf16[160,1152]{1,0:T(8,128)(2,1)}, bf16[160,1152]{1,0:T(8,128)(2,1)}, bf16[160,1152]{1,0:T(8,128)(2,1)}) custom-call(bf16[160,1152]{1,0:T(8,128)(2,1)S(1)} %bitcast.33, bf16[160,1152]{1,0:T(8,128)(2,1)S(1)} %bitcast.36, bf16[160,1152]{1,0:T(8,128)(2,1)S(1)} %bitcast.39, bf16[160,1152]{1,0:T(8,128)(2,1)S(1)} %bitcast.22, ...), custom_call_target="tpu_custom_call" | custom-call | flops 20000000000 | bytes 10 | tf_op jit(solution)/shard_map/pallas_call | solution.py:274
  97.5 0.3 collective-permute-done.21.refs_1_
  97.8 0.1 collective-permute-start.22
  97.9 0.0 collective-permute-done.19.refs_1_
  97.9 1.4 %shard_map.155 = (bf16[4,40,1152]{2,1,0:T(8,128)(2,1)}, bf16[4,40,1152]{2,1,0:T(8,128)(2,1)}, bf16[4,40,1152]{2,1,0:T(8,128)(2,1)}) custom-call(s32[2]{0:T(128)S(1)} %pad_add_fusion.where_ref, bf16[3,40,1152]{2,1,0:T(8,128)(2,1)S(1)} %collective-permute-done.18.refs_0_, ...), custom_call_target="tpu_custom_call", output_to_operand_aliasing={{0}: (3, {}), {1}: (4, {}), {2}: (5, {})} | custom-call | flops 20000000000 | bytes 10 | tf_op jit(solution)/shard_map/pallas_call | solution.py:255
  99.3 0.2 collective-permute-done.22.other_ref
  99.6 1.8 %shard_map.158 = f32[4,72,1152]{2,1,0:T(8,128)} custom-call(s32[2]{0:T(128)S(1)} %pad_add_fusion.where_ref, bf16[4,72,640]{2,1,0:T(8,128)(2,1)S(1)} %shard_map.157.mine_ref, bf16[4,72,640]{2,1,0:T(8,128)(2,1)S(1)} %collective-permute-done.22.other_ref), custom_call_target="tpu_custom_call" | custom-call | flops 10 | bytes 10 | tf_op jit(solution)/shard_map/pallas_call | solution.py:274
  (27 shorter events, 0.2 us)
Async XLA Ops:
  0.7 1.0 copy-start.1
  1.7 1.0 copy-start.3
  2.7 1.0 copy-start.5
  4.3 27.6 %collective-permute-start.4 = (bf16[3,40,1152]{2,1,0:T(8,128)(2,1)S(1)}, bf16[3,40,1152]{2,1,0:T(8,128)(2,1)S(1)}, u32[]{:S(2)}, u32[]{:S(2)}) collective-permute-start(bf16[3,40,1152]{2,1,0:T(8,128)(2,1)S(1)} %get-tuple-element.72), channel_id=1, source_target_pairs={{0,2},{1,3},{2,0},{3,1},{4,6},{5,7},{6,4},{7,5},{8,10},{9,11},{10,... | collective-permute-start | bytes 829448 | tf_op jit(solution)/shard_map/ppermute | solution.py:287
  8.4 24.9 %collective-permute-start.5 = (bf16[3,40,1152]{2,1,0:T(8,128)(2,1)S(1)}, bf16[3,40,1152]{2,1,0:T(8,128)(2,1)S(1)}, u32[]{:S(2)}, u32[]{:S(2)}) collective-permute-start(bf16[3,40,1152]{2,1,0:T(8,128)(2,1)S(1)} %get-tuple-element.73), channel_id=1, source_target_pairs={{0,3},{1,2},{2,1},{3,0},{4,7},{5,6},{6,5},{7,4},{8,11},{9,10},{10,... | collective-permute-start | bytes 829448 | tf_op jit(solution)/shard_map/ppermute | solution.py:287
  9.7 23.6 %collective-permute-start.3 = (bf16[3,40,1152]{2,1,0:T(8,128)(2,1)S(1)}, bf16[3,40,1152]{2,1,0:T(8,128)(2,1)S(1)}, u32[]{:S(2)}, u32[]{:S(2)}) collective-permute-start(bf16[3,40,1152]{2,1,0:T(8,128)(2,1)S(1)} %get-tuple-element.69), channel_id=1, source_target_pairs={{0,1},{1,0},{2,3},{3,2},{4,5},{5,4},{6,7},{7,6},{8,9},{9,8},{10,11... | collective-permute-start | bytes 829448 | tf_op jit(solution)/shard_map/ppermute | solution.py:287
  10.0 1.0 copy-start.9
  10.9 1.6 %copy-start.2 = (bf16[1,160,1152]{2,1,0:T(8,128)(2,1)S(1)}, bf16[1,160,1152]{2,1,0:T(8,128)(2,1)}, u32[]{:S(2)}) copy-start(bf16[1,160,1152]{2,1,0:T(8,128)(2,1)} %param.11) | copy-start | bytes 1105924
  10.9 1.6 %copy-start.4 = (bf16[1,160,1152]{2,1,0:T(8,128)(2,1)S(1)}, bf16[1,160,1152]{2,1,0:T(8,128)(2,1)}, u32[]{:S(2)}) copy-start(bf16[1,160,1152]{2,1,0:T(8,128)(2,1)} %param.12) | copy-start | bytes 1105924
  11.0 7.2 %collective-permute-start.6 = (bf16[1,144,1152]{2,1,0:T(8,128)(2,1)S(1)}, bf16[1,144,1152]{2,1,0:T(8,128)(2,1)S(1)}, u32[]{:S(2)}, u32[]{:S(2)}) collective-permute-start(bf16[1,144,1152]{2,1,0:T(8,128)(2,1)S(1)} %shard_map.140.refs_0_), channel_id=1, source_target_pairs={{0,8},{4,20},{8,0},{12,28},{16,24},{20,4},{24,16},{28,12},{1,9},{5... | collective-permute-start | bytes 995336 | tf_op jit(solution)/shard_map/ppermute | solution.py:302
  13.1 6.7 %copy-start.6 = (bf16[1,160,1152]{2,1,0:T(8,128)(2,1)S(1)}, bf16[1,160,1152]{2,1,0:T(8,128)(2,1)}, u32[]{:S(2)}) copy-start(bf16[1,160,1152]{2,1,0:T(8,128)(2,1)} %param.8) | copy-start | bytes 1105924
  13.1 6.7 %copy-start.7 = (bf16[1,160,1152]{2,1,0:T(8,128)(2,1)S(1)}, bf16[1,160,1152]{2,1,0:T(8,128)(2,1)}, u32[]{:S(2)}) copy-start(bf16[1,160,1152]{2,1,0:T(8,128)(2,1)} %param.9) | copy-start | bytes 1105924
  13.1 6.7 %copy-start.8 = (bf16[1,160,1152]{2,1,0:T(8,128)(2,1)S(1)}, bf16[1,160,1152]{2,1,0:T(8,128)(2,1)}, u32[]{:S(2)}) copy-start(bf16[1,160,1152]{2,1,0:T(8,128)(2,1)} %param.10) | copy-start | bytes 1105924
  18.2 10.7 %collective-permute-start.7 = (bf16[2,144,1152]{2,1,0:T(8,128)(2,1)S(1)}, bf16[2,144,1152]{2,1,0:T(8,128)(2,1)S(1)}, u32[]{:S(2)}, u32[]{:S(2)}) collective-permute-start(bf16[2,144,1152]{2,1,0:T(8,128)(2,1)S(1)} %shard_map.141.refs_0_), channel_id=1, source_target_pairs={{0,16},{4,12},{8,24},{12,4},{16,0},{20,28},{24,8},{28,20},{1,17},{... | collective-permute-start | bytes 1990664 | tf_op jit(solution)/shard_map/ppermute | solution.py:302
  19.8 1.9 %copy-start = (bf16[1,160,1152]{2,1,0:T(8,128)(2,1)S(1)}, bf16[1,160,1152]{2,1,0:T(8,128)(2,1)}, u32[]{:S(2)}) copy-start(bf16[1,160,1152]{2,1,0:T(8,128)(2,1)} %param.15) | copy-start | bytes 1105924
  22.3 14.8 %collective-permute-start = (bf16[2,40,1152]{2,1,0:T(8,128)(2,1)S(1)}, bf16[2,40,1152]{2,1,0:T(8,128)(2,1)S(1)}, u32[]{:S(2)}, u32[]{:S(2)}) collective-permute-start(bf16[2,40,1152]{2,1,0:T(8,128)(2,1)S(1)} %get-tuple-element.66), channel_id=1, source_target_pairs={{0,1},{1,0},{2,3},{3,2},{4,5},{5,4},{6,7},{7,6},{8,9},{9,8},{10,11... | collective-permute-start | bytes 552968 | tf_op jit(solution)/shard_map/ppermute | solution.py:287
  29.0 16.5 %collective-permute-start.1 = (bf16[2,40,1152]{2,1,0:T(8,128)(2,1)S(1)}, bf16[2,40,1152]{2,1,0:T(8,128)(2,1)S(1)}, u32[]{:S(2)}, u32[]{:S(2)}) collective-permute-start(bf16[2,40,1152]{2,1,0:T(8,128)(2,1)S(1)} %get-tuple-element.67), channel_id=1, source_target_pairs={{0,2},{1,3},{2,0},{3,1},{4,6},{5,7},{6,4},{7,5},{8,10},{9,11},{10,... | collective-permute-start | bytes 552968 | tf_op jit(solution)/shard_map/ppermute | solution.py:287
  31.9 13.6 %collective-permute-start.2 = (bf16[2,40,1152]{2,1,0:T(8,128)(2,1)S(1)}, bf16[2,40,1152]{2,1,0:T(8,128)(2,1)S(1)}, u32[]{:S(2)}, u32[]{:S(2)}) collective-permute-start(bf16[2,40,1152]{2,1,0:T(8,128)(2,1)S(1)} %get-tuple-element.68), channel_id=1, source_target_pairs={{0,3},{1,2},{2,1},{3,0},{4,7},{5,6},{6,5},{7,4},{8,11},{9,10},{10,... | collective-permute-start | bytes 552968 | tf_op jit(solution)/shard_map/ppermute | solution.py:287
  33.3 3.1 %collective-permute-start.8 = (bf16[4,144,1152]{2,1,0:T(8,128)(2,1)S(1)}, bf16[4,144,1152]{2,1,0:T(8,128)(2,1)S(1)}, u32[]{:S(2)}, u32[]{:S(2)}) collective-permute-start(bf16[4,144,1152]{2,1,0:T(8,128)(2,1)S(1)} %shard_map.142.mine_ref), channel_id=1, source_target_pairs={{0,4},{4,0},{8,12},{12,8},{16,20},{20,16},{24,28},{28,24},{1,5},{5... | collective-permute-start | bytes 3981320 | tf_op jit(solution)/shard_map/ppermute | solution.py:287
  47.1 3.0 %collective-permute-start.9 = (bf16[2,160,1152]{2,1,0:T(8,128)(2,1)S(1)}, bf16[2,160,1152]{2,1,0:T(8,128)(2,1)S(1)}, u32[]{:S(2)}, u32[]{:S(2)}) collective-permute-start(bf16[2,160,1152]{2,1,0:T(8,128)(2,1)S(1)} %get-tuple-element.79.mine_ref), channel_id=1, source_target_pairs={{0,4},{4,0},{8,12},{12,8},{16,20},{20,16},{24,28},{28,24},{1,5},{5... | collective-permute-start | bytes 2211848 | tf_op jit(solution)/shard_map/ppermute | solution.py:287
  47.1 15.7 %collective-permute-start.12 = (bf16[1,40,1152]{2,1,0:T(8,128)(2,1)S(1)}, bf16[1,40,1152]{2,1,0:T(8,128)(2,1)S(1)}, u32[]{:S(2)}, u32[]{:S(2)}) collective-permute-start(bf16[1,40,1152]{2,1,0:T(8,128)(2,1)S(1)} %get-tuple-element.86), channel_id=1, source_target_pairs={{0,3},{1,2},{2,1},{3,0},{4,7},{5,6},{6,5},{7,4},{8,11},{9,10},{10,... | collective-permute-start | bytes 276488 | tf_op jit(solution)/shard_map/ppermute | solution.py:287
  51.9 11.5 %collective-permute-start.13 = (bf16[2,4,72,640]{3,2,1,0:T(8,128)(2,1)S(1)}, bf16[2,4,72,640]{3,2,1,0:T(8,128)(2,1)S(1)}, u32[]{:S(2)}, u32[]{:S(2)}) collective-permute-start(bf16[2,4,72,640]{3,2,1,0:T(8,128)(2,1)S(1)} %get-tuple-element.80), channel_id=1, source_target_pairs={{0,8},{4,20},{8,0},{12,28},{16,24},{20,4},{24,16},{28,12},{1,9},{5... | collective-permute-start | bytes 2211848 | tf_op jit(solution)/shard_map/ppermute | solution.py:302
  53.4 9.5 %collective-permute-start.10 = (bf16[1,40,1152]{2,1,0:T(8,128)(2,1)S(1)}, bf16[1,40,1152]{2,1,0:T(8,128)(2,1)S(1)}, u32[]{:S(2)}, u32[]{:S(2)}) collective-permute-start(bf16[1,40,1152]{2,1,0:T(8,128)(2,1)S(1)} %get-tuple-element.83), channel_id=1, source_target_pairs={{0,1},{1,0},{2,3},{3,2},{4,5},{5,4},{6,7},{7,6},{8,9},{9,8},{10,11... | collective-permute-start | bytes 276488 | tf_op jit(solution)/shard_map/ppermute | solution.py:287
  56.9 6.4 %collective-permute-start.11 = (bf16[1,40,1152]{2,1,0:T(8,128)(2,1)S(1)}, bf16[1,40,1152]{2,1,0:T(8,128)(2,1)S(1)}, u32[]{:S(2)}, u32[]{:S(2)}) collective-permute-start(bf16[1,40,1152]{2,1,0:T(8,128)(2,1)S(1)} %get-tuple-element.85), channel_id=1, source_target_pairs={{0,2},{1,3},{2,0},{3,1},{4,6},{5,7},{6,4},{7,5},{8,10},{9,11},{10,... | collective-permute-start | bytes 276488 | tf_op jit(solution)/shard_map/ppermute | solution.py:287
  63.5 7.6 %collective-permute-start.14 = (bf16[1,4,72,640]{3,2,1,0:T(8,128)(2,1)S(1)}, bf16[1,4,72,640]{3,2,1,0:T(8,128)(2,1)S(1)}, u32[]{:S(2)}, u32[]{:S(2)}) collective-permute-start(bf16[1,4,72,640]{3,2,1,0:T(8,128)(2,1)S(1)} %get-tuple-element.94), channel_id=1, source_target_pairs={{0,16},{4,12},{8,24},{12,4},{16,0},{20,28},{24,8},{28,20},{1,17},{... | collective-permute-start | bytes 1105928 | tf_op jit(solution)/shard_map/ppermute | solution.py:302
  65.1 18.8 %collective-permute-start.16 = (bf16[3,40,1152]{2,1,0:T(8,128)(2,1)S(1)}, bf16[3,40,1152]{2,1,0:T(8,128)(2,1)S(1)}, u32[]{:S(2)}, u32[]{:S(2)}) collective-permute-start(bf16[3,40,1152]{2,1,0:T(8,128)(2,1)S(1)} %get-tuple-element.102), channel_id=1, source_target_pairs={{0,3},{1,2},{2,1},{3,0},{4,7},{5,6},{6,5},{7,4},{8,11},{9,10},{10,... | collective-permute-start | bytes 829448 | tf_op jit(solution)/shard_map/ppermute | solution.py:287
  71.8 7.3 %collective-permute-start.15 = (bf16[2,72,640]{2,1,0:T(8,128)(2,1)S(1)}, bf16[2,72,640]{2,1,0:T(8,128)(2,1)S(1)}, u32[]{:S(2)}, u32[]{:S(2)}) collective-permute-start(bf16[2,72,640]{2,1,0:T(8,128)(2,1)S(1)} %get-tuple-element.100), channel_id=1, source_target_pairs={{0,1},{1,0},{2,3},{3,2},{4,5},{5,4},{6,7},{7,6},{8,9},{9,8},{10,11... | collective-permute-start | bytes 552968 | tf_op jit(solution)/shard_map/ppermute | solution.py:287
  79.2 6.5 %collective-permute-start.17 = (bf16[1,72,640]{2,1,0:T(8,128)(2,1)S(1)}, bf16[1,72,640]{2,1,0:T(8,128)(2,1)S(1)}, u32[]{:S(2)}, u32[]{:S(2)}) collective-permute-start(bf16[1,72,640]{2,1,0:T(8,128)(2,1)S(1)} %get-tuple-element.104), channel_id=1, source_target_pairs={{0,2},{1,3},{2,0},{3,1},{4,6},{5,7},{6,4},{7,5},{8,10},{9,11},{10,... | collective-permute-start | bytes 276488 | tf_op jit(solution)/shard_map/ppermute | solution.py:287
  82.6 15.3 %collective-permute-start.18 = (bf16[3,40,1152]{2,1,0:T(8,128)(2,1)S(1)}, bf16[3,40,1152]{2,1,0:T(8,128)(2,1)S(1)}, u32[]{:S(2)}, u32[]{:S(2)}) collective-permute-start(bf16[3,40,1152]{2,1,0:T(8,128)(2,1)S(1)} %get-tuple-element.111), channel_id=1, source_target_pairs={{0,1},{1,0},{2,3},{3,2},{4,5},{5,4},{6,7},{7,6},{8,9},{9,8},{10,11... | collective-permute-start | bytes 829448 | tf_op jit(solution)/shard_map/ppermute | solution.py:287
  83.3 14.6 %collective-permute-start.19 = (bf16[3,40,1152]{2,1,0:T(8,128)(2,1)S(1)}, bf16[3,40,1152]{2,1,0:T(8,128)(2,1)S(1)}, u32[]{:S(2)}, u32[]{:S(2)}) collective-permute-start(bf16[3,40,1152]{2,1,0:T(8,128)(2,1)S(1)} %get-tuple-element.112), channel_id=1, source_target_pairs={{0,2},{1,3},{2,0},{3,1},{4,6},{5,7},{6,4},{7,5},{8,10},{9,11},{10,... | collective-permute-start | bytes 829448 | tf_op jit(solution)/shard_map/ppermute | solution.py:287
  85.7 6.4 %collective-permute-start.20 = (bf16[1,72,640]{2,1,0:T(8,128)(2,1)S(1)}, bf16[1,72,640]{2,1,0:T(8,128)(2,1)S(1)}, u32[]{:S(2)}, u32[]{:S(2)}) collective-permute-start(bf16[1,72,640]{2,1,0:T(8,128)(2,1)S(1)} %shard_map.152.refs_0_), channel_id=1, source_target_pairs={{0,8},{4,20},{8,0},{12,28},{16,24},{20,4},{24,16},{28,12},{1,9},{5... | collective-permute-start | bytes 276488 | tf_op jit(solution)/shard_map/ppermute | solution.py:302
  92.1 5.6 %collective-permute-start.21 = (bf16[2,72,640]{2,1,0:T(8,128)(2,1)S(1)}, bf16[2,72,640]{2,1,0:T(8,128)(2,1)S(1)}, u32[]{:S(2)}, u32[]{:S(2)}) collective-permute-start(bf16[2,72,640]{2,1,0:T(8,128)(2,1)S(1)} %shard_map.156.refs_0_), channel_id=1, source_target_pairs={{0,16},{4,12},{8,24},{12,4},{16,0},{20,28},{24,8},{28,20},{1,17},{... | collective-permute-start | bytes 552968 | tf_op jit(solution)/shard_map/ppermute | solution.py:302
  97.8 1.8 %collective-permute-start.22 = (bf16[4,72,640]{2,1,0:T(8,128)(2,1)S(1)}, bf16[4,72,640]{2,1,0:T(8,128)(2,1)S(1)}, u32[]{:S(2)}, u32[]{:S(2)}) collective-permute-start(bf16[4,72,640]{2,1,0:T(8,128)(2,1)S(1)} %shard_map.157.mine_ref), channel_id=1, source_target_pairs={{0,4},{4,0},{8,12},{12,8},{16,20},{20,16},{24,28},{28,24},{1,5},{5... | collective-permute-start | bytes 1105928 | tf_op jit(solution)/shard_map/ppermute | solution.py:287

commit v6 on v5

--- a/solution.py
+++ b/solution.py
@@ -368,6 +368,7 @@
     keep = after(keep, *earlier)
     for step in range(count - 1):
         keep, send = halved(keep, swap_ways(send, step, count))
+    keep = after(keep, between)
     order = halving(seq_bits)
     cut = (groups // 2, rows, size)
     keep, send = call(
@@ -379,7 +380,6 @@
         swap_ways(send, count - 1, count),
         cost=SMALL,
     )
-    keep = after(keep, between)
     for bit in seq_bits[:-1]:
         keep, send = halved(keep, swap(send, "seq", bit))
     keep = after(keep, back[-1])

time: 102 us -> 102 us (level)
    ppermute x6, waiting for transfers between devices: 14.8 us -> 11.7 us  [swap_ways(): lax.ppermute(array, 'dp', [(i, i ^ bits[i % 2]) for i in range(size)])]
    ppermute x17, waiting for transfers between devices: 12.8 us -> 15.8 us  [swap(): return lax.ppermute(array, axis, [(i, i ^ bits) for i in range(size)])]
where the time goes in v6:
time: 102 us; the launch traced here: 101 us
  starting transfers between devices  42.9 us (42%)
  waiting for transfers between devices  27.5 us (27%)
  Pallas kernels  26 us (25%)
  local copies, waits for them, and re-layouts  3.96 us (4%)
    ppermute x17, starting transfers between devices, swap(): return lax.ppermute(array, axis, [(i, i ^ bits) for i in range(size)])  30.7 us
    pallas_call x22, Pallas kernels, call(): pl.pallas_call(body, out_shape=tuple((jax.ShapeDtypeStruct(*out) for out...  23.2 us
    ppermute x17, waiting for transfers between devices, swap(): return lax.ppermute(array, axis, [(i, i ^ bits) for i in range(size)])  15.8 us
    ppermute x6, starting transfers between devices, swap_ways(): lax.ppermute(array, 'dp', [(i, i ^ bits[i % 2]) for i in range(size)])  12.3 us
    ppermute x6, waiting for transfers between devices, swap_ways(): lax.ppermute(array, 'dp', [(i, i ^ bits[i % 2]) for i in range(size)])  11.7 us
    unnamed x20, local copies, waits for them, and re-layouts  3.96 us
    pallas_call x2, Pallas kernels, place(): pl.pallas_call(functools.partial(place_kernel, slots), out_shape=(jax.Sha...  2.77 us
  transfers between devices with their start and end apart: 23, of which 11 were waited for; matrix products, arithmetic and copies ran while one was open for 0% of the time, Pallas kernels for 22%

profile of v6, /device:TPU:0, one launch (start us, length us, event | category | flops | bytes accessed | tf_op | source)
XLA Modules:
  0.0 101.3 jit_solution(3295157953105375744)
XLA Ops:
  0.6 0.1 pad_add_fusion.where_ref
  0.7 1.0 copy-done.1
  1.7 1.0 copy-done.3
  2.7 1.0 copy-done.5
  3.7 0.6 shard_map.137
  4.3 4.1 %collective-permute-start.4 = (bf16[3,40,1152]{2,1,0:T(8,128)(2,1)S(1)}, bf16[3,40,1152]{2,1,0:T(8,128)(2,1)S(1)}, u32[]{:S(2)}, u32[]{:S(2)}) collective-permute-start(bf16[3,40,1152]{2,1,0:T(8,128)(2,1)S(1)} %get-tuple-element.72), channel_id=1, source_target_pairs={{0,2},{1,3},{2,0},{3,1},{4,6},{5,7},{6,4},{7,5},{8,10},{9,11},{10,... | collective-permute-start | bytes 829448 | tf_op jit(solution)/shard_map/ppermute | solution.py:287
  8.4 1.3 %collective-permute-start.5 = (bf16[3,40,1152]{2,1,0:T(8,128)(2,1)S(1)}, bf16[3,40,1152]{2,1,0:T(8,128)(2,1)S(1)}, u32[]{:S(2)}, u32[]{:S(2)}) collective-permute-start(bf16[3,40,1152]{2,1,0:T(8,128)(2,1)S(1)} %get-tuple-element.73), channel_id=1, source_target_pairs={{0,3},{1,2},{2,1},{3,0},{4,7},{5,6},{6,5},{7,4},{8,11},{9,10},{10,... | collective-permute-start | bytes 829448 | tf_op jit(solution)/shard_map/ppermute | solution.py:287
  9.7 0.2 collective-permute-start.3
  10.0 1.0 copy-done.9
  11.0 1.6 %collective-permute-start.6 = (bf16[1,144,1152]{2,1,0:T(8,128)(2,1)S(1)}, bf16[1,144,1152]{2,1,0:T(8,128)(2,1)S(1)}, u32[]{:S(2)}, u32[]{:S(2)}) collective-permute-start(bf16[1,144,1152]{2,1,0:T(8,128)(2,1)S(1)} %shard_map.140.refs_0_), channel_id=1, source_target_pairs={{0,8},{4,20},{8,0},{12,28},{16,24},{20,4},{24,16},{28,12},{1,9},{5... | collective-permute-start | bytes 995336 | tf_op jit(solution)/shard_map/ppermute | solution.py:302
  12.5 0.6 shard_map.138.refs_0_
  13.1 0.0 copy-start.6
  13.1 0.0 copy-start.7
  13.1 0.0 copy-start.8
  13.1 5.0 %collective-permute-done.6.refs_1_ = bf16[1,144,1152]{2,1,0:T(8,128)(2,1)S(1)} collective-permute-done((bf16[1,144,1152]{2,1,0:T(8,128)(2,1)S(1)}, bf16[1,144,1152]{2,1,0:T(8,128)(2,1)S(1)}, u32[]{:S(2)}, u32[]{:S(2)}) %collective-permute-start.6) | collective-permute-done | bytes 331808 | tf_op jit(solution)/shard_map/ppermute | solution.py:302
  18.2 1.6 %collective-permute-start.7 = (bf16[2,144,1152]{2,1,0:T(8,128)(2,1)S(1)}, bf16[2,144,1152]{2,1,0:T(8,128)(2,1)S(1)}, u32[]{:S(2)}, u32[]{:S(2)}) collective-permute-start(bf16[2,144,1152]{2,1,0:T(8,128)(2,1)S(1)} %shard_map.141.refs_0_), channel_id=1, source_target_pairs={{0,16},{4,12},{8,24},{12,4},{16,0},{20,28},{24,8},{28,20},{1,17},{... | collective-permute-start | bytes 1990664 | tf_op jit(solution)/shard_map/ppermute | solution.py:302
  19.8 1.9 %shard_map.135 = (bf16[160,1152]{1,0:T(8,128)(2,1)S(1)}, f32[16,160,160]{2,1,0:T(8,128)S(1)}) custom-call(bf16[160,1152]{1,0:T(8,128)(2,1)S(1)} %bitcast.31, bf16[160,1152]{1,0:T(8,128)(2,1)S(1)} %bitcast.34, bf16[160,1152]{1,0:T(8,128)(2,1)S(1)} %bitcast.37), custom_call_target="tpu_custom_call" | custom-call | flops 20000000000 | bytes 10 | tf_op jit(solution)/shard_map/pallas_call | solution.py:274
  21.7 0.6 shard_map.136
  22.3 1.9 %collective-permute-start = (bf16[2,40,1152]{2,1,0:T(8,128)(2,1)S(1)}, bf16[2,40,1152]{2,1,0:T(8,128)(2,1)S(1)}, u32[]{:S(2)}, u32[]{:S(2)}) collective-permute-start(bf16[2,40,1152]{2,1,0:T(8,128)(2,1)S(1)} %get-tuple-element.66), channel_id=1, source_target_pairs={{0,1},{1,0},{2,3},{3,2},{4,5},{5,4},{6,7},{7,6},{8,9},{9,8},{10,11... | collective-permute-start | bytes 552968 | tf_op jit(solution)/shard_map/ppermute | solution.py:287
  24.2 4.8 %collective-permute-done.7.refs_1_ = bf16[2,144,1152]{2,1,0:T(8,128)(2,1)S(1)} collective-permute-done((bf16[2,144,1152]{2,1,0:T(8,128)(2,1)S(1)}, bf16[2,144,1152]{2,1,0:T(8,128)(2,1)S(1)}, u32[]{:S(2)}, u32[]{:S(2)}) %collective-permute-start.7) | collective-permute-done | bytes 663584 | tf_op jit(solution)/shard_map/ppermute | solution.py:302
  29.0 2.8 %collective-permute-start.1 = (bf16[2,40,1152]{2,1,0:T(8,128)(2,1)S(1)}, bf16[2,40,1152]{2,1,0:T(8,128)(2,1)S(1)}, u32[]{:S(2)}, u32[]{:S(2)}) collective-permute-start(bf16[2,40,1152]{2,1,0:T(8,128)(2,1)S(1)} %get-tuple-element.67), channel_id=1, source_target_pairs={{0,2},{1,3},{2,0},{3,1},{4,6},{5,7},{6,4},{7,5},{8,10},{9,11},{10,... | collective-permute-start | bytes 552968 | tf_op jit(solution)/shard_map/ppermute | solution.py:287
  31.8 0.1 shard_map.142.mine_ref
  31.9 0.0 collective-permute-done.4.refs_2_
  31.9 1.4 %collective-permute-start.2 = (bf16[2,40,1152]{2,1,0:T(8,128)(2,1)S(1)}, bf16[2,40,1152]{2,1,0:T(8,128)(2,1)S(1)}, u32[]{:S(2)}, u32[]{:S(2)}) collective-permute-start(bf16[2,40,1152]{2,1,0:T(8,128)(2,1)S(1)} %get-tuple-element.68), channel_id=1, source_target_pairs={{0,3},{1,2},{2,1},{3,0},{4,7},{5,6},{6,5},{7,4},{8,11},{9,10},{10,... | collective-permute-start | bytes 552968 | tf_op jit(solution)/shard_map/ppermute | solution.py:287
  33.3 2.0 %shard_map.139 = (f32[16,160,160]{2,1,0:T(8,128)S(1)}, bf16[3,160,1152]{2,1,0:T(8,128)(2,1)S(1)}, f32[160,1152]{1,0:T(8,128)S(1)}) custom-call(bf16[3,40,1152]{2,1,0:T(8,128)(2,1)S(1)} %shard_map.138.refs_0_, bf16[3,40,1152]{2,1,0:T(8,128)(2,1)S(1)} %collective-permute-done.3.refs_1_, bf16[3,40,1152]{2,1,0:T(8,128)(2,1)S(1)} %collective-permute-done.4.refs_2_, ...), custom_call_target="tpu_custom_call" | custom-call | flops 20000000000 | bytes 10 | tf_op jit(solution)/shard_map/pallas_call | solution.py:274
  35.3 1.1 %collective-permute-done.8.other_ref = bf16[4,144,1152]{2,1,0:T(8,128)(2,1)S(1)} collective-permute-done((bf16[4,144,1152]{2,1,0:T(8,128)(2,1)S(1)}, bf16[4,144,1152]{2,1,0:T(8,128)(2,1)S(1)}, u32[]{:S(2)}, u32[]{:S(2)}) %collective-permute-start.8) | collective-permute-done | bytes 1327136 | tf_op jit(solution)/shard_map/ppermute | solution.py:287
  36.3 0.7 shard_map.143
  37.1 0.0 collective-permute-done.refs_1_
  37.1 8.4 %collective-permute-done.1.refs_2_ = bf16[2,40,1152]{2,1,0:T(8,128)(2,1)S(1)} collective-permute-done((bf16[2,40,1152]{2,1,0:T(8,128)(2,1)S(1)}, bf16[2,40,1152]{2,1,0:T(8,128)(2,1)S(1)}, u32[]{:S(2)}, u32[]{:S(2)}) %collective-permute-start.1) | collective-permute-done | bytes 184352 | tf_op jit(solution)/shard_map/ppermute | solution.py:287
  45.5 0.0 collective-permute-done.2.refs_3_
  45.5 1.6 %shard_map.144 = (bf16[2,160,1152]{2,1,0:T(8,128)(2,1)S(1)}, bf16[160,1152]{1,0:T(8,128)(2,1)S(1)}, bf16[1,40,1152]{2,1,0:T(8,128)(2,1)S(1)}, bf16[1,40,1152]{2,...) custom-call(bf16[2,40,1152]{2,1,0:T(8,128)(2,1)S(1)} %get-tuple-element.65.refs_0_, ...), custom_call_target="tpu_custom_call" | custom-call | flops 20000000000 | bytes 10 | tf_op jit(solution)/shard_map/pallas_call | solution.py:274
  47.1 0.1 collective-permute-start.9
  47.1 2.9 %collective-permute-start.12 = (bf16[1,40,1152]{2,1,0:T(8,128)(2,1)S(1)}, bf16[1,40,1152]{2,1,0:T(8,128)(2,1)S(1)}, u32[]{:S(2)}, u32[]{:S(2)}) collective-permute-start(bf16[1,40,1152]{2,1,0:T(8,128)(2,1)S(1)} %get-tuple-element.86), channel_id=1, source_target_pairs={{0,3},{1,2},{2,1},{3,0},{4,7},{5,6},{6,5},{7,4},{8,11},{9,10},{10,... | collective-permute-start | bytes 276488 | tf_op jit(solution)/shard_map/ppermute | solution.py:287
  50.0 1.8 %shard_map.145 = (f32[2,4,72,640]{3,2,1,0:T(8,128)S(1)}, bf16[2,4,72,640]{3,2,1,0:T(8,128)(2,1)S(1)}) custom-call(s32[2]{0:T(128)S(1)} %pad_add_fusion.where_ref, bf16[2,160,1152]{2,1,0:T(8,128)(2,1)S(1)} %get-tuple-element.79.mine_ref, bf16[2,160,1152]{2,1,0:T(8,128)(2,1)S(1)} %collective-permute-done.9.other_ref), custom_call_target="tpu_custom_call" | custom-call | flops 20000000000 | bytes 10 | tf_op jit(solution)/shard_map/pallas_call | solution.py:274
  51.9 1.6 %collective-permute-start.13 = (bf16[2,4,72,640]{3,2,1,0:T(8,128)(2,1)S(1)}, bf16[2,4,72,640]{3,2,1,0:T(8,128)(2,1)S(1)}, u32[]{:S(2)}, u32[]{:S(2)}) collective-permute-start(bf16[2,4,72,640]{3,2,1,0:T(8,128)(2,1)S(1)} %get-tuple-element.80), channel_id=1, source_target_pairs={{0,8},{4,20},{8,0},{12,28},{16,24},{20,4},{24,16},{28,12},{1,9},{5... | collective-permute-start | bytes 2211848 | tf_op jit(solution)/shard_map/ppermute | solution.py:302
  53.4 3.5 %collective-permute-start.10 = (bf16[1,40,1152]{2,1,0:T(8,128)(2,1)S(1)}, bf16[1,40,1152]{2,1,0:T(8,128)(2,1)S(1)}, u32[]{:S(2)}, u32[]{:S(2)}) collective-permute-start(bf16[1,40,1152]{2,1,0:T(8,128)(2,1)S(1)} %get-tuple-element.83), channel_id=1, source_target_pairs={{0,1},{1,0},{2,3},{3,2},{4,5},{5,4},{6,7},{7,6},{8,9},{9,8},{10,11... | collective-permute-start | bytes 276488 | tf_op jit(solution)/shard_map/ppermute | solution.py:287
  56.9 1.6 %collective-permute-start.11 = (bf16[1,40,1152]{2,1,0:T(8,128)(2,1)S(1)}, bf16[1,40,1152]{2,1,0:T(8,128)(2,1)S(1)}, u32[]{:S(2)}, u32[]{:S(2)}) collective-permute-start(bf16[1,40,1152]{2,1,0:T(8,128)(2,1)S(1)} %get-tuple-element.85), channel_id=1, source_target_pairs={{0,2},{1,3},{2,0},{3,1},{4,6},{5,7},{6,4},{7,5},{8,10},{9,11},{10,... | collective-permute-start | bytes 276488 | tf_op jit(solution)/shard_map/ppermute | solution.py:287
  58.5 4.3 %shard_map.147 = (bf16[3,40,1152]{2,1,0:T(8,128)(2,1)S(1)}, bf16[3,40,1152]{2,1,0:T(8,128)(2,1)S(1)}, bf16[3,40,1152]{2,1,0:T(8,128)(2,1)S(1)}, bf16[3,40,1152]{2,1,0:T(8,128)(2,1)S(1)}) custom-call(bf16[160,1152]{1,0:T(8,128)(2,1)S(1)} %get-tuple-element.88.step_ref, bf16[3,160,1152]{2,1,0:T(8,128)(2,1)S(1)} %get-tuple-element.89.qkv_ref, ...), custom_call_target="tpu_custom_call" | custom-call | flops 20000000000 | bytes 10 | tf_op jit(solution)/shard_map/pallas_call | solution.py:274
  62.9 0.5 collective-permute-done.11.refs_2_
  63.4 0.0 collective-permute-done.13.came_ref
  63.4 0.1 shard_map.148
  63.5 1.6 %collective-permute-start.14 = (bf16[1,4,72,640]{3,2,1,0:T(8,128)(2,1)S(1)}, bf16[1,4,72,640]{3,2,1,0:T(8,128)(2,1)S(1)}, u32[]{:S(2)}, u32[]{:S(2)}) collective-permute-start(bf16[1,4,72,640]{3,2,1,0:T(8,128)(2,1)S(1)} %get-tuple-element.98), channel_id=1, source_target_pairs={{0,16},{4,12},{8,24},{12,4},{16,0},{20,28},{24,8},{28,20},{1,17},{... | collective-permute-start | bytes 1105928 | tf_op jit(solution)/shard_map/ppermute | solution.py:302
  65.1 2.5 %collective-permute-start.16 = (bf16[3,40,1152]{2,1,0:T(8,128)(2,1)S(1)}, bf16[3,40,1152]{2,1,0:T(8,128)(2,1)S(1)}, u32[]{:S(2)}, u32[]{:S(2)}) collective-permute-start(bf16[3,40,1152]{2,1,0:T(8,128)(2,1)S(1)} %get-tuple-element.102), channel_id=1, source_target_pairs={{0,3},{1,2},{2,1},{3,0},{4,7},{5,6},{6,5},{7,4},{8,11},{9,10},{10,... | collective-permute-start | bytes 829448 | tf_op jit(solution)/shard_map/ppermute | solution.py:287
  67.6 0.6 shard_map.146
  68.1 2.4 %shard_map.149 = (f32[160,1152]{1,0:T(8,128)S(1)}, f32[160,1152]{1,0:T(8,128)S(1)}, f32[160,1152]{1,0:T(8,128)S(1)}) custom-call(bf16[160,1152]{1,0:T(8,128)(2,1)S(1)} %bitcast.32, bf16[160,1152]{1,0:T(8,128)(2,1)S(1)} %bitcast.35, bf16[160,1152]{1,0:T(8,128)(2,1)S(1)} %bitcast.38, bf16[160,1152]{1,0:T(8,128)(2,1)S(1)} %bitcast.21, ...), custom_call_target="tpu_custom_call" | custom-call | flops 10 | bytes 10 | tf_op jit(solution)/shard_map/pallas_call | solution.py:274
  70.6 0.5 collective-permute-done.14.came_ref
  71.1 0.7 shard_map.150
  71.8 3.6 %collective-permute-start.15 = (bf16[2,72,640]{2,1,0:T(8,128)(2,1)S(1)}, bf16[2,72,640]{2,1,0:T(8,128)(2,1)S(1)}, u32[]{:S(2)}, u32[]{:S(2)}) collective-permute-start(bf16[2,72,640]{2,1,0:T(8,128)(2,1)S(1)} %get-tuple-element.100), channel_id=1, source_target_pairs={{0,1},{1,0},{2,3},{3,2},{4,5},{5,4},{6,7},{7,6},{8,9},{9,8},{10,11... | collective-permute-start | bytes 552968 | tf_op jit(solution)/shard_map/ppermute | solution.py:287
  75.3 3.8 %collective-permute-done.15.came_ref = bf16[2,72,640]{2,1,0:T(8,128)(2,1)S(1)} collective-permute-done((bf16[2,72,640]{2,1,0:T(8,128)(2,1)S(1)}, bf16[2,72,640]{2,1,0:T(8,128)(2,1)S(1)}, u32[]{:S(2)}, u32[]{:S(2)}) %collective-permute-start.15) | collective-permute-done | bytes 184352 | tf_op jit(solution)/shard_map/ppermute | solution.py:287
  79.2 3.4 %collective-permute-start.17 = (bf16[1,72,640]{2,1,0:T(8,128)(2,1)S(1)}, bf16[1,72,640]{2,1,0:T(8,128)(2,1)S(1)}, u32[]{:S(2)}, u32[]{:S(2)}) collective-permute-start(bf16[1,72,640]{2,1,0:T(8,128)(2,1)S(1)} %get-tuple-element.104), channel_id=1, source_target_pairs={{0,2},{1,3},{2,0},{3,1},{4,6},{5,7},{6,4},{7,5},{8,10},{9,11},{10,... | collective-permute-start | bytes 276488 | tf_op jit(solution)/shard_map/ppermute | solution.py:287
  82.6 0.8 collective-permute-start.18
  83.3 0.6 collective-permute-start.19
  83.9 1.8 %collective-permute-done.17.came_ref = bf16[1,72,640]{2,1,0:T(8,128)(2,1)S(1)} collective-permute-done((bf16[1,72,640]{2,1,0:T(8,128)(2,1)S(1)}, bf16[1,72,640]{2,1,0:T(8,128)(2,1)S(1)}, u32[]{:S(2)}, u32[]{:S(2)}) %collective-permute-start.17) | collective-permute-done | bytes 92192 | tf_op jit(solution)/shard_map/ppermute | solution.py:287
  85.7 3.9 %collective-permute-start.20 = (bf16[1,72,640]{2,1,0:T(8,128)(2,1)S(1)}, bf16[1,72,640]{2,1,0:T(8,128)(2,1)S(1)}, u32[]{:S(2)}, u32[]{:S(2)}) collective-permute-start(bf16[1,72,640]{2,1,0:T(8,128)(2,1)S(1)} %shard_map.152.refs_0_), channel_id=1, source_target_pairs={{0,8},{4,20},{8,0},{12,28},{16,24},{20,4},{24,16},{28,12},{1,9},{5... | collective-permute-start | bytes 276488 | tf_op jit(solution)/shard_map/ppermute | solution.py:302
  89.6 1.4 %shard_map.154 = (bf16[4,40,1152]{2,1,0:T(8,128)(2,1)}, bf16[4,40,1152]{2,1,0:T(8,128)(2,1)}, bf16[4,40,1152]{2,1,0:T(8,128)(2,1)}) custom-call(s32[2]{0:T(128)S(1)} %pad_add_fusion.where_ref, bf16[3,40,1152]{2,1,0:T(8,128)(2,1)S(1)} %get-tuple-element.91.refs_0_, bf16[3,40,1152]{2,1,0:T(8,128)(2,1)S(1)} %collective-permute-done.16.refs_1_), custom_call_target="tpu_custom_call" | custom-call | flops 20000000000 | bytes 10 | tf_op jit(solution)/shard_map/pallas_call | solution.py:255
  91.0 1.1 %collective-permute-done.20.refs_1_ = bf16[1,72,640]{2,1,0:T(8,128)(2,1)S(1)} collective-permute-done((bf16[1,72,640]{2,1,0:T(8,128)(2,1)S(1)}, bf16[1,72,640]{2,1,0:T(8,128)(2,1)S(1)}, u32[]{:S(2)}, u32[]{:S(2)}) %collective-permute-start.20) | collective-permute-done | bytes 92192 | tf_op jit(solution)/shard_map/ppermute | solution.py:302
  92.1 2.1 %collective-permute-start.21 = (bf16[2,72,640]{2,1,0:T(8,128)(2,1)S(1)}, bf16[2,72,640]{2,1,0:T(8,128)(2,1)S(1)}, u32[]{:S(2)}, u32[]{:S(2)}) collective-permute-start(bf16[2,72,640]{2,1,0:T(8,128)(2,1)S(1)} %shard_map.156.refs_0_), channel_id=1, source_target_pairs={{0,16},{4,12},{8,24},{12,4},{16,0},{20,28},{24,8},{28,20},{1,17},{... | collective-permute-start | bytes 552968 | tf_op jit(solution)/shard_map/ppermute | solution.py:302
  94.2 3.2 %shard_map.153 = (bf16[160,1152]{1,0:T(8,128)(2,1)}, bf16[160,1152]{1,0:T(8,128)(2,1)}, bf16[160,1152]{1,0:T(8,128)(2,1)}) custom-call(bf16[160,1152]{1,0:T(8,128)(2,1)S(1)} %bitcast.33, bf16[160,1152]{1,0:T(8,128)(2,1)S(1)} %bitcast.36, bf16[160,1152]{1,0:T(8,128)(2,1)S(1)} %bitcast.39, bf16[160,1152]{1,0:T(8,128)(2,1)S(1)} %bitcast.22, ...), custom_call_target="tpu_custom_call" | custom-call | flops 20000000000 | bytes 10 | tf_op jit(solution)/shard_map/pallas_call | solution.py:274
  97.5 0.3 collective-permute-done.21.refs_1_
  97.8 0.1 collective-permute-start.22
  97.9 0.0 collective-permute-done.19.refs_1_
  97.9 1.4 %shard_map.155 = (bf16[4,40,1152]{2,1,0:T(8,128)(2,1)}, bf16[4,40,1152]{2,1,0:T(8,128)(2,1)}, bf16[4,40,1152]{2,1,0:T(8,128)(2,1)}) custom-call(s32[2]{0:T(128)S(1)} %pad_add_fusion.where_ref, bf16[3,40,1152]{2,1,0:T(8,128)(2,1)S(1)} %collective-permute-done.18.refs_0_, ...), custom_call_target="tpu_custom_call", output_to_operand_aliasing={{0}: (3, {}), {1}: (4, {}), {2}: (5, {})} | custom-call | flops 20000000000 | bytes 10 | tf_op jit(solution)/shard_map/pallas_call | solution.py:255
  99.3 0.2 collective-permute-done.22.other_ref
  99.6 1.8 %shard_map.158 = f32[4,72,1152]{2,1,0:T(8,128)} custom-call(s32[2]{0:T(128)S(1)} %pad_add_fusion.where_ref, bf16[4,72,640]{2,1,0:T(8,128)(2,1)S(1)} %shard_map.157.mine_ref, bf16[4,72,640]{2,1,0:T(8,128)(2,1)S(1)} %collective-permute-done.22.other_ref), custom_call_target="tpu_custom_call" | custom-call | flops 10 | bytes 10 | tf_op jit(solution)/shard_map/pallas_call | solution.py:274
  (27 shorter events, 0.2 us)
Async XLA Ops:
  0.7 1.0 copy-start.1
  1.7 1.0 copy-start.3
  2.7 1.0 copy-start.5
  4.3 27.6 %collective-permute-start.4 = (bf16[3,40,1152]{2,1,0:T(8,128)(2,1)S(1)}, bf16[3,40,1152]{2,1,0:T(8,128)(2,1)S(1)}, u32[]{:S(2)}, u32[]{:S(2)}) collective-permute-start(bf16[3,40,1152]{2,1,0:T(8,128)(2,1)S(1)} %get-tuple-element.72), channel_id=1, source_target_pairs={{0,2},{1,3},{2,0},{3,1},{4,6},{5,7},{6,4},{7,5},{8,10},{9,11},{10,... | collective-permute-start | bytes 829448 | tf_op jit(solution)/shard_map/ppermute | solution.py:287
  8.4 24.9 %collective-permute-start.5 = (bf16[3,40,1152]{2,1,0:T(8,128)(2,1)S(1)}, bf16[3,40,1152]{2,1,0:T(8,128)(2,1)S(1)}, u32[]{:S(2)}, u32[]{:S(2)}) collective-permute-start(bf16[3,40,1152]{2,1,0:T(8,128)(2,1)S(1)} %get-tuple-element.73), channel_id=1, source_target_pairs={{0,3},{1,2},{2,1},{3,0},{4,7},{5,6},{6,5},{7,4},{8,11},{9,10},{10,... | collective-permute-start | bytes 829448 | tf_op jit(solution)/shard_map/ppermute | solution.py:287
  9.7 23.6 %collective-permute-start.3 = (bf16[3,40,1152]{2,1,0:T(8,128)(2,1)S(1)}, bf16[3,40,1152]{2,1,0:T(8,128)(2,1)S(1)}, u32[]{:S(2)}, u32[]{:S(2)}) collective-permute-start(bf16[3,40,1152]{2,1,0:T(8,128)(2,1)S(1)} %get-tuple-element.69), channel_id=1, source_target_pairs={{0,1},{1,0},{2,3},{3,2},{4,5},{5,4},{6,7},{7,6},{8,9},{9,8},{10,11... | collective-permute-start | bytes 829448 | tf_op jit(solution)/shard_map/ppermute | solution.py:287
  10.0 1.0 copy-start.9
  10.9 1.6 %copy-start.2 = (bf16[1,160,1152]{2,1,0:T(8,128)(2,1)S(1)}, bf16[1,160,1152]{2,1,0:T(8,128)(2,1)}, u32[]{:S(2)}) copy-start(bf16[1,160,1152]{2,1,0:T(8,128)(2,1)} %param.11) | copy-start | bytes 1105924
  10.9 1.6 %copy-start.4 = (bf16[1,160,1152]{2,1,0:T(8,128)(2,1)S(1)}, bf16[1,160,1152]{2,1,0:T(8,128)(2,1)}, u32[]{:S(2)}) copy-start(bf16[1,160,1152]{2,1,0:T(8,128)(2,1)} %param.12) | copy-start | bytes 1105924
  11.0 7.2 %collective-permute-start.6 = (bf16[1,144,1152]{2,1,0:T(8,128)(2,1)S(1)}, bf16[1,144,1152]{2,1,0:T(8,128)(2,1)S(1)}, u32[]{:S(2)}, u32[]{:S(2)}) collective-permute-start(bf16[1,144,1152]{2,1,0:T(8,128)(2,1)S(1)} %shard_map.140.refs_0_), channel_id=1, source_target_pairs={{0,8},{4,20},{8,0},{12,28},{16,24},{20,4},{24,16},{28,12},{1,9},{5... | collective-permute-start | bytes 995336 | tf_op jit(solution)/shard_map/ppermute | solution.py:302
  13.1 6.7 %copy-start.6 = (bf16[1,160,1152]{2,1,0:T(8,128)(2,1)S(1)}, bf16[1,160,1152]{2,1,0:T(8,128)(2,1)}, u32[]{:S(2)}) copy-start(bf16[1,160,1152]{2,1,0:T(8,128)(2,1)} %param.8) | copy-start | bytes 1105924
  13.1 6.7 %copy-start.7 = (bf16[1,160,1152]{2,1,0:T(8,128)(2,1)S(1)}, bf16[1,160,1152]{2,1,0:T(8,128)(2,1)}, u32[]{:S(2)}) copy-start(bf16[1,160,1152]{2,1,0:T(8,128)(2,1)} %param.9) | copy-start | bytes 1105924
  13.1 6.7 %copy-start.8 = (bf16[1,160,1152]{2,1,0:T(8,128)(2,1)S(1)}, bf16[1,160,1152]{2,1,0:T(8,128)(2,1)}, u32[]{:S(2)}) copy-start(bf16[1,160,1152]{2,1,0:T(8,128)(2,1)} %param.10) | copy-start | bytes 1105924
  18.2 10.7 %collective-permute-start.7 = (bf16[2,144,1152]{2,1,0:T(8,128)(2,1)S(1)}, bf16[2,144,1152]{2,1,0:T(8,128)(2,1)S(1)}, u32[]{:S(2)}, u32[]{:S(2)}) collective-permute-start(bf16[2,144,1152]{2,1,0:T(8,128)(2,1)S(1)} %shard_map.141.refs_0_), channel_id=1, source_target_pairs={{0,16},{4,12},{8,24},{12,4},{16,0},{20,28},{24,8},{28,20},{1,17},{... | collective-permute-start | bytes 1990664 | tf_op jit(solution)/shard_map/ppermute | solution.py:302
  19.8 1.9 %copy-start = (bf16[1,160,1152]{2,1,0:T(8,128)(2,1)S(1)}, bf16[1,160,1152]{2,1,0:T(8,128)(2,1)}, u32[]{:S(2)}) copy-start(bf16[1,160,1152]{2,1,0:T(8,128)(2,1)} %param.15) | copy-start | bytes 1105924
  22.3 14.8 %collective-permute-start = (bf16[2,40,1152]{2,1,0:T(8,128)(2,1)S(1)}, bf16[2,40,1152]{2,1,0:T(8,128)(2,1)S(1)}, u32[]{:S(2)}, u32[]{:S(2)}) collective-permute-start(bf16[2,40,1152]{2,1,0:T(8,128)(2,1)S(1)} %get-tuple-element.66), channel_id=1, source_target_pairs={{0,1},{1,0},{2,3},{3,2},{4,5},{5,4},{6,7},{7,6},{8,9},{9,8},{10,11... | collective-permute-start | bytes 552968 | tf_op jit(solution)/shard_map/ppermute | solution.py:287
  29.0 16.5 %collective-permute-start.1 = (bf16[2,40,1152]{2,1,0:T(8,128)(2,1)S(1)}, bf16[2,40,1152]{2,1,0:T(8,128)(2,1)S(1)}, u32[]{:S(2)}, u32[]{:S(2)}) collective-permute-start(bf16[2,40,1152]{2,1,0:T(8,128)(2,1)S(1)} %get-tuple-element.67), channel_id=1, source_target_pairs={{0,2},{1,3},{2,0},{3,1},{4,6},{5,7},{6,4},{7,5},{8,10},{9,11},{10,... | collective-permute-start | bytes 552968 | tf_op jit(solution)/shard_map/ppermute | solution.py:287
  31.9 13.6 %collective-permute-start.2 = (bf16[2,40,1152]{2,1,0:T(8,128)(2,1)S(1)}, bf16[2,40,1152]{2,1,0:T(8,128)(2,1)S(1)}, u32[]{:S(2)}, u32[]{:S(2)}) collective-permute-start(bf16[2,40,1152]{2,1,0:T(8,128)(2,1)S(1)} %get-tuple-element.68), channel_id=1, source_target_pairs={{0,3},{1,2},{2,1},{3,0},{4,7},{5,6},{6,5},{7,4},{8,11},{9,10},{10,... | collective-permute-start | bytes 552968 | tf_op jit(solution)/shard_map/ppermute | solution.py:287
  33.3 3.1 %collective-permute-start.8 = (bf16[4,144,1152]{2,1,0:T(8,128)(2,1)S(1)}, bf16[4,144,1152]{2,1,0:T(8,128)(2,1)S(1)}, u32[]{:S(2)}, u32[]{:S(2)}) collective-permute-start(bf16[4,144,1152]{2,1,0:T(8,128)(2,1)S(1)} %shard_map.142.mine_ref), channel_id=1, source_target_pairs={{0,4},{4,0},{8,12},{12,8},{16,20},{20,16},{24,28},{28,24},{1,5},{5... | collective-permute-start | bytes 3981320 | tf_op jit(solution)/shard_map/ppermute | solution.py:287
  47.1 3.0 %collective-permute-start.9 = (bf16[2,160,1152]{2,1,0:T(8,128)(2,1)S(1)}, bf16[2,160,1152]{2,1,0:T(8,128)(2,1)S(1)}, u32[]{:S(2)}, u32[]{:S(2)}) collective-permute-start(bf16[2,160,1152]{2,1,0:T(8,128)(2,1)S(1)} %get-tuple-element.79.mine_ref), channel_id=1, source_target_pairs={{0,4},{4,0},{8,12},{12,8},{16,20},{20,16},{24,28},{28,24},{1,5},{5... | collective-permute-start | bytes 2211848 | tf_op jit(solution)/shard_map/ppermute | solution.py:287
  47.1 15.7 %collective-permute-start.12 = (bf16[1,40,1152]{2,1,0:T(8,128)(2,1)S(1)}, bf16[1,40,1152]{2,1,0:T(8,128)(2,1)S(1)}, u32[]{:S(2)}, u32[]{:S(2)}) collective-permute-start(bf16[1,40,1152]{2,1,0:T(8,128)(2,1)S(1)} %get-tuple-element.86), channel_id=1, source_target_pairs={{0,3},{1,2},{2,1},{3,0},{4,7},{5,6},{6,5},{7,4},{8,11},{9,10},{10,... | collective-permute-start | bytes 276488 | tf_op jit(solution)/shard_map/ppermute | solution.py:287
  51.9 11.5 %collective-permute-start.13 = (bf16[2,4,72,640]{3,2,1,0:T(8,128)(2,1)S(1)}, bf16[2,4,72,640]{3,2,1,0:T(8,128)(2,1)S(1)}, u32[]{:S(2)}, u32[]{:S(2)}) collective-permute-start(bf16[2,4,72,640]{3,2,1,0:T(8,128)(2,1)S(1)} %get-tuple-element.80), channel_id=1, source_target_pairs={{0,8},{4,20},{8,0},{12,28},{16,24},{20,4},{24,16},{28,12},{1,9},{5... | collective-permute-start | bytes 2211848 | tf_op jit(solution)/shard_map/ppermute | solution.py:302
  53.4 9.5 %collective-permute-start.10 = (bf16[1,40,1152]{2,1,0:T(8,128)(2,1)S(1)}, bf16[1,40,1152]{2,1,0:T(8,128)(2,1)S(1)}, u32[]{:S(2)}, u32[]{:S(2)}) collective-permute-start(bf16[1,40,1152]{2,1,0:T(8,128)(2,1)S(1)} %get-tuple-element.83), channel_id=1, source_target_pairs={{0,1},{1,0},{2,3},{3,2},{4,5},{5,4},{6,7},{7,6},{8,9},{9,8},{10,11... | collective-permute-start | bytes 276488 | tf_op jit(solution)/shard_map/ppermute | solution.py:287
  56.9 6.4 %collective-permute-start.11 = (bf16[1,40,1152]{2,1,0:T(8,128)(2,1)S(1)}, bf16[1,40,1152]{2,1,0:T(8,128)(2,1)S(1)}, u32[]{:S(2)}, u32[]{:S(2)}) collective-permute-start(bf16[1,40,1152]{2,1,0:T(8,128)(2,1)S(1)} %get-tuple-element.85), channel_id=1, source_target_pairs={{0,2},{1,3},{2,0},{3,1},{4,6},{5,7},{6,4},{7,5},{8,10},{9,11},{10,... | collective-permute-start | bytes 276488 | tf_op jit(solution)/shard_map/ppermute | solution.py:287
  63.5 7.6 %collective-permute-start.14 = (bf16[1,4,72,640]{3,2,1,0:T(8,128)(2,1)S(1)}, bf16[1,4,72,640]{3,2,1,0:T(8,128)(2,1)S(1)}, u32[]{:S(2)}, u32[]{:S(2)}) collective-permute-start(bf16[1,4,72,640]{3,2,1,0:T(8,128)(2,1)S(1)} %get-tuple-element.98), channel_id=1, source_target_pairs={{0,16},{4,12},{8,24},{12,4},{16,0},{20,28},{24,8},{28,20},{1,17},{... | collective-permute-start | bytes 1105928 | tf_op jit(solution)/shard_map/ppermute | solution.py:302
  65.1 18.8 %collective-permute-start.16 = (bf16[3,40,1152]{2,1,0:T(8,128)(2,1)S(1)}, bf16[3,40,1152]{2,1,0:T(8,128)(2,1)S(1)}, u32[]{:S(2)}, u32[]{:S(2)}) collective-permute-start(bf16[3,40,1152]{2,1,0:T(8,128)(2,1)S(1)} %get-tuple-element.102), channel_id=1, source_target_pairs={{0,3},{1,2},{2,1},{3,0},{4,7},{5,6},{6,5},{7,4},{8,11},{9,10},{10,... | collective-permute-start | bytes 829448 | tf_op jit(solution)/shard_map/ppermute | solution.py:287
  71.8 7.3 %collective-permute-start.15 = (bf16[2,72,640]{2,1,0:T(8,128)(2,1)S(1)}, bf16[2,72,640]{2,1,0:T(8,128)(2,1)S(1)}, u32[]{:S(2)}, u32[]{:S(2)}) collective-permute-start(bf16[2,72,640]{2,1,0:T(8,128)(2,1)S(1)} %get-tuple-element.100), channel_id=1, source_target_pairs={{0,1},{1,0},{2,3},{3,2},{4,5},{5,4},{6,7},{7,6},{8,9},{9,8},{10,11... | collective-permute-start | bytes 552968 | tf_op jit(solution)/shard_map/ppermute | solution.py:287
  79.2 6.5 %collective-permute-start.17 = (bf16[1,72,640]{2,1,0:T(8,128)(2,1)S(1)}, bf16[1,72,640]{2,1,0:T(8,128)(2,1)S(1)}, u32[]{:S(2)}, u32[]{:S(2)}) collective-permute-start(bf16[1,72,640]{2,1,0:T(8,128)(2,1)S(1)} %get-tuple-element.104), channel_id=1, source_target_pairs={{0,2},{1,3},{2,0},{3,1},{4,6},{5,7},{6,4},{7,5},{8,10},{9,11},{10,... | collective-permute-start | bytes 276488 | tf_op jit(solution)/shard_map/ppermute | solution.py:287
  82.6 15.3 %collective-permute-start.18 = (bf16[3,40,1152]{2,1,0:T(8,128)(2,1)S(1)}, bf16[3,40,1152]{2,1,0:T(8,128)(2,1)S(1)}, u32[]{:S(2)}, u32[]{:S(2)}) collective-permute-start(bf16[3,40,1152]{2,1,0:T(8,128)(2,1)S(1)} %get-tuple-element.111), channel_id=1, source_target_pairs={{0,1},{1,0},{2,3},{3,2},{4,5},{5,4},{6,7},{7,6},{8,9},{9,8},{10,11... | collective-permute-start | bytes 829448 | tf_op jit(solution)/shard_map/ppermute | solution.py:287
  83.3 14.6 %collective-permute-start.19 = (bf16[3,40,1152]{2,1,0:T(8,128)(2,1)S(1)}, bf16[3,40,1152]{2,1,0:T(8,128)(2,1)S(1)}, u32[]{:S(2)}, u32[]{:S(2)}) collective-permute-start(bf16[3,40,1152]{2,1,0:T(8,128)(2,1)S(1)} %get-tuple-element.112), channel_id=1, source_target_pairs={{0,2},{1,3},{2,0},{3,1},{4,6},{5,7},{6,4},{7,5},{8,10},{9,11},{10,... | collective-permute-start | bytes 829448 | tf_op jit(solution)/shard_map/ppermute | solution.py:287
  85.7 6.4 %collective-permute-start.20 = (bf16[1,72,640]{2,1,0:T(8,128)(2,1)S(1)}, bf16[1,72,640]{2,1,0:T(8,128)(2,1)S(1)}, u32[]{:S(2)}, u32[]{:S(2)}) collective-permute-start(bf16[1,72,640]{2,1,0:T(8,128)(2,1)S(1)} %shard_map.152.refs_0_), channel_id=1, source_target_pairs={{0,8},{4,20},{8,0},{12,28},{16,24},{20,4},{24,16},{28,12},{1,9},{5... | collective-permute-start | bytes 276488 | tf_op jit(solution)/shard_map/ppermute | solution.py:302
  92.1 5.6 %collective-permute-start.21 = (bf16[2,72,640]{2,1,0:T(8,128)(2,1)S(1)}, bf16[2,72,640]{2,1,0:T(8,128)(2,1)S(1)}, u32[]{:S(2)}, u32[]{:S(2)}) collective-permute-start(bf16[2,72,640]{2,1,0:T(8,128)(2,1)S(1)} %shard_map.156.refs_0_), channel_id=1, source_target_pairs={{0,16},{4,12},{8,24},{12,4},{16,0},{20,28},{24,8},{28,20},{1,17},{... | collective-permute-start | bytes 552968 | tf_op jit(solution)/shard_map/ppermute | solution.py:302
  97.8 1.8 %collective-permute-start.22 = (bf16[4,72,640]{2,1,0:T(8,128)(2,1)S(1)}, bf16[4,72,640]{2,1,0:T(8,128)(2,1)S(1)}, u32[]{:S(2)}, u32[]{:S(2)}) collective-permute-start(bf16[4,72,640]{2,1,0:T(8,128)(2,1)S(1)} %shard_map.157.mine_ref), channel_id=1, source_target_pairs={{0,4},{4,0},{8,12},{12,8},{16,20},{20,16},{24,28},{28,24},{1,5},{5... | collective-permute-start | bytes 1105928 | tf_op jit(solution)/shard_map/ppermute | solution.py:287

commit v7 on v5

--- a/solution.py
+++ b/solution.py
@@ -95,7 +95,7 @@
 def space_first_kernel(q_ref, k_ref, v_ref, g_ref, probs_ref, *sums):
     for item in sums:
         item[...] = jnp.zeros_like(item)
-    backward(q_ref, k_ref, v_ref, g_ref, probs_ref, *sums, heads=slice(probs_ref.shape[0] // 2))
+    backward(q_ref, k_ref, v_ref, g_ref, probs_ref, *sums, heads=slice(probs_ref.shape[0] * 5 // 8))
 
 
 def space_backward_kernel(q_ref, k_ref, v_ref, g_ref, probs_ref, *refs):
@@ -103,7 +103,7 @@
     for first, item in zip(firsts, sums):
         item[...] = first[...]
     backward(
-        q_ref, k_ref, v_ref, g_ref, probs_ref, *sums, heads=slice(probs_ref.shape[0] // 2, None)
+        q_ref, k_ref, v_ref, g_ref, probs_ref, *sums, heads=slice(probs_ref.shape[0] * 5 // 8, None)
     )
     scaling = 1.0 / math.sqrt(HEAD_DIM)
     dq_ref[...] = (sums[0][...] * scaling).astype(BF16)

time: 102 us -> 102 us (level)
  no operation moved by 1% of the time
where the time goes in v7:
time: 102 us; the launch traced here: 101 us
  starting transfers between devices  42.9 us (42%)
  waiting for transfers between devices  27.4 us (27%)
  Pallas kernels  26.1 us (26%)
  local copies, waits for them, and re-layouts  3.96 us (4%)
    ppermute x17, starting transfers between devices, swap(): return lax.ppermute(array, axis, [(i, i ^ bits) for i in range(size)])  30.7 us
    pallas_call x22, Pallas kernels, call(): pl.pallas_call(body, out_shape=tuple((jax.ShapeDtypeStruct(*out) for out...  23.3 us
    ppermute x6, waiting for transfers between devices, swap_ways(): lax.ppermute(array, 'dp', [(i, i ^ bits[i % 2]) for i in range(size)])  15.2 us
    ppermute x6, starting transfers between devices, swap_ways(): lax.ppermute(array, 'dp', [(i, i ^ bits[i % 2]) for i in range(size)])  12.3 us
    ppermute x17, waiting for transfers between devices, swap(): return lax.ppermute(array, axis, [(i, i ^ bits) for i in range(size)])  12.2 us
    unnamed x20, local copies, waits for them, and re-layouts  3.96 us
    pallas_call x2, Pallas kernels, place(): pl.pallas_call(functools.partial(place_kernel, slots), out_shape=(jax.Sha...  2.77 us
  transfers between devices with their start and end apart: 23, of which 11 were waited for; matrix products, arithmetic and copies ran while one was open for 0% of the time, Pallas kernels for 22%

profile of v7, /device:TPU:0, one launch (start us, length us, event | category | flops | bytes accessed | tf_op | source)
XLA Modules:
  0.0 101.3 jit_solution(2252698826137618555)
XLA Ops:
  0.6 0.1 pad_add_fusion.where_ref
  0.7 1.0 copy-done.1
  1.7 1.0 copy-done.3
  2.7 1.0 copy-done.5
  3.7 0.6 shard_map.137
  4.3 4.1 %collective-permute-start.4 = (bf16[3,40,1152]{2,1,0:T(8,128)(2,1)S(1)}, bf16[3,40,1152]{2,1,0:T(8,128)(2,1)S(1)}, u32[]{:S(2)}, u32[]{:S(2)}) collective-permute-start(bf16[3,40,1152]{2,1,0:T(8,128)(2,1)S(1)} %get-tuple-element.72), channel_id=1, source_target_pairs={{0,2},{1,3},{2,0},{3,1},{4,6},{5,7},{6,4},{7,5},{8,10},{9,11},{10,... | collective-permute-start | bytes 829448 | tf_op jit(solution)/shard_map/ppermute | solution.py:287
  8.4 1.3 %collective-permute-start.5 = (bf16[3,40,1152]{2,1,0:T(8,128)(2,1)S(1)}, bf16[3,40,1152]{2,1,0:T(8,128)(2,1)S(1)}, u32[]{:S(2)}, u32[]{:S(2)}) collective-permute-start(bf16[3,40,1152]{2,1,0:T(8,128)(2,1)S(1)} %get-tuple-element.73), channel_id=1, source_target_pairs={{0,3},{1,2},{2,1},{3,0},{4,7},{5,6},{6,5},{7,4},{8,11},{9,10},{10,... | collective-permute-start | bytes 829448 | tf_op jit(solution)/shard_map/ppermute | solution.py:287
  9.7 0.2 collective-permute-start.3
  10.0 1.0 copy-done.9
  11.0 1.6 %collective-permute-start.6 = (bf16[1,144,1152]{2,1,0:T(8,128)(2,1)S(1)}, bf16[1,144,1152]{2,1,0:T(8,128)(2,1)S(1)}, u32[]{:S(2)}, u32[]{:S(2)}) collective-permute-start(bf16[1,144,1152]{2,1,0:T(8,128)(2,1)S(1)} %shard_map.140.refs_0_), channel_id=1, source_target_pairs={{0,8},{4,20},{8,0},{12,28},{16,24},{20,4},{24,16},{28,12},{1,9},{5... | collective-permute-start | bytes 995336 | tf_op jit(solution)/shard_map/ppermute | solution.py:302
  12.5 0.6 shard_map.138.refs_0_
  13.1 0.0 copy-start.6
  13.1 0.0 copy-start.7
  13.1 0.0 copy-start.8
  13.1 5.0 %collective-permute-done.6.refs_1_ = bf16[1,144,1152]{2,1,0:T(8,128)(2,1)S(1)} collective-permute-done((bf16[1,144,1152]{2,1,0:T(8,128)(2,1)S(1)}, bf16[1,144,1152]{2,1,0:T(8,128)(2,1)S(1)}, u32[]{:S(2)}, u32[]{:S(2)}) %collective-permute-start.6) | collective-permute-done | bytes 331808 | tf_op jit(solution)/shard_map/ppermute | solution.py:302
  18.2 1.6 %collective-permute-start.7 = (bf16[2,144,1152]{2,1,0:T(8,128)(2,1)S(1)}, bf16[2,144,1152]{2,1,0:T(8,128)(2,1)S(1)}, u32[]{:S(2)}, u32[]{:S(2)}) collective-permute-start(bf16[2,144,1152]{2,1,0:T(8,128)(2,1)S(1)} %shard_map.141.refs_0_), channel_id=1, source_target_pairs={{0,16},{4,12},{8,24},{12,4},{16,0},{20,28},{24,8},{28,20},{1,17},{... | collective-permute-start | bytes 1990664 | tf_op jit(solution)/shard_map/ppermute | solution.py:302
  19.8 1.9 %shard_map.135 = (bf16[160,1152]{1,0:T(8,128)(2,1)S(1)}, f32[16,160,160]{2,1,0:T(8,128)S(1)}) custom-call(bf16[160,1152]{1,0:T(8,128)(2,1)S(1)} %bitcast.31, bf16[160,1152]{1,0:T(8,128)(2,1)S(1)} %bitcast.34, bf16[160,1152]{1,0:T(8,128)(2,1)S(1)} %bitcast.37), custom_call_target="tpu_custom_call" | custom-call | flops 20000000000 | bytes 10 | tf_op jit(solution)/shard_map/pallas_call | solution.py:274
  21.7 0.6 shard_map.136
  22.3 1.9 %collective-permute-start = (bf16[2,40,1152]{2,1,0:T(8,128)(2,1)S(1)}, bf16[2,40,1152]{2,1,0:T(8,128)(2,1)S(1)}, u32[]{:S(2)}, u32[]{:S(2)}) collective-permute-start(bf16[2,40,1152]{2,1,0:T(8,128)(2,1)S(1)} %get-tuple-element.66), channel_id=1, source_target_pairs={{0,1},{1,0},{2,3},{3,2},{4,5},{5,4},{6,7},{7,6},{8,9},{9,8},{10,11... | collective-permute-start | bytes 552968 | tf_op jit(solution)/shard_map/ppermute | solution.py:287
  24.2 4.8 %collective-permute-done.7.refs_1_ = bf16[2,144,1152]{2,1,0:T(8,128)(2,1)S(1)} collective-permute-done((bf16[2,144,1152]{2,1,0:T(8,128)(2,1)S(1)}, bf16[2,144,1152]{2,1,0:T(8,128)(2,1)S(1)}, u32[]{:S(2)}, u32[]{:S(2)}) %collective-permute-start.7) | collective-permute-done | bytes 663584 | tf_op jit(solution)/shard_map/ppermute | solution.py:302
  29.0 2.8 %collective-permute-start.1 = (bf16[2,40,1152]{2,1,0:T(8,128)(2,1)S(1)}, bf16[2,40,1152]{2,1,0:T(8,128)(2,1)S(1)}, u32[]{:S(2)}, u32[]{:S(2)}) collective-permute-start(bf16[2,40,1152]{2,1,0:T(8,128)(2,1)S(1)} %get-tuple-element.67), channel_id=1, source_target_pairs={{0,2},{1,3},{2,0},{3,1},{4,6},{5,7},{6,4},{7,5},{8,10},{9,11},{10,... | collective-permute-start | bytes 552968 | tf_op jit(solution)/shard_map/ppermute | solution.py:287
  31.8 0.1 shard_map.142.mine_ref
  31.9 1.4 %collective-permute-start.2 = (bf16[2,40,1152]{2,1,0:T(8,128)(2,1)S(1)}, bf16[2,40,1152]{2,1,0:T(8,128)(2,1)S(1)}, u32[]{:S(2)}, u32[]{:S(2)}) collective-permute-start(bf16[2,40,1152]{2,1,0:T(8,128)(2,1)S(1)} %get-tuple-element.68), channel_id=1, source_target_pairs={{0,3},{1,2},{2,1},{3,0},{4,7},{5,6},{6,5},{7,4},{8,11},{9,10},{10,... | collective-permute-start | bytes 552968 | tf_op jit(solution)/shard_map/ppermute | solution.py:287
  33.3 0.0 collective-permute-done.5.refs_3_
  33.3 0.0 collective-permute-start.8
  33.3 0.0 collective-permute-done.3.refs_1_
  33.3 2.0 %shard_map.139 = (f32[16,160,160]{2,1,0:T(8,128)S(1)}, bf16[3,160,1152]{2,1,0:T(8,128)(2,1)S(1)}, f32[160,1152]{1,0:T(8,128)S(1)}) custom-call(bf16[3,40,1152]{2,1,0:T(8,128)(2,1)S(1)} %shard_map.138.refs_0_, bf16[3,40,1152]{2,1,0:T(8,128)(2,1)S(1)} %collective-permute-done.3.refs_1_, bf16[3,40,1152]{2,1,0:T(8,128)(2,1)S(1)} %collective-permute-done.4.refs_2_, ...), custom_call_target="tpu_custom_call" | custom-call | flops 20000000000 | bytes 10 | tf_op jit(solution)/shard_map/pallas_call | solution.py:274
  35.3 1.1 %collective-permute-done.8.other_ref = bf16[4,144,1152]{2,1,0:T(8,128)(2,1)S(1)} collective-permute-done((bf16[4,144,1152]{2,1,0:T(8,128)(2,1)S(1)}, bf16[4,144,1152]{2,1,0:T(8,128)(2,1)S(1)}, u32[]{:S(2)}, u32[]{:S(2)}) %collective-permute-start.8) | collective-permute-done | bytes 1327136 | tf_op jit(solution)/shard_map/ppermute | solution.py:287
  36.3 0.7 shard_map.143
  37.1 8.4 %collective-permute-done.1.refs_2_ = bf16[2,40,1152]{2,1,0:T(8,128)(2,1)S(1)} collective-permute-done((bf16[2,40,1152]{2,1,0:T(8,128)(2,1)S(1)}, bf16[2,40,1152]{2,1,0:T(8,128)(2,1)S(1)}, u32[]{:S(2)}, u32[]{:S(2)}) %collective-permute-start.1) | collective-permute-done | bytes 184352 | tf_op jit(solution)/shard_map/ppermute | solution.py:287
  45.5 1.6 %shard_map.144 = (bf16[2,160,1152]{2,1,0:T(8,128)(2,1)S(1)}, bf16[160,1152]{1,0:T(8,128)(2,1)S(1)}, bf16[1,40,1152]{2,1,0:T(8,128)(2,1)S(1)}, bf16[1,40,1152]{2,...) custom-call(bf16[2,40,1152]{2,1,0:T(8,128)(2,1)S(1)} %get-tuple-element.65.refs_0_, ...), custom_call_target="tpu_custom_call" | custom-call | flops 20000000000 | bytes 10 | tf_op jit(solution)/shard_map/pallas_call | solution.py:274
  47.1 0.1 collective-permute-start.9
  47.1 2.9 %collective-permute-start.12 = (bf16[1,40,1152]{2,1,0:T(8,128)(2,1)S(1)}, bf16[1,40,1152]{2,1,0:T(8,128)(2,1)S(1)}, u32[]{:S(2)}, u32[]{:S(2)}) collective-permute-start(bf16[1,40,1152]{2,1,0:T(8,128)(2,1)S(1)} %get-tuple-element.86), channel_id=1, source_target_pairs={{0,3},{1,2},{2,1},{3,0},{4,7},{5,6},{6,5},{7,4},{8,11},{9,10},{10,... | collective-permute-start | bytes 276488 | tf_op jit(solution)/shard_map/ppermute | solution.py:287
  50.0 1.8 %shard_map.145 = (f32[2,4,72,640]{3,2,1,0:T(8,128)S(1)}, bf16[2,4,72,640]{3,2,1,0:T(8,128)(2,1)S(1)}) custom-call(s32[2]{0:T(128)S(1)} %pad_add_fusion.where_ref, bf16[2,160,1152]{2,1,0:T(8,128)(2,1)S(1)} %get-tuple-element.79.mine_ref, bf16[2,160,1152]{2,1,0:T(8,128)(2,1)S(1)} %collective-permute-done.9.other_ref), custom_call_target="tpu_custom_call" | custom-call | flops 20000000000 | bytes 10 | tf_op jit(solution)/shard_map/pallas_call | solution.py:274
  51.9 1.6 %collective-permute-start.13 = (bf16[2,4,72,640]{3,2,1,0:T(8,128)(2,1)S(1)}, bf16[2,4,72,640]{3,2,1,0:T(8,128)(2,1)S(1)}, u32[]{:S(2)}, u32[]{:S(2)}) collective-permute-start(bf16[2,4,72,640]{3,2,1,0:T(8,128)(2,1)S(1)} %get-tuple-element.80), channel_id=1, source_target_pairs={{0,8},{4,20},{8,0},{12,28},{16,24},{20,4},{24,16},{28,12},{1,9},{5... | collective-permute-start | bytes 2211848 | tf_op jit(solution)/shard_map/ppermute | solution.py:302
  53.4 3.5 %collective-permute-start.10 = (bf16[1,40,1152]{2,1,0:T(8,128)(2,1)S(1)}, bf16[1,40,1152]{2,1,0:T(8,128)(2,1)S(1)}, u32[]{:S(2)}, u32[]{:S(2)}) collective-permute-start(bf16[1,40,1152]{2,1,0:T(8,128)(2,1)S(1)} %get-tuple-element.83), channel_id=1, source_target_pairs={{0,1},{1,0},{2,3},{3,2},{4,5},{5,4},{6,7},{7,6},{8,9},{9,8},{10,11... | collective-permute-start | bytes 276488 | tf_op jit(solution)/shard_map/ppermute | solution.py:287
  56.9 1.6 %collective-permute-start.11 = (bf16[1,40,1152]{2,1,0:T(8,128)(2,1)S(1)}, bf16[1,40,1152]{2,1,0:T(8,128)(2,1)S(1)}, u32[]{:S(2)}, u32[]{:S(2)}) collective-permute-start(bf16[1,40,1152]{2,1,0:T(8,128)(2,1)S(1)} %get-tuple-element.85), channel_id=1, source_target_pairs={{0,2},{1,3},{2,0},{3,1},{4,6},{5,7},{6,4},{7,5},{8,10},{9,11},{10,... | collective-permute-start | bytes 276488 | tf_op jit(solution)/shard_map/ppermute | solution.py:287
  58.5 4.3 %shard_map.147 = (bf16[3,40,1152]{2,1,0:T(8,128)(2,1)S(1)}, bf16[3,40,1152]{2,1,0:T(8,128)(2,1)S(1)}, bf16[3,40,1152]{2,1,0:T(8,128)(2,1)S(1)}, bf16[3,40,1152]{2,1,0:T(8,128)(2,1)S(1)}) custom-call(bf16[160,1152]{1,0:T(8,128)(2,1)S(1)} %get-tuple-element.88.step_ref, bf16[3,160,1152]{2,1,0:T(8,128)(2,1)S(1)} %get-tuple-element.89.qkv_ref, ...), custom_call_target="tpu_custom_call" | custom-call | flops 20000000000 | bytes 10 | tf_op jit(solution)/shard_map/pallas_call | solution.py:274
  62.9 0.5 collective-permute-done.11.refs_2_
  63.4 0.0 collective-permute-done.13.came_ref
  63.4 0.1 shard_map.148
  63.5 1.6 %collective-permute-start.14 = (bf16[1,4,72,640]{3,2,1,0:T(8,128)(2,1)S(1)}, bf16[1,4,72,640]{3,2,1,0:T(8,128)(2,1)S(1)}, u32[]{:S(2)}, u32[]{:S(2)}) collective-permute-start(bf16[1,4,72,640]{3,2,1,0:T(8,128)(2,1)S(1)} %get-tuple-element.94), channel_id=1, source_target_pairs={{0,16},{4,12},{8,24},{12,4},{16,0},{20,28},{24,8},{28,20},{1,17},{... | collective-permute-start | bytes 1105928 | tf_op jit(solution)/shard_map/ppermute | solution.py:302
  65.1 2.5 %collective-permute-start.16 = (bf16[3,40,1152]{2,1,0:T(8,128)(2,1)S(1)}, bf16[3,40,1152]{2,1,0:T(8,128)(2,1)S(1)}, u32[]{:S(2)}, u32[]{:S(2)}) collective-permute-start(bf16[3,40,1152]{2,1,0:T(8,128)(2,1)S(1)} %get-tuple-element.102), channel_id=1, source_target_pairs={{0,3},{1,2},{2,1},{3,0},{4,7},{5,6},{6,5},{7,4},{8,11},{9,10},{10,... | collective-permute-start | bytes 829448 | tf_op jit(solution)/shard_map/ppermute | solution.py:287
  67.6 3.5 %collective-permute-done.14.came_ref = bf16[1,4,72,640]{3,2,1,0:T(8,128)(2,1)S(1)} collective-permute-done((bf16[1,4,72,640]{3,2,1,0:T(8,128)(2,1)S(1)}, bf16[1,4,72,640]{3,2,1,0:T(8,128)(2,1)S(1)}, u32[]{:S(2)}, u32[]{:S(2)}) %collective-permute-start.14) | collective-permute-done | bytes 368672 | tf_op jit(solution)/shard_map/ppermute | solution.py:302
  71.1 0.7 shard_map.149
  71.8 3.6 %collective-permute-start.15 = (bf16[2,72,640]{2,1,0:T(8,128)(2,1)S(1)}, bf16[2,72,640]{2,1,0:T(8,128)(2,1)S(1)}, u32[]{:S(2)}, u32[]{:S(2)}) collective-permute-start(bf16[2,72,640]{2,1,0:T(8,128)(2,1)S(1)} %get-tuple-element.100), channel_id=1, source_target_pairs={{0,1},{1,0},{2,3},{3,2},{4,5},{5,4},{6,7},{7,6},{8,9},{9,8},{10,11... | collective-permute-start | bytes 552968 | tf_op jit(solution)/shard_map/ppermute | solution.py:287
  75.3 0.6 shard_map.146
  75.9 3.0 %shard_map.150 = (f32[160,1152]{1,0:T(8,128)S(1)}, f32[160,1152]{1,0:T(8,128)S(1)}, f32[160,1152]{1,0:T(8,128)S(1)}) custom-call(bf16[160,1152]{1,0:T(8,128)(2,1)S(1)} %bitcast.32, bf16[160,1152]{1,0:T(8,128)(2,1)S(1)} %bitcast.35, bf16[160,1152]{1,0:T(8,128)(2,1)S(1)} %bitcast.38, bf16[160,1152]{1,0:T(8,128)(2,1)S(1)} %bitcast.21, ...), custom_call_target="tpu_custom_call" | custom-call | flops 10 | bytes 10 | tf_op jit(solution)/shard_map/pallas_call | solution.py:274
  78.9 0.2 collective-permute-done.15.came_ref
  79.2 3.4 %collective-permute-start.17 = (bf16[1,72,640]{2,1,0:T(8,128)(2,1)S(1)}, bf16[1,72,640]{2,1,0:T(8,128)(2,1)S(1)}, u32[]{:S(2)}, u32[]{:S(2)}) collective-permute-start(bf16[1,72,640]{2,1,0:T(8,128)(2,1)S(1)} %get-tuple-element.104), channel_id=1, source_target_pairs={{0,2},{1,3},{2,0},{3,1},{4,6},{5,7},{6,4},{7,5},{8,10},{9,11},{10,... | collective-permute-start | bytes 276488 | tf_op jit(solution)/shard_map/ppermute | solution.py:287
  82.6 0.8 collective-permute-start.18
  83.3 0.6 collective-permute-start.19
  83.9 1.8 %collective-permute-done.17.came_ref = bf16[1,72,640]{2,1,0:T(8,128)(2,1)S(1)} collective-permute-done((bf16[1,72,640]{2,1,0:T(8,128)(2,1)S(1)}, bf16[1,72,640]{2,1,0:T(8,128)(2,1)S(1)}, u32[]{:S(2)}, u32[]{:S(2)}) %collective-permute-start.17) | collective-permute-done | bytes 92192 | tf_op jit(solution)/shard_map/ppermute | solution.py:287
  85.7 3.9 %collective-permute-start.20 = (bf16[1,72,640]{2,1,0:T(8,128)(2,1)S(1)}, bf16[1,72,640]{2,1,0:T(8,128)(2,1)S(1)}, u32[]{:S(2)}, u32[]{:S(2)}) collective-permute-start(bf16[1,72,640]{2,1,0:T(8,128)(2,1)S(1)} %shard_map.152.refs_0_), channel_id=1, source_target_pairs={{0,8},{4,20},{8,0},{12,28},{16,24},{20,4},{24,16},{28,12},{1,9},{5... | collective-permute-start | bytes 276488 | tf_op jit(solution)/shard_map/ppermute | solution.py:302
  89.6 1.4 %shard_map.154 = (bf16[4,40,1152]{2,1,0:T(8,128)(2,1)}, bf16[4,40,1152]{2,1,0:T(8,128)(2,1)}, bf16[4,40,1152]{2,1,0:T(8,128)(2,1)}) custom-call(s32[2]{0:T(128)S(1)} %pad_add_fusion.where_ref, bf16[3,40,1152]{2,1,0:T(8,128)(2,1)S(1)} %get-tuple-element.91.refs_0_, bf16[3,40,1152]{2,1,0:T(8,128)(2,1)S(1)} %collective-permute-done.16.refs_1_), custom_call_target="tpu_custom_call" | custom-call | flops 20000000000 | bytes 10 | tf_op jit(solution)/shard_map/pallas_call | solution.py:255
  91.0 1.1 %collective-permute-done.20.refs_1_ = bf16[1,72,640]{2,1,0:T(8,128)(2,1)S(1)} collective-permute-done((bf16[1,72,640]{2,1,0:T(8,128)(2,1)S(1)}, bf16[1,72,640]{2,1,0:T(8,128)(2,1)S(1)}, u32[]{:S(2)}, u32[]{:S(2)}) %collective-permute-start.20) | collective-permute-done | bytes 92192 | tf_op jit(solution)/shard_map/ppermute | solution.py:302
  92.1 2.1 %collective-permute-start.21 = (bf16[2,72,640]{2,1,0:T(8,128)(2,1)S(1)}, bf16[2,72,640]{2,1,0:T(8,128)(2,1)S(1)}, u32[]{:S(2)}, u32[]{:S(2)}) collective-permute-start(bf16[2,72,640]{2,1,0:T(8,128)(2,1)S(1)} %shard_map.156.refs_0_), channel_id=1, source_target_pairs={{0,16},{4,12},{8,24},{12,4},{16,0},{20,28},{24,8},{28,20},{1,17},{... | collective-permute-start | bytes 552968 | tf_op jit(solution)/shard_map/ppermute | solution.py:302
  94.3 2.8 %shard_map.153 = (bf16[160,1152]{1,0:T(8,128)(2,1)}, bf16[160,1152]{1,0:T(8,128)(2,1)}, bf16[160,1152]{1,0:T(8,128)(2,1)}) custom-call(bf16[160,1152]{1,0:T(8,128)(2,1)S(1)} %bitcast.33, bf16[160,1152]{1,0:T(8,128)(2,1)S(1)} %bitcast.36, bf16[160,1152]{1,0:T(8,128)(2,1)S(1)} %bitcast.39, bf16[160,1152]{1,0:T(8,128)(2,1)S(1)} %bitcast.22, ...), custom_call_target="tpu_custom_call" | custom-call | flops 20000000000 | bytes 10 | tf_op jit(solution)/shard_map/pallas_call | solution.py:274
  97.1 0.7 collective-permute-done.21.refs_1_
  97.8 0.1 collective-permute-start.22
  97.9 0.0 collective-permute-done.19.refs_1_
  97.9 1.4 %shard_map.155 = (bf16[4,40,1152]{2,1,0:T(8,128)(2,1)}, bf16[4,40,1152]{2,1,0:T(8,128)(2,1)}, bf16[4,40,1152]{2,1,0:T(8,128)(2,1)}) custom-call(s32[2]{0:T(128)S(1)} %pad_add_fusion.where_ref, bf16[3,40,1152]{2,1,0:T(8,128)(2,1)S(1)} %collective-permute-done.18.refs_0_, ...), custom_call_target="tpu_custom_call", output_to_operand_aliasing={{0}: (3, {}), {1}: (4, {}), {2}: (5, {})} | custom-call | flops 20000000000 | bytes 10 | tf_op jit(solution)/shard_map/pallas_call | solution.py:255
  99.3 0.2 collective-permute-done.22.other_ref
  99.6 1.8 %shard_map.158 = f32[4,72,1152]{2,1,0:T(8,128)} custom-call(s32[2]{0:T(128)S(1)} %pad_add_fusion.where_ref, bf16[4,72,640]{2,1,0:T(8,128)(2,1)S(1)} %shard_map.157.mine_ref, bf16[4,72,640]{2,1,0:T(8,128)(2,1)S(1)} %collective-permute-done.22.other_ref), custom_call_target="tpu_custom_call" | custom-call | flops 10 | bytes 10 | tf_op jit(solution)/shard_map/pallas_call | solution.py:274
  (27 shorter events, 0.2 us)
Async XLA Ops:
  0.7 1.0 copy-start.1
  1.7 1.0 copy-start.3
  2.7 1.0 copy-start.5
  4.3 27.6 %collective-permute-start.4 = (bf16[3,40,1152]{2,1,0:T(8,128)(2,1)S(1)}, bf16[3,40,1152]{2,1,0:T(8,128)(2,1)S(1)}, u32[]{:S(2)}, u32[]{:S(2)}) collective-permute-start(bf16[3,40,1152]{2,1,0:T(8,128)(2,1)S(1)} %get-tuple-element.72), channel_id=1, source_target_pairs={{0,2},{1,3},{2,0},{3,1},{4,6},{5,7},{6,4},{7,5},{8,10},{9,11},{10,... | collective-permute-start | bytes 829448 | tf_op jit(solution)/shard_map/ppermute | solution.py:287
  8.4 24.9 %collective-permute-start.5 = (bf16[3,40,1152]{2,1,0:T(8,128)(2,1)S(1)}, bf16[3,40,1152]{2,1,0:T(8,128)(2,1)S(1)}, u32[]{:S(2)}, u32[]{:S(2)}) collective-permute-start(bf16[3,40,1152]{2,1,0:T(8,128)(2,1)S(1)} %get-tuple-element.73), channel_id=1, source_target_pairs={{0,3},{1,2},{2,1},{3,0},{4,7},{5,6},{6,5},{7,4},{8,11},{9,10},{10,... | collective-permute-start | bytes 829448 | tf_op jit(solution)/shard_map/ppermute | solution.py:287
  9.7 23.6 %collective-permute-start.3 = (bf16[3,40,1152]{2,1,0:T(8,128)(2,1)S(1)}, bf16[3,40,1152]{2,1,0:T(8,128)(2,1)S(1)}, u32[]{:S(2)}, u32[]{:S(2)}) collective-permute-start(bf16[3,40,1152]{2,1,0:T(8,128)(2,1)S(1)} %get-tuple-element.69), channel_id=1, source_target_pairs={{0,1},{1,0},{2,3},{3,2},{4,5},{5,4},{6,7},{7,6},{8,9},{9,8},{10,11... | collective-permute-start | bytes 829448 | tf_op jit(solution)/shard_map/ppermute | solution.py:287
  10.0 1.0 copy-start.9
  10.9 1.6 %copy-start.2 = (bf16[1,160,1152]{2,1,0:T(8,128)(2,1)S(1)}, bf16[1,160,1152]{2,1,0:T(8,128)(2,1)}, u32[]{:S(2)}) copy-start(bf16[1,160,1152]{2,1,0:T(8,128)(2,1)} %param.11) | copy-start | bytes 1105924
  10.9 1.6 %copy-start.4 = (bf16[1,160,1152]{2,1,0:T(8,128)(2,1)S(1)}, bf16[1,160,1152]{2,1,0:T(8,128)(2,1)}, u32[]{:S(2)}) copy-start(bf16[1,160,1152]{2,1,0:T(8,128)(2,1)} %param.12) | copy-start | bytes 1105924
  11.0 7.2 %collective-permute-start.6 = (bf16[1,144,1152]{2,1,0:T(8,128)(2,1)S(1)}, bf16[1,144,1152]{2,1,0:T(8,128)(2,1)S(1)}, u32[]{:S(2)}, u32[]{:S(2)}) collective-permute-start(bf16[1,144,1152]{2,1,0:T(8,128)(2,1)S(1)} %shard_map.140.refs_0_), channel_id=1, source_target_pairs={{0,8},{4,20},{8,0},{12,28},{16,24},{20,4},{24,16},{28,12},{1,9},{5... | collective-permute-start | bytes 995336 | tf_op jit(solution)/shard_map/ppermute | solution.py:302
  13.1 6.7 %copy-start.6 = (bf16[1,160,1152]{2,1,0:T(8,128)(2,1)S(1)}, bf16[1,160,1152]{2,1,0:T(8,128)(2,1)}, u32[]{:S(2)}) copy-start(bf16[1,160,1152]{2,1,0:T(8,128)(2,1)} %param.8) | copy-start | bytes 1105924
  13.1 6.7 %copy-start.7 = (bf16[1,160,1152]{2,1,0:T(8,128)(2,1)S(1)}, bf16[1,160,1152]{2,1,0:T(8,128)(2,1)}, u32[]{:S(2)}) copy-start(bf16[1,160,1152]{2,1,0:T(8,128)(2,1)} %param.9) | copy-start | bytes 1105924
  13.1 6.7 %copy-start.8 = (bf16[1,160,1152]{2,1,0:T(8,128)(2,1)S(1)}, bf16[1,160,1152]{2,1,0:T(8,128)(2,1)}, u32[]{:S(2)}) copy-start(bf16[1,160,1152]{2,1,0:T(8,128)(2,1)} %param.10) | copy-start | bytes 1105924
  18.2 10.7 %collective-permute-start.7 = (bf16[2,144,1152]{2,1,0:T(8,128)(2,1)S(1)}, bf16[2,144,1152]{2,1,0:T(8,128)(2,1)S(1)}, u32[]{:S(2)}, u32[]{:S(2)}) collective-permute-start(bf16[2,144,1152]{2,1,0:T(8,128)(2,1)S(1)} %shard_map.141.refs_0_), channel_id=1, source_target_pairs={{0,16},{4,12},{8,24},{12,4},{16,0},{20,28},{24,8},{28,20},{1,17},{... | collective-permute-start | bytes 1990664 | tf_op jit(solution)/shard_map/ppermute | solution.py:302
  19.8 1.9 %copy-start = (bf16[1,160,1152]{2,1,0:T(8,128)(2,1)S(1)}, bf16[1,160,1152]{2,1,0:T(8,128)(2,1)}, u32[]{:S(2)}) copy-start(bf16[1,160,1152]{2,1,0:T(8,128)(2,1)} %param.15) | copy-start | bytes 1105924
  22.3 14.8 %collective-permute-start = (bf16[2,40,1152]{2,1,0:T(8,128)(2,1)S(1)}, bf16[2,40,1152]{2,1,0:T(8,128)(2,1)S(1)}, u32[]{:S(2)}, u32[]{:S(2)}) collective-permute-start(bf16[2,40,1152]{2,1,0:T(8,128)(2,1)S(1)} %get-tuple-element.66), channel_id=1, source_target_pairs={{0,1},{1,0},{2,3},{3,2},{4,5},{5,4},{6,7},{7,6},{8,9},{9,8},{10,11... | collective-permute-start | bytes 552968 | tf_op jit(solution)/shard_map/ppermute | solution.py:287
  29.0 16.5 %collective-permute-start.1 = (bf16[2,40,1152]{2,1,0:T(8,128)(2,1)S(1)}, bf16[2,40,1152]{2,1,0:T(8,128)(2,1)S(1)}, u32[]{:S(2)}, u32[]{:S(2)}) collective-permute-start(bf16[2,40,1152]{2,1,0:T(8,128)(2,1)S(1)} %get-tuple-element.67), channel_id=1, source_target_pairs={{0,2},{1,3},{2,0},{3,1},{4,6},{5,7},{6,4},{7,5},{8,10},{9,11},{10,... | collective-permute-start | bytes 552968 | tf_op jit(solution)/shard_map/ppermute | solution.py:287
  31.9 13.6 %collective-permute-start.2 = (bf16[2,40,1152]{2,1,0:T(8,128)(2,1)S(1)}, bf16[2,40,1152]{2,1,0:T(8,128)(2,1)S(1)}, u32[]{:S(2)}, u32[]{:S(2)}) collective-permute-start(bf16[2,40,1152]{2,1,0:T(8,128)(2,1)S(1)} %get-tuple-element.68), channel_id=1, source_target_pairs={{0,3},{1,2},{2,1},{3,0},{4,7},{5,6},{6,5},{7,4},{8,11},{9,10},{10,... | collective-permute-start | bytes 552968 | tf_op jit(solution)/shard_map/ppermute | solution.py:287
  33.3 3.1 %collective-permute-start.8 = (bf16[4,144,1152]{2,1,0:T(8,128)(2,1)S(1)}, bf16[4,144,1152]{2,1,0:T(8,128)(2,1)S(1)}, u32[]{:S(2)}, u32[]{:S(2)}) collective-permute-start(bf16[4,144,1152]{2,1,0:T(8,128)(2,1)S(1)} %shard_map.142.mine_ref), channel_id=1, source_target_pairs={{0,4},{4,0},{8,12},{12,8},{16,20},{20,16},{24,28},{28,24},{1,5},{5... | collective-permute-start | bytes 3981320 | tf_op jit(solution)/shard_map/ppermute | solution.py:287
  47.1 3.0 %collective-permute-start.9 = (bf16[2,160,1152]{2,1,0:T(8,128)(2,1)S(1)}, bf16[2,160,1152]{2,1,0:T(8,128)(2,1)S(1)}, u32[]{:S(2)}, u32[]{:S(2)}) collective-permute-start(bf16[2,160,1152]{2,1,0:T(8,128)(2,1)S(1)} %get-tuple-element.79.mine_ref), channel_id=1, source_target_pairs={{0,4},{4,0},{8,12},{12,8},{16,20},{20,16},{24,28},{28,24},{1,5},{5... | collective-permute-start | bytes 2211848 | tf_op jit(solution)/shard_map/ppermute | solution.py:287
  47.1 15.7 %collective-permute-start.12 = (bf16[1,40,1152]{2,1,0:T(8,128)(2,1)S(1)}, bf16[1,40,1152]{2,1,0:T(8,128)(2,1)S(1)}, u32[]{:S(2)}, u32[]{:S(2)}) collective-permute-start(bf16[1,40,1152]{2,1,0:T(8,128)(2,1)S(1)} %get-tuple-element.86), channel_id=1, source_target_pairs={{0,3},{1,2},{2,1},{3,0},{4,7},{5,6},{6,5},{7,4},{8,11},{9,10},{10,... | collective-permute-start | bytes 276488 | tf_op jit(solution)/shard_map/ppermute | solution.py:287
  51.9 11.5 %collective-permute-start.13 = (bf16[2,4,72,640]{3,2,1,0:T(8,128)(2,1)S(1)}, bf16[2,4,72,640]{3,2,1,0:T(8,128)(2,1)S(1)}, u32[]{:S(2)}, u32[]{:S(2)}) collective-permute-start(bf16[2,4,72,640]{3,2,1,0:T(8,128)(2,1)S(1)} %get-tuple-element.80), channel_id=1, source_target_pairs={{0,8},{4,20},{8,0},{12,28},{16,24},{20,4},{24,16},{28,12},{1,9},{5... | collective-permute-start | bytes 2211848 | tf_op jit(solution)/shard_map/ppermute | solution.py:302
  53.4 9.5 %collective-permute-start.10 = (bf16[1,40,1152]{2,1,0:T(8,128)(2,1)S(1)}, bf16[1,40,1152]{2,1,0:T(8,128)(2,1)S(1)}, u32[]{:S(2)}, u32[]{:S(2)}) collective-permute-start(bf16[1,40,1152]{2,1,0:T(8,128)(2,1)S(1)} %get-tuple-element.83), channel_id=1, source_target_pairs={{0,1},{1,0},{2,3},{3,2},{4,5},{5,4},{6,7},{7,6},{8,9},{9,8},{10,11... | collective-permute-start | bytes 276488 | tf_op jit(solution)/shard_map/ppermute | solution.py:287
  56.9 6.4 %collective-permute-start.11 = (bf16[1,40,1152]{2,1,0:T(8,128)(2,1)S(1)}, bf16[1,40,1152]{2,1,0:T(8,128)(2,1)S(1)}, u32[]{:S(2)}, u32[]{:S(2)}) collective-permute-start(bf16[1,40,1152]{2,1,0:T(8,128)(2,1)S(1)} %get-tuple-element.85), channel_id=1, source_target_pairs={{0,2},{1,3},{2,0},{3,1},{4,6},{5,7},{6,4},{7,5},{8,10},{9,11},{10,... | collective-permute-start | bytes 276488 | tf_op jit(solution)/shard_map/ppermute | solution.py:287
  63.5 7.6 %collective-permute-start.14 = (bf16[1,4,72,640]{3,2,1,0:T(8,128)(2,1)S(1)}, bf16[1,4,72,640]{3,2,1,0:T(8,128)(2,1)S(1)}, u32[]{:S(2)}, u32[]{:S(2)}) collective-permute-start(bf16[1,4,72,640]{3,2,1,0:T(8,128)(2,1)S(1)} %get-tuple-element.94), channel_id=1, source_target_pairs={{0,16},{4,12},{8,24},{12,4},{16,0},{20,28},{24,8},{28,20},{1,17},{... | collective-permute-start | bytes 1105928 | tf_op jit(solution)/shard_map/ppermute | solution.py:302
  65.1 18.8 %collective-permute-start.16 = (bf16[3,40,1152]{2,1,0:T(8,128)(2,1)S(1)}, bf16[3,40,1152]{2,1,0:T(8,128)(2,1)S(1)}, u32[]{:S(2)}, u32[]{:S(2)}) collective-permute-start(bf16[3,40,1152]{2,1,0:T(8,128)(2,1)S(1)} %get-tuple-element.102), channel_id=1, source_target_pairs={{0,3},{1,2},{2,1},{3,0},{4,7},{5,6},{6,5},{7,4},{8,11},{9,10},{10,... | collective-permute-start | bytes 829448 | tf_op jit(solution)/shard_map/ppermute | solution.py:287
  71.8 7.3 %collective-permute-start.15 = (bf16[2,72,640]{2,1,0:T(8,128)(2,1)S(1)}, bf16[2,72,640]{2,1,0:T(8,128)(2,1)S(1)}, u32[]{:S(2)}, u32[]{:S(2)}) collective-permute-start(bf16[2,72,640]{2,1,0:T(8,128)(2,1)S(1)} %get-tuple-element.100), channel_id=1, source_target_pairs={{0,1},{1,0},{2,3},{3,2},{4,5},{5,4},{6,7},{7,6},{8,9},{9,8},{10,11... | collective-permute-start | bytes 552968 | tf_op jit(solution)/shard_map/ppermute | solution.py:287
  79.2 6.5 %collective-permute-start.17 = (bf16[1,72,640]{2,1,0:T(8,128)(2,1)S(1)}, bf16[1,72,640]{2,1,0:T(8,128)(2,1)S(1)}, u32[]{:S(2)}, u32[]{:S(2)}) collective-permute-start(bf16[1,72,640]{2,1,0:T(8,128)(2,1)S(1)} %get-tuple-element.104), channel_id=1, source_target_pairs={{0,2},{1,3},{2,0},{3,1},{4,6},{5,7},{6,4},{7,5},{8,10},{9,11},{10,... | collective-permute-start | bytes 276488 | tf_op jit(solution)/shard_map/ppermute | solution.py:287
  82.6 15.3 %collective-permute-start.18 = (bf16[3,40,1152]{2,1,0:T(8,128)(2,1)S(1)}, bf16[3,40,1152]{2,1,0:T(8,128)(2,1)S(1)}, u32[]{:S(2)}, u32[]{:S(2)}) collective-permute-start(bf16[3,40,1152]{2,1,0:T(8,128)(2,1)S(1)} %get-tuple-element.111), channel_id=1, source_target_pairs={{0,1},{1,0},{2,3},{3,2},{4,5},{5,4},{6,7},{7,6},{8,9},{9,8},{10,11... | collective-permute-start | bytes 829448 | tf_op jit(solution)/shard_map/ppermute | solution.py:287
  83.3 14.6 %collective-permute-start.19 = (bf16[3,40,1152]{2,1,0:T(8,128)(2,1)S(1)}, bf16[3,40,1152]{2,1,0:T(8,128)(2,1)S(1)}, u32[]{:S(2)}, u32[]{:S(2)}) collective-permute-start(bf16[3,40,1152]{2,1,0:T(8,128)(2,1)S(1)} %get-tuple-element.112), channel_id=1, source_target_pairs={{0,2},{1,3},{2,0},{3,1},{4,6},{5,7},{6,4},{7,5},{8,10},{9,11},{10,... | collective-permute-start | bytes 829448 | tf_op jit(solution)/shard_map/ppermute | solution.py:287
  85.7 6.4 %collective-permute-start.20 = (bf16[1,72,640]{2,1,0:T(8,128)(2,1)S(1)}, bf16[1,72,640]{2,1,0:T(8,128)(2,1)S(1)}, u32[]{:S(2)}, u32[]{:S(2)}) collective-permute-start(bf16[1,72,640]{2,1,0:T(8,128)(2,1)S(1)} %shard_map.152.refs_0_), channel_id=1, source_target_pairs={{0,8},{4,20},{8,0},{12,28},{16,24},{20,4},{24,16},{28,12},{1,9},{5... | collective-permute-start | bytes 276488 | tf_op jit(solution)/shard_map/ppermute | solution.py:302
  92.1 5.6 %collective-permute-start.21 = (bf16[2,72,640]{2,1,0:T(8,128)(2,1)S(1)}, bf16[2,72,640]{2,1,0:T(8,128)(2,1)S(1)}, u32[]{:S(2)}, u32[]{:S(2)}) collective-permute-start(bf16[2,72,640]{2,1,0:T(8,128)(2,1)S(1)} %shard_map.156.refs_0_), channel_id=1, source_target_pairs={{0,16},{4,12},{8,24},{12,4},{16,0},{20,28},{24,8},{28,20},{1,17},{... | collective-permute-start | bytes 552968 | tf_op jit(solution)/shard_map/ppermute | solution.py:302
  97.8 1.8 %collective-permute-start.22 = (bf16[4,72,640]{2,1,0:T(8,128)(2,1)S(1)}, bf16[4,72,640]{2,1,0:T(8,128)(2,1)S(1)}, u32[]{:S(2)}, u32[]{:S(2)}) collective-permute-start(bf16[4,72,640]{2,1,0:T(8,128)(2,1)S(1)} %shard_map.157.mine_ref), channel_id=1, source_target_pairs={{0,4},{4,0},{8,12},{12,8},{16,20},{20,16},{24,28},{28,24},{1,5},{5... | collective-permute-start | bytes 1105928 | tf_op jit(solution)/shard_map/ppermute | solution.py:287
